TPU v7x, 32 devices: a whole 2x2x4 slice. The times are simulated.
32 devices in a mesh: groups: 2 (over y), member: 4 (over x, core), shard: 4 (over z).
Axes of the slice: x: 2, y: 2, z: 4, core: 2. Of those that a mesh axis runs over, the one named last changes fastest.
Arguments:
- context: bfloat16 [8, 2048, 1024], P(('groups', 'member'), 'shard'), parts along dimension 0, may hold values from -6 to 6
- out_grad: bfloat16 [8, 2048, 1024], P(('groups', 'member'), 'shard'), parts along dimension 0, may hold values from -4 to 4
- weight: float32 [8, 1024, 1024], P(('groups', 'member'), 'shard'), parts along dimension 0, may hold values from -5 to 5
- first: float32 [8, 1024, 1024], P(('groups', 'member'), 'shard'), parts along dimension 0, may hold values from -3 to 3
- second: float32 [8, 1024, 1024], P(('groups', 'member'), 'shard'), parts along dimension 0, may hold values from 0.05 to 2
- rates: float32 [8], P('groups'), parts along dimension 0, may hold values from 0.01 to 0.1
- decays: float32 [8], P('groups'), parts along dimension 0, may hold values from 0.1 to 1
- steps: int32 [8], P('groups'), parts along dimension 0, may hold values from 10 to 3000
- donor: int32 [8], P('groups'), parts along dimension 0, may hold values from -1 to 3, as said below
Outputs:
- context_grad: bfloat16 [8, 2048, 1024], P(('groups', 'member'), 'shard'), parts along dimension 0
- new_weight: float32 [8, 1024, 1024], P(('groups', 'member'), 'shard'), parts along dimension 0
- new_first: float32 [8, 1024, 1024], P(('groups', 'member'), 'shard'), parts along dimension 0
- new_second: float32 [8, 1024, 1024], P(('groups', 'member'), 'shard'), parts along dimension 0
There are 2 independent parts, one for each index of `groups`. A program takes and returns all parts, laid end to end along the dimension named above; each array names one. Nothing has to cross between parts.
Inputs may be any that keep to these rules, and one draw needn't show every extreme that they name: Exactly 2 entries are not -1; each of those names a member whose own entry is -1. Member 4 - 1 is always some loser's donor.
All inputs are finite; a program needn't handle non-finite values.
Results may differ from a plain program's by a relative error of at most 0.0049.
Values may be sent and summed in bfloat16 or wider, within the bound.
No kernel may reach another device: no remote copies, remote signals or barrier semaphores. Data moves between devices by JAX's collectives and lax.ppermute only.
A program may use at most 64 MiB of HBM per device.

v0:
```python
import jax
import jax.numpy as jnp
from jax import lax
from jax.sharding import PartitionSpec as P

beta_one = 0.9
beta_two = 0.999
epsilon = 1e-08


def lookup(table, index):
    positions = jnp.arange(table.shape[0], dtype=jnp.int32)
    return jnp.sum(jnp.where(positions == index, table, jnp.zeros_like(table)))


def adam_update(weight_rows, first_rows, second_rows, grad_rows, rates, decays, steps, index):
    rate = lookup(rates, index)
    decay = lookup(decays, index)
    count = (lookup(steps, index) + 1).astype(jnp.float32)
    first_step = beta_one * first_rows + (1.0 - beta_one) * grad_rows
    second_step = beta_two * second_rows + (1.0 - beta_two) * grad_rows * grad_rows
    first_hat = first_step / (1.0 - jnp.power(beta_one, count))
    second_hat = second_step / (1.0 - jnp.power(beta_two, count))
    weight_step = weight_rows - rate * (
        first_hat / (jnp.sqrt(second_hat) + epsilon) + decay * weight_rows
    )
    return (weight_step, first_step, second_step)


def on_device(context, out_grad, weight, first, second, rates, decays, steps, donor):
    context_rows = context[0]
    cotangent = out_grad[0]
    width = context_rows.shape[1]
    scale = width ** (-0.5)
    member_index = lax.axis_index("member")
    own_donor = lookup(donor, member_index)
    source = jnp.where(own_donor >= 0, own_donor, member_index)
    half_weight = weight[0].astype(jnp.bfloat16)
    columns = lax.dot_general(
        cotangent,
        lax.all_gather(half_weight, "shard", axis=0, tiled=True),
        (((1,), (1,)), ((), ())),
        preferred_element_type=jnp.float32,
    )
    context_grad = (columns * scale).astype(jnp.bfloat16)[None]
    grad_rows = lax.psum_scatter(
        scale
        * lax.dot_general(
            context_rows, cotangent, (((0,), (0,)), ((), ())), preferred_element_type=jnp.float32
        ),
        "shard",
        scatter_dimension=0,
        tiled=True,
    )
    weight_step, first_step, second_step = adam_update(
        weight[0], first[0], second[0], grad_rows, rates, decays, steps, member_index
    )
    gathered = (
        lax.all_gather(weight_step[None], "member", axis=0, tiled=True),
        lax.all_gather(first_step[None], "member", axis=0, tiled=True),
        lax.all_gather(second_step[None], "member", axis=0, tiled=True),
    )
    weight_new = lax.dynamic_index_in_dim(gathered[0], source, 0, keepdims=False)
    first_new = lax.dynamic_index_in_dim(gathered[1], source, 0, keepdims=False)
    second_new = lax.dynamic_index_in_dim(gathered[2], source, 0, keepdims=False)
    return (context_grad, weight_new[None], first_new[None], second_new[None])


def solution(mesh):
    in_specs = (
        P(("groups", "member"), "shard", None),
        P(("groups", "member"), "shard", None),
        P(("groups", "member"), "shard", None),
        P(("groups", "member"), "shard", None),
        P(("groups", "member"), "shard", None),
        P("groups"),
        P("groups"),
        P("groups"),
        P("groups"),
    )
    out_specs = (
        P(("groups", "member"), "shard", None),
        P(("groups", "member"), "shard", None),
        P(("groups", "member"), "shard", None),
        P(("groups", "member"), "shard", None),
    )
    return jax.shard_map(
        on_device, mesh=mesh, in_specs=in_specs, out_specs=out_specs, check_vma=False
    )
```

profile of v0, /device:TPU:1, one launch (start us, length us, event | category | flops | bytes accessed | tf_op | source)
XLA Modules:
  0.0 258.5 jit_solution(9673098122536787532)
XLA Ops:
  7.2 0.0 copy-start
  7.2 0.0 copy-start.1
  7.2 0.0 reduce-scatter.2.cloned.1.call-start
  7.2 1.2 copy-done
  8.4 4.5 %convolution_multiply_fusion = f32[1024,1024]{1,0:T(8,128)} fusion(bf16[1,512,1024]{2,1,0:T(8,128)(2,1)} %param.9, bf16[1,512,1024]{2,1,0:T(8,128)(2,1)S(1)} %copy-done), kind=kOutput, calls=%fused_computation | convolution fusion | flops 1074790400 | bytes 6291456 | tf_op jit(solution)/shard_map/dot_general | solution.py:48
  12.9 0.0 copy-start.2
  12.9 0.0 reduce-scatter.2.cloned.1.call-update
  12.9 0.0 all-gather.8.cloned.1.call-start
  13.0 0.0 copy-done.1
  13.0 0.9 bitcast_convert_fusion
  13.8 0.0 all-gather.8.cloned.1.call-update
  13.9 0.0 all-gather.14.cloned.1.call-start
  13.9 0.0 copy-done.3
  13.9 0.0 copy-done.4
  13.9 0.6 select_reduce_fusion
  15.3 0.7 select_reduce_fusion.1
  16.0 76.0 %reduce-scatter.2.cloned.1.call-done = f32[256,1024]{1,0:T(8,128)} async-done(((f32[1024,1024]{1,0:T(8,128)}), f32[256,1024]{1,0:T(8,128)}) %reduce-scatter.2.cloned.1.call-update) | async-done | bytes 1048592 | tf_op jit(solution)/shard_map/reduce_scatter | solution.py:46
  92.0 0.0 copy-done.2
  92.0 5.1 %bitcast_subtract_fusion = (f32[256,1024]{1,0:T(8,128)}, f32[256,1024]{1,0:T(8,128)}, f32[256,1024]{1,0:T(8,128)}) fusion(f32[1,256,1024]{2,1,0:T(8,128)S(1)} %copy-done.1, f32[]{:T(128)} %get-tuple-element.9, f32[]{:T(128)S(6)} %sub.10, f32[]{:T(128)S(6)} %sub.9, f32[]{:T(128)} %get-tuple-element.10, f32[256,1024]{1,0:T(8,128)} %reduce-scatter.2.cloned.1.call-done, ...), kind=kLoop, calls=%fused_computation.7 | loop fusion | flops 3932160 | bytes 7340048 | tf_op jit(solution)/shard_map/sub | solution.py:24
  97.0 0.0 all-gather.14.cloned.1.call-update
  97.0 0.0 all-gather.12.cloned.1.call-start
  97.1 0.5 all-gather.12.cloned.1.call-update
  97.6 0.0 all-gather.10.cloned.1.call-start
  97.7 0.5 all-gather.10.cloned.1.call-update
  99.3 41.3 %all-gather.8.cloned.1.call-done = bf16[1024,1024]{1,0:T(8,128)(2,1)} async-done(((bf16[256,1024]{1,0:T(8,128)(2,1)}), bf16[1024,1024]{1,0:T(8,128)(2,1)}) %all-gather.8.cloned.1.call-update) | async-done | bytes 2097168 | tf_op jit(solution)/shard_map/all_gather | solution.py:41
  140.6 3.8 %fusion = bf16[1,512,1024]{2,1,0:T(8,128)(2,1)} fusion(bf16[1024,1024]{1,0:T(8,128)(2,1)} %all-gather.8.cloned.1.call-done, bf16[1,512,1024]{2,1,0:T(8,128)(2,1)S(1)} %copy-done), kind=kOutput, calls=%fused_computation.3 | convolution fusion | flops 1074790400 | bytes 4194304 | tf_op jit(solution)/shard_map/dot_general | solution.py:39
  144.5 32.0 %all-gather.14.cloned.1.call-done = f32[1024,1024]{1,0:T(8,128)} async-done(((f32[256,1024]{1,0:T(8,128)}), f32[1024,1024]{1,0:T(8,128)}) %all-gather.14.cloned.1.call-update) | async-done | bytes 4194320 | tf_op jit(solution)/shard_map/all_gather | solution.py:61
  176.5 2.3 constant_dynamic-slice_fusion
  178.8 34.3 %all-gather.12.cloned.1.call-done = f32[1024,1024]{1,0:T(8,128)} async-done(((f32[256,1024]{1,0:T(8,128)}), f32[1024,1024]{1,0:T(8,128)}) %all-gather.12.cloned.1.call-update) | async-done | bytes 4194320 | tf_op jit(solution)/shard_map/all_gather | solution.py:60
  213.0 2.3 constant_dynamic-slice_fusion.1
  215.4 34.3 %all-gather.10.cloned.1.call-done = f32[1024,1024]{1,0:T(8,128)} async-done(((f32[256,1024]{1,0:T(8,128)}), f32[1024,1024]{1,0:T(8,128)}) %all-gather.10.cloned.1.call-update) | async-done | bytes 4194320 | tf_op jit(solution)/shard_map/all_gather | solution.py:59
  249.6 2.3 constant_dynamic-slice_fusion.2
  (6 shorter events, 0.0 us)
Async XLA Ops:
  7.2 1.2 copy-start
  7.2 5.8 %copy-start.1 = (f32[1,256,1024]{2,1,0:T(8,128)S(1)}, f32[1,256,1024]{2,1,0:T(8,128)}, u32[]{:S(2)}) copy-start(f32[1,256,1024]{2,1,0:T(8,128)} %param.11) | copy-start | bytes 3145732
  7.2 84.8 %reduce-scatter.2.cloned.1.call-start = ((), (), s32[]{:S(2)}) async-start(), calls=%async_computation.2 | async-start | bytes 5242880 | tf_op jit(solution)/shard_map/reduce_scatter | solution.py:46
  12.9 1.1 copy-start.3
  12.9 1.1 copy-start.4
  12.9 2.4 copy-start.5
  12.9 2.5 copy-start.6
  12.9 79.1 %copy-start.2 = (f32[1,256,1024]{2,1,0:T(8,128)S(1)}, f32[1,256,1024]{2,1,0:T(8,128)}, u32[]{:S(2)}) copy-start(f32[1,256,1024]{2,1,0:T(8,128)} %param.13) | copy-start | bytes 3145732
  12.9 127.7 %all-gather.8.cloned.1.call-start = ((), (), s32[]{:S(2)}) async-start(), calls=%async_computation.1 | async-start | bytes 2621440 | tf_op jit(solution)/shard_map/all_gather | solution.py:41
  13.9 162.6 %all-gather.14.cloned.1.call-start = ((), (), s32[]{:S(2)}) async-start(), calls=%async_computation.5 | async-start | bytes 5242880 | tf_op jit(solution)/shard_map/all_gather | solution.py:61
  97.0 116.0 %all-gather.12.cloned.1.call-start = ((), (), s32[]{:S(2)}) async-start(), calls=%async_computation.4 | async-start | bytes 5242880 | tf_op jit(solution)/shard_map/all_gather | solution.py:60
  97.6 152.0 %all-gather.10.cloned.1.call-start = ((), (), s32[]{:S(2)}) async-start(), calls=%async_computation.3 | async-start | bytes 5242880 | tf_op jit(solution)/shard_map/all_gather | solution.py:59
Sparse Core Ops, SparseCore 0:
  13.0 78.8 reduce-scatter.1
  94.2 46.3 all-gather.7
  142.8 33.5 all-gather.13
  178.5 34.4 all-gather.11
  215.1 34.4 all-gather.9
where the time goes:
time: 259 us; the launch traced here: 258 us
  waiting for transfers between devices  219 us (85%)
  between operations  15.7 us (6%)
  matrix products  8.31 us (3%)
  local copies, waits for them, and re-layouts  8.11 us (3%)
  other arithmetic  7.23 us (3%)
    reduce_scatter x1, waiting for transfers between devices, on_device(): lax.psum_scatter(scale * lax.dot_general(context_rows, cotangent, (((0,),...  76 us
    all_gather x1, waiting for transfers between devices, on_device(): lax.all_gather(half_weight, 'shard', axis=0, tiled=True)  41.3 us
    all_gather x1, waiting for transfers between devices, on_device(): lax.all_gather(first_step[None], 'member', axis=0, tiled=True)  34.3 us
    all_gather x1, waiting for transfers between devices, on_device(): lax.all_gather(weight_step[None], 'member', axis=0, tiled=True)  34.3 us
    all_gather x1, waiting for transfers between devices, on_device(): lax.all_gather(second_step[None], 'member', axis=0, tiled=True)  32 us
  transfers between devices with their start and end apart: 5, of which 5 were waited for; matrix products, arithmetic and copies ran while one was open for 6% of the time, Pallas kernels for 0%

commit v1 on v0

v1 whole, which is shorter than its diff:
```python
import jax
import jax.numpy as jnp
from jax import lax
from jax.sharding import PartitionSpec as P

beta_one = 0.9
beta_two = 0.999
epsilon = 1e-08


def lookup(table, index):
    positions = jnp.arange(table.shape[0], dtype=jnp.int32)
    return jnp.sum(jnp.where(positions == index, table, jnp.zeros_like(table)))


def adam_update(weight_rows, first_rows, second_rows, grad_rows, rates, decays, steps, index):
    rate = lookup(rates, index)
    decay = lookup(decays, index)
    count = (lookup(steps, index) + 1).astype(jnp.float32)
    first_step = beta_one * first_rows + (1.0 - beta_one) * grad_rows
    second_step = beta_two * second_rows + (1.0 - beta_two) * grad_rows * grad_rows
    first_hat = first_step / (1.0 - jnp.power(beta_one, count))
    second_hat = second_step / (1.0 - jnp.power(beta_two, count))
    weight_step = weight_rows - rate * (
        first_hat / (jnp.sqrt(second_hat) + epsilon) + decay * weight_rows
    )
    return (weight_step, first_step, second_step)


def on_device(n, members, context, out_grad, weight, first, second, rates, decays, steps, donor):
    context_rows = context[0]
    cotangent = out_grad[0]
    width = context_rows.shape[1]
    rows = weight.shape[1]
    scale = width ** (-0.5)
    half = jnp.bfloat16
    me = lax.axis_index("shard")
    member = lax.axis_index("member")
    donor_of = lookup(donor, member)
    source = jnp.where(donor_of >= 0, donor_of, member)
    mate = jnp.bitwise_xor(member, 1)
    across = jnp.bitwise_xor(member, 2)
    mate_donor = lookup(donor, mate)
    mate_source = jnp.where(mate_donor >= 0, mate_donor, mate)

    swap_across = [(m, m ^ 2) for m in range(members)]
    swap_mates = [(m, m ^ 1) for m in range(members)]
    to_right = [(s, s + 1) for s in range(n - 1)]
    to_left = [(s + 1, s) for s in range(n - 1)]

    def from_donor(own):
        far = lax.ppermute(own, "member", swap_across)
        near = lax.ppermute(jnp.where(mate_source == across, far, own), "member", swap_mates)
        return jnp.where(source == across, far, near)

    half_weight = weight[0].astype(half)
    state = jnp.concatenate([half_weight, first[0].astype(half), second[0].astype(half)], axis=0)

    partial = scale * lax.dot_general(
        context_rows, cotangent, (((0,), (0,)), ((), ())), preferred_element_type=jnp.float32
    )

    def partial_block(block):
        start = jnp.clip(block, 0, n - 1) * rows
        return lax.dynamic_slice_in_dim(partial, start, rows, 0)

    from_left, from_right = [half_weight], [half_weight]
    for slot in range(1, n + 1):
        right, left = from_left[-1], from_right[-1]
        if slot > 1:
            add_right = jnp.where(me >= slot - 1, 0.0, partial_block(n + 1 + me - slot))
            add_left = jnp.where(n - 1 - me >= slot - 1, 0.0, partial_block(me + slot - n - 1))
            right = (right.astype(jnp.float32) + add_right).astype(half)
            left = (left.astype(jnp.float32) + add_left).astype(half)
        from_left.append(lax.ppermute(right, "shard", to_right))
        from_right.append(lax.ppermute(left, "shard", to_left))

    donor_state = from_donor(state)

    window = jnp.concatenate(from_left[n - 1:0:-1] + [half_weight] + from_right[1:n], axis=0)
    full_weight = lax.dynamic_slice_in_dim(window, (n - 1 - me) * rows, n * rows, 0)
    columns = lax.dot_general(
        cotangent, full_weight, (((1,), (1,)), ((), ())), preferred_element_type=jnp.float32
    )
    context_grad = (columns * scale).astype(half)[None]

    grad = partial_block(me) + from_left[n].astype(jnp.float32) + from_right[n].astype(jnp.float32)
    donor_grad = from_donor(grad.astype(half))

    keeps = source == member
    donor_state = donor_state.astype(jnp.float32)
    updated = adam_update(
        jnp.where(keeps, weight[0], donor_state[:rows]),
        jnp.where(keeps, first[0], donor_state[rows:2 * rows]),
        jnp.where(keeps, second[0], donor_state[2 * rows:]),
        jnp.where(keeps, grad, donor_grad.astype(jnp.float32)),
        rates, decays, steps, source,
    )
    return (context_grad,) + tuple(array[None] for array in updated)


def solution(mesh):
    whole = P(("groups", "member"), "shard", None)
    n, members = mesh.shape["shard"], mesh.shape["member"]

    def run(*args):
        return on_device(n, members, *args)

    return jax.shard_map(
        run, mesh=mesh, in_specs=(whole,) * 5 + (P("groups"),) * 4, out_specs=(whole,) * 4, check_vma=False
    )
```

time: 259 us -> 103 us (0.40)
  waiting for transfers between devices: 219 us -> 29.6 us
  starting transfers between devices: 0.2 us -> 31.2 us
  other arithmetic: 7.23 us -> 21.4 us
  between operations: 15.7 us -> 4.09 us
  matrix products: 8.31 us -> 4.79 us
    all_gather x4 -> x0, waiting for transfers between devices: 142 us -> none  [the longest x1 41.3 us: on_device(): lax.all_gather(half_weight, 'shard', axis=0, tiled=True)]
    reduce_scatter x1 -> x0, waiting for transfers between devices: 76 us -> none  [on_device(): lax.psum_scatter(scale * lax.dot_general(context_rows, cotangent, (((0,),...]
    ppermute x0 -> x12, starting transfers between devices: none -> 31.2 us  [the longest x4 13 us: on_device(): from_left.append(lax.ppermute(right, 'shard', to_right))]
    ppermute x0 -> x12, waiting for transfers between devices: none -> 29.6 us  [the longest x4 13.1 us: on_device(): from_right.append(lax.ppermute(left, 'shard', to_left))]
    convert_element_type x1 -> x7, other arithmetic: 0.87 us -> 11.5 us  [the longest x2 4.53 us: on_device(): left = (left.astype(jnp.float32) + add_left).astype(half)]
    unnamed x14 -> x50, local copies, waits for them, and re-layouts: 1.19 us -> 8.78 us
    dynamic_slice x3 -> x0, local copies, waits for them, and re-layouts: 6.92 us -> none  [the longest x1 2.31 us: on_device(): first_new = lax.dynamic_index_in_dim(gathered[1], source, 0, keepdims=False)]
    sub x1 -> x0, other arithmetic: 5.06 us -> none  [adam_update(): weight_rows - rate * (first_hat / (jnp.sqrt(second_hat) + epsilon) + deca...]
  transfers between devices with their start and end apart: 5 -> 12, of which waited for: 5 -> 7; matrix products, arithmetic and copies ran while one was open for 6% -> 26% of each run, Pallas kernels for 0% -> 0%
where the time goes in v1:
time: 103 us; the launch traced here: 101 us
  starting transfers between devices  31.2 us (30%)
  waiting for transfers between devices  29.6 us (29%)
  other arithmetic  21.4 us (21%)
  local copies, waits for them, and re-layouts  9.86 us (10%)
  matrix products  4.79 us (5%)
  between operations  4.09 us (4%)
    ppermute x4, waiting for transfers between devices, on_device(): from_right.append(lax.ppermute(left, 'shard', to_left))  13.1 us
    ppermute x4, starting transfers between devices, on_device(): from_left.append(lax.ppermute(right, 'shard', to_right))  13 us
    ppermute x4, waiting for transfers between devices, on_device(): from_left.append(lax.ppermute(right, 'shard', to_right))  12 us
    ppermute x2, starting transfers between devices, from_donor(): lax.ppermute(jnp.where(mate_source == across, far, own), 'member', swap_m...  10.6 us
    unnamed x50, local copies, waits for them, and re-layouts  8.78 us
    ppermute x4, starting transfers between devices, on_device(): from_right.append(lax.ppermute(left, 'shard', to_left))  5.14 us
    convert_element_type x2, other arithmetic, on_device(): left = (left.astype(jnp.float32) + add_left).astype(half)  4.53 us
    ppermute x2, waiting for transfers between devices, from_donor(): far = lax.ppermute(own, 'member', swap_across)  4.53 us
  transfers between devices with their start and end apart: 12, of which 7 were waited for; matrix products, arithmetic and copies ran while one was open for 26% of the time, Pallas kernels for 0%

profile of v1, /device:TPU:1, one launch (start us, length us, event | category | flops | bytes accessed | tf_op | source)
XLA Modules:
  0.0 100.9 jit_solution(14271592020169649600)
XLA Ops:
  0.6 1.4 %bitcast_convert_fusion.2 = bf16[256,1024]{1,0:T(8,128)(2,1)S(1)} fusion(f32[1,256,1024]{2,1,0:T(8,128)} %param.11), kind=kLoop, calls=%fused_computation.21 | loop fusion | flops 262144 | bytes 1572864 | tf_op jit(solution)/shard_map/convert_element_type | solution.py:56
  2.0 4.1 %collective-permute-start = (bf16[256,1024]{1,0:T(8,128)(2,1)S(1)}, bf16[256,1024]{1,0:T(8,128)(2,1)S(1)}, u32[]{:S(2)}, u32[]{:S(2)}) collective-permute-start(bf16[256,1024]{1,0:T(8,128)(2,1)S(1)} %bitcast_convert_fusion.2), channel_id=1, source_target_pairs={{0,1},{1,2},{2,3},{4,5},{5,6},{6,7},{8,9},{9,10},{10,11},{12,13},{... | collective-permute-start | bytes 1572872 | tf_op jit(solution)/shard_map/ppermute | solution.py:75
  6.1 1.3 %collective-permute-start.3 = (bf16[256,1024]{1,0:T(8,128)(2,1)S(1)}, bf16[256,1024]{1,0:T(8,128)(2,1)S(1)}, u32[]{:S(2)}, u32[]{:S(2)}) collective-permute-start(bf16[256,1024]{1,0:T(8,128)(2,1)S(1)} %bitcast_convert_fusion.2), channel_id=1, source_target_pairs={{1,0},{2,1},{3,2},{5,4},{6,5},{7,6},{9,8},{10,9},{11,10},{13,12},{... | collective-permute-start | bytes 1572872 | tf_op jit(solution)/shard_map/ppermute | solution.py:76
  7.4 2.5 %convolution_multiply_fusion = f32[1024,1024]{1,0:T(8,128)S(1)} fusion(bf16[1,512,1024]{2,1,0:T(8,128)(2,1)S(1)} %copy-done, bf16[1,512,1024]{2,1,0:T(8,128)(2,1)} %param.9), kind=kOutput, calls=%fused_computation | convolution fusion | flops 1074790400 | bytes 6291456 | tf_op jit(solution)/shard_map/dot_general | solution.py:59
  10.0 6.7 %collective-permute-done = bf16[256,1024]{1,0:T(8,128)(2,1)S(1)} collective-permute-done((bf16[256,1024]{1,0:T(8,128)(2,1)S(1)}, bf16[256,1024]{1,0:T(8,128)(2,1)S(1)}, u32[]{:S(2)}, u32[]{:S(2)}) %collective-permute-start) | collective-permute-done | bytes 524320 | tf_op jit(solution)/shard_map/ppermute | solution.py:75
  16.6 3.8 %collective-permute-done.3 = bf16[256,1024]{1,0:T(8,128)(2,1)S(1)} collective-permute-done((bf16[256,1024]{1,0:T(8,128)(2,1)S(1)}, bf16[256,1024]{1,0:T(8,128)(2,1)S(1)}, u32[]{:S(2)}, u32[]{:S(2)}) %collective-permute-start.3) | collective-permute-done | bytes 524320 | tf_op jit(solution)/shard_map/ppermute | solution.py:76
  20.5 1.4 %add_convert_fusion.3 = (bf16[256,1024]{1,0:T(8,128)(2,1)}, bf16[256,1024]{1,0:T(8,128)(2,1)}) fusion(f32[1024,1024]{1,0:T(8,128)S(1)} %convolution_multiply_fusion, s32[]{:T(128)S(6)} %select_n.141, bf16[256,1024]{1,0:T(8,128)(2,1)S(1)} %collective-permute-done.3, pred[]{:T(512)S(6)} %ge.26, s32[]{:T(128)S(6)} %select_n.135, pred[]{:T(512)S(6)} %ge.24, ...), kind=kLoop, calls=%fused_computation.28 | loop fusion | flops 2097152 | bytes 4194314 | tf_op jit(solution)/shard_map/convert_element_type | solution.py:74
  21.8 4.0 %collective-permute-start.1 = (bf16[256,1024]{1,0:T(8,128)(2,1)}, bf16[256,1024]{1,0:T(8,128)(2,1)}, u32[]{:S(2)}, u32[]{:S(2)}) collective-permute-start(bf16[256,1024]{1,0:T(8,128)(2,1)} %get-tuple-element.20), channel_id=1, source_target_pairs={{0,1},{1,2},{2,3},{4,5},{5,6},{6,7},{8,9},{9,10},{10,11},{12,13},{... | collective-permute-start | bytes 1572872 | tf_op jit(solution)/shard_map/ppermute | solution.py:75
  25.8 1.3 %collective-permute-start.4 = (bf16[256,1024]{1,0:T(8,128)(2,1)}, bf16[256,1024]{1,0:T(8,128)(2,1)}, u32[]{:S(2)}, u32[]{:S(2)}) collective-permute-start(bf16[256,1024]{1,0:T(8,128)(2,1)} %get-tuple-element.19), channel_id=1, source_target_pairs={{1,0},{2,1},{3,2},{5,4},{6,5},{7,6},{9,8},{10,9},{11,10},{13,12},{... | collective-permute-start | bytes 1572872 | tf_op jit(solution)/shard_map/ppermute | solution.py:76
  28.1 1.3 %pad_maximum_fusion = bf16[768,1024]{1,0:T(8,128)(2,1)} fusion(bf16[256,1024]{1,0:T(8,128)(2,1)S(1)} %get-tuple-element.21, bf16[256,1024]{1,0:T(8,128)(2,1)S(1)} %get-tuple-element.22, bf16[256,1024]{1,0:T(8,128)(2,1)S(1)} %bitcast_convert_fusion.2), kind=kLoop, calls=%fused_computation.4 | loop fusion | flops 4718592 | bytes 3145728 | tf_op jit(solution)/shard_map/concatenate | solution.py:57
  29.4 1.2 %collective-permute-start.6 = (bf16[768,1024]{1,0:T(8,128)(2,1)}, bf16[768,1024]{1,0:T(8,128)(2,1)S(1)}, u32[]{:S(2)}, u32[]{:S(2)}) collective-permute-start(bf16[768,1024]{1,0:T(8,128)(2,1)} %pad_maximum_fusion), channel_id=1, source_target_pairs={{0,8},{4,12},{8,0},{12,4},{1,9},{5,13},{9,1},{13,5},{2,10},{6,14},... | collective-permute-start | bytes 4718600 | tf_op jit(solution)/shard_map/ppermute | solution.py:52
  30.6 4.0 %collective-permute-done.1 = bf16[256,1024]{1,0:T(8,128)(2,1)} collective-permute-done((bf16[256,1024]{1,0:T(8,128)(2,1)}, bf16[256,1024]{1,0:T(8,128)(2,1)}, u32[]{:S(2)}, u32[]{:S(2)}) %collective-permute-start.1) | collective-permute-done | bytes 524320 | tf_op jit(solution)/shard_map/ppermute | solution.py:75
  34.7 4.6 %collective-permute-done.4 = bf16[256,1024]{1,0:T(8,128)(2,1)} collective-permute-done((bf16[256,1024]{1,0:T(8,128)(2,1)}, bf16[256,1024]{1,0:T(8,128)(2,1)}, u32[]{:S(2)}, u32[]{:S(2)}) %collective-permute-start.4) | collective-permute-done | bytes 524320 | tf_op jit(solution)/shard_map/ppermute | solution.py:76
  39.3 3.2 %add_convert_fusion.2 = (bf16[256,1024]{1,0:T(8,128)(2,1)}, bf16[256,1024]{1,0:T(8,128)(2,1)}) fusion(f32[1024,1024]{1,0:T(8,128)} %copy-done.1, s32[]{:T(128)S(6)} %select_n.144, bf16[256,1024]{1,0:T(8,128)(2,1)} %collective-permute-done.4, pred[]{:T(512)S(6)} %ge.27, s32[]{:T(128)S(6)} %select_n.138, pred[]{:T(512)S(6)} %ge.25, ...), kind=kLoop, calls=%fused_computation.27 | loop fusion | flops 2097152 | bytes 4194314 | tf_op jit(solution)/shard_map/convert_element_type | solution.py:74
  42.4 3.2 %collective-permute-start.2 = (bf16[256,1024]{1,0:T(8,128)(2,1)}, bf16[256,1024]{1,0:T(8,128)(2,1)}, u32[]{:S(2)}, u32[]{:S(2)}) collective-permute-start(bf16[256,1024]{1,0:T(8,128)(2,1)} %get-tuple-element.18), channel_id=1, source_target_pairs={{0,1},{1,2},{2,3},{4,5},{5,6},{6,7},{8,9},{9,10},{10,11},{12,13},{... | collective-permute-start | bytes 1572872 | tf_op jit(solution)/shard_map/ppermute | solution.py:75
  45.7 1.3 %collective-permute-start.5 = (bf16[256,1024]{1,0:T(8,128)(2,1)}, bf16[256,1024]{1,0:T(8,128)(2,1)}, u32[]{:S(2)}, u32[]{:S(2)}) collective-permute-start(bf16[256,1024]{1,0:T(8,128)(2,1)} %get-tuple-element.17), channel_id=1, source_target_pairs={{1,0},{2,1},{3,2},{5,4},{6,5},{7,6},{9,8},{10,9},{11,10},{13,12},{... | collective-permute-start | bytes 1572872 | tf_op jit(solution)/shard_map/ppermute | solution.py:76
  52.0 1.3 %collective-permute-done.2 = bf16[256,1024]{1,0:T(8,128)(2,1)} collective-permute-done((bf16[256,1024]{1,0:T(8,128)(2,1)}, bf16[256,1024]{1,0:T(8,128)(2,1)}, u32[]{:S(2)}, u32[]{:S(2)}) %collective-permute-start.2) | collective-permute-done | bytes 524320 | tf_op jit(solution)/shard_map/ppermute | solution.py:75
  53.3 4.6 %collective-permute-done.5 = bf16[256,1024]{1,0:T(8,128)(2,1)} collective-permute-done((bf16[256,1024]{1,0:T(8,128)(2,1)}, bf16[256,1024]{1,0:T(8,128)(2,1)}, u32[]{:S(2)}, u32[]{:S(2)}) %collective-permute-start.5) | collective-permute-done | bytes 524320 | tf_op jit(solution)/shard_map/ppermute | solution.py:76
  57.9 2.2 %add_convert_fusion.1 = (bf16[256,1024]{1,0:T(8,128)(2,1)S(1)}, bf16[256,1024]{1,0:T(8,128)(2,1)S(1)}) fusion(f32[1024,1024]{1,0:T(8,128)} %copy-done.1, s32[]{:T(128)S(6)} %select_n.161, bf16[256,1024]{1,0:T(8,128)(2,1)} %collective-permute-done.2, pred[]{:T(512)S(6)} %ge.30, s32[]{:T(128)S(6)} %select_n.164, pred[]{:T(512)S(6)} %ge.31, ...), kind=kLoop, calls=%fused_computation.26 | loop fusion | flops 2097152 | bytes 4194314 | tf_op jit(solution)/shard_map/convert_element_type | solution.py:73
  60.1 1.7 %collective-permute-start.8 = (bf16[256,1024]{1,0:T(8,128)(2,1)S(1)}, bf16[256,1024]{1,0:T(8,128)(2,1)S(1)}, u32[]{:S(2)}, u32[]{:S(2)}) collective-permute-start(bf16[256,1024]{1,0:T(8,128)(2,1)S(1)} %get-tuple-element.15), channel_id=1, source_target_pairs={{0,1},{1,2},{2,3},{4,5},{5,6},{6,7},{8,9},{9,10},{10,11},{12,13},{... | collective-permute-start | bytes 1572872 | tf_op jit(solution)/shard_map/ppermute | solution.py:75
  61.9 1.3 %collective-permute-start.9 = (bf16[256,1024]{1,0:T(8,128)(2,1)S(1)}, bf16[256,1024]{1,0:T(8,128)(2,1)S(1)}, u32[]{:S(2)}, u32[]{:S(2)}) collective-permute-start(bf16[256,1024]{1,0:T(8,128)(2,1)S(1)} %get-tuple-element.16), channel_id=1, source_target_pairs={{1,0},{2,1},{3,2},{5,4},{6,5},{7,6},{9,8},{10,9},{11,10},{13,12},{... | collective-permute-start | bytes 1572872 | tf_op jit(solution)/shard_map/ppermute | solution.py:76
  65.4 1.2 %copy-done.3 = bf16[768,1024]{1,0:T(8,128)(2,1)} copy-done((bf16[768,1024]{1,0:T(8,128)(2,1)}, bf16[768,1024]{1,0:T(8,128)(2,1)S(1)}, u32[]{:S(2)}) %copy-start.3) | copy-done | bytes 1572888
  66.6 1.9 %broadcast_select_fusion = bf16[768,1024]{1,0:T(8,128)(2,1)} fusion(bf16[768,1024]{1,0:T(8,128)(2,1)S(1)} %collective-permute-done.6, pred[]{:T(512)S(6)} %eq.39, bf16[256,1024]{1,0:T(8,128)(2,1)S(1)} %copy-done.5, bf16[256,1024]{1,0:T(8,128)(2,1)S(1)} %copy-done.7, bf16[256,1024]{1,0:T(8,128)(2,1)S(1)} %bitcast_convert_fusion.2), kind=kLoop, calls=%fused_computation.7 | loop fusion | flops 5505024 | bytes 4718593 | tf_op jit(solution)/shard_map/jit(_where)/select_n | solution.py:53
  68.5 4.3 %collective-permute-start.7 = (bf16[768,1024]{1,0:T(8,128)(2,1)}, bf16[768,1024]{1,0:T(8,128)(2,1)}, u32[]{:S(2)}, u32[]{:S(2)}) collective-permute-start(bf16[768,1024]{1,0:T(8,128)(2,1)} %broadcast_select_fusion), channel_id=1, source_target_pairs={{0,4},{4,0},{8,12},{12,8},{1,5},{5,1},{9,13},{13,9},{2,6},{6,2},{1... | collective-permute-start | bytes 4718600 | tf_op jit(solution)/shard_map/ppermute | solution.py:53
  72.9 1.5 %fusion.19 = (bf16[256,1024]{1,0:T(8,128)(2,1)S(1)}, f32[256,1024]{1,0:T(8,128)S(1)}) fusion(bf16[256,1024]{1,0:T(8,128)(2,1)S(1)} %collective-permute-done.9, bf16[256,1024]{1,0:T(8,128)(2,1)S(1)} %collective-permute-done.8, f32[1024,1024]{1,0:T(8,128)} %copy-done.1, s32[]{:T(128)S(6)} %select_n.159), kind=kLoop, calls=%fused_computation.49 | loop fusion | flops 1310720 | bytes 3670020 | tf_op jit(solution)/shard_map/convert_element_type | solution.py:88
  74.4 1.3 %collective-permute-start.10 = (bf16[256,1024]{1,0:T(8,128)(2,1)S(1)}, bf16[256,1024]{1,0:T(8,128)(2,1)S(1)}, u32[]{:S(2)}, u32[]{:S(2)}) collective-permute-start(bf16[256,1024]{1,0:T(8,128)(2,1)S(1)} %get-tuple-element.13), channel_id=1, source_target_pairs={{0,8},{4,12},{8,0},{12,4},{1,9},{5,13},{9,1},{13,5},{2,10},{6,14},... | collective-permute-start | bytes 1572872 | tf_op jit(solution)/shard_map/ppermute | solution.py:52
  78.0 4.5 %collective-permute-done.10 = bf16[256,1024]{1,0:T(8,128)(2,1)S(1)} collective-permute-done((bf16[256,1024]{1,0:T(8,128)(2,1)S(1)}, bf16[256,1024]{1,0:T(8,128)(2,1)S(1)}, u32[]{:S(2)}, u32[]{:S(2)}) %collective-permute-start.10) | collective-permute-done | bytes 524320 | tf_op jit(solution)/shard_map/ppermute | solution.py:52
  84.2 6.3 %collective-permute-start.11 = (bf16[256,1024]{1,0:T(8,128)(2,1)}, bf16[256,1024]{1,0:T(8,128)(2,1)}, u32[]{:S(2)}, u32[]{:S(2)}) collective-permute-start(bf16[256,1024]{1,0:T(8,128)(2,1)} %broadcast_select_fusion.1), channel_id=1, source_target_pairs={{0,4},{4,0},{8,12},{12,8},{1,5},{5,1},{9,13},{13,9},{2,6},{6,2},{1... | collective-permute-start | bytes 1572872 | tf_op jit(solution)/shard_map/ppermute | solution.py:53
  90.5 2.3 %fusion.4 = bf16[1,512,1024]{1,2,0:T(8,128)(2,1)} fusion(bf16[1792,1024]{1,0:T(8,128)(2,1)S(1)} %constant_dynamic-update-slice_fusion, s32[]{:T(128)S(6)} %select_n.146, bf16[1,512,1024]{2,1,0:T(8,128)(2,1)S(1)} %copy-done), kind=kOutput, calls=%fused_computation.8 | convolution fusion | flops 1074790400 | bytes 4194308 | tf_op jit(solution)/shard_map/dot_general | solution.py:82
  92.8 2.3 %copy.13 = bf16[1,512,1024]{2,1,0:T(8,128)(2,1)} copy(bf16[1,512,1024]{1,2,0:T(8,128)(2,1)} %fusion.4) | data formatting | bytes 2097152
  95.1 1.8 %select_convert_fusion = f32[768,1024]{1,0:T(8,128)S(1)} fusion(bf16[768,1024]{1,0:T(8,128)(2,1)} %copy-done.3, bf16[768,1024]{1,0:T(8,128)(2,1)} %collective-permute-done.7, pred[]{:T(512)S(6)} %eq.36), kind=kLoop, calls=%fused_computation.6 | loop fusion | flops 1572864 | bytes 6291457 | tf_op jit(solution)/shard_map/convert_element_type | solution.py:91
  97.2 3.7 %subtract_bitcast_fusion = (f32[1,256,1024]{2,1,0:T(8,128)}, f32[256,1024]{1,0:T(8,128)}, f32[256,1024]{1,0:T(8,128)}) fusion(f32[768,1024]{1,0:T(8,128)S(1)} %select_convert_fusion, f32[1,256,1024]{2,1,0:T(8,128)S(1)} %copy-done.2, f32[]{:T(128)} %get-tuple-element.23, f32[]{:T(128)S(6)} %sub.44, f32[]{:T(128)S(6)} %sub.43, f32[]{:T(128)} %get-tuple-element.24, ...), kind=kLoop, calls=%fused_computation.22 | loop fusion | flops 5505024 | bytes 11534354 | tf_op jit(solution)/shard_map/broadcast_in_dim | solution.py:99
  (60 shorter events, 9.4 us)
Async XLA Ops:
  0.6 6.8 %copy-start = (bf16[1,512,1024]{2,1,0:T(8,128)(2,1)S(1)}, bf16[1,512,1024]{2,1,0:T(8,128)(2,1)}, u32[]{:S(2)}) copy-start(bf16[1,512,1024]{2,1,0:T(8,128)(2,1)} %param.10) | copy-start | bytes 3145732
  2.0 14.6 %collective-permute-start = (bf16[256,1024]{1,0:T(8,128)(2,1)S(1)}, bf16[256,1024]{1,0:T(8,128)(2,1)S(1)}, u32[]{:S(2)}, u32[]{:S(2)}) collective-permute-start(bf16[256,1024]{1,0:T(8,128)(2,1)S(1)} %bitcast_convert_fusion.2), channel_id=1, source_target_pairs={{0,1},{1,2},{2,3},{4,5},{5,6},{6,7},{8,9},{9,10},{10,11},{12,13},{... | collective-permute-start | bytes 1572872 | tf_op jit(solution)/shard_map/ppermute | solution.py:75
  6.1 14.4 %collective-permute-start.3 = (bf16[256,1024]{1,0:T(8,128)(2,1)S(1)}, bf16[256,1024]{1,0:T(8,128)(2,1)S(1)}, u32[]{:S(2)}, u32[]{:S(2)}) collective-permute-start(bf16[256,1024]{1,0:T(8,128)(2,1)S(1)} %bitcast_convert_fusion.2), channel_id=1, source_target_pairs={{1,0},{2,1},{3,2},{5,4},{6,5},{7,6},{9,8},{10,9},{11,10},{13,12},{... | collective-permute-start | bytes 1572872 | tf_op jit(solution)/shard_map/ppermute | solution.py:76
  10.0 17.3 %copy-start.1 = (f32[1024,1024]{1,0:T(8,128)}, f32[1024,1024]{1,0:T(8,128)S(1)}, u32[]{:S(2)}) copy-start(f32[1024,1024]{1,0:T(8,128)S(1)} %convolution_multiply_fusion) | copy-start | bytes 12582916
  10.0 17.1 %copy-start.8 = (f32[1,256,1024]{2,1,0:T(8,128)S(1)}, f32[1,256,1024]{2,1,0:T(8,128)}, u32[]{:S(2)}) copy-start(f32[1,256,1024]{2,1,0:T(8,128)} %param.13) | copy-start | bytes 3145732
  10.0 17.1 %copy-start.10 = (f32[1,256,1024]{2,1,0:T(8,128)S(1)}, f32[1,256,1024]{2,1,0:T(8,128)}, u32[]{:S(2)}) copy-start(f32[1,256,1024]{2,1,0:T(8,128)} %param.12) | copy-start | bytes 3145732
  16.6 10.6 %copy-start.16 = (bf16[256,1024]{1,0:T(8,128)(2,1)}, bf16[256,1024]{1,0:T(8,128)(2,1)S(1)}, u32[]{:S(2)}) copy-start(bf16[256,1024]{1,0:T(8,128)(2,1)S(1)} %collective-permute-done) | copy-start | bytes 1572868
  20.5 6.8 %copy-start.14 = (bf16[256,1024]{1,0:T(8,128)(2,1)}, bf16[256,1024]{1,0:T(8,128)(2,1)S(1)}, u32[]{:S(2)}) copy-start(bf16[256,1024]{1,0:T(8,128)(2,1)S(1)} %collective-permute-done.3) | copy-start | bytes 1572868
  21.8 12.8 %collective-permute-start.1 = (bf16[256,1024]{1,0:T(8,128)(2,1)}, bf16[256,1024]{1,0:T(8,128)(2,1)}, u32[]{:S(2)}, u32[]{:S(2)}) collective-permute-start(bf16[256,1024]{1,0:T(8,128)(2,1)} %get-tuple-element.20), channel_id=1, source_target_pairs={{0,1},{1,2},{2,3},{4,5},{5,6},{6,7},{8,9},{9,10},{10,11},{12,13},{... | collective-permute-start | bytes 1572872 | tf_op jit(solution)/shard_map/ppermute | solution.py:75
  25.8 13.5 %collective-permute-start.4 = (bf16[256,1024]{1,0:T(8,128)(2,1)}, bf16[256,1024]{1,0:T(8,128)(2,1)}, u32[]{:S(2)}, u32[]{:S(2)}) collective-permute-start(bf16[256,1024]{1,0:T(8,128)(2,1)} %get-tuple-element.19), channel_id=1, source_target_pairs={{1,0},{2,1},{3,2},{5,4},{6,5},{7,6},{9,8},{10,9},{11,10},{13,12},{... | collective-permute-start | bytes 1572872 | tf_op jit(solution)/shard_map/ppermute | solution.py:76
  27.3 2.1 %copy-start.6 = (bf16[256,1024]{1,0:T(8,128)(2,1)}, bf16[256,1024]{1,0:T(8,128)(2,1)S(1)}, u32[]{:S(2)}) copy-start(bf16[256,1024]{1,0:T(8,128)(2,1)S(1)} %get-tuple-element.22) | copy-start | bytes 1572868
  28.1 18.9 %copy-start.18 = (s32[4]{0:T(128)S(1)}, s32[4]{0:T(128)}, u32[]{:S(2)}) copy-start(s32[4]{0:T(128)} %param.17) | copy-start | bytes 52
  28.1 22.0 %copy-start.21 = (s32[4]{0:T(128)S(1)}, s32[4]{0:T(128)}, u32[]{:S(2)}) copy-start(s32[4]{0:T(128)} %param.16) | copy-start | bytes 52
  28.1 23.3 %copy-start.19 = (f32[4]{0:T(128)S(1)}, f32[4]{0:T(128)}, u32[]{:S(2)}) copy-start(f32[4]{0:T(128)} %param.15) | copy-start | bytes 52
  28.1 23.3 %copy-start.20 = (f32[4]{0:T(128)S(1)}, f32[4]{0:T(128)}, u32[]{:S(2)}) copy-start(f32[4]{0:T(128)} %param.14) | copy-start | bytes 52
  29.4 36.0 %collective-permute-start.6 = (bf16[768,1024]{1,0:T(8,128)(2,1)}, bf16[768,1024]{1,0:T(8,128)(2,1)S(1)}, u32[]{:S(2)}, u32[]{:S(2)}) collective-permute-start(bf16[768,1024]{1,0:T(8,128)(2,1)} %pad_maximum_fusion), channel_id=1, source_target_pairs={{0,8},{4,12},{8,0},{12,4},{1,9},{5,13},{9,1},{13,5},{2,10},{6,14},... | collective-permute-start | bytes 4718600 | tf_op jit(solution)/shard_map/ppermute | solution.py:52
  42.4 10.9 %collective-permute-start.2 = (bf16[256,1024]{1,0:T(8,128)(2,1)}, bf16[256,1024]{1,0:T(8,128)(2,1)}, u32[]{:S(2)}, u32[]{:S(2)}) collective-permute-start(bf16[256,1024]{1,0:T(8,128)(2,1)} %get-tuple-element.18), channel_id=1, source_target_pairs={{0,1},{1,2},{2,3},{4,5},{5,6},{6,7},{8,9},{9,10},{10,11},{12,13},{... | collective-permute-start | bytes 1572872 | tf_op jit(solution)/shard_map/ppermute | solution.py:75
  45.7 12.3 %collective-permute-start.5 = (bf16[256,1024]{1,0:T(8,128)(2,1)}, bf16[256,1024]{1,0:T(8,128)(2,1)}, u32[]{:S(2)}, u32[]{:S(2)}) collective-permute-start(bf16[256,1024]{1,0:T(8,128)(2,1)} %get-tuple-element.17), channel_id=1, source_target_pairs={{1,0},{2,1},{3,2},{5,4},{6,5},{7,6},{9,8},{10,9},{11,10},{13,12},{... | collective-permute-start | bytes 1572872 | tf_op jit(solution)/shard_map/ppermute | solution.py:76
  52.0 14.6 %copy-start.5 = (bf16[256,1024]{1,0:T(8,128)(2,1)S(1)}, bf16[256,1024]{1,0:T(8,128)(2,1)}, u32[]{:S(2)}) copy-start(bf16[256,1024]{1,0:T(8,128)(2,1)} %copy-done.4) | copy-start | bytes 1572868
  52.0 14.6 %copy-start.7 = (bf16[256,1024]{1,0:T(8,128)(2,1)S(1)}, bf16[256,1024]{1,0:T(8,128)(2,1)}, u32[]{:S(2)}) copy-start(bf16[256,1024]{1,0:T(8,128)(2,1)} %copy-done.6) | copy-start | bytes 1572868
  60.1 12.7 %collective-permute-start.8 = (bf16[256,1024]{1,0:T(8,128)(2,1)S(1)}, bf16[256,1024]{1,0:T(8,128)(2,1)S(1)}, u32[]{:S(2)}, u32[]{:S(2)}) collective-permute-start(bf16[256,1024]{1,0:T(8,128)(2,1)S(1)} %get-tuple-element.15), channel_id=1, source_target_pairs={{0,1},{1,2},{2,3},{4,5},{5,6},{6,7},{8,9},{9,10},{10,11},{12,13},{... | collective-permute-start | bytes 1572872 | tf_op jit(solution)/shard_map/ppermute | solution.py:75
  61.9 11.0 %collective-permute-start.9 = (bf16[256,1024]{1,0:T(8,128)(2,1)S(1)}, bf16[256,1024]{1,0:T(8,128)(2,1)S(1)}, u32[]{:S(2)}, u32[]{:S(2)}) collective-permute-start(bf16[256,1024]{1,0:T(8,128)(2,1)S(1)} %get-tuple-element.16), channel_id=1, source_target_pairs={{1,0},{2,1},{3,2},{5,4},{6,5},{7,6},{9,8},{10,9},{11,10},{13,12},{... | collective-permute-start | bytes 1572872 | tf_op jit(solution)/shard_map/ppermute | solution.py:76
  64.2 8.6 %copy-start.17 = (bf16[256,1024]{1,0:T(8,128)(2,1)S(1)}, bf16[256,1024]{1,0:T(8,128)(2,1)}, u32[]{:S(2)}) copy-start(bf16[256,1024]{1,0:T(8,128)(2,1)} %copy-done.16) | copy-start | bytes 1572868
  65.4 1.2 %copy-start.3 = (bf16[768,1024]{1,0:T(8,128)(2,1)}, bf16[768,1024]{1,0:T(8,128)(2,1)S(1)}, u32[]{:S(2)}) copy-start(bf16[768,1024]{1,0:T(8,128)(2,1)S(1)} %collective-permute-done.6) | copy-start | bytes 4718596
  68.5 7.2 %copy-start.2 = (f32[1,256,1024]{2,1,0:T(8,128)S(1)}, f32[1,256,1024]{2,1,0:T(8,128)}, u32[]{:S(2)}) copy-start(f32[1,256,1024]{2,1,0:T(8,128)} %param.11) | copy-start | bytes 3145732
  68.5 7.2 %copy-start.15 = (bf16[256,1024]{1,0:T(8,128)(2,1)S(1)}, bf16[256,1024]{1,0:T(8,128)(2,1)}, u32[]{:S(2)}) copy-start(bf16[256,1024]{1,0:T(8,128)(2,1)} %copy-done.14) | copy-start | bytes 1572868
  68.5 26.5 %collective-permute-start.7 = (bf16[768,1024]{1,0:T(8,128)(2,1)}, bf16[768,1024]{1,0:T(8,128)(2,1)}, u32[]{:S(2)}, u32[]{:S(2)}) collective-permute-start(bf16[768,1024]{1,0:T(8,128)(2,1)} %broadcast_select_fusion), channel_id=1, source_target_pairs={{0,4},{4,0},{8,12},{12,8},{1,5},{5,1},{9,13},{13,9},{2,6},{6,2},{1... | collective-permute-start | bytes 4718600 | tf_op jit(solution)/shard_map/ppermute | solution.py:53
  74.4 8.1 %collective-permute-start.10 = (bf16[256,1024]{1,0:T(8,128)(2,1)S(1)}, bf16[256,1024]{1,0:T(8,128)(2,1)S(1)}, u32[]{:S(2)}, u32[]{:S(2)}) collective-permute-start(bf16[256,1024]{1,0:T(8,128)(2,1)S(1)} %get-tuple-element.13), channel_id=1, source_target_pairs={{0,8},{4,12},{8,0},{12,4},{1,9},{5,13},{9,1},{13,5},{2,10},{6,14},... | collective-permute-start | bytes 1572872 | tf_op jit(solution)/shard_map/ppermute | solution.py:52
  84.2 12.7 %collective-permute-start.11 = (bf16[256,1024]{1,0:T(8,128)(2,1)}, bf16[256,1024]{1,0:T(8,128)(2,1)}, u32[]{:S(2)}, u32[]{:S(2)}) collective-permute-start(bf16[256,1024]{1,0:T(8,128)(2,1)} %broadcast_select_fusion.1), channel_id=1, source_target_pairs={{0,4},{4,0},{8,12},{12,8},{1,5},{5,1},{9,13},{13,9},{2,6},{6,2},{1... | collective-permute-start | bytes 1572872 | tf_op jit(solution)/shard_map/ppermute | solution.py:53
  95.0 1.8 %copy-start.9 = (f32[1,256,1024]{2,1,0:T(8,128)S(1)}, f32[1,256,1024]{2,1,0:T(8,128)}, u32[]{:S(2)}) copy-start(f32[1,256,1024]{2,1,0:T(8,128)} %param.13) | copy-start | bytes 3145732
  95.1 2.0 %copy-start.11 = (f32[1,256,1024]{2,1,0:T(8,128)S(1)}, f32[1,256,1024]{2,1,0:T(8,128)}, u32[]{:S(2)}) copy-start(f32[1,256,1024]{2,1,0:T(8,128)} %param.12) | copy-start | bytes 3145732
  95.1 2.1 %copy-start.13 = (bf16[256,1024]{1,0:T(8,128)(2,1)S(1)}, bf16[256,1024]{1,0:T(8,128)(2,1)}, u32[]{:S(2)}) copy-start(bf16[256,1024]{1,0:T(8,128)(2,1)} %copy-done.12) | copy-start | bytes 1572868
  (2 other events, 1.6 us)

commit v2 on v1

v2 whole, which is shorter than its diff:
```python
import functools
import math

import jax
import jax.numpy as jnp
from jax import lax
from jax.experimental import pallas as pl
from jax.experimental.pallas import tpu as pltpu
from jax.sharding import PartitionSpec as P

beta_one = 0.9
beta_two = 0.999
epsilon = 1e-08

MIB = 1 << 20
SMEM = pl.BlockSpec(memory_space=pltpu.SMEM)
VMEM = pl.BlockSpec(memory_space=pltpu.VMEM)
ANY = pl.BlockSpec(memory_space=pl.ANY)


def cost(flops, moved):
    return pl.CostEstimate(flops=flops, bytes_accessed=moved, transcendentals=0)


def partial_kernel(n, chains, scale, where_ref, context_ref, cotangent_ref, *refs):
    blocks, (product, sems) = refs[:-2], refs[-2:]
    width = product.shape[0]
    rows = width // n
    part = rows // chains
    me = where_ref[0]
    tile = min(256, width)
    for start in range(0, width, tile):
        product[start:start + tile, :] = scale * lax.dot_general(
            context_ref[:, start:start + tile], cotangent_ref[...],
            (((0,), (0,)), ((), ())), preferred_element_type=jnp.float32,
        )
    copies = []
    for i in range(n):
        for c in range(chains):
            first_row = pl.multiple_of(lax.rem(me + i, n) * rows + c * part, part)
            copies.append(pltpu.make_async_copy(
                product.at[pl.ds(first_row, part), :], blocks[i * chains + c], sems.at[i * chains + c]
            ))
            copies[-1].start()
    for copy in copies:
        copy.wait()


def partial_blocks(n, chains, scale, where, context_rows, cotangent):
    tokens, width = context_rows.shape
    depth = cotangent.shape[1]
    part = width // n // chains
    return pl.pallas_call(
        functools.partial(partial_kernel, n, chains, scale),
        out_shape=[jax.ShapeDtypeStruct((part, depth), jnp.float32)] * (n * chains),
        in_specs=[SMEM, VMEM, VMEM],
        out_specs=[ANY] * (n * chains),
        scratch_shapes=[pltpu.VMEM((width, depth), jnp.float32), pltpu.SemaphoreType.DMA((n * chains,))],
        compiler_params=pltpu.CompilerParams(vmem_limit_bytes=20 * MIB),
        cost_estimate=cost(2 * tokens * width * depth, 6 * MIB),
        name="partial_blocks",
    )(where, context_rows, cotangent)


def columns_kernel(n, chains, scale, where_ref, cotangent_ref, *refs):
    blocks, (out_ref, full, sems) = refs[:-3], refs[-3:]
    rows = full.shape[0] // n
    part = rows // chains
    me = where_ref[0]
    moves = []
    for k in range(2 * n - 1):
        shard = me + (k - (n - 1))
        there = jnp.logical_and(shard >= 0, shard < n)
        for c in range(chains):
            first_row = pl.multiple_of(jnp.clip(shard, 0, n - 1) * rows + c * part, part)
            moves.append((there, pltpu.make_async_copy(
                blocks[k * chains + c], full.at[pl.ds(first_row, part), :], sems.at[k * chains + c]
            )))
    for there, copy in moves:
        pl.when(there)(copy.start)
    for there, copy in moves:
        pl.when(there)(copy.wait)
    width = full.shape[0]
    tile = min(256, width)
    for start in range(0, width, tile):
        out_ref[:, start:start + tile] = (scale * lax.dot_general(
            cotangent_ref[...], full[start:start + tile, :],
            (((1,), (1,)), ((), ())), preferred_element_type=jnp.float32,
        )).astype(out_ref.dtype)


def columns(n, chains, scale, where, cotangent, blocks):
    tokens, depth = cotangent.shape
    width = blocks[0].shape[0] * n * chains
    return pl.pallas_call(
        functools.partial(columns_kernel, n, chains, scale),
        out_shape=jax.ShapeDtypeStruct((tokens, width), cotangent.dtype),
        in_specs=[SMEM, VMEM] + [ANY] * len(blocks),
        out_specs=VMEM,
        scratch_shapes=[pltpu.VMEM((width, depth), cotangent.dtype), pltpu.SemaphoreType.DMA((len(blocks),))],
        compiler_params=pltpu.CompilerParams(vmem_limit_bytes=20 * MIB),
        cost_estimate=cost(2 * tokens * width * depth, 4 * MIB),
        name="context_grad",
    )(where, cotangent, *blocks)


def adam_kernel(chain, part, filled, where_ref, rates_ref, decays_ref, steps_ref, donor_ref, *refs):
    own, donated, grads = refs[:3], refs[3:6], refs[6:10]
    refs = refs[10 + (3 if filled else 0):]
    outs, (kept, taken, grad, stepped, sems, out_sems) = refs[:3], refs[3:]
    rows = own[0].shape[0]
    member = where_ref[1]
    donor = donor_ref[member]
    source = jnp.where(donor >= 0, donor, member)
    way = jnp.bitwise_xor(source, member)
    rate, decay = rates_ref[source], decays_ref[source]
    count = jnp.full((1, grad.shape[1]), (steps_ref[source] + 1).astype(jnp.float32))
    scale_one = 1.0 / (1.0 - jnp.exp(count * math.log(beta_one)))
    scale_two = 1.0 / (1.0 - jnp.exp(count * math.log(beta_two)))
    mine = pl.ds(chain * part, part)

    def own_copy(k):
        return pltpu.make_async_copy(own[k].at[mine, :], kept.at[k], sems.at[k])

    def donated_copy(w, k):
        return pltpu.make_async_copy(
            donated[w - 1].at[pl.ds(k * rows + chain * part, part), :], taken.at[k], sems.at[k]
        )

    def grad_copy(w):
        return pltpu.make_async_copy(grads[w], grad, sems.at[3])

    def step(i, from_own):
        at = pl.ds(pl.multiple_of(i * 16, 16), 16)
        load = lambda k: kept[k, at, :] if from_own else taken[k, at, :].astype(jnp.float32)
        g = grad[at, :].astype(jnp.float32)
        w = load(0)
        first_step = beta_one * load(1) + (1.0 - beta_one) * g
        second_step = beta_two * load(2) + (1.0 - beta_two) * g * g
        ratio = (first_step * scale_one) / (jnp.sqrt(second_step * scale_two) + epsilon)
        stepped[0, at, :] = w - rate * (ratio + decay * w)
        stepped[1, at, :] = first_step
        stepped[2, at, :] = second_step

    for w in range(4):
        @pl.when(way == w)
        def _():
            grad_copy(w).start()
            for k in range(3):
                (own_copy(k) if w == 0 else donated_copy(w, k)).start()
            grad_copy(w).wait()
            for k in range(3):
                (own_copy(k) if w == 0 else donated_copy(w, k)).wait()

    @pl.when(way == 0)
    def _():
        pl.loop(0, part // 16)(lambda i: step(i, True))

    @pl.when(way != 0)
    def _():
        pl.loop(0, part // 16)(lambda i: step(i, False))

    writes = [
        pltpu.make_async_copy(stepped.at[k], outs[k].at[mine, :], out_sems.at[k]) for k in range(3)
    ]
    for write in writes:
        write.start()
    for write in writes:
        write.wait()


def adam_update(chain, part, where, tables, own, donated, grads, filled):
    rows, depth = own[0].shape
    shape = jax.ShapeDtypeStruct((rows, depth), jnp.float32)
    before = 5 + 3 + 3 + 4
    return pl.pallas_call(
        functools.partial(adam_kernel, chain, part, bool(filled)),
        out_shape=[shape] * 3,
        in_specs=[SMEM] * 5 + [ANY] * (10 + len(filled)),
        out_specs=[ANY] * 3,
        scratch_shapes=[
            pltpu.VMEM((3, part, depth), jnp.float32),
            pltpu.VMEM((3, part, depth), jnp.bfloat16),
            pltpu.VMEM((part, depth), jnp.bfloat16),
            pltpu.VMEM((3, part, depth), jnp.float32),
            pltpu.SemaphoreType.DMA((4,)),
            pltpu.SemaphoreType.DMA((3,)),
        ],
        input_output_aliases={before + k: k for k in range(len(filled))},
        compiler_params=pltpu.CompilerParams(vmem_limit_bytes=16 * MIB),
        cost_estimate=cost(30 * part * depth, 26 * part * depth),
        name="adam",
    )(where, *tables, *own, *donated, *grads, *filled)


def on_device(n, members, context, out_grad, weight, first, second, rates, decays, steps, donor):
    context_rows = context[0]
    cotangent = out_grad[0]
    scale = context_rows.shape[1] ** (-0.5)
    rows = weight.shape[1]
    chains = 2 if rows % 32 == 0 else 1
    part = rows // chains
    half = jnp.bfloat16
    me = lax.axis_index("shard")
    where = jnp.stack([me, lax.axis_index("member")]).astype(jnp.int32)

    swap_across = [(m, m ^ 2) for m in range(members)]
    swap_mates = [(m, m ^ 1) for m in range(members)]
    to_right = [(s, s + 1) for s in range(n - 1)]
    to_left = [(s + 1, s) for s in range(n - 1)]

    def from_members(own):
        across = lax.ppermute(own, "member", swap_across)
        mate = lax.ppermute(own, "member", swap_mates)
        return mate, across, lax.ppermute(across, "member", swap_mates)

    half_weight = weight[0].astype(half)
    pieces = [half_weight[c * part:(c + 1) * part] for c in range(chains)]
    partial = partial_blocks(n, chains, scale, where, context_rows, cotangent)

    from_left, from_right = [pieces], [pieces]
    for slot in range(1, n + 1):
        right, left = from_left[-1], from_right[-1]
        if slot > 1:
            def added(arrived, block, forwards):
                term = jnp.where(forwards, 0.0, block)
                return (arrived.astype(jnp.float32) + term).astype(half)

            right = [
                added(right[c], partial[(n + 1 - slot) * chains + c], me >= slot - 1)
                for c in range(chains)
            ]
            left = [
                added(left[c], partial[(slot - 1) * chains + c], n - 1 - me >= slot - 1)
                for c in range(chains)
            ]
        arrived = [
            (lax.ppermute(right[c], "shard", to_right), lax.ppermute(left[c], "shard", to_left))
            for c in range(chains)
        ]
        from_left.append([pair[0] for pair in arrived])
        from_right.append([pair[1] for pair in arrived])

    state = jnp.concatenate([half_weight, first[0].astype(half), second[0].astype(half)], axis=0)
    donated = from_members(state)

    blocks = from_left[n - 1:0:-1] + [pieces] + from_right[1:n]
    context_grad = columns(n, chains, scale, where, cotangent, [b for pair in blocks for b in pair])

    tables = (rates, decays, steps, donor)
    updated = ()
    for c in range(chains):
        grad = partial[c] + from_left[n][c].astype(jnp.float32) + from_right[n][c].astype(jnp.float32)
        grad = grad.astype(half)
        updated = adam_update(
            c, part, where, tables, (weight[0], first[0], second[0]), donated,
            (grad,) + from_members(grad), updated,
        )
    return (context_grad[None],) + tuple(array[None] for array in updated)


def solution(mesh):
    whole = P(("groups", "member"), "shard", None)
    n, members = mesh.shape["shard"], mesh.shape["member"]
    return jax.shard_map(
        functools.partial(on_device, n, members),
        mesh=mesh,
        in_specs=(whole,) * 5 + (P("groups"),) * 4,
        out_specs=(whole,) * 4,
        check_vma=False,
    )
```

time: 103 us -> 112 us (1.087)
  starting transfers between devices: 31.2 us -> 56.1 us
  waiting for transfers between devices: 29.6 us -> 12.2 us
  Pallas kernels: 0 us -> 13.6 us
  matrix products: 4.79 us -> 0 us
  between operations: 4.09 us -> 1.09 us
  other arithmetic: 21.4 us -> 19.2 us
    ppermute x12 -> x25, starting transfers between devices: 31.2 us -> 56.1 us  [the longest x8 30.2 us: on_device(): lax.ppermute(right[c], 'shard', to_right)]
    ppermute x12 -> x25, waiting for transfers between devices: 29.6 us -> 12.2 us  [the longest x8 7.13 us: on_device(): lax.ppermute(left[c], 'shard', to_left)]
    pallas_call x0 -> x4, Pallas kernels: none -> 13.6 us  [the longest x2 7 us: adam_update(): pl.pallas_call(functools.partial(adam_kernel, chain, part, bool(filled)),...]
    convert_element_type x5 -> x12, other arithmetic: 10 us -> 16.3 us  [the longest x10 16.1 us: added(): return (arrived.astype(jnp.float32) + term).astype(half)]
    dot_general x2 -> x0, matrix products: 4.79 us -> none  [the longest x1 2.52 us: on_device(): lax.dot_general(context_rows, cotangent, (((0,), (0,)), ((), ())), prefer...]
    broadcast_in_dim x1 -> x0, other arithmetic: 3.72 us -> none  [on_device(): return (context_grad,) + tuple((array[None] for array in updated))]
    select_n x2 -> x0, other arithmetic: 2.79 us -> none  [from_donor(): jnp.where(mate_source == across, far, own)]
    reduce_sum x3 -> x0, other arithmetic: 1.91 us -> none  [lookup(): return jnp.sum(jnp.where(positions == index, table, jnp.zeros_like(table)))]
  transfers between devices with their start and end apart: 12 -> 25, of which waited for: 7 -> 5; matrix products, arithmetic and copies ran while one was open for 26% -> 16% of each run, Pallas kernels for 0% -> 9%
where the time goes in v2:
time: 112 us; the launch traced here: 111 us
  starting transfers between devices  56.1 us (50%)
  other arithmetic  19.2 us (17%)
  Pallas kernels  13.6 us (12%)
  waiting for transfers between devices  12.2 us (11%)
  local copies, waits for them, and re-layouts  8.77 us (8%)
    ppermute x8, starting transfers between devices, on_device(): lax.ppermute(right[c], 'shard', to_right)  30.2 us
    convert_element_type x10, other arithmetic, added(): return (arrived.astype(jnp.float32) + term).astype(half)  16.1 us
    ppermute x8, starting transfers between devices, on_device(): lax.ppermute(left[c], 'shard', to_left)  10.4 us
    unnamed x42, local copies, waits for them, and re-layouts  8 us
    ppermute x3, starting transfers between devices, from_members(): return (mate, across, lax.ppermute(across, 'member', swap_mates))  7.61 us
    ppermute x8, waiting for transfers between devices, on_device(): lax.ppermute(left[c], 'shard', to_left)  7.13 us
    pallas_call x2, Pallas kernels, adam_update(): pl.pallas_call(functools.partial(adam_kernel, chain, part, bool(filled)),...  7 us
    ppermute x3, starting transfers between devices, from_members(): mate = lax.ppermute(own, 'member', swap_mates)  6.13 us
  transfers between devices with their start and end apart: 25, of which 5 were waited for; matrix products, arithmetic and copies ran while one was open for 16% of the time, Pallas kernels for 9%

profile of v2, /device:TPU:1, one launch (start us, length us, event | category | flops | bytes accessed | tf_op | source)
XLA Modules:
  0.0 111.0 jit_solution(17507897177111680631)
XLA Ops:
  0.7 1.4 %bitcast_convert_fusion.2 = bf16[256,1024]{1,0:T(8,128)(2,1)S(1)} fusion(f32[1,256,1024]{2,1,0:T(8,128)} %param.11), kind=kLoop, calls=%fused_computation.18 | loop fusion | flops 262144 | bytes 1572864 | tf_op jit(solution)/shard_map/convert_element_type | solution.py:217
  2.9 4.7 %collective-permute-start.3 = (bf16[128,1024]{1,0:T(8,128)(2,1)S(1)}, bf16[128,1024]{1,0:T(8,128)(2,1)}, u32[]{:S(2)}, u32[]{:S(2)}) collective-permute-start(bf16[128,1024]{1,0:T(8,128)(2,1)S(1)} %get-tuple-element.36.refs_7_), channel_id=1, source_target_pairs={{0,1},{1,2},{2,3},{4,5},{5,6},{6,7},{8,9},{9,10},{10,11},{12,13},{... | collective-permute-start | bytes 786440 | tf_op jit(solution)/shard_map/ppermute | solution.py:238
  7.6 3.2 %collective-permute-start = (bf16[128,1024]{1,0:T(8,128)(2,1)}, bf16[128,1024]{1,0:T(8,128)(2,1)}, u32[]{:S(2)}, u32[]{:S(2)}) collective-permute-start(bf16[128,1024]{1,0:T(8,128)(2,1)} %get-tuple-element.37.refs_6_), channel_id=1, source_target_pairs={{0,1},{1,2},{2,3},{4,5},{5,6},{6,7},{8,9},{9,10},{10,11},{12,13},{... | collective-permute-start | bytes 786440 | tf_op jit(solution)/shard_map/ppermute | solution.py:238
  16.0 2.2 %partial_blocks.1 = (f32[128,1024]{1,0:T(8,128)S(1)}, f32[128,1024]{1,0:T(8,128)S(1)}, f32[128,1024]{1,0:T(8,128)S(1)}, f32[128,1024]{1,0:T(8,128)S(1)}, f32[128...) custom-call(s32[2]{0:T(128)S(1)} %pad_add_fusion.where_ref, ...), custom_call_target="tpu_custom_call" | custom-call | flops 1073741824 | bytes 6291456 | tf_op jit(solution)/shard_map/partial_blocks/pallas_call | solution.py:53
  23.0 1.7 %add_convert_fusion.13 = bf16[128,1024]{1,0:T(8,128)(2,1)} fusion(f32[128,1024]{1,0:T(8,128)S(1)} %get-tuple-element.18, bf16[128,1024]{1,0:T(8,128)(2,1)} %collective-permute-done.refs_4_, pred[]{:T(512)S(6)} %ge.24), kind=kLoop, calls=%fused_computation.14 | loop fusion | flops 524288 | bytes 1048577 | tf_op jit(solution)/shard_map/convert_element_type | solution.py:227
  24.8 3.2 %collective-permute-start.1 = (bf16[128,1024]{1,0:T(8,128)(2,1)}, bf16[128,1024]{1,0:T(8,128)(2,1)}, u32[]{:S(2)}, u32[]{:S(2)}) collective-permute-start(bf16[128,1024]{1,0:T(8,128)(2,1)} %add_convert_fusion.13), channel_id=1, source_target_pairs={{0,1},{1,2},{2,3},{4,5},{5,6},{6,7},{8,9},{9,10},{10,11},{12,13},{... | collective-permute-start | bytes 786440 | tf_op jit(solution)/shard_map/ppermute | solution.py:238
  28.0 1.3 %collective-permute-start.6 = (bf16[128,1024]{1,0:T(8,128)(2,1)}, bf16[128,1024]{1,0:T(8,128)(2,1)}, u32[]{:S(2)}, u32[]{:S(2)}) collective-permute-start(bf16[128,1024]{1,0:T(8,128)(2,1)} %get-tuple-element.37.refs_6_), channel_id=1, source_target_pairs={{1,0},{2,1},{3,2},{5,4},{6,5},{7,6},{9,8},{10,9},{11,10},{13,12},{... | collective-permute-start | bytes 786440 | tf_op jit(solution)/shard_map/ppermute | solution.py:238
  29.3 1.7 %add_convert_fusion.11 = bf16[128,1024]{1,0:T(8,128)(2,1)} fusion(f32[128,1024]{1,0:T(8,128)S(1)} %get-tuple-element.20, bf16[128,1024]{1,0:T(8,128)(2,1)} %collective-permute-done.3.refs_5_, pred[]{:T(512)S(6)} %ge.24), kind=kLoop, calls=%fused_computation.12 | loop fusion | flops 524288 | bytes 1048577 | tf_op jit(solution)/shard_map/convert_element_type | solution.py:227
  31.0 4.7 %collective-permute-start.4 = (bf16[128,1024]{1,0:T(8,128)(2,1)}, bf16[128,1024]{1,0:T(8,128)(2,1)}, u32[]{:S(2)}, u32[]{:S(2)}) collective-permute-start(bf16[128,1024]{1,0:T(8,128)(2,1)} %add_convert_fusion.11), channel_id=1, source_target_pairs={{0,1},{1,2},{2,3},{4,5},{5,6},{6,7},{8,9},{9,10},{10,11},{12,13},{... | collective-permute-start | bytes 786440 | tf_op jit(solution)/shard_map/ppermute | solution.py:238
  35.7 1.9 %add_convert_fusion.12 = bf16[128,1024]{1,0:T(8,128)(2,1)} fusion(f32[128,1024]{1,0:T(8,128)} %copy-done.4, bf16[128,1024]{1,0:T(8,128)(2,1)} %collective-permute-done.1.refs_2_, pred[]{:T(512)S(6)} %ge.25), kind=kLoop, calls=%fused_computation.13 | loop fusion | flops 524288 | bytes 1048577 | tf_op jit(solution)/shard_map/convert_element_type | solution.py:227
  37.6 2.0 %collective-permute-start.2 = (bf16[128,1024]{1,0:T(8,128)(2,1)}, bf16[128,1024]{1,0:T(8,128)(2,1)}, u32[]{:S(2)}, u32[]{:S(2)}) collective-permute-start(bf16[128,1024]{1,0:T(8,128)(2,1)} %add_convert_fusion.12), channel_id=1, source_target_pairs={{0,1},{1,2},{2,3},{4,5},{5,6},{6,7},{8,9},{9,10},{10,11},{12,13},{... | collective-permute-start | bytes 786440 | tf_op jit(solution)/shard_map/ppermute | solution.py:238
  39.6 1.3 %collective-permute-start.7 = (bf16[128,1024]{1,0:T(8,128)(2,1)S(1)}, bf16[128,1024]{1,0:T(8,128)(2,1)}, u32[]{:S(2)}, u32[]{:S(2)}) collective-permute-start(bf16[128,1024]{1,0:T(8,128)(2,1)S(1)} %get-tuple-element.36.refs_7_), channel_id=1, source_target_pairs={{1,0},{2,1},{3,2},{5,4},{6,5},{7,6},{9,8},{10,9},{11,10},{13,12},{... | collective-permute-start | bytes 786440 | tf_op jit(solution)/shard_map/ppermute | solution.py:238
  42.1 4.0 %collective-permute-start.5 = (bf16[128,1024]{1,0:T(8,128)(2,1)S(1)}, bf16[128,1024]{1,0:T(8,128)(2,1)S(1)}, u32[]{:S(2)}, u32[]{:S(2)}) collective-permute-start(bf16[128,1024]{1,0:T(8,128)(2,1)S(1)} %add_convert_fusion.10), channel_id=1, source_target_pairs={{0,1},{1,2},{2,3},{4,5},{5,6},{6,7},{8,9},{9,10},{10,11},{12,13},{... | collective-permute-start | bytes 786440 | tf_op jit(solution)/shard_map/ppermute | solution.py:238
  46.1 2.1 %add_convert_fusion.2 = (bf16[128,1024]{1,0:T(8,128)(2,1)}, bf16[128,1024]{1,0:T(8,128)(2,1)}) fusion(f32[128,1024]{1,0:T(8,128)} %copy-done.15, bf16[128,1024]{1,0:T(8,128)(2,1)} %collective-permute-done.2.refs_0_, pred[]{:T(512)S(6)} %ge.28, pred[]{:T(512)S(6)} %ge.26, bf16[128,1024]{1,0:T(8,128)(2,1)} %collective-permute-done.6.refs_8_), kind=kLoop, calls=%fused_computation.3 | loop fusion | flops 1048576 | bytes 1572866 | tf_op jit(solution)/shard_map/convert_element_type | solution.py:227
  49.7 1.9 %add_convert_fusion.5 = (bf16[128,1024]{1,0:T(8,128)(2,1)}, bf16[128,1024]{1,0:T(8,128)(2,1)}) fusion(f32[128,1024]{1,0:T(8,128)S(1)} %copy-done.14, bf16[128,1024]{1,0:T(8,128)(2,1)S(1)} %collective-permute-done.5.refs_1_, pred[]{:T(512)S(6)} %ge.28, pred[]{:T(512)S(6)} %ge.26, bf16[128,1024]{1,0:T(8,128)(2,1)} %collective-permute-done.7.refs_9_), kind=kLoop, calls=%fused_computation.6 | loop fusion | flops 1048576 | bytes 1572866 | tf_op jit(solution)/shard_map/convert_element_type | solution.py:227
  53.6 3.3 %collective-permute-start.12 = (bf16[768,1024]{1,0:T(8,128)(2,1)}, bf16[768,1024]{1,0:T(8,128)(2,1)}, u32[]{:S(2)}, u32[]{:S(2)}) collective-permute-start(bf16[768,1024]{1,0:T(8,128)(2,1)} %pad_maximum_fusion), channel_id=1, source_target_pairs={{0,4},{4,0},{8,12},{12,8},{1,5},{5,1},{9,13},{13,9},{2,6},{6,2},{1... | collective-permute-start | bytes 4718600 | tf_op jit(solution)/shard_map/ppermute | solution.py:214
  57.0 1.7 %add_convert_fusion.7 = bf16[128,1024]{1,0:T(8,128)(2,1)} fusion(f32[128,1024]{1,0:T(8,128)} %copy-done.4, bf16[128,1024]{1,0:T(8,128)(2,1)} %collective-permute-done.8.refs_10_, pred[]{:T(512)S(6)} %ge.27), kind=kLoop, calls=%fused_computation.8 | loop fusion | flops 524288 | bytes 1048577 | tf_op jit(solution)/shard_map/convert_element_type | solution.py:227
  60.0 4.7 %collective-permute-start.14 = (bf16[768,1024]{1,0:T(8,128)(2,1)}, bf16[768,1024]{1,0:T(8,128)(2,1)}, u32[]{:S(2)}, u32[]{:S(2)}) collective-permute-start(bf16[768,1024]{1,0:T(8,128)(2,1)} %collective-permute-done.13.refs_4_), channel_id=1, source_target_pairs={{0,4},{4,0},{8,12},{12,8},{1,5},{5,1},{9,13},{13,9},{2,6},{6,2},{1... | collective-permute-start | bytes 4718600 | tf_op jit(solution)/shard_map/ppermute | solution.py:215
  64.7 1.7 %add_convert_fusion.6 = bf16[128,1024]{1,0:T(8,128)(2,1)} fusion(f32[128,1024]{1,0:T(8,128)} %copy-done.3, bf16[128,1024]{1,0:T(8,128)(2,1)} %collective-permute-done.9.refs_11_, pred[]{:T(512)S(6)} %ge.27), kind=kLoop, calls=%fused_computation.7 | loop fusion | flops 524288 | bytes 1048577 | tf_op jit(solution)/shard_map/convert_element_type | solution.py:227
  67.7 5.0 %collective-permute-start.20 = (bf16[128,1024]{1,0:T(8,128)(2,1)}, bf16[128,1024]{1,0:T(8,128)(2,1)S(1)}, u32[]{:S(2)}, u32[]{:S(2)}) collective-permute-start(bf16[128,1024]{1,0:T(8,128)(2,1)} %get-tuple-element.32), channel_id=1, source_target_pairs={{0,1},{1,2},{2,3},{4,5},{5,6},{6,7},{8,9},{9,10},{10,11},{12,13},{... | collective-permute-start | bytes 786440 | tf_op jit(solution)/shard_map/ppermute | solution.py:238
  73.8 1.3 %collective-permute-start.21 = (bf16[128,1024]{1,0:T(8,128)(2,1)S(1)}, bf16[128,1024]{1,0:T(8,128)(2,1)S(1)}, u32[]{:S(2)}, u32[]{:S(2)}) collective-permute-start(bf16[128,1024]{1,0:T(8,128)(2,1)S(1)} %add_convert_fusion.1), channel_id=1, source_target_pairs={{1,0},{2,1},{3,2},{5,4},{6,5},{7,6},{9,8},{10,9},{11,10},{13,12},{... | collective-permute-start | bytes 786440 | tf_op jit(solution)/shard_map/ppermute | solution.py:238
  75.1 2.4 %collective-permute-done.11.refs_13_ = bf16[128,1024]{1,0:T(8,128)(2,1)} collective-permute-done((bf16[128,1024]{1,0:T(8,128)(2,1)}, bf16[128,1024]{1,0:T(8,128)(2,1)}, u32[]{:S(2)}, u32[]{:S(2)}) %collective-permute-start.11) | collective-permute-done | bytes 262176 | tf_op jit(solution)/shard_map/ppermute | solution.py:238
  77.5 3.3 %collective-permute-start.15 = (bf16[128,1024]{1,0:T(8,128)(2,1)}, bf16[128,1024]{1,0:T(8,128)(2,1)S(1)}, u32[]{:S(2)}, u32[]{:S(2)}) collective-permute-start(bf16[128,1024]{1,0:T(8,128)(2,1)} %get-tuple-element.34), channel_id=1, source_target_pairs={{0,1},{1,2},{2,3},{4,5},{5,6},{6,7},{8,9},{9,10},{10,11},{12,13},{... | collective-permute-start | bytes 786440 | tf_op jit(solution)/shard_map/ppermute | solution.py:238
  81.8 1.4 %collective-permute-start.16 = (bf16[128,1024]{1,0:T(8,128)(2,1)S(1)}, bf16[128,1024]{1,0:T(8,128)(2,1)S(1)}, u32[]{:S(2)}, u32[]{:S(2)}) collective-permute-start(bf16[128,1024]{1,0:T(8,128)(2,1)S(1)} %add_convert_fusion.4), channel_id=1, source_target_pairs={{1,0},{2,1},{3,2},{5,4},{6,5},{7,6},{9,8},{10,9},{11,10},{13,12},{... | collective-permute-start | bytes 786440 | tf_op jit(solution)/shard_map/ppermute | solution.py:238
  83.7 2.1 %collective-permute-done.15 = bf16[128,1024]{1,0:T(8,128)(2,1)S(1)} collective-permute-done((bf16[128,1024]{1,0:T(8,128)(2,1)}, bf16[128,1024]{1,0:T(8,128)(2,1)S(1)}, u32[]{:S(2)}, u32[]{:S(2)}) %collective-permute-start.15) | collective-permute-done | bytes 262176 | tf_op jit(solution)/shard_map/ppermute | solution.py:238
  85.9 4.7 %collective-permute-done.16 = bf16[128,1024]{1,0:T(8,128)(2,1)S(1)} collective-permute-done((bf16[128,1024]{1,0:T(8,128)(2,1)S(1)}, bf16[128,1024]{1,0:T(8,128)(2,1)S(1)}, u32[]{:S(2)}, u32[]{:S(2)}) %collective-permute-start.16) | collective-permute-done | bytes 262176 | tf_op jit(solution)/shard_map/ppermute | solution.py:238
  91.1 2.3 %collective-permute-start.22 = (bf16[128,1024]{1,0:T(8,128)(2,1)S(1)}, bf16[128,1024]{1,0:T(8,128)(2,1)S(1)}, u32[]{:S(2)}, u32[]{:S(2)}) collective-permute-start(bf16[128,1024]{1,0:T(8,128)(2,1)S(1)} %add_convert_fusion.refs_6_), channel_id=1, source_target_pairs={{0,4},{4,0},{8,12},{12,8},{1,5},{5,1},{9,13},{13,9},{2,6},{6,2},{1... | collective-permute-start | bytes 786440 | tf_op jit(solution)/shard_map/ppermute | solution.py:214
  93.9 2.7 %collective-permute-done.18.refs_8_ = bf16[128,1024]{1,0:T(8,128)(2,1)S(1)} collective-permute-done((bf16[128,1024]{1,0:T(8,128)(2,1)S(1)}, bf16[128,1024]{1,0:T(8,128)(2,1)S(1)}, u32[]{:S(2)}, u32[]{:S(2)}) %collective-permute-start.18) | collective-permute-done | bytes 262176 | tf_op jit(solution)/shard_map/ppermute | solution.py:213
  96.6 2.9 %collective-permute-start.19 = (bf16[128,1024]{1,0:T(8,128)(2,1)S(1)}, bf16[128,1024]{1,0:T(8,128)(2,1)S(1)}, u32[]{:S(2)}, u32[]{:S(2)}) collective-permute-start(bf16[128,1024]{1,0:T(8,128)(2,1)S(1)} %collective-permute-done.18.refs_8_), channel_id=1, source_target_pairs={{0,4},{4,0},{8,12},{12,8},{1,5},{5,1},{9,13},{13,9},{2,6},{6,2},{1... | collective-permute-start | bytes 786440 | tf_op jit(solution)/shard_map/ppermute | solution.py:215
  99.5 4.4 %context_grad.1 = bf16[512,1024]{1,0:T(8,128)(2,1)} custom-call(s32[2]{0:T(128)S(1)} %pad_add_fusion.where_ref, bf16[512,1024]{1,0:T(8,128)(2,1)S(1)} %bitcast.21, bf16[128,1024]{1,0:T(8,128)(2,1)} %collective-permute-done.2.refs_0_, bf16[128,1024]{1,0:T(8,128)(2,1)S(1)} %copy-done.6, bf16[128,1024]{1,0:T(8,128)(2,1)} %collective-permute-done.1.refs_2_, ...), custom_call_target="tpu_custom_call" | custom-call | flops 1073741824 | bytes 4194304 | tf_op jit(solution)/shard_map/context_grad/pallas_call | solution.py:95
  104.0 3.5 %adam.2 = (f32[256,1024]{1,0:T(8,128)}, f32[256,1024]{1,0:T(8,128)}, f32[256,1024]{1,0:T(8,128)}) custom-call(s32[2]{0:T(128)S(1)} %pad_add_fusion.where_ref, f32[4]{0:T(128)S(1)} %copy-done.16, f32[4]{0:T(128)S(1)} %copy-done.17, s32[4]{0:T(128)S(1)} %copy-done.18, s32[4]{0:T(128)S(1)} %copy-done.19, f32[256,1024]{1,0:T(8,128)S(1)} %bitcast.18, ...), custom_call_target="tpu_custom_call" | custom-call | flops 3932160 | bytes 3407872 | tf_op jit(solution)/shard_map/adam/pallas_call | solution.py:176
  107.5 3.5 %adam.3 = (f32[256,1024]{1,0:T(8,128)}, f32[256,1024]{1,0:T(8,128)}, f32[256,1024]{1,0:T(8,128)}) custom-call(s32[2]{0:T(128)S(1)} %pad_add_fusion.where_ref, f32[4]{0:T(128)S(1)} %copy-done.16, f32[4]{0:T(128)S(1)} %copy-done.17, s32[4]{0:T(128)S(1)} %copy-done.18, s32[4]{0:T(128)S(1)} %copy-done.19, ...), custom_call_target="tpu_custom_call", output_to_operand_aliasing={{0}: (15, {}), {1}: (16, {}), {2}: (17, {})} | custom-call | flops 3932160 | bytes 3407872 | tf_op jit(solution)/shard_map/adam/pallas_call | solution.py:176
  (81 shorter events, 21.5 us)
Async XLA Ops:
  2.9 26.4 %collective-permute-start.3 = (bf16[128,1024]{1,0:T(8,128)(2,1)S(1)}, bf16[128,1024]{1,0:T(8,128)(2,1)}, u32[]{:S(2)}, u32[]{:S(2)}) collective-permute-start(bf16[128,1024]{1,0:T(8,128)(2,1)S(1)} %get-tuple-element.36.refs_7_), channel_id=1, source_target_pairs={{0,1},{1,2},{2,3},{4,5},{5,6},{6,7},{8,9},{9,10},{10,11},{12,13},{... | collective-permute-start | bytes 786440 | tf_op jit(solution)/shard_map/ppermute | solution.py:238
  7.6 15.4 %collective-permute-start = (bf16[128,1024]{1,0:T(8,128)(2,1)}, bf16[128,1024]{1,0:T(8,128)(2,1)}, u32[]{:S(2)}, u32[]{:S(2)}) collective-permute-start(bf16[128,1024]{1,0:T(8,128)(2,1)} %get-tuple-element.37.refs_6_), channel_id=1, source_target_pairs={{0,1},{1,2},{2,3},{4,5},{5,6},{6,7},{8,9},{9,10},{10,11},{12,13},{... | collective-permute-start | bytes 786440 | tf_op jit(solution)/shard_map/ppermute | solution.py:238
  12.3 47.7 %collective-permute-start.13 = (bf16[768,1024]{1,0:T(8,128)(2,1)}, bf16[768,1024]{1,0:T(8,128)(2,1)}, u32[]{:S(2)}, u32[]{:S(2)}) collective-permute-start(bf16[768,1024]{1,0:T(8,128)(2,1)} %pad_maximum_fusion), channel_id=1, source_target_pairs={{0,8},{4,12},{8,0},{12,4},{1,9},{5,13},{9,1},{13,5},{2,10},{6,14},... | collective-permute-start | bytes 4718600 | tf_op jit(solution)/shard_map/ppermute | solution.py:213
  24.8 10.9 %collective-permute-start.1 = (bf16[128,1024]{1,0:T(8,128)(2,1)}, bf16[128,1024]{1,0:T(8,128)(2,1)}, u32[]{:S(2)}, u32[]{:S(2)}) collective-permute-start(bf16[128,1024]{1,0:T(8,128)(2,1)} %add_convert_fusion.13), channel_id=1, source_target_pairs={{0,1},{1,2},{2,3},{4,5},{5,6},{6,7},{8,9},{9,10},{10,11},{12,13},{... | collective-permute-start | bytes 786440 | tf_op jit(solution)/shard_map/ppermute | solution.py:238
  28.0 18.2 %collective-permute-start.6 = (bf16[128,1024]{1,0:T(8,128)(2,1)}, bf16[128,1024]{1,0:T(8,128)(2,1)}, u32[]{:S(2)}, u32[]{:S(2)}) collective-permute-start(bf16[128,1024]{1,0:T(8,128)(2,1)} %get-tuple-element.37.refs_6_), channel_id=1, source_target_pairs={{1,0},{2,1},{3,2},{5,4},{6,5},{7,6},{9,8},{10,9},{11,10},{13,12},{... | collective-permute-start | bytes 786440 | tf_op jit(solution)/shard_map/ppermute | solution.py:238
  31.0 9.9 %collective-permute-start.4 = (bf16[128,1024]{1,0:T(8,128)(2,1)}, bf16[128,1024]{1,0:T(8,128)(2,1)}, u32[]{:S(2)}, u32[]{:S(2)}) collective-permute-start(bf16[128,1024]{1,0:T(8,128)(2,1)} %add_convert_fusion.11), channel_id=1, source_target_pairs={{0,1},{1,2},{2,3},{4,5},{5,6},{6,7},{8,9},{9,10},{10,11},{12,13},{... | collective-permute-start | bytes 786440 | tf_op jit(solution)/shard_map/ppermute | solution.py:238
  37.6 8.6 %collective-permute-start.2 = (bf16[128,1024]{1,0:T(8,128)(2,1)}, bf16[128,1024]{1,0:T(8,128)(2,1)}, u32[]{:S(2)}, u32[]{:S(2)}) collective-permute-start(bf16[128,1024]{1,0:T(8,128)(2,1)} %add_convert_fusion.12), channel_id=1, source_target_pairs={{0,1},{1,2},{2,3},{4,5},{5,6},{6,7},{8,9},{9,10},{10,11},{12,13},{... | collective-permute-start | bytes 786440 | tf_op jit(solution)/shard_map/ppermute | solution.py:238
  39.6 10.0 %collective-permute-start.7 = (bf16[128,1024]{1,0:T(8,128)(2,1)S(1)}, bf16[128,1024]{1,0:T(8,128)(2,1)}, u32[]{:S(2)}, u32[]{:S(2)}) collective-permute-start(bf16[128,1024]{1,0:T(8,128)(2,1)S(1)} %get-tuple-element.36.refs_7_), channel_id=1, source_target_pairs={{1,0},{2,1},{3,2},{5,4},{6,5},{7,6},{9,8},{10,9},{11,10},{13,12},{... | collective-permute-start | bytes 786440 | tf_op jit(solution)/shard_map/ppermute | solution.py:238
  42.1 7.6 %collective-permute-start.5 = (bf16[128,1024]{1,0:T(8,128)(2,1)S(1)}, bf16[128,1024]{1,0:T(8,128)(2,1)S(1)}, u32[]{:S(2)}, u32[]{:S(2)}) collective-permute-start(bf16[128,1024]{1,0:T(8,128)(2,1)S(1)} %add_convert_fusion.10), channel_id=1, source_target_pairs={{0,1},{1,2},{2,3},{4,5},{5,6},{6,7},{8,9},{9,10},{10,11},{12,13},{... | collective-permute-start | bytes 786440 | tf_op jit(solution)/shard_map/ppermute | solution.py:238
  48.3 8.7 %collective-permute-start.8 = (bf16[128,1024]{1,0:T(8,128)(2,1)}, bf16[128,1024]{1,0:T(8,128)(2,1)}, u32[]{:S(2)}, u32[]{:S(2)}) collective-permute-start(bf16[128,1024]{1,0:T(8,128)(2,1)} %get-tuple-element.33), channel_id=1, source_target_pairs={{1,0},{2,1},{3,2},{5,4},{6,5},{7,6},{9,8},{10,9},{11,10},{13,12},{... | collective-permute-start | bytes 786440 | tf_op jit(solution)/shard_map/ppermute | solution.py:238
  52.3 12.3 %collective-permute-start.9 = (bf16[128,1024]{1,0:T(8,128)(2,1)}, bf16[128,1024]{1,0:T(8,128)(2,1)}, u32[]{:S(2)}, u32[]{:S(2)}) collective-permute-start(bf16[128,1024]{1,0:T(8,128)(2,1)} %get-tuple-element.35), channel_id=1, source_target_pairs={{1,0},{2,1},{3,2},{5,4},{6,5},{7,6},{9,8},{10,9},{11,10},{13,12},{... | collective-permute-start | bytes 786440 | tf_op jit(solution)/shard_map/ppermute | solution.py:238
  53.6 39.7 %collective-permute-start.12 = (bf16[768,1024]{1,0:T(8,128)(2,1)}, bf16[768,1024]{1,0:T(8,128)(2,1)}, u32[]{:S(2)}, u32[]{:S(2)}) collective-permute-start(bf16[768,1024]{1,0:T(8,128)(2,1)} %pad_maximum_fusion), channel_id=1, source_target_pairs={{0,4},{4,0},{8,12},{12,8},{1,5},{5,1},{9,13},{13,9},{2,6},{6,2},{1... | collective-permute-start | bytes 4718600 | tf_op jit(solution)/shard_map/ppermute | solution.py:214
  58.7 14.1 %collective-permute-start.10 = (bf16[128,1024]{1,0:T(8,128)(2,1)}, bf16[128,1024]{1,0:T(8,128)(2,1)}, u32[]{:S(2)}, u32[]{:S(2)}) collective-permute-start(bf16[128,1024]{1,0:T(8,128)(2,1)} %add_convert_fusion.7), channel_id=1, source_target_pairs={{1,0},{2,1},{3,2},{5,4},{6,5},{7,6},{9,8},{10,9},{11,10},{13,12},{... | collective-permute-start | bytes 786440 | tf_op jit(solution)/shard_map/ppermute | solution.py:238
  60.0 44.0 %collective-permute-start.14 = (bf16[768,1024]{1,0:T(8,128)(2,1)}, bf16[768,1024]{1,0:T(8,128)(2,1)}, u32[]{:S(2)}, u32[]{:S(2)}) collective-permute-start(bf16[768,1024]{1,0:T(8,128)(2,1)} %collective-permute-done.13.refs_4_), channel_id=1, source_target_pairs={{0,4},{4,0},{8,12},{12,8},{1,5},{5,1},{9,13},{13,9},{2,6},{6,2},{1... | collective-permute-start | bytes 4718600 | tf_op jit(solution)/shard_map/ppermute | solution.py:215
  66.4 11.1 %collective-permute-start.11 = (bf16[128,1024]{1,0:T(8,128)(2,1)}, bf16[128,1024]{1,0:T(8,128)(2,1)}, u32[]{:S(2)}, u32[]{:S(2)}) collective-permute-start(bf16[128,1024]{1,0:T(8,128)(2,1)} %add_convert_fusion.6), channel_id=1, source_target_pairs={{1,0},{2,1},{3,2},{5,4},{6,5},{7,6},{9,8},{10,9},{11,10},{13,12},{... | collective-permute-start | bytes 786440 | tf_op jit(solution)/shard_map/ppermute | solution.py:238
  67.7 15.6 %copy-start.12 = (f32[128,1024]{1,0:T(8,128)S(1)}, f32[128,1024]{1,0:T(8,128)}, u32[]{:S(2)}) copy-start(f32[128,1024]{1,0:T(8,128)} %copy-done.11) | copy-start | bytes 1572868
  67.7 22.9 %copy-start.10 = (f32[128,1024]{1,0:T(8,128)S(1)}, f32[128,1024]{1,0:T(8,128)}, u32[]{:S(2)}) copy-start(f32[128,1024]{1,0:T(8,128)} %copy-done.9) | copy-start | bytes 1572868
  67.7 14.1 %collective-permute-start.20 = (bf16[128,1024]{1,0:T(8,128)(2,1)}, bf16[128,1024]{1,0:T(8,128)(2,1)S(1)}, u32[]{:S(2)}, u32[]{:S(2)}) collective-permute-start(bf16[128,1024]{1,0:T(8,128)(2,1)} %get-tuple-element.32), channel_id=1, source_target_pairs={{0,1},{1,2},{2,3},{4,5},{5,6},{6,7},{8,9},{9,10},{10,11},{12,13},{... | collective-permute-start | bytes 786440 | tf_op jit(solution)/shard_map/ppermute | solution.py:238
  73.8 9.5 %collective-permute-start.21 = (bf16[128,1024]{1,0:T(8,128)(2,1)S(1)}, bf16[128,1024]{1,0:T(8,128)(2,1)S(1)}, u32[]{:S(2)}, u32[]{:S(2)}) collective-permute-start(bf16[128,1024]{1,0:T(8,128)(2,1)S(1)} %add_convert_fusion.1), channel_id=1, source_target_pairs={{1,0},{2,1},{3,2},{5,4},{6,5},{7,6},{9,8},{10,9},{11,10},{13,12},{... | collective-permute-start | bytes 786440 | tf_op jit(solution)/shard_map/ppermute | solution.py:238
  77.5 8.4 %collective-permute-start.15 = (bf16[128,1024]{1,0:T(8,128)(2,1)}, bf16[128,1024]{1,0:T(8,128)(2,1)S(1)}, u32[]{:S(2)}, u32[]{:S(2)}) collective-permute-start(bf16[128,1024]{1,0:T(8,128)(2,1)} %get-tuple-element.34), channel_id=1, source_target_pairs={{0,1},{1,2},{2,3},{4,5},{5,6},{6,7},{8,9},{9,10},{10,11},{12,13},{... | collective-permute-start | bytes 786440 | tf_op jit(solution)/shard_map/ppermute | solution.py:238
  81.8 17.7 %copy-start.6 = (bf16[128,1024]{1,0:T(8,128)(2,1)S(1)}, bf16[128,1024]{1,0:T(8,128)(2,1)}, u32[]{:S(2)}) copy-start(bf16[128,1024]{1,0:T(8,128)(2,1)} %copy-done.5) | copy-start | bytes 786436
  81.8 17.7 %copy-start.8 = (bf16[1,512,1024]{2,1,0:T(8,128)(2,1)S(1)}, bf16[1,512,1024]{2,1,0:T(8,128)(2,1)}, u32[]{:S(2)}) copy-start(bf16[1,512,1024]{2,1,0:T(8,128)(2,1)} %param.10) | copy-start | bytes 3145732
  81.8 8.7 %collective-permute-start.16 = (bf16[128,1024]{1,0:T(8,128)(2,1)S(1)}, bf16[128,1024]{1,0:T(8,128)(2,1)S(1)}, u32[]{:S(2)}, u32[]{:S(2)}) collective-permute-start(bf16[128,1024]{1,0:T(8,128)(2,1)S(1)} %add_convert_fusion.4), channel_id=1, source_target_pairs={{1,0},{2,1},{3,2},{5,4},{6,5},{7,6},{9,8},{10,9},{11,10},{13,12},{... | collective-permute-start | bytes 786440 | tf_op jit(solution)/shard_map/ppermute | solution.py:238
  83.4 10.0 %collective-permute-start.23 = (bf16[128,1024]{1,0:T(8,128)(2,1)S(1)}, bf16[128,1024]{1,0:T(8,128)(2,1)S(1)}, u32[]{:S(2)}, u32[]{:S(2)}) collective-permute-start(bf16[128,1024]{1,0:T(8,128)(2,1)S(1)} %add_convert_fusion.refs_6_), channel_id=1, source_target_pairs={{0,8},{4,12},{8,0},{12,4},{1,9},{5,13},{9,1},{13,5},{2,10},{6,14},... | collective-permute-start | bytes 786440 | tf_op jit(solution)/shard_map/ppermute | solution.py:213
  90.7 13.3 %copy-start.2 = (f32[1,256,1024]{2,1,0:T(8,128)S(1)}, f32[1,256,1024]{2,1,0:T(8,128)}, u32[]{:S(2)}) copy-start(f32[1,256,1024]{2,1,0:T(8,128)} %param.11) | copy-start | bytes 3145732
  90.7 13.3 %copy-start.16 = (f32[4]{0:T(128)S(1)}, f32[4]{0:T(128)}, u32[]{:S(2)}) copy-start(f32[4]{0:T(128)} %rates_ref.3) | copy-start | bytes 52
  90.7 13.3 %copy-start.17 = (f32[4]{0:T(128)S(1)}, f32[4]{0:T(128)}, u32[]{:S(2)}) copy-start(f32[4]{0:T(128)} %decays_ref.3) | copy-start | bytes 52
  90.7 5.8 %collective-permute-start.18 = (bf16[128,1024]{1,0:T(8,128)(2,1)S(1)}, bf16[128,1024]{1,0:T(8,128)(2,1)S(1)}, u32[]{:S(2)}, u32[]{:S(2)}) collective-permute-start(bf16[128,1024]{1,0:T(8,128)(2,1)S(1)} %add_convert_fusion.3.refs_6_), channel_id=1, source_target_pairs={{0,8},{4,12},{8,0},{12,4},{1,9},{5,13},{9,1},{13,5},{2,10},{6,14},... | collective-permute-start | bytes 786440 | tf_op jit(solution)/shard_map/ppermute | solution.py:213
  91.1 12.9 %collective-permute-start.22 = (bf16[128,1024]{1,0:T(8,128)(2,1)S(1)}, bf16[128,1024]{1,0:T(8,128)(2,1)S(1)}, u32[]{:S(2)}, u32[]{:S(2)}) collective-permute-start(bf16[128,1024]{1,0:T(8,128)(2,1)S(1)} %add_convert_fusion.refs_6_), channel_id=1, source_target_pairs={{0,4},{4,0},{8,12},{12,8},{1,5},{5,1},{9,13},{13,9},{2,6},{6,2},{1... | collective-permute-start | bytes 786440 | tf_op jit(solution)/shard_map/ppermute | solution.py:214
  93.4 10.6 %collective-permute-start.24 = (bf16[128,1024]{1,0:T(8,128)(2,1)S(1)}, bf16[128,1024]{1,0:T(8,128)(2,1)S(1)}, u32[]{:S(2)}, u32[]{:S(2)}) collective-permute-start(bf16[128,1024]{1,0:T(8,128)(2,1)S(1)} %collective-permute-done.23.refs_8_), channel_id=1, source_target_pairs={{0,4},{4,0},{8,12},{12,8},{1,5},{5,1},{9,13},{13,9},{2,6},{6,2},{1... | collective-permute-start | bytes 786440 | tf_op jit(solution)/shard_map/ppermute | solution.py:215
  93.4 14.1 %collective-permute-start.17 = (bf16[128,1024]{1,0:T(8,128)(2,1)S(1)}, bf16[128,1024]{1,0:T(8,128)(2,1)S(1)}, u32[]{:S(2)}, u32[]{:S(2)}) collective-permute-start(bf16[128,1024]{1,0:T(8,128)(2,1)S(1)} %add_convert_fusion.3.refs_6_), channel_id=1, source_target_pairs={{0,4},{4,0},{8,12},{12,8},{1,5},{5,1},{9,13},{13,9},{2,6},{6,2},{1... | collective-permute-start | bytes 786440 | tf_op jit(solution)/shard_map/ppermute | solution.py:214
  96.6 10.9 %collective-permute-start.19 = (bf16[128,1024]{1,0:T(8,128)(2,1)S(1)}, bf16[128,1024]{1,0:T(8,128)(2,1)S(1)}, u32[]{:S(2)}, u32[]{:S(2)}) collective-permute-start(bf16[128,1024]{1,0:T(8,128)(2,1)S(1)} %collective-permute-done.18.refs_8_), channel_id=1, source_target_pairs={{0,4},{4,0},{8,12},{12,8},{1,5},{5,1},{9,13},{13,9},{2,6},{6,2},{1... | collective-permute-start | bytes 786440 | tf_op jit(solution)/shard_map/ppermute | solution.py:215
  (14 other events, 63.8 us)

commit v3 on v2

--- a/solution.py
+++ b/solution.py
@@ -18,15 +18,13 @@
 ANY = pl.BlockSpec(memory_space=pl.ANY)
 
 
-def cost(flops, moved):
-    return pl.CostEstimate(flops=flops, bytes_accessed=moved, transcendentals=0)
-
-
-def partial_kernel(n, chains, scale, where_ref, context_ref, cotangent_ref, *refs):
+SMALL = pl.CostEstimate(flops=0, bytes_accessed=1024, transcendentals=0)
+
+
+def partial_kernel(n, scale, order, where_ref, context_ref, cotangent_ref, *refs):
     blocks, (product, sems) = refs[:-2], refs[-2:]
     width = product.shape[0]
     rows = width // n
-    part = rows // chains
     me = where_ref[0]
     tile = min(256, width)
     for start in range(0, width, tile):
@@ -35,47 +33,94 @@
             (((0,), (0,)), ((), ())), preferred_element_type=jnp.float32,
         )
     copies = []
-    for i in range(n):
-        for c in range(chains):
-            first_row = pl.multiple_of(lax.rem(me + i, n) * rows + c * part, part)
-            copies.append(pltpu.make_async_copy(
-                product.at[pl.ds(first_row, part), :], blocks[i * chains + c], sems.at[i * chains + c]
-            ))
-            copies[-1].start()
+    for k, ahead in enumerate(order):
+        first_row = pl.multiple_of(lax.rem(me + ahead, n) * rows, rows)
+        copies.append(pltpu.make_async_copy(product.at[pl.ds(first_row, rows), :], blocks[k], sems.at[k]))
+        copies[-1].start()
     for copy in copies:
         copy.wait()
 
 
-def partial_blocks(n, chains, scale, where, context_rows, cotangent):
-    tokens, width = context_rows.shape
-    depth = cotangent.shape[1]
-    part = width // n // chains
-    return pl.pallas_call(
-        functools.partial(partial_kernel, n, chains, scale),
-        out_shape=[jax.ShapeDtypeStruct((part, depth), jnp.float32)] * (n * chains),
+def partial_blocks(n, scale, order, where, context_rows, cotangent):
+    width, depth = context_rows.shape[1], cotangent.shape[1]
+    return pl.pallas_call(
+        functools.partial(partial_kernel, n, scale, order),
+        out_shape=[jax.ShapeDtypeStruct((width // n, depth), jnp.float32)] * len(order),
         in_specs=[SMEM, VMEM, VMEM],
-        out_specs=[ANY] * (n * chains),
-        scratch_shapes=[pltpu.VMEM((width, depth), jnp.float32), pltpu.SemaphoreType.DMA((n * chains,))],
+        out_specs=[ANY] * len(order),
+        scratch_shapes=[pltpu.VMEM((width, depth), jnp.float32), pltpu.SemaphoreType.DMA((len(order),))],
         compiler_params=pltpu.CompilerParams(vmem_limit_bytes=20 * MIB),
-        cost_estimate=cost(2 * tokens * width * depth, 6 * MIB),
+        cost_estimate=SMALL,
         name="partial_blocks",
     )(where, context_rows, cotangent)
 
 
-def columns_kernel(n, chains, scale, where_ref, cotangent_ref, *refs):
+def send_kernel(slot, n, to_right, where_ref, arrived_ref, term_ref, out_ref):
+    place = where_ref[0] if to_right else n - 1 - where_ref[0]
+    forwards = place >= slot - 1
+
+    @pl.when(forwards)
+    def _():
+        out_ref[...] = arrived_ref[...]
+
+    @pl.when(jnp.logical_not(forwards))
+    def _():
+        @pl.loop(0, out_ref.shape[0] // 16)
+        def _(i):
+            at = pl.ds(pl.multiple_of(i * 16, 16), 16)
+            out_ref[at, :] = (arrived_ref[at, :].astype(jnp.float32) + term_ref[at, :]).astype(out_ref.dtype)
+
+
+def to_send(slot, n, to_right, where, arrived, term, c, part):
+    block = pl.BlockSpec((part, arrived.shape[1]), lambda i: (c, 0))
+    return pl.pallas_call(
+        functools.partial(send_kernel, slot, n, to_right),
+        grid=(1,),
+        out_shape=jax.ShapeDtypeStruct((part, arrived.shape[1]), arrived.dtype),
+        in_specs=[SMEM, block, block],
+        out_specs=pl.BlockSpec((part, arrived.shape[1]), lambda i: (0, 0)),
+        compiler_params=pltpu.CompilerParams(vmem_limit_bytes=8 * MIB),
+        cost_estimate=SMALL,
+        name="to_send",
+    )(where, arrived, term)
+
+
+def grad_kernel(term_ref, left_ref, right_ref, _, out_ref):
+    @pl.loop(0, out_ref.shape[0] // 16)
+    def _(i):
+        at = pl.ds(pl.multiple_of(i * 16, 16), 16)
+        arrived = left_ref[at, :].astype(jnp.float32) + right_ref[at, :].astype(jnp.float32)
+        out_ref[at, :] = (term_ref[at, :] + arrived).astype(out_ref.dtype)
+
+
+def summed_grad(term, from_left, from_right, after, c):
+    part, depth = from_left.shape
+    own = pl.BlockSpec((part, depth), lambda i: (c, 0))
+    block = pl.BlockSpec((part, depth), lambda i: (0, 0))
+    return pl.pallas_call(
+        grad_kernel,
+        grid=(1,),
+        out_shape=jax.ShapeDtypeStruct((part, depth), from_left.dtype),
+        in_specs=[own, block, block, ANY],
+        out_specs=block,
+        compiler_params=pltpu.CompilerParams(vmem_limit_bytes=8 * MIB),
+        cost_estimate=SMALL,
+        name="summed_grad",
+    )(term, from_left, from_right, after)
+
+
+def columns_kernel(n, scale, where_ref, cotangent_ref, *refs):
     blocks, (out_ref, full, sems) = refs[:-3], refs[-3:]
     rows = full.shape[0] // n
-    part = rows // chains
     me = where_ref[0]
     moves = []
     for k in range(2 * n - 1):
         shard = me + (k - (n - 1))
         there = jnp.logical_and(shard >= 0, shard < n)
-        for c in range(chains):
-            first_row = pl.multiple_of(jnp.clip(shard, 0, n - 1) * rows + c * part, part)
-            moves.append((there, pltpu.make_async_copy(
-                blocks[k * chains + c], full.at[pl.ds(first_row, part), :], sems.at[k * chains + c]
-            )))
+        first_row = pl.multiple_of(jnp.clip(shard, 0, n - 1) * rows, rows)
+        moves.append((there, pltpu.make_async_copy(
+            blocks[k], full.at[pl.ds(first_row, rows), :], sems.at[k]
+        )))
     for there, copy in moves:
         pl.when(there)(copy.start)
     for there, copy in moves:
@@ -89,17 +134,17 @@
         )).astype(out_ref.dtype)
 
 
-def columns(n, chains, scale, where, cotangent, blocks):
+def columns(n, scale, where, cotangent, blocks):
     tokens, depth = cotangent.shape
-    width = blocks[0].shape[0] * n * chains
-    return pl.pallas_call(
-        functools.partial(columns_kernel, n, chains, scale),
+    width = blocks[0].shape[0] * n
+    return pl.pallas_call(
+        functools.partial(columns_kernel, n, scale),
         out_shape=jax.ShapeDtypeStruct((tokens, width), cotangent.dtype),
         in_specs=[SMEM, VMEM] + [ANY] * len(blocks),
         out_specs=VMEM,
         scratch_shapes=[pltpu.VMEM((width, depth), cotangent.dtype), pltpu.SemaphoreType.DMA((len(blocks),))],
         compiler_params=pltpu.CompilerParams(vmem_limit_bytes=20 * MIB),
-        cost_estimate=cost(2 * tokens * width * depth, 4 * MIB),
+        cost_estimate=SMALL,
         name="context_grad",
     )(where, cotangent, *blocks)
 
@@ -188,7 +233,7 @@
         ],
         input_output_aliases={before + k: k for k in range(len(filled))},
         compiler_params=pltpu.CompilerParams(vmem_limit_bytes=16 * MIB),
-        cost_estimate=cost(30 * part * depth, 26 * part * depth),
+        cost_estimate=SMALL,
         name="adam",
     )(where, *tables, *own, *donated, *grads, *filled)
 
@@ -215,43 +260,35 @@
         return mate, across, lax.ppermute(across, "member", swap_mates)
 
     half_weight = weight[0].astype(half)
-    pieces = [half_weight[c * part:(c + 1) * part] for c in range(chains)]
-    partial = partial_blocks(n, chains, scale, where, context_rows, cotangent)
-
-    from_left, from_right = [pieces], [pieces]
-    for slot in range(1, n + 1):
+    order = list(range(n - 1, 0, -1)) + list(range(1, n)) + [0]
+    terms = partial_blocks(n, scale, order, where, context_rows, cotangent)
+    right_terms, left_terms, own_term = terms[:n - 1], terms[n - 1:-1], terms[-1]
+
+    from_left, from_right = [half_weight], [half_weight]
+    for slot in range(1, n):
         right, left = from_left[-1], from_right[-1]
         if slot > 1:
-            def added(arrived, block, forwards):
-                term = jnp.where(forwards, 0.0, block)
-                return (arrived.astype(jnp.float32) + term).astype(half)
-
-            right = [
-                added(right[c], partial[(n + 1 - slot) * chains + c], me >= slot - 1)
-                for c in range(chains)
-            ]
-            left = [
-                added(left[c], partial[(slot - 1) * chains + c], n - 1 - me >= slot - 1)
-                for c in range(chains)
-            ]
-        arrived = [
-            (lax.ppermute(right[c], "shard", to_right), lax.ppermute(left[c], "shard", to_left))
-            for c in range(chains)
-        ]
-        from_left.append([pair[0] for pair in arrived])
-        from_right.append([pair[1] for pair in arrived])
+            right = to_send(slot, n, True, where, right, right_terms[slot - 2], 0, rows)
+            left = to_send(slot, n, False, where, left, left_terms[slot - 2], 0, rows)
+        from_left.append(lax.ppermute(right, "shard", to_right))
+        from_right.append(lax.ppermute(left, "shard", to_left))
+    last_left, last_right = [], []
+    for c in range(chains):
+        right = to_send(n, n, True, where, from_left[-1], right_terms[-1], c, part)
+        left = to_send(n, n, False, where, from_right[-1], left_terms[-1], c, part)
+        last_left.append(lax.ppermute(right, "shard", to_right))
+        last_right.append(lax.ppermute(left, "shard", to_left))
 
     state = jnp.concatenate([half_weight, first[0].astype(half), second[0].astype(half)], axis=0)
     donated = from_members(state)
 
-    blocks = from_left[n - 1:0:-1] + [pieces] + from_right[1:n]
-    context_grad = columns(n, chains, scale, where, cotangent, [b for pair in blocks for b in pair])
+    blocks = from_left[n - 1:0:-1] + [half_weight] + from_right[1:n]
+    context_grad = columns(n, scale, where, cotangent, blocks)
 
     tables = (rates, decays, steps, donor)
     updated = ()
     for c in range(chains):
-        grad = partial[c] + from_left[n][c].astype(jnp.float32) + from_right[n][c].astype(jnp.float32)
-        grad = grad.astype(half)
+        grad = summed_grad(own_term, last_left[c], last_right[c], context_grad, c)
         updated = adam_update(
             c, part, where, tables, (weight[0], first[0], second[0]), donated,
             (grad,) + from_members(grad), updated,

time: 112 us -> 97 us (0.87)
  other arithmetic: 19.2 us -> 4.12 us
  waiting for transfers between devices: 12.2 us -> 25.2 us
  starting transfers between devices: 56.1 us -> 44.4 us
  local copies, waits for them, and re-layouts: 8.77 us -> 3.86 us
  Pallas kernels: 13.6 us -> 17.7 us
    convert_element_type x12 -> x0, other arithmetic: 16.3 us -> none  [the longest x10 16.1 us: added(): return (arrived.astype(jnp.float32) + term).astype(half)]
    ppermute x16 -> x10, starting transfers between devices: 40.6 us -> 26.3 us  [the longest x3 11.6 us: on_device(): from_left.append(lax.ppermute(right, 'shard', to_right))]
    ppermute x3, waiting for transfers between devices: 2.71 us -> 12.5 us  [from_members(): across = lax.ppermute(own, 'member', swap_across)]
    pallas_call x2 -> x12, Pallas kernels: 6.61 us -> 12.7 us  [the longest x8 6.05 us: to_send(): pl.pallas_call(functools.partial(send_kernel, slot, n, to_right), grid=(1...]
    unnamed x42 -> x22, local copies, waits for them, and re-layouts: 8 us -> 3.86 us
    ppermute x16 -> x10, waiting for transfers between devices: 9.45 us -> 12.7 us  [the longest x3 12.6 us: on_device(): from_left.append(lax.ppermute(right, 'shard', to_right))]
    ppermute x3, starting transfers between devices: 1.85 us -> 4.59 us  [from_members(): across = lax.ppermute(own, 'member', swap_across)]
    pallas_call x2, Pallas kernels: 7 us -> 4.98 us  [adam_update(): pl.pallas_call(functools.partial(adam_kernel, chain, part, bool(filled)),...]
  transfers between devices with their start and end apart: 25 -> 19, of which waited for: 5 -> 5; matrix products, arithmetic and copies ran while one was open for 16% -> 0% of each run, Pallas kernels for 9% -> 16%
where the time goes in v3:
time: 97 us; the launch traced here: 96.3 us
  starting transfers between devices  44.4 us (46%)
  waiting for transfers between devices  25.2 us (26%)
  Pallas kernels  17.7 us (18%)
  other arithmetic  4.12 us (4%)
  local copies, waits for them, and re-layouts  3.86 us (4%)
  between operations  1.02 us (1%)
    ppermute x3, waiting for transfers between devices, on_device(): from_left.append(lax.ppermute(right, 'shard', to_right))  12.6 us
    ppermute x3, waiting for transfers between devices, from_members(): across = lax.ppermute(own, 'member', swap_across)  12.5 us
    ppermute x3, starting transfers between devices, on_device(): from_left.append(lax.ppermute(right, 'shard', to_right))  11.6 us
    ppermute x3, starting transfers between devices, from_members(): return (mate, across, lax.ppermute(across, 'member', swap_mates))  8.48 us
    ppermute x2, starting transfers between devices, on_device(): last_left.append(lax.ppermute(right, 'shard', to_right))  8.12 us
    pallas_call x8, Pallas kernels, to_send(): pl.pallas_call(functools.partial(send_kernel, slot, n, to_right), grid=(1...  6.05 us
    ppermute x3, starting transfers between devices, from_members(): mate = lax.ppermute(own, 'member', swap_mates)  5.04 us
    pallas_call x2, Pallas kernels, adam_update(): pl.pallas_call(functools.partial(adam_kernel, chain, part, bool(filled)),...  4.98 us
  transfers between devices with their start and end apart: 19, of which 5 were waited for; matrix products, arithmetic and copies ran while one was open for 0% of the time, Pallas kernels for 16%

profile of v3, /device:TPU:1, one launch (start us, length us, event | category | flops | bytes accessed | tf_op | source)
XLA Modules:
  0.0 96.3 jit_solution(18258334416760702402)
XLA Ops:
  0.6 1.4 %bitcast_convert_fusion.2.refs_3_ = bf16[256,1024]{1,0:T(8,128)(2,1)S(1)} fusion(f32[1,256,1024]{2,1,0:T(8,128)} %param.11), kind=kLoop, calls=%fused_computation.4 | loop fusion | flops 262144 | bytes 1572864 | tf_op jit(solution)/shard_map/convert_element_type | solution.py:262
  2.2 1.4 %bitcast_convert_fusion = (bf16[256,1024]{1,0:T(8,128)(2,1)S(1)}, bf16[256,1024]{1,0:T(8,128)(2,1)S(1)}) fusion(f32[1,256,1024]{2,1,0:T(8,128)} %param.13, f32[1,256,1024]{2,1,0:T(8,128)S(1)} %copy-done), kind=kLoop, calls=%fused_computation.2 | loop fusion | flops 524288 | bytes 3145728 | tf_op jit(solution)/shard_map/convert_element_type | solution.py:282
  3.5 1.3 %pad_maximum_fusion = bf16[768,1024]{1,0:T(8,128)(2,1)} fusion(bf16[256,1024]{1,0:T(8,128)(2,1)S(1)} %get-tuple-element.30, bf16[256,1024]{1,0:T(8,128)(2,1)S(1)} %get-tuple-element.31, bf16[256,1024]{1,0:T(8,128)(2,1)S(1)} %bitcast_convert_fusion.2.refs_3_), kind=kLoop, calls=%fused_computation | loop fusion | flops 4718592 | bytes 3145728 | tf_op jit(solution)/shard_map/concatenate | solution.py:282
  4.8 2.0 %collective-permute-start.7 = (bf16[768,1024]{1,0:T(8,128)(2,1)}, bf16[768,1024]{1,0:T(8,128)(2,1)S(1)}, u32[]{:S(2)}, u32[]{:S(2)}) collective-permute-start(bf16[768,1024]{1,0:T(8,128)(2,1)} %pad_maximum_fusion), channel_id=1, source_target_pairs={{0,8},{4,12},{8,0},{12,4},{1,9},{5,13},{9,1},{13,5},{2,10},{6,14},... | collective-permute-start | bytes 4718600 | tf_op jit(solution)/shard_map/ppermute | solution.py:258
  6.9 4.0 %collective-permute-start = (bf16[256,1024]{1,0:T(8,128)(2,1)S(1)}, bf16[256,1024]{1,0:T(8,128)(2,1)}, u32[]{:S(2)}, u32[]{:S(2)}) collective-permute-start(bf16[256,1024]{1,0:T(8,128)(2,1)S(1)} %bitcast_convert_fusion.2.refs_3_), channel_id=1, source_target_pairs={{0,1},{1,2},{2,3},{4,5},{5,6},{6,7},{8,9},{9,10},{10,11},{12,13},{... | collective-permute-start | bytes 1572872 | tf_op jit(solution)/shard_map/ppermute | solution.py:273
  10.9 1.3 %collective-permute-start.3 = (bf16[256,1024]{1,0:T(8,128)(2,1)S(1)}, bf16[256,1024]{1,0:T(8,128)(2,1)}, u32[]{:S(2)}, u32[]{:S(2)}) collective-permute-start(bf16[256,1024]{1,0:T(8,128)(2,1)S(1)} %bitcast_convert_fusion.2.refs_3_), channel_id=1, source_target_pairs={{1,0},{2,1},{3,2},{5,4},{6,5},{7,6},{9,8},{10,9},{11,10},{13,12},{... | collective-permute-start | bytes 1572872 | tf_op jit(solution)/shard_map/ppermute | solution.py:274
  12.2 1.2 %copy-done.4 = bf16[1,512,1024]{2,1,0:T(8,128)(2,1)S(1)} copy-done((bf16[1,512,1024]{2,1,0:T(8,128)(2,1)S(1)}, bf16[1,512,1024]{2,1,0:T(8,128)(2,1)}, u32[]{:S(2)}) %copy-start.4) | copy-done | bytes 1048600
  13.5 1.2 %copy-done.6 = bf16[1,512,1024]{2,1,0:T(8,128)(2,1)S(1)} copy-done((bf16[1,512,1024]{2,1,0:T(8,128)(2,1)S(1)}, bf16[1,512,1024]{2,1,0:T(8,128)(2,1)}, u32[]{:S(2)}) %copy-start.6) | copy-done | bytes 1048600
  14.7 2.4 %partial_blocks.1 = (f32[256,1024]{1,0:T(8,128)S(1)}, f32[256,1024]{1,0:T(8,128)S(1)}, f32[256,1024]{1,0:T(8,128)S(1)}, f32[256,1024]{1,0:T(8,128)S(1)}, f32[256...) custom-call(s32[2]{0:T(128)S(1)} %pad_add_fusion.where_ref, bf16[512,1024]{1,0:T(8,128)(2,1)S(1)} %bitcast.23, ...), custom_call_target="tpu_custom_call" | custom-call | bytes 1024 | tf_op jit(solution)/shard_map/partial_blocks/pallas_call | solution.py:46
  17.1 3.2 %collective-permute-done.arrived_ref.refs_2_ = bf16[256,1024]{1,0:T(8,128)(2,1)} collective-permute-done((bf16[256,1024]{1,0:T(8,128)(2,1)S(1)}, bf16[256,1024]{1,0:T(8,128)(2,1)}, u32[]{:S(2)}, u32[]{:S(2)}) %collective-permute-start) | collective-permute-done | bytes 524320 | tf_op jit(solution)/shard_map/ppermute | solution.py:273
  20.3 1.2 %to_send.8 = bf16[256,1024]{1,0:T(8,128)(2,1)S(1)} custom-call(s32[2]{0:T(128)S(1)} %pad_add_fusion.where_ref, bf16[256,1024]{1,0:T(8,128)(2,1)} %collective-permute-done.arrived_ref.refs_2_, f32[256,1024]{1,0:T(8,128)S(1)} %get-tuple-element.17.term_ref), custom_call_target="tpu_custom_call" | custom-call | bytes 1024 | tf_op jit(solution)/shard_map/to_send/pallas_call | solution.py:76
  21.6 4.1 %collective-permute-start.1 = (bf16[256,1024]{1,0:T(8,128)(2,1)S(1)}, bf16[256,1024]{1,0:T(8,128)(2,1)S(1)}, u32[]{:S(2)}, u32[]{:S(2)}) collective-permute-start(bf16[256,1024]{1,0:T(8,128)(2,1)S(1)} %to_send.8), channel_id=1, source_target_pairs={{0,1},{1,2},{2,3},{4,5},{5,6},{6,7},{8,9},{9,10},{10,11},{12,13},{... | collective-permute-start | bytes 1572872 | tf_op jit(solution)/shard_map/ppermute | solution.py:273
  26.8 1.3 %collective-permute-start.4 = (bf16[256,1024]{1,0:T(8,128)(2,1)S(1)}, bf16[256,1024]{1,0:T(8,128)(2,1)S(1)}, u32[]{:S(2)}, u32[]{:S(2)}) collective-permute-start(bf16[256,1024]{1,0:T(8,128)(2,1)S(1)} %to_send.10), channel_id=1, source_target_pairs={{1,0},{2,1},{3,2},{5,4},{6,5},{7,6},{9,8},{10,9},{11,10},{13,12},{... | collective-permute-start | bytes 1572872 | tf_op jit(solution)/shard_map/ppermute | solution.py:274
  28.1 2.2 %collective-permute-start.6 = (bf16[768,1024]{1,0:T(8,128)(2,1)}, bf16[768,1024]{1,0:T(8,128)(2,1)S(1)}, u32[]{:S(2)}, u32[]{:S(2)}) collective-permute-start(bf16[768,1024]{1,0:T(8,128)(2,1)} %pad_maximum_fusion), channel_id=1, source_target_pairs={{0,4},{4,0},{8,12},{12,8},{1,5},{5,1},{9,13},{13,9},{2,6},{6,2},{1... | collective-permute-start | bytes 4718600 | tf_op jit(solution)/shard_map/ppermute | solution.py:259
  30.3 10.9 %collective-permute-done.7.refs_4_ = bf16[768,1024]{1,0:T(8,128)(2,1)S(1)} collective-permute-done((bf16[768,1024]{1,0:T(8,128)(2,1)}, bf16[768,1024]{1,0:T(8,128)(2,1)S(1)}, u32[]{:S(2)}, u32[]{:S(2)}) %collective-permute-start.7) | collective-permute-done | bytes 1572896 | tf_op jit(solution)/shard_map/ppermute | solution.py:258
  41.2 1.2 %collective-permute-start.8 = (bf16[768,1024]{1,0:T(8,128)(2,1)S(1)}, bf16[768,1024]{1,0:T(8,128)(2,1)S(1)}, u32[]{:S(2)}, u32[]{:S(2)}) collective-permute-start(bf16[768,1024]{1,0:T(8,128)(2,1)S(1)} %collective-permute-done.7.refs_4_), channel_id=1, source_target_pairs={{0,4},{4,0},{8,12},{12,8},{1,5},{5,1},{9,13},{13,9},{2,6},{6,2},{1... | collective-permute-start | bytes 4718600 | tf_op jit(solution)/shard_map/ppermute | solution.py:260
  43.2 3.5 %collective-permute-start.2 = (bf16[256,1024]{1,0:T(8,128)(2,1)S(1)}, bf16[256,1024]{1,0:T(8,128)(2,1)S(1)}, u32[]{:S(2)}, u32[]{:S(2)}) collective-permute-start(bf16[256,1024]{1,0:T(8,128)(2,1)S(1)} %to_send.9), channel_id=1, source_target_pairs={{0,1},{1,2},{2,3},{4,5},{5,6},{6,7},{8,9},{9,10},{10,11},{12,13},{... | collective-permute-start | bytes 1572872 | tf_op jit(solution)/shard_map/ppermute | solution.py:273
  47.3 1.3 %collective-permute-start.5 = (bf16[256,1024]{1,0:T(8,128)(2,1)S(1)}, bf16[256,1024]{1,0:T(8,128)(2,1)S(1)}, u32[]{:S(2)}, u32[]{:S(2)}) collective-permute-start(bf16[256,1024]{1,0:T(8,128)(2,1)S(1)} %to_send.11), channel_id=1, source_target_pairs={{1,0},{2,1},{3,2},{5,4},{6,5},{7,6},{9,8},{10,9},{11,10},{13,12},{... | collective-permute-start | bytes 1572872 | tf_op jit(solution)/shard_map/ppermute | solution.py:274
  48.6 9.4 %collective-permute-done.2.refs_0_.arrived_ref = bf16[256,1024]{1,0:T(8,128)(2,1)S(1)} collective-permute-done((bf16[256,1024]{1,0:T(8,128)(2,1)S(1)}, bf16[256,1024]{1,0:T(8,128)(2,1)S(1)}, u32[]{:S(2)}, u32[]{:S(2)}) %collective-permute-start.2) | collective-permute-done | bytes 524320 | tf_op jit(solution)/shard_map/ppermute | solution.py:273
  58.6 4.1 %collective-permute-start.14 = (bf16[128,1024]{1,0:T(8,128)(2,1)S(1)}, bf16[128,1024]{1,0:T(8,128)(2,1)S(1)}, u32[]{:S(2)}, u32[]{:S(2)}) collective-permute-start(bf16[128,1024]{1,0:T(8,128)(2,1)S(1)} %to_send.14), channel_id=1, source_target_pairs={{0,1},{1,2},{2,3},{4,5},{5,6},{6,7},{8,9},{9,10},{10,11},{12,13},{... | collective-permute-start | bytes 786440 | tf_op jit(solution)/shard_map/ppermute | solution.py:279
  63.3 1.4 %collective-permute-start.15 = (bf16[128,1024]{1,0:T(8,128)(2,1)S(1)}, bf16[128,1024]{1,0:T(8,128)(2,1)S(1)}, u32[]{:S(2)}, u32[]{:S(2)}) collective-permute-start(bf16[128,1024]{1,0:T(8,128)(2,1)S(1)} %to_send.15), channel_id=1, source_target_pairs={{1,0},{2,1},{3,2},{5,4},{6,5},{7,6},{9,8},{10,9},{11,10},{13,12},{... | collective-permute-start | bytes 786440 | tf_op jit(solution)/shard_map/ppermute | solution.py:280
  65.4 4.0 %collective-permute-start.9 = (bf16[128,1024]{1,0:T(8,128)(2,1)S(1)}, bf16[128,1024]{1,0:T(8,128)(2,1)S(1)}, u32[]{:S(2)}, u32[]{:S(2)}) collective-permute-start(bf16[128,1024]{1,0:T(8,128)(2,1)S(1)} %to_send.12), channel_id=1, source_target_pairs={{0,1},{1,2},{2,3},{4,5},{5,6},{6,7},{8,9},{9,10},{10,11},{12,13},{... | collective-permute-start | bytes 786440 | tf_op jit(solution)/shard_map/ppermute | solution.py:279
  70.0 1.3 %collective-permute-start.10 = (bf16[128,1024]{1,0:T(8,128)(2,1)S(1)}, bf16[128,1024]{1,0:T(8,128)(2,1)S(1)}, u32[]{:S(2)}, u32[]{:S(2)}) collective-permute-start(bf16[128,1024]{1,0:T(8,128)(2,1)S(1)} %to_send.13), channel_id=1, source_target_pairs={{1,0},{2,1},{3,2},{5,4},{6,5},{7,6},{9,8},{10,9},{11,10},{13,12},{... | collective-permute-start | bytes 786440 | tf_op jit(solution)/shard_map/ppermute | solution.py:280
  71.3 4.0 %context_grad.1._ = bf16[512,1024]{1,0:T(8,128)(2,1)} custom-call(s32[2]{0:T(128)S(1)} %pad_add_fusion.where_ref, bf16[512,1024]{1,0:T(8,128)(2,1)S(1)} %bitcast.22, bf16[256,1024]{1,0:T(8,128)(2,1)S(1)} %collective-permute-done.2.refs_0_.arrived_ref, bf16[256,1024]{1,0:T(8,128)(2,1)S(1)} %collective-permute-done.1.arrived_ref.refs_1_, ...), custom_call_target="tpu_custom_call" | custom-call | bytes 1024 | tf_op jit(solution)/shard_map/context_grad/pallas_call | solution.py:140
  75.4 1.2 %copy-done.3 = bf16[512,1024]{1,0:T(8,128)(2,1)S(1)} copy-done((bf16[512,1024]{1,0:T(8,128)(2,1)S(1)}, bf16[512,1024]{1,0:T(8,128)(2,1)}, u32[]{:S(2)}) %copy-start.3) | copy-done | bytes 1048600
  76.8 1.3 %collective-permute-start.17 = (bf16[128,1024]{1,0:T(8,128)(2,1)S(1)}, bf16[128,1024]{1,0:T(8,128)(2,1)S(1)}, u32[]{:S(2)}, u32[]{:S(2)}) collective-permute-start(bf16[128,1024]{1,0:T(8,128)(2,1)S(1)} %summed_grad.3.refs_6_), channel_id=1, source_target_pairs={{0,8},{4,12},{8,0},{12,4},{1,9},{5,13},{9,1},{13,5},{2,10},{6,14},... | collective-permute-start | bytes 786440 | tf_op jit(solution)/shard_map/ppermute | solution.py:258
  78.2 1.3 %collective-permute-start.12 = (bf16[128,1024]{1,0:T(8,128)(2,1)S(1)}, bf16[128,1024]{1,0:T(8,128)(2,1)S(1)}, u32[]{:S(2)}, u32[]{:S(2)}) collective-permute-start(bf16[128,1024]{1,0:T(8,128)(2,1)S(1)} %summed_grad.2.refs_6_), channel_id=1, source_target_pairs={{0,8},{4,12},{8,0},{12,4},{1,9},{5,13},{9,1},{13,5},{2,10},{6,14},... | collective-permute-start | bytes 786440 | tf_op jit(solution)/shard_map/ppermute | solution.py:258
  79.5 2.8 %collective-permute-start.16 = (bf16[128,1024]{1,0:T(8,128)(2,1)S(1)}, bf16[128,1024]{1,0:T(8,128)(2,1)S(1)}, u32[]{:S(2)}, u32[]{:S(2)}) collective-permute-start(bf16[128,1024]{1,0:T(8,128)(2,1)S(1)} %summed_grad.3.refs_6_), channel_id=1, source_target_pairs={{0,4},{4,0},{8,12},{12,8},{1,5},{5,1},{9,13},{13,9},{2,6},{6,2},{1... | collective-permute-start | bytes 786440 | tf_op jit(solution)/shard_map/ppermute | solution.py:259
  83.0 4.7 %collective-permute-start.18 = (bf16[128,1024]{1,0:T(8,128)(2,1)S(1)}, bf16[128,1024]{1,0:T(8,128)(2,1)S(1)}, u32[]{:S(2)}, u32[]{:S(2)}) collective-permute-start(bf16[128,1024]{1,0:T(8,128)(2,1)S(1)} %collective-permute-done.17.refs_8_), channel_id=1, source_target_pairs={{0,4},{4,0},{8,12},{12,8},{1,5},{5,1},{9,13},{13,9},{2,6},{6,2},{1... | collective-permute-start | bytes 786440 | tf_op jit(solution)/shard_map/ppermute | solution.py:260
  88.6 2.6 %collective-permute-start.13 = (bf16[128,1024]{1,0:T(8,128)(2,1)S(1)}, bf16[128,1024]{1,0:T(8,128)(2,1)S(1)}, u32[]{:S(2)}, u32[]{:S(2)}) collective-permute-start(bf16[128,1024]{1,0:T(8,128)(2,1)S(1)} %collective-permute-done.12.refs_8_), channel_id=1, source_target_pairs={{0,4},{4,0},{8,12},{12,8},{1,5},{5,1},{9,13},{13,9},{2,6},{6,2},{1... | collective-permute-start | bytes 786440 | tf_op jit(solution)/shard_map/ppermute | solution.py:260
  91.2 2.5 %adam.2 = (f32[256,1024]{1,0:T(8,128)}, f32[256,1024]{1,0:T(8,128)}, f32[256,1024]{1,0:T(8,128)}) custom-call(s32[2]{0:T(128)S(1)} %pad_add_fusion.where_ref, f32[4]{0:T(128)S(1)} %copy-done.7, f32[4]{0:T(128)S(1)} %copy-done.8, s32[4]{0:T(128)S(1)} %copy-done.9, s32[4]{0:T(128)S(1)} %copy-done.10, f32[256,1024]{1,0:T(8,128)S(1)} %bitcast.18, ...), custom_call_target="tpu_custom_call" | custom-call | bytes 1024 | tf_op jit(solution)/shard_map/adam/pallas_call | solution.py:221
  93.8 2.5 %adam.3 = (f32[256,1024]{1,0:T(8,128)}, f32[256,1024]{1,0:T(8,128)}, f32[256,1024]{1,0:T(8,128)}) custom-call(s32[2]{0:T(128)S(1)} %pad_add_fusion.where_ref, f32[4]{0:T(128)S(1)} %copy-done.7, f32[4]{0:T(128)S(1)} %copy-done.8, s32[4]{0:T(128)S(1)} %copy-done.9, s32[4]{0:T(128)S(1)} %copy-done.10, ...), custom_call_target="tpu_custom_call", output_to_operand_aliasing={{0}: (15, {}), {1}: (16, {}), {2}: (17, {})} | custom-call | bytes 1024 | tf_op jit(solution)/shard_map/adam/pallas_call | solution.py:221
  (46 shorter events, 7.0 us)
Async XLA Ops:
  0.6 1.5 %copy-start = (f32[1,256,1024]{2,1,0:T(8,128)S(1)}, f32[1,256,1024]{2,1,0:T(8,128)}, u32[]{:S(2)}) copy-start(f32[1,256,1024]{2,1,0:T(8,128)} %param.12) | copy-start | bytes 3145732
  4.8 36.4 %collective-permute-start.7 = (bf16[768,1024]{1,0:T(8,128)(2,1)}, bf16[768,1024]{1,0:T(8,128)(2,1)S(1)}, u32[]{:S(2)}, u32[]{:S(2)}) collective-permute-start(bf16[768,1024]{1,0:T(8,128)(2,1)} %pad_maximum_fusion), channel_id=1, source_target_pairs={{0,8},{4,12},{8,0},{12,4},{1,9},{5,13},{9,1},{13,5},{2,10},{6,14},... | collective-permute-start | bytes 4718600 | tf_op jit(solution)/shard_map/ppermute | solution.py:258
  6.9 13.5 %collective-permute-start = (bf16[256,1024]{1,0:T(8,128)(2,1)S(1)}, bf16[256,1024]{1,0:T(8,128)(2,1)}, u32[]{:S(2)}, u32[]{:S(2)}) collective-permute-start(bf16[256,1024]{1,0:T(8,128)(2,1)S(1)} %bitcast_convert_fusion.2.refs_3_), channel_id=1, source_target_pairs={{0,1},{1,2},{2,3},{4,5},{5,6},{6,7},{8,9},{9,10},{10,11},{12,13},{... | collective-permute-start | bytes 1572872 | tf_op jit(solution)/shard_map/ppermute | solution.py:273
  10.9 14.8 %collective-permute-start.3 = (bf16[256,1024]{1,0:T(8,128)(2,1)S(1)}, bf16[256,1024]{1,0:T(8,128)(2,1)}, u32[]{:S(2)}, u32[]{:S(2)}) collective-permute-start(bf16[256,1024]{1,0:T(8,128)(2,1)S(1)} %bitcast_convert_fusion.2.refs_3_), channel_id=1, source_target_pairs={{1,0},{2,1},{3,2},{5,4},{6,5},{7,6},{9,8},{10,9},{11,10},{13,12},{... | collective-permute-start | bytes 1572872 | tf_op jit(solution)/shard_map/ppermute | solution.py:274
  12.2 1.2 %copy-start.4 = (bf16[1,512,1024]{2,1,0:T(8,128)(2,1)S(1)}, bf16[1,512,1024]{2,1,0:T(8,128)(2,1)}, u32[]{:S(2)}) copy-start(bf16[1,512,1024]{2,1,0:T(8,128)(2,1)} %param.10) | copy-start | bytes 3145732
  13.5 1.2 %copy-start.6 = (bf16[1,512,1024]{2,1,0:T(8,128)(2,1)S(1)}, bf16[1,512,1024]{2,1,0:T(8,128)(2,1)}, u32[]{:S(2)}) copy-start(bf16[1,512,1024]{2,1,0:T(8,128)(2,1)} %param.9) | copy-start | bytes 3145732
  21.6 20.9 %collective-permute-start.1 = (bf16[256,1024]{1,0:T(8,128)(2,1)S(1)}, bf16[256,1024]{1,0:T(8,128)(2,1)S(1)}, u32[]{:S(2)}, u32[]{:S(2)}) collective-permute-start(bf16[256,1024]{1,0:T(8,128)(2,1)S(1)} %to_send.8), channel_id=1, source_target_pairs={{0,1},{1,2},{2,3},{4,5},{5,6},{6,7},{8,9},{9,10},{10,11},{12,13},{... | collective-permute-start | bytes 1572872 | tf_op jit(solution)/shard_map/ppermute | solution.py:273
  26.8 19.9 %collective-permute-start.4 = (bf16[256,1024]{1,0:T(8,128)(2,1)S(1)}, bf16[256,1024]{1,0:T(8,128)(2,1)S(1)}, u32[]{:S(2)}, u32[]{:S(2)}) collective-permute-start(bf16[256,1024]{1,0:T(8,128)(2,1)S(1)} %to_send.10), channel_id=1, source_target_pairs={{1,0},{2,1},{3,2},{5,4},{6,5},{7,6},{9,8},{10,9},{11,10},{13,12},{... | collective-permute-start | bytes 1572872 | tf_op jit(solution)/shard_map/ppermute | solution.py:274
  28.1 59.6 %collective-permute-start.6 = (bf16[768,1024]{1,0:T(8,128)(2,1)}, bf16[768,1024]{1,0:T(8,128)(2,1)S(1)}, u32[]{:S(2)}, u32[]{:S(2)}) collective-permute-start(bf16[768,1024]{1,0:T(8,128)(2,1)} %pad_maximum_fusion), channel_id=1, source_target_pairs={{0,4},{4,0},{8,12},{12,8},{1,5},{5,1},{9,13},{13,9},{2,6},{6,2},{1... | collective-permute-start | bytes 4718600 | tf_op jit(solution)/shard_map/ppermute | solution.py:259
  41.2 50.0 %collective-permute-start.8 = (bf16[768,1024]{1,0:T(8,128)(2,1)S(1)}, bf16[768,1024]{1,0:T(8,128)(2,1)S(1)}, u32[]{:S(2)}, u32[]{:S(2)}) collective-permute-start(bf16[768,1024]{1,0:T(8,128)(2,1)S(1)} %collective-permute-done.7.refs_4_), channel_id=1, source_target_pairs={{0,4},{4,0},{8,12},{12,8},{1,5},{5,1},{9,13},{13,9},{2,6},{6,2},{1... | collective-permute-start | bytes 4718600 | tf_op jit(solution)/shard_map/ppermute | solution.py:260
  43.2 14.8 %collective-permute-start.2 = (bf16[256,1024]{1,0:T(8,128)(2,1)S(1)}, bf16[256,1024]{1,0:T(8,128)(2,1)S(1)}, u32[]{:S(2)}, u32[]{:S(2)}) collective-permute-start(bf16[256,1024]{1,0:T(8,128)(2,1)S(1)} %to_send.9), channel_id=1, source_target_pairs={{0,1},{1,2},{2,3},{4,5},{5,6},{6,7},{8,9},{9,10},{10,11},{12,13},{... | collective-permute-start | bytes 1572872 | tf_op jit(solution)/shard_map/ppermute | solution.py:273
  47.3 15.5 %collective-permute-start.5 = (bf16[256,1024]{1,0:T(8,128)(2,1)S(1)}, bf16[256,1024]{1,0:T(8,128)(2,1)S(1)}, u32[]{:S(2)}, u32[]{:S(2)}) collective-permute-start(bf16[256,1024]{1,0:T(8,128)(2,1)S(1)} %to_send.11), channel_id=1, source_target_pairs={{1,0},{2,1},{3,2},{5,4},{6,5},{7,6},{9,8},{10,9},{11,10},{13,12},{... | collective-permute-start | bytes 1572872 | tf_op jit(solution)/shard_map/ppermute | solution.py:274
  58.6 11.4 %collective-permute-start.14 = (bf16[128,1024]{1,0:T(8,128)(2,1)S(1)}, bf16[128,1024]{1,0:T(8,128)(2,1)S(1)}, u32[]{:S(2)}, u32[]{:S(2)}) collective-permute-start(bf16[128,1024]{1,0:T(8,128)(2,1)S(1)} %to_send.14), channel_id=1, source_target_pairs={{0,1},{1,2},{2,3},{4,5},{5,6},{6,7},{8,9},{9,10},{10,11},{12,13},{... | collective-permute-start | bytes 786440 | tf_op jit(solution)/shard_map/ppermute | solution.py:279
  63.3 8.0 %copy-start.5 = (bf16[1,512,1024]{2,1,0:T(8,128)(2,1)S(1)}, bf16[1,512,1024]{2,1,0:T(8,128)(2,1)}, u32[]{:S(2)}) copy-start(bf16[1,512,1024]{2,1,0:T(8,128)(2,1)} %param.10) | copy-start | bytes 3145732
  63.3 12.0 %collective-permute-start.15 = (bf16[128,1024]{1,0:T(8,128)(2,1)S(1)}, bf16[128,1024]{1,0:T(8,128)(2,1)S(1)}, u32[]{:S(2)}, u32[]{:S(2)}) collective-permute-start(bf16[128,1024]{1,0:T(8,128)(2,1)S(1)} %to_send.15), channel_id=1, source_target_pairs={{1,0},{2,1},{3,2},{5,4},{6,5},{7,6},{9,8},{10,9},{11,10},{13,12},{... | collective-permute-start | bytes 786440 | tf_op jit(solution)/shard_map/ppermute | solution.py:280
  65.4 12.6 %collective-permute-start.9 = (bf16[128,1024]{1,0:T(8,128)(2,1)S(1)}, bf16[128,1024]{1,0:T(8,128)(2,1)S(1)}, u32[]{:S(2)}, u32[]{:S(2)}) collective-permute-start(bf16[128,1024]{1,0:T(8,128)(2,1)S(1)} %to_send.12), channel_id=1, source_target_pairs={{0,1},{1,2},{2,3},{4,5},{5,6},{6,7},{8,9},{9,10},{10,11},{12,13},{... | collective-permute-start | bytes 786440 | tf_op jit(solution)/shard_map/ppermute | solution.py:279
  70.0 8.1 %collective-permute-start.10 = (bf16[128,1024]{1,0:T(8,128)(2,1)S(1)}, bf16[128,1024]{1,0:T(8,128)(2,1)S(1)}, u32[]{:S(2)}, u32[]{:S(2)}) collective-permute-start(bf16[128,1024]{1,0:T(8,128)(2,1)S(1)} %to_send.13), channel_id=1, source_target_pairs={{1,0},{2,1},{3,2},{5,4},{6,5},{7,6},{9,8},{10,9},{11,10},{13,12},{... | collective-permute-start | bytes 786440 | tf_op jit(solution)/shard_map/ppermute | solution.py:280
  75.3 1.2 %copy-start.3 = (bf16[512,1024]{1,0:T(8,128)(2,1)S(1)}, bf16[512,1024]{1,0:T(8,128)(2,1)}, u32[]{:S(2)}) copy-start(bf16[512,1024]{1,0:T(8,128)(2,1)} %context_grad.1._) | copy-start | bytes 3145732
  76.7 14.5 %copy-start.1 = (f32[1,256,1024]{2,1,0:T(8,128)S(1)}, f32[1,256,1024]{2,1,0:T(8,128)}, u32[]{:S(2)}) copy-start(f32[1,256,1024]{2,1,0:T(8,128)} %param.13) | copy-start | bytes 3145732
  76.7 14.5 %copy-start.2 = (f32[1,256,1024]{2,1,0:T(8,128)S(1)}, f32[1,256,1024]{2,1,0:T(8,128)}, u32[]{:S(2)}) copy-start(f32[1,256,1024]{2,1,0:T(8,128)} %param.11) | copy-start | bytes 3145732
  76.7 14.5 %copy-start.7 = (f32[4]{0:T(128)S(1)}, f32[4]{0:T(128)}, u32[]{:S(2)}) copy-start(f32[4]{0:T(128)} %rates_ref.3) | copy-start | bytes 52
  76.7 14.5 %copy-start.8 = (f32[4]{0:T(128)S(1)}, f32[4]{0:T(128)}, u32[]{:S(2)}) copy-start(f32[4]{0:T(128)} %decays_ref.3) | copy-start | bytes 52
  76.7 14.5 %copy-start.9 = (s32[4]{0:T(128)S(1)}, s32[4]{0:T(128)}, u32[]{:S(2)}) copy-start(s32[4]{0:T(128)} %steps_ref.3) | copy-start | bytes 52
  76.8 14.5 %copy-start.10 = (s32[4]{0:T(128)S(1)}, s32[4]{0:T(128)}, u32[]{:S(2)}) copy-start(s32[4]{0:T(128)} %donor_ref.3) | copy-start | bytes 52
  76.8 6.2 %collective-permute-start.17 = (bf16[128,1024]{1,0:T(8,128)(2,1)S(1)}, bf16[128,1024]{1,0:T(8,128)(2,1)S(1)}, u32[]{:S(2)}, u32[]{:S(2)}) collective-permute-start(bf16[128,1024]{1,0:T(8,128)(2,1)S(1)} %summed_grad.3.refs_6_), channel_id=1, source_target_pairs={{0,8},{4,12},{8,0},{12,4},{1,9},{5,13},{9,1},{13,5},{2,10},{6,14},... | collective-permute-start | bytes 786440 | tf_op jit(solution)/shard_map/ppermute | solution.py:258
  78.2 10.4 %collective-permute-start.12 = (bf16[128,1024]{1,0:T(8,128)(2,1)S(1)}, bf16[128,1024]{1,0:T(8,128)(2,1)S(1)}, u32[]{:S(2)}, u32[]{:S(2)}) collective-permute-start(bf16[128,1024]{1,0:T(8,128)(2,1)S(1)} %summed_grad.2.refs_6_), channel_id=1, source_target_pairs={{0,8},{4,12},{8,0},{12,4},{1,9},{5,13},{9,1},{13,5},{2,10},{6,14},... | collective-permute-start | bytes 786440 | tf_op jit(solution)/shard_map/ppermute | solution.py:258
  79.5 11.7 %collective-permute-start.16 = (bf16[128,1024]{1,0:T(8,128)(2,1)S(1)}, bf16[128,1024]{1,0:T(8,128)(2,1)S(1)}, u32[]{:S(2)}, u32[]{:S(2)}) collective-permute-start(bf16[128,1024]{1,0:T(8,128)(2,1)S(1)} %summed_grad.3.refs_6_), channel_id=1, source_target_pairs={{0,4},{4,0},{8,12},{12,8},{1,5},{5,1},{9,13},{13,9},{2,6},{6,2},{1... | collective-permute-start | bytes 786440 | tf_op jit(solution)/shard_map/ppermute | solution.py:259
  83.0 8.2 %collective-permute-start.18 = (bf16[128,1024]{1,0:T(8,128)(2,1)S(1)}, bf16[128,1024]{1,0:T(8,128)(2,1)S(1)}, u32[]{:S(2)}, u32[]{:S(2)}) collective-permute-start(bf16[128,1024]{1,0:T(8,128)(2,1)S(1)} %collective-permute-done.17.refs_8_), channel_id=1, source_target_pairs={{0,4},{4,0},{8,12},{12,8},{1,5},{5,1},{9,13},{13,9},{2,6},{6,2},{1... | collective-permute-start | bytes 786440 | tf_op jit(solution)/shard_map/ppermute | solution.py:260
  87.7 6.0 %collective-permute-start.11 = (bf16[128,1024]{1,0:T(8,128)(2,1)S(1)}, bf16[128,1024]{1,0:T(8,128)(2,1)S(1)}, u32[]{:S(2)}, u32[]{:S(2)}) collective-permute-start(bf16[128,1024]{1,0:T(8,128)(2,1)S(1)} %summed_grad.2.refs_6_), channel_id=1, source_target_pairs={{0,4},{4,0},{8,12},{12,8},{1,5},{5,1},{9,13},{13,9},{2,6},{6,2},{1... | collective-permute-start | bytes 786440 | tf_op jit(solution)/shard_map/ppermute | solution.py:259
  88.6 5.1 %collective-permute-start.13 = (bf16[128,1024]{1,0:T(8,128)(2,1)S(1)}, bf16[128,1024]{1,0:T(8,128)(2,1)S(1)}, u32[]{:S(2)}, u32[]{:S(2)}) collective-permute-start(bf16[128,1024]{1,0:T(8,128)(2,1)S(1)} %collective-permute-done.12.refs_8_), channel_id=1, source_target_pairs={{0,4},{4,0},{8,12},{12,8},{1,5},{5,1},{9,13},{13,9},{2,6},{6,2},{1... | collective-permute-start | bytes 786440 | tf_op jit(solution)/shard_map/ppermute | solution.py:260

commit v4 on v3

v4 whole, which is shorter than its diff:
```python
import functools
import math

import jax
import jax.numpy as jnp
from jax import lax
from jax.experimental import pallas as pl
from jax.experimental.pallas import tpu as pltpu
from jax.sharding import PartitionSpec as P

beta_one = 0.9
beta_two = 0.999
epsilon = 1e-08

MIB = 1 << 20
SMEM = pl.BlockSpec(memory_space=pltpu.SMEM)
VMEM = pl.BlockSpec(memory_space=pltpu.VMEM)
ANY = pl.BlockSpec(memory_space=pl.ANY)


SMALL = pl.CostEstimate(flops=0, bytes_accessed=1024, transcendentals=0)


def halves_kernel(parts, weight_ref, first_ref, second_ref, state_ref, *own_refs):
    rows = weight_ref.shape[0]
    for (start, size), own_ref in zip(parts, own_refs):
        own_ref[...] = weight_ref[start:start + size, :].astype(own_ref.dtype)
    for k, ref in enumerate((weight_ref, first_ref, second_ref)):
        state_ref[k * rows:(k + 1) * rows, :] = ref[...].astype(state_ref.dtype)


def halves(parts, weight, first, second):
    rows, depth = weight.shape
    sizes = [3 * rows] + [size for _, size in parts]
    return pl.pallas_call(
        functools.partial(halves_kernel, parts),
        out_shape=[jax.ShapeDtypeStruct((size, depth), jnp.bfloat16) for size in sizes],
        in_specs=[VMEM] * 3,
        out_specs=[VMEM] * len(sizes),
        compiler_params=pltpu.CompilerParams(vmem_limit_bytes=12 * MIB),
        cost_estimate=SMALL,
        name="halves",
    )(weight, first, second)


def source_of(member, donor_ref):
    donor = donor_ref[member]
    return jnp.where(donor >= 0, donor, member)


def pick_kernel(where_ref, donor_ref, own_ref, mate_ref, after_ref, out_ref, sem):
    member = where_ref[1]
    wants_mate = source_of(jnp.bitwise_xor(member, 2), donor_ref) == jnp.bitwise_xor(member, 1)
    for ref, wanted in ((own_ref, jnp.logical_not(wants_mate)), (mate_ref, wants_mate)):
        @pl.when(wanted)
        def _():
            copy = pltpu.make_async_copy(ref, out_ref, sem.at[0])
            copy.start()
            copy.wait()


def pick(where, donor, own, mate, after):
    return pl.pallas_call(
        pick_kernel,
        out_shape=jax.ShapeDtypeStruct(own.shape, own.dtype),
        in_specs=[SMEM, SMEM, ANY, ANY, ANY],
        out_specs=ANY,
        scratch_shapes=[pltpu.SemaphoreType.DMA((1,))],
        cost_estimate=SMALL,
        name="pick",
    )(where, donor, own, mate, after)


def partial_kernel(n, scale, parts, order, where_ref, context_ref, cotangent_ref, *refs):
    blocks, (product, sems) = refs[:-2], refs[-2:]
    width = product.shape[0]
    rows = width // n
    me = where_ref[0]
    even = lax.rem(me, 2) == 0
    tile = min(256, width)
    for start in range(0, width, tile):
        product[start:start + tile, :] = scale * lax.dot_general(
            context_ref[:, start:start + tile], cotangent_ref[...],
            (((0,), (0,)), ((), ())), preferred_element_type=jnp.float32,
        )
    copies = []
    for k, (if_even, if_odd) in enumerate(order):
        block = lax.rem(me + jnp.where(even, if_even, if_odd), n)
        for c, (first, size) in enumerate(parts):
            at = k * len(parts) + c
            first_row = pl.multiple_of(block * rows + first, 8)
            copies.append(pltpu.make_async_copy(
                product.at[pl.ds(first_row, size), :], blocks[at], sems.at[at]
            ))
            copies[-1].start()
    for copy in copies:
        copy.wait()


def partial_blocks(n, scale, parts, order, where, context_rows, cotangent):
    width, depth = context_rows.shape[1], cotangent.shape[1]
    outs = len(order) * len(parts)
    flat = pl.pallas_call(
        functools.partial(partial_kernel, n, scale, parts, order),
        out_shape=[jax.ShapeDtypeStruct((size, depth), jnp.float32) for _, size in parts] * len(order),
        in_specs=[SMEM, VMEM, VMEM],
        out_specs=[ANY] * outs,
        scratch_shapes=[pltpu.VMEM((width, depth), jnp.float32), pltpu.SemaphoreType.DMA((outs,))],
        compiler_params=pltpu.CompilerParams(vmem_limit_bytes=20 * MIB),
        cost_estimate=SMALL,
        name="partial_blocks",
    )(where, context_rows, cotangent)
    return [flat[k * len(parts):(k + 1) * len(parts)] for k in range(len(order))]


def send_kernel(slot, n, swap, where_ref, arrived_ref, term_ref, after_ref, out_ref):
    me = where_ref[0]
    place = jnp.where(lax.rem(me + swap, 2) == 0, me, n - 1 - me)
    forwards = place >= slot - 1

    @pl.when(forwards)
    def _():
        out_ref[...] = arrived_ref[...]

    @pl.when(jnp.logical_not(forwards))
    def _():
        @pl.loop(0, out_ref.shape[0] // 16)
        def _(i):
            at = pl.ds(pl.multiple_of(i * 16, 16), 16)
            out_ref[at, :] = (arrived_ref[at, :].astype(jnp.float32) + term_ref[at, :]).astype(out_ref.dtype)


def to_send(slot, n, swap, where, arrived, term, after):
    return pl.pallas_call(
        functools.partial(send_kernel, slot, n, swap),
        out_shape=jax.ShapeDtypeStruct(arrived.shape, arrived.dtype),
        in_specs=[SMEM, VMEM, VMEM, ANY],
        out_specs=VMEM,
        compiler_params=pltpu.CompilerParams(vmem_limit_bytes=8 * MIB),
        cost_estimate=SMALL,
        name="to_send",
    )(where, arrived, term, after)


def grad_kernel(term_ref, one_ref, other_ref, after_ref, out_ref):
    @pl.loop(0, out_ref.shape[0] // 16)
    def _(i):
        at = pl.ds(pl.multiple_of(i * 16, 16), 16)
        arrived = one_ref[at, :].astype(jnp.float32) + other_ref[at, :].astype(jnp.float32)
        out_ref[at, :] = (term_ref[at, :] + arrived).astype(out_ref.dtype)


def summed_grad(term, one, other, after):
    return pl.pallas_call(
        grad_kernel,
        out_shape=jax.ShapeDtypeStruct(one.shape, one.dtype),
        in_specs=[VMEM, VMEM, VMEM, ANY],
        out_specs=VMEM,
        compiler_params=pltpu.CompilerParams(vmem_limit_bytes=8 * MIB),
        cost_estimate=SMALL,
        name="summed_grad",
    )(term, one, other, after)


def columns_kernel(n, scale, parts, where_ref, cotangent_ref, after_ref, *refs):
    blocks, (out_ref, token_ref, full, result, sems, out_sems) = refs[:-6], refs[-6:]
    token_ref[...] = jnp.zeros_like(token_ref)
    width = full.shape[0]
    rows = width // n
    me = where_ref[0]
    even = lax.rem(me, 2) == 0
    moves = []
    for k in range(2 * n - 1):
        slot, swap = (k + 1) // 2, (k + 1) % 2
        shard = me + (jnp.where(even, slot, -slot) if swap == 0 else jnp.where(even, -slot, slot))
        there = jnp.logical_and(shard >= 0, shard < n)
        for c, (first, size) in enumerate(parts):
            at = k * len(parts) + c
            first_row = pl.multiple_of(jnp.clip(shard, 0, n - 1) * rows + first, 8)
            moves.append((there, pltpu.make_async_copy(
                blocks[at], full.at[pl.ds(first_row, size), :], sems.at[at]
            )))
    for there, copy in moves:
        pl.when(there)(copy.start)
    for there, copy in moves:
        pl.when(there)(copy.wait)
    tile = min(256, width)
    writes = []
    for i, start in enumerate(range(0, width, tile)):
        result[:, start:start + tile] = (scale * lax.dot_general(
            cotangent_ref[...], full[start:start + tile, :],
            (((1,), (1,)), ((), ())), preferred_element_type=jnp.float32,
        )).astype(out_ref.dtype)
        writes.append(pltpu.make_async_copy(
            result.at[:, start:start + tile], out_ref.at[:, start:start + tile], out_sems.at[i]
        ))
        writes[-1].start()
    for write in writes:
        write.wait()


def columns(n, scale, parts, where, cotangent, after, blocks):
    tokens, depth = cotangent.shape
    width = n * sum(size for _, size in parts)
    return pl.pallas_call(
        functools.partial(columns_kernel, n, scale, parts),
        out_shape=[
            jax.ShapeDtypeStruct((tokens, width), cotangent.dtype), jax.ShapeDtypeStruct((8, 128), jnp.float32)
        ],
        in_specs=[SMEM, VMEM, ANY] + [ANY] * len(blocks),
        out_specs=[pl.BlockSpec(memory_space=pltpu.HBM), VMEM],
        scratch_shapes=[
            pltpu.VMEM((width, depth), cotangent.dtype),
            pltpu.VMEM((tokens, width), cotangent.dtype),
            pltpu.SemaphoreType.DMA((len(blocks),)),
            pltpu.SemaphoreType.DMA((width // min(256, width),)),
        ],
        compiler_params=pltpu.CompilerParams(vmem_limit_bytes=20 * MIB),
        cost_estimate=SMALL,
        name="context_grad",
    )(where, cotangent, after, *blocks)


def adam_kernel(first_row, part, filled, where_ref, rates_ref, decays_ref, steps_ref, donor_ref, *refs):
    own, donated, grads = refs[:3], refs[3:5], refs[5:8]
    refs = refs[9 + (3 if filled else 0):]
    outs, (kept, taken, grad, stepped, sems, out_sems) = refs[:3], refs[3:]
    rows = own[0].shape[0]
    member = where_ref[1]
    source = source_of(member, donor_ref)
    way = jnp.minimum(jnp.bitwise_xor(source, member), 2)
    rate, decay = rates_ref[source], decays_ref[source]
    count = jnp.full((1, grad.shape[1]), (steps_ref[source] + 1).astype(jnp.float32))
    scale_one = 1.0 / (1.0 - jnp.exp(count * math.log(beta_one)))
    scale_two = 1.0 / (1.0 - jnp.exp(count * math.log(beta_two)))
    mine = pl.ds(first_row, part)

    def own_copy(k):
        return pltpu.make_async_copy(own[k].at[mine, :], kept.at[k], sems.at[k])

    def donated_copy(w, k):
        return pltpu.make_async_copy(
            donated[w - 1].at[pl.ds(k * rows + first_row, part), :], taken.at[k], sems.at[k]
        )

    def grad_copy(w):
        return pltpu.make_async_copy(grads[w], grad, sems.at[3])

    def step(i, from_own):
        at = pl.ds(pl.multiple_of(i * 16, 16), 16)
        load = lambda k: kept[k, at, :] if from_own else taken[k, at, :].astype(jnp.float32)
        g = grad[at, :].astype(jnp.float32)
        w = load(0)
        first_step = beta_one * load(1) + (1.0 - beta_one) * g
        second_step = beta_two * load(2) + (1.0 - beta_two) * g * g
        ratio = (first_step * scale_one) / (jnp.sqrt(second_step * scale_two) + epsilon)
        stepped[0, at, :] = w - rate * (ratio + decay * w)
        stepped[1, at, :] = first_step
        stepped[2, at, :] = second_step

    for w in range(3):
        @pl.when(way == w)
        def _():
            grad_copy(w).start()
            for k in range(3):
                (own_copy(k) if w == 0 else donated_copy(w, k)).start()
            grad_copy(w).wait()
            for k in range(3):
                (own_copy(k) if w == 0 else donated_copy(w, k)).wait()

    @pl.when(way == 0)
    def _():
        pl.loop(0, part // 16)(lambda i: step(i, True))

    @pl.when(way != 0)
    def _():
        pl.loop(0, part // 16)(lambda i: step(i, False))

    writes = [
        pltpu.make_async_copy(stepped.at[k], outs[k].at[mine, :], out_sems.at[k]) for k in range(3)
    ]
    for write in writes:
        write.start()
    for write in writes:
        write.wait()


def adam_update(first_row, part, where, tables, own, donated, grads, after, filled):
    rows, depth = own[0].shape
    shape = jax.ShapeDtypeStruct((rows, depth), jnp.float32)
    before = 5 + 3 + 2 + 3 + 1
    return pl.pallas_call(
        functools.partial(adam_kernel, first_row, part, bool(filled)),
        out_shape=[shape] * 3,
        in_specs=[SMEM] * 5 + [ANY] * (9 + len(filled)),
        out_specs=[ANY] * 3,
        scratch_shapes=[
            pltpu.VMEM((3, part, depth), jnp.float32),
            pltpu.VMEM((3, part, depth), jnp.bfloat16),
            pltpu.VMEM((part, depth), jnp.bfloat16),
            pltpu.VMEM((3, part, depth), jnp.float32),
            pltpu.SemaphoreType.DMA((4,)),
            pltpu.SemaphoreType.DMA((3,)),
        ],
        input_output_aliases={before + k: k for k in range(len(filled))},
        compiler_params=pltpu.CompilerParams(vmem_limit_bytes=16 * MIB),
        cost_estimate=SMALL,
        name="adam",
    )(where, *tables, *own, *donated, *grads, after, *filled)


def on_device(n, members, context, out_grad, weight, first, second, rates, decays, steps, donor):
    context_rows = context[0]
    cotangent = out_grad[0]
    scale = context_rows.shape[1] ** (-0.5)
    rows = weight.shape[1]
    chains = 2 if rows % 32 == 0 else 1
    parts = [(c * rows // chains, rows // chains) for c in range(chains)]
    where = jnp.stack([lax.axis_index("shard"), lax.axis_index("member")]).astype(jnp.int32)

    swap_across = [(m, m ^ 2) for m in range(members)]
    swap_mates = [(m, m ^ 1) for m in range(members)]
    swaps = []
    for swap in range(2):
        pairs = [(s, s + 1) for s in range(swap, n - 1, 2)]
        swaps.append(pairs + [(b, a) for a, b in pairs])

    state, *own = halves(parts, weight[0], first[0], second[0])
    order = []
    for slot in range(2, n + 1):
        order += [(n + 1 - slot, slot - 1), (slot - 1, n + 1 - slot)]
    terms = partial_blocks(n, scale, parts, order + [(0, 0)], where, context_rows, cotangent)

    arrived = [[own, own]]
    for slot in range(1, n + 1):
        now = [[], []]
        for c in range(len(parts)):
            for swap in range(2):
                block = arrived[-1][1 - swap][c]
                if slot > 1:
                    block = to_send(slot, n, swap, where, block, terms[2 * (slot - 2) + swap][c], sent)
                now[swap].append(lax.ppermute(block, "shard", swaps[swap]))
                sent = block
                if slot <= 2 and c == 0:
                    early = block
        arrived.append(now)

    def from_members(own, after):
        mate = lax.ppermute(own, "member", swap_mates)
        return mate, lax.ppermute(pick(where, donor, own, mate, after), "member", swap_across)

    donated = from_members(state, early)

    grads = []
    for c in range(len(parts)):
        sent = summed_grad(terms[-1][c], arrived[n][0][c], arrived[n][1][c], sent)
        grads.append(sent)
    blocks = list(own)
    for slot in range(1, n):
        blocks += arrived[slot][0] + arrived[slot][1]
    context_grad, computed = columns(n, scale, parts, where, cotangent, grads[-1], blocks)

    tables = (rates, decays, steps, donor)
    updated = ()
    for (first_row, size), grad in zip(parts, grads):
        updated = adam_update(
            first_row, size, where, tables, (weight[0], first[0], second[0]), donated,
            (grad,) + from_members(grad, grad), computed, updated,
        )
    return (context_grad[None],) + tuple(array[None] for array in updated)


def solution(mesh):
    whole = P(("groups", "member"), "shard", None)
    n, members = mesh.shape["shard"], mesh.shape["member"]
    return jax.shard_map(
        functools.partial(on_device, n, members),
        mesh=mesh,
        in_specs=(whole,) * 5 + (P("groups"),) * 4,
        out_specs=(whole,) * 4,
        check_vma=False,
    )
```

time: 97 us -> 162 us (1.67); the launches traced: 96.3 us -> 159 us
  Pallas kernels: 17.7 us -> 90.4 us
  waiting for transfers between devices: 25.2 us -> 3.03 us
  local copies, waits for them, and re-layouts: 3.86 us -> 25.7 us
  starting transfers between devices: 44.4 us -> 38.7 us
  other arithmetic: 4.12 us -> 0.07 us
    pallas_call x14 -> x22, Pallas kernels: 17.7 us -> 90.4 us  [the longest x3 69 us: pick(): pl.pallas_call(pick_kernel, out_shape=jax.ShapeDtypeStruct(own.shape, own...]
    ppermute x16 -> x19, waiting for transfers between devices: 25.2 us -> 3.02 us  [the longest x16 3.01 us: on_device(): now[swap].append(lax.ppermute(block, 'shard', swaps[swap]))]
    unnamed x22 -> x134, local copies, waits for them, and re-layouts: 3.86 us -> 25.7 us
    ppermute x16 -> x19, starting transfers between devices: 39.4 us -> 30 us  [the longest x16 27.1 us: on_device(): now[swap].append(lax.ppermute(block, 'shard', swaps[swap]))]
    ppermute x3, starting transfers between devices: 5.04 us -> 8.72 us  [from_members(): mate = lax.ppermute(own, 'member', swap_mates)]
    convert_element_type x2 -> x0, other arithmetic: 2.74 us -> none  [the longest x1 1.38 us: on_device(): half_weight = weight[0].astype(half)]
  transfers between devices with their start and end apart: 19 -> 22, of which waited for: 5 -> 2; matrix products, arithmetic and copies ran while one was open for 0% -> 0% of each run, Pallas kernels for 16% -> 54%
where the time goes in v4:
time: 162 us; the launch traced here: 159 us
  Pallas kernels  90.4 us (56%)
  starting transfers between devices  38.7 us (24%)
  local copies, waits for them, and re-layouts  25.7 us (16%)
  waiting for transfers between devices  3.03 us (2%)
    pallas_call x3, Pallas kernels, pick(): pl.pallas_call(pick_kernel, out_shape=jax.ShapeDtypeStruct(own.shape, own...  69 us
    ppermute x16, starting transfers between devices, on_device(): now[swap].append(lax.ppermute(block, 'shard', swaps[swap]))  27.1 us
    unnamed x134, local copies, waits for them, and re-layouts  25.7 us
    ppermute x3, starting transfers between devices, from_members(): mate = lax.ppermute(own, 'member', swap_mates)  8.72 us
    pallas_call x12, Pallas kernels, to_send(): pl.pallas_call(functools.partial(send_kernel, slot, n, swap), out_shape=j...  8.19 us
    pallas_call x2, Pallas kernels, adam_update(): pl.pallas_call(functools.partial(adam_kernel, first_row, part, bool(fille...  4.97 us
    pallas_call x1, Pallas kernels, columns(): pl.pallas_call(functools.partial(columns_kernel, n, scale, parts), out_sh...  3.96 us
  transfers between devices with their start and end apart: 22, of which 2 were waited for; matrix products, arithmetic and copies ran while one was open for 0% of the time, Pallas kernels for 54%

profile of v4, /device:TPU:1, one launch (start us, length us, event | category | flops | bytes accessed | tf_op | source)
XLA Modules:
  0.0 159.2 jit_solution(10404419143211700006)
XLA Ops:
  0.6 1.2 copy-done.2
  1.9 1.2 copy-done.4
  3.1 1.2 copy-done.6
  4.3 1.5 halves.1
  6.6 5.3 %collective-permute-start.1 = (bf16[128,1024]{1,0:T(8,128)(2,1)}, bf16[128,1024]{1,0:T(8,128)(2,1)S(1)}, u32[]{:S(2)}, u32[]{:S(2)}) collective-permute-start(bf16[128,1024]{1,0:T(8,128)(2,1)} %get-tuple-element.32.refs_0_), channel_id=1, source_target_pairs={{0,1},{2,3},{1,0},{3,2},{4,5},{6,7},{5,4},{7,6},{8,9},{10,11},{9,8... | collective-permute-start | bytes 786440 | tf_op jit(solution)/shard_map/ppermute | solution.py:342
  11.9 1.4 collective-permute-start
  14.2 1.2 copy-done.35
  15.4 2.5 %partial_blocks.1 = (f32[128,1024]{1,0:T(8,128)S(1)}, f32[128,1024]{1,0:T(8,128)S(1)}, f32[128,1024]{1,0:T(8,128)S(1)}, f32[128,1024]{1,0:T(8,128)S(1)}, f32[128...) custom-call(s32[2]{0:T(128)S(1)} %pad_add_fusion.where_ref, ...), custom_call_target="tpu_custom_call" | custom-call | bytes 1024 | tf_op jit(solution)/shard_map/partial_blocks/pallas_call | solution.py:103
  28.0 1.1 copy-done
  29.2 49.6 %pick.3 = bf16[768,1024]{1,0:T(8,128)(2,1)} custom-call(s32[2]{0:T(128)} %copy-done.60, s32[4]{0:T(128)} %donor_ref.9, bf16[768,1024]{1,0:T(8,128)(2,1)} %get-tuple-element.46.own_ref, bf16[768,1024]{1,0:T(8,128)(2,1)} %copy-done, bf16[128,1024]{1,0:T(8,128)(2,1)} %copy-done.13), custom_call_target="tpu_custom_call" | custom-call | bytes 1024 | tf_op jit(solution)/shard_map/pick/pallas_call | solution.py:63
  78.8 1.3 collective-permute-start.17
  80.7 2.6 %collective-permute-start.6 = (bf16[128,1024]{1,0:T(8,128)(2,1)S(1)}, bf16[128,1024]{1,0:T(8,128)(2,1)S(1)}, u32[]{:S(2)}, u32[]{:S(2)}) collective-permute-start(bf16[128,1024]{1,0:T(8,128)(2,1)S(1)} %to_send.12.after_ref), channel_id=1, source_target_pairs={{0,1},{2,3},{1,0},{3,2},{4,5},{6,7},{5,4},{7,6},{8,9},{10,11},{9,8... | collective-permute-start | bytes 786440 | tf_op jit(solution)/shard_map/ppermute | solution.py:342
  83.3 1.0 copy-done.59
  84.4 1.1 to_send.14.after_ref
  85.5 1.0 to_send.15.after_ref
  87.4 2.1 %collective-permute-start.3 = (bf16[128,1024]{1,0:T(8,128)(2,1)S(1)}, bf16[128,1024]{1,0:T(8,128)(2,1)S(1)}, u32[]{:S(2)}, u32[]{:S(2)}) collective-permute-start(bf16[128,1024]{1,0:T(8,128)(2,1)S(1)} %to_send.14.after_ref), channel_id=1, source_target_pairs={{0,1},{2,3},{1,0},{3,2},{4,5},{6,7},{5,4},{7,6},{8,9},{10,11},{9,8... | collective-permute-start | bytes 786440 | tf_op jit(solution)/shard_map/ppermute | solution.py:342
  91.5 2.1 %collective-permute-start.9 = (bf16[128,1024]{1,0:T(8,128)(2,1)S(1)}, bf16[128,1024]{1,0:T(8,128)(2,1)S(1)}, u32[]{:S(2)}, u32[]{:S(2)}) collective-permute-start(bf16[128,1024]{1,0:T(8,128)(2,1)S(1)} %to_send.16.after_ref), channel_id=1, source_target_pairs={{0,1},{2,3},{1,0},{3,2},{4,5},{6,7},{5,4},{7,6},{8,9},{10,11},{9,8... | collective-permute-start | bytes 786440 | tf_op jit(solution)/shard_map/ppermute | solution.py:342
  95.8 3.5 %collective-permute-start.12 = (bf16[128,1024]{1,0:T(8,128)(2,1)S(1)}, bf16[128,1024]{1,0:T(8,128)(2,1)S(1)}, u32[]{:S(2)}, u32[]{:S(2)}) collective-permute-start(bf16[128,1024]{1,0:T(8,128)(2,1)S(1)} %to_send.18.after_ref), channel_id=1, source_target_pairs={{0,1},{2,3},{1,0},{3,2},{4,5},{6,7},{5,4},{7,6},{8,9},{10,11},{9,8... | collective-permute-start | bytes 786440 | tf_op jit(solution)/shard_map/ppermute | solution.py:342
  99.9 2.0 %collective-permute-start.14 = (bf16[128,1024]{1,0:T(8,128)(2,1)S(1)}, bf16[128,1024]{1,0:T(8,128)(2,1)S(1)}, u32[]{:S(2)}, u32[]{:S(2)}) collective-permute-start(bf16[128,1024]{1,0:T(8,128)(2,1)S(1)} %to_send.20.after_ref), channel_id=1, source_target_pairs={{0,1},{2,3},{1,0},{3,2},{4,5},{6,7},{5,4},{7,6},{8,9},{10,11},{9,8... | collective-permute-start | bytes 786440 | tf_op jit(solution)/shard_map/ppermute | solution.py:342
  104.0 2.2 %collective-permute-start.11 = (bf16[128,1024]{1,0:T(8,128)(2,1)S(1)}, bf16[128,1024]{1,0:T(8,128)(2,1)S(1)}, u32[]{:S(2)}, u32[]{:S(2)}) collective-permute-start(bf16[128,1024]{1,0:T(8,128)(2,1)S(1)} %to_send.22.after_ref), channel_id=1, source_target_pairs={{0,1},{2,3},{1,0},{3,2},{4,5},{6,7},{5,4},{7,6},{8,9},{10,11},{9,8... | collective-permute-start | bytes 786440 | tf_op jit(solution)/shard_map/ppermute | solution.py:342
  107.5 2.9 %collective-permute-done.14.one_ref = bf16[128,1024]{1,0:T(8,128)(2,1)S(1)} collective-permute-done((bf16[128,1024]{1,0:T(8,128)(2,1)S(1)}, bf16[128,1024]{1,0:T(8,128)(2,1)S(1)}, u32[]{:S(2)}, u32[]{:S(2)}) %collective-permute-start.14) | collective-permute-done | bytes 262176 | tf_op jit(solution)/shard_map/ppermute | solution.py:342
  110.6 6.0 %collective-permute-start.20 = (bf16[128,1024]{1,0:T(8,128)(2,1)S(1)}, bf16[128,1024]{1,0:T(8,128)(2,1)}, u32[]{:S(2)}, u32[]{:S(2)}) collective-permute-start(bf16[128,1024]{1,0:T(8,128)(2,1)S(1)} %summed_grad.2.after_ref.own_ref.refs_5_), channel_id=1, source_target_pairs={{0,4},{4,0},{8,12},{12,8},{1,5},{5,1},{9,13},{13,9},{2,6},{6,2},{1... | collective-permute-start | bytes 786440 | tf_op jit(solution)/shard_map/ppermute | solution.py:349
  116.7 2.7 %collective-permute-start.18 = (bf16[128,1024]{1,0:T(8,128)(2,1)S(1)}, bf16[128,1024]{1,0:T(8,128)(2,1)}, u32[]{:S(2)}, u32[]{:S(2)}) collective-permute-start(bf16[128,1024]{1,0:T(8,128)(2,1)S(1)} %summed_grad.3.after_ref.own_ref.refs_5_), channel_id=1, source_target_pairs={{0,4},{4,0},{8,12},{12,8},{1,5},{5,1},{9,13},{13,9},{2,6},{6,2},{1... | collective-permute-start | bytes 786440 | tf_op jit(solution)/shard_map/ppermute | solution.py:349
  119.4 9.7 %pick.5 = bf16[128,1024]{1,0:T(8,128)(2,1)} custom-call(s32[2]{0:T(128)} %copy-done.60, s32[4]{0:T(128)} %donor_ref.9, bf16[128,1024]{1,0:T(8,128)(2,1)} %copy-done.10, bf16[128,1024]{1,0:T(8,128)(2,1)} %collective-permute-done.20.mate_ref.refs_6_, bf16[128,1024]{1,0:T(8,128)(2,1)} %copy-done.10), custom_call_target="tpu_custom_call" | custom-call | bytes 1024 | tf_op jit(solution)/shard_map/pick/pallas_call | solution.py:63
  129.5 9.7 %pick.4 = bf16[128,1024]{1,0:T(8,128)(2,1)} custom-call(s32[2]{0:T(128)} %copy-done.60, s32[4]{0:T(128)} %donor_ref.9, bf16[128,1024]{1,0:T(8,128)(2,1)} %copy-done.8, bf16[128,1024]{1,0:T(8,128)(2,1)} %collective-permute-done.18.mate_ref.refs_6_, bf16[128,1024]{1,0:T(8,128)(2,1)} %copy-done.8), custom_call_target="tpu_custom_call" | custom-call | bytes 1024 | tf_op jit(solution)/shard_map/pick/pallas_call | solution.py:63
  139.3 1.3 collective-permute-start.19
  140.6 1.0 copy-done.9
  142.5 0.9 copy-done.20
  143.5 0.9 copy-done.22
  150.2 4.0 %context_grad.1 = (bf16[512,1024]{1,0:T(8,128)(2,1)}, f32[8,128]{1,0:T(8,128)S(1)}) custom-call(s32[2]{0:T(128)S(1)} %copy-done.62, bf16[512,1024]{1,0:T(8,128)(2,1)S(1)} %bitcast.21, bf16[128,1024]{1,0:T(8,128)(2,1)S(1)} %copy-done.9, bf16[128,1024]{1,0:T(8,128)(2,1)} %get-tuple-element.32.refs_0_, bf16[128,1024]{1,0:T(8,128)(2,1)} %get-tuple-element.30.after_ref.refs_1_, ...), custom_call_target="tpu_custom_call" | custom-call | bytes 1024 | tf_op jit(solution)/shard_map/context_grad/pallas_call | solution.py:205
  154.2 2.5 %adam.2 = (f32[256,1024]{1,0:T(8,128)}, f32[256,1024]{1,0:T(8,128)}, f32[256,1024]{1,0:T(8,128)}) custom-call(s32[2]{0:T(128)S(1)} %copy-done.62, f32[4]{0:T(128)S(1)} %copy-done.64, f32[4]{0:T(128)S(1)} %copy-done.65, s32[4]{0:T(128)S(1)} %copy-done.66, s32[4]{0:T(128)S(1)} %copy-done.63, f32[256,1024]{1,0:T(8,128)S(1)} %bitcast.12, ...), custom_call_target="tpu_custom_call" | custom-call | bytes 1024 | tf_op jit(solution)/shard_map/adam/pallas_call | solution.py:292
  156.7 2.5 %adam.3 = (f32[256,1024]{1,0:T(8,128)}, f32[256,1024]{1,0:T(8,128)}, f32[256,1024]{1,0:T(8,128)}) custom-call(s32[2]{0:T(128)S(1)} %copy-done.62, f32[4]{0:T(128)S(1)} %copy-done.64, f32[4]{0:T(128)S(1)} %copy-done.65, s32[4]{0:T(128)S(1)} %copy-done.66, s32[4]{0:T(128)S(1)} %copy-done.63, ...), custom_call_target="tpu_custom_call", output_to_operand_aliasing={{0}: (14, {}), {1}: (15, {}), {2}: (16, {})} | custom-call | bytes 1024 | tf_op jit(solution)/shard_map/adam/pallas_call | solution.py:292
  (169 shorter events, 28.6 us)
Async XLA Ops:
  5.8 22.2 %collective-permute-start.16 = (bf16[768,1024]{1,0:T(8,128)(2,1)}, bf16[768,1024]{1,0:T(8,128)(2,1)S(1)}, u32[]{:S(2)}, u32[]{:S(2)}) collective-permute-start(bf16[768,1024]{1,0:T(8,128)(2,1)} %get-tuple-element.46.own_ref), channel_id=1, source_target_pairs={{0,4},{4,0},{8,12},{12,8},{1,5},{5,1},{9,13},{13,9},{2,6},{6,2},{1... | collective-permute-start | bytes 4718600 | tf_op jit(solution)/shard_map/ppermute | solution.py:349
  5.9 20.1 %collective-permute-start.2 = (bf16[128,1024]{1,0:T(8,128)(2,1)}, bf16[128,1024]{1,0:T(8,128)(2,1)S(1)}, u32[]{:S(2)}, u32[]{:S(2)}) collective-permute-start(bf16[128,1024]{1,0:T(8,128)(2,1)} %get-tuple-element.32.refs_0_), channel_id=1, source_target_pairs={{1,2},{2,1},{5,6},{6,5},{9,10},{10,9},{13,14},{14,13},{17,18},{18,... | collective-permute-start | bytes 786440 | tf_op jit(solution)/shard_map/ppermute | solution.py:342
  6.6 20.1 %collective-permute-start.1 = (bf16[128,1024]{1,0:T(8,128)(2,1)}, bf16[128,1024]{1,0:T(8,128)(2,1)S(1)}, u32[]{:S(2)}, u32[]{:S(2)}) collective-permute-start(bf16[128,1024]{1,0:T(8,128)(2,1)} %get-tuple-element.32.refs_0_), channel_id=1, source_target_pairs={{0,1},{2,3},{1,0},{3,2},{4,5},{6,7},{5,4},{7,6},{8,9},{10,11},{9,8... | collective-permute-start | bytes 786440 | tf_op jit(solution)/shard_map/ppermute | solution.py:342
  11.9 71.4 %collective-permute-start = (bf16[128,1024]{1,0:T(8,128)(2,1)}, bf16[128,1024]{1,0:T(8,128)(2,1)}, u32[]{:S(2)}, u32[]{:S(2)}) collective-permute-start(bf16[128,1024]{1,0:T(8,128)(2,1)} %get-tuple-element.30.after_ref.refs_1_), channel_id=1, source_target_pairs={{1,2},{2,1},{5,6},{6,5},{9,10},{10,9},{13,14},{14,13},{17,18},{18,... | collective-permute-start | bytes 786440 | tf_op jit(solution)/shard_map/ppermute | solution.py:342
  13.3 72.2 %collective-permute-start.4 = (bf16[128,1024]{1,0:T(8,128)(2,1)}, bf16[128,1024]{1,0:T(8,128)(2,1)}, u32[]{:S(2)}, u32[]{:S(2)}) collective-permute-start(bf16[128,1024]{1,0:T(8,128)(2,1)} %get-tuple-element.30.after_ref.refs_1_), channel_id=1, source_target_pairs={{0,1},{2,3},{1,0},{3,2},{4,5},{6,7},{5,4},{7,6},{8,9},{10,11},{9,8... | collective-permute-start | bytes 786440 | tf_op jit(solution)/shard_map/ppermute | solution.py:342
  14.1 12.6 %copy-start.60 = (s32[2]{0:T(128)}, s32[2]{0:T(128)S(1)}, u32[]{:S(2)}) copy-start(s32[2]{0:T(128)S(1)} %pad_add_fusion.where_ref) | copy-start | bytes 28
  28.0 55.3 %copy-start.61 = (s32[2]{0:T(128)S(1)}, s32[2]{0:T(128)}, u32[]{:S(2)}) copy-start(s32[2]{0:T(128)} %copy-done.60) | copy-start | bytes 28
  29.2 50.9 %copy-start.14 = (bf16[128,1024]{1,0:T(8,128)(2,1)S(1)}, bf16[128,1024]{1,0:T(8,128)(2,1)}, u32[]{:S(2)}) copy-start(bf16[128,1024]{1,0:T(8,128)(2,1)} %copy-done.13) | copy-start | bytes 786436
  78.8 75.4 %collective-permute-start.17 = (bf16[768,1024]{1,0:T(8,128)(2,1)}, bf16[768,1024]{1,0:T(8,128)(2,1)S(1)}, u32[]{:S(2)}, u32[]{:S(2)}) collective-permute-start(bf16[768,1024]{1,0:T(8,128)(2,1)} %pick.3), channel_id=1, source_target_pairs={{0,8},{4,12},{8,0},{12,4},{1,9},{5,13},{9,1},{13,5},{2,10},{6,14},... | collective-permute-start | bytes 4718600 | tf_op jit(solution)/shard_map/ppermute | solution.py:350
  80.0 9.4 %collective-permute-start.7 = (bf16[128,1024]{1,0:T(8,128)(2,1)S(1)}, bf16[128,1024]{1,0:T(8,128)(2,1)S(1)}, u32[]{:S(2)}, u32[]{:S(2)}) collective-permute-start(bf16[128,1024]{1,0:T(8,128)(2,1)S(1)} %copy-done.14), channel_id=1, source_target_pairs={{1,2},{2,1},{5,6},{6,5},{9,10},{10,9},{13,14},{14,13},{17,18},{18,... | collective-permute-start | bytes 786440 | tf_op jit(solution)/shard_map/ppermute | solution.py:342
  80.7 9.4 %collective-permute-start.6 = (bf16[128,1024]{1,0:T(8,128)(2,1)S(1)}, bf16[128,1024]{1,0:T(8,128)(2,1)S(1)}, u32[]{:S(2)}, u32[]{:S(2)}) collective-permute-start(bf16[128,1024]{1,0:T(8,128)(2,1)S(1)} %to_send.12.after_ref), channel_id=1, source_target_pairs={{0,1},{2,3},{1,0},{3,2},{4,5},{6,7},{5,4},{7,6},{8,9},{10,11},{9,8... | collective-permute-start | bytes 786440 | tf_op jit(solution)/shard_map/ppermute | solution.py:342
  86.5 7.1 %collective-permute-start.5 = (bf16[128,1024]{1,0:T(8,128)(2,1)S(1)}, bf16[128,1024]{1,0:T(8,128)(2,1)S(1)}, u32[]{:S(2)}, u32[]{:S(2)}) collective-permute-start(bf16[128,1024]{1,0:T(8,128)(2,1)S(1)} %to_send.15.after_ref), channel_id=1, source_target_pairs={{1,2},{2,1},{5,6},{6,5},{9,10},{10,9},{13,14},{14,13},{17,18},{18,... | collective-permute-start | bytes 786440 | tf_op jit(solution)/shard_map/ppermute | solution.py:342
  87.4 7.0 %collective-permute-start.3 = (bf16[128,1024]{1,0:T(8,128)(2,1)S(1)}, bf16[128,1024]{1,0:T(8,128)(2,1)S(1)}, u32[]{:S(2)}, u32[]{:S(2)}) collective-permute-start(bf16[128,1024]{1,0:T(8,128)(2,1)S(1)} %to_send.14.after_ref), channel_id=1, source_target_pairs={{0,1},{2,3},{1,0},{3,2},{4,5},{6,7},{5,4},{7,6},{8,9},{10,11},{9,8... | collective-permute-start | bytes 786440 | tf_op jit(solution)/shard_map/ppermute | solution.py:342
  90.7 8.5 %collective-permute-start.10 = (bf16[128,1024]{1,0:T(8,128)(2,1)S(1)}, bf16[128,1024]{1,0:T(8,128)(2,1)S(1)}, u32[]{:S(2)}, u32[]{:S(2)}) collective-permute-start(bf16[128,1024]{1,0:T(8,128)(2,1)S(1)} %to_send.17.after_ref), channel_id=1, source_target_pairs={{1,2},{2,1},{5,6},{6,5},{9,10},{10,9},{13,14},{14,13},{17,18},{18,... | collective-permute-start | bytes 786440 | tf_op jit(solution)/shard_map/ppermute | solution.py:342
  91.5 10.4 %collective-permute-start.9 = (bf16[128,1024]{1,0:T(8,128)(2,1)S(1)}, bf16[128,1024]{1,0:T(8,128)(2,1)S(1)}, u32[]{:S(2)}, u32[]{:S(2)}) collective-permute-start(bf16[128,1024]{1,0:T(8,128)(2,1)S(1)} %to_send.16.after_ref), channel_id=1, source_target_pairs={{0,1},{2,3},{1,0},{3,2},{4,5},{6,7},{5,4},{7,6},{8,9},{10,11},{9,8... | collective-permute-start | bytes 786440 | tf_op jit(solution)/shard_map/ppermute | solution.py:342
  95.0 8.4 %collective-permute-start.8 = (bf16[128,1024]{1,0:T(8,128)(2,1)S(1)}, bf16[128,1024]{1,0:T(8,128)(2,1)S(1)}, u32[]{:S(2)}, u32[]{:S(2)}) collective-permute-start(bf16[128,1024]{1,0:T(8,128)(2,1)S(1)} %to_send.19.after_ref), channel_id=1, source_target_pairs={{1,2},{2,1},{5,6},{6,5},{9,10},{10,9},{13,14},{14,13},{17,18},{18,... | collective-permute-start | bytes 786440 | tf_op jit(solution)/shard_map/ppermute | solution.py:342
  95.8 10.4 %collective-permute-start.12 = (bf16[128,1024]{1,0:T(8,128)(2,1)S(1)}, bf16[128,1024]{1,0:T(8,128)(2,1)S(1)}, u32[]{:S(2)}, u32[]{:S(2)}) collective-permute-start(bf16[128,1024]{1,0:T(8,128)(2,1)S(1)} %to_send.18.after_ref), channel_id=1, source_target_pairs={{0,1},{2,3},{1,0},{3,2},{4,5},{6,7},{5,4},{7,6},{8,9},{10,11},{9,8... | collective-permute-start | bytes 786440 | tf_op jit(solution)/shard_map/ppermute | solution.py:342
  99.9 10.5 %collective-permute-start.14 = (bf16[128,1024]{1,0:T(8,128)(2,1)S(1)}, bf16[128,1024]{1,0:T(8,128)(2,1)S(1)}, u32[]{:S(2)}, u32[]{:S(2)}) collective-permute-start(bf16[128,1024]{1,0:T(8,128)(2,1)S(1)} %to_send.20.after_ref), channel_id=1, source_target_pairs={{0,1},{2,3},{1,0},{3,2},{4,5},{6,7},{5,4},{7,6},{8,9},{10,11},{9,8... | collective-permute-start | bytes 786440 | tf_op jit(solution)/shard_map/ppermute | solution.py:342
  102.5 7.9 %collective-permute-start.15 = (bf16[128,1024]{1,0:T(8,128)(2,1)S(1)}, bf16[128,1024]{1,0:T(8,128)(2,1)S(1)}, u32[]{:S(2)}, u32[]{:S(2)}) collective-permute-start(bf16[128,1024]{1,0:T(8,128)(2,1)S(1)} %to_send.21.after_ref), channel_id=1, source_target_pairs={{1,2},{2,1},{5,6},{6,5},{9,10},{10,9},{13,14},{14,13},{17,18},{18,... | collective-permute-start | bytes 786440 | tf_op jit(solution)/shard_map/ppermute | solution.py:342
  104.0 12.5 %collective-permute-start.11 = (bf16[128,1024]{1,0:T(8,128)(2,1)S(1)}, bf16[128,1024]{1,0:T(8,128)(2,1)S(1)}, u32[]{:S(2)}, u32[]{:S(2)}) collective-permute-start(bf16[128,1024]{1,0:T(8,128)(2,1)S(1)} %to_send.22.after_ref), channel_id=1, source_target_pairs={{0,1},{2,3},{1,0},{3,2},{4,5},{6,7},{5,4},{7,6},{8,9},{10,11},{9,8... | collective-permute-start | bytes 786440 | tf_op jit(solution)/shard_map/ppermute | solution.py:342
  106.8 9.7 %collective-permute-start.13 = (bf16[128,1024]{1,0:T(8,128)(2,1)S(1)}, bf16[128,1024]{1,0:T(8,128)(2,1)S(1)}, u32[]{:S(2)}, u32[]{:S(2)}) collective-permute-start(bf16[128,1024]{1,0:T(8,128)(2,1)S(1)} %to_send.23.after_ref), channel_id=1, source_target_pairs={{1,2},{2,1},{5,6},{6,5},{9,10},{10,9},{13,14},{14,13},{17,18},{18,... | collective-permute-start | bytes 786440 | tf_op jit(solution)/shard_map/ppermute | solution.py:342
  110.6 8.9 %collective-permute-start.20 = (bf16[128,1024]{1,0:T(8,128)(2,1)S(1)}, bf16[128,1024]{1,0:T(8,128)(2,1)}, u32[]{:S(2)}, u32[]{:S(2)}) collective-permute-start(bf16[128,1024]{1,0:T(8,128)(2,1)S(1)} %summed_grad.2.after_ref.own_ref.refs_5_), channel_id=1, source_target_pairs={{0,4},{4,0},{8,12},{12,8},{1,5},{5,1},{9,13},{13,9},{2,6},{6,2},{1... | collective-permute-start | bytes 786440 | tf_op jit(solution)/shard_map/ppermute | solution.py:349
  116.5 24.0 %copy-start.16 = (bf16[128,1024]{1,0:T(8,128)(2,1)S(1)}, bf16[128,1024]{1,0:T(8,128)(2,1)}, u32[]{:S(2)}) copy-start(bf16[128,1024]{1,0:T(8,128)(2,1)} %copy-done.15) | copy-start | bytes 786436
  116.5 24.0 %copy-start.62 = (s32[2]{0:T(128)S(1)}, s32[2]{0:T(128)}, u32[]{:S(2)}) copy-start(s32[2]{0:T(128)} %copy-done.60) | copy-start | bytes 28
  116.7 12.8 %copy-start.8 = (bf16[128,1024]{1,0:T(8,128)(2,1)}, bf16[128,1024]{1,0:T(8,128)(2,1)S(1)}, u32[]{:S(2)}) copy-start(bf16[128,1024]{1,0:T(8,128)(2,1)S(1)} %summed_grad.3.after_ref.own_ref.refs_5_) | copy-start | bytes 786436
  116.7 12.8 %collective-permute-start.18 = (bf16[128,1024]{1,0:T(8,128)(2,1)S(1)}, bf16[128,1024]{1,0:T(8,128)(2,1)}, u32[]{:S(2)}, u32[]{:S(2)}) collective-permute-start(bf16[128,1024]{1,0:T(8,128)(2,1)S(1)} %summed_grad.3.after_ref.own_ref.refs_5_), channel_id=1, source_target_pairs={{0,4},{4,0},{8,12},{12,8},{1,5},{5,1},{9,13},{13,9},{2,6},{6,2},{1... | collective-permute-start | bytes 786440 | tf_op jit(solution)/shard_map/ppermute | solution.py:349
  129.2 25.0 %collective-permute-start.21 = (bf16[128,1024]{1,0:T(8,128)(2,1)}, bf16[128,1024]{1,0:T(8,128)(2,1)S(1)}, u32[]{:S(2)}, u32[]{:S(2)}) collective-permute-start(bf16[128,1024]{1,0:T(8,128)(2,1)} %pick.5), channel_id=1, source_target_pairs={{0,8},{4,12},{8,0},{12,4},{1,9},{5,13},{9,1},{13,5},{2,10},{6,14},... | collective-permute-start | bytes 786440 | tf_op jit(solution)/shard_map/ppermute | solution.py:350
  139.2 14.9 %copy-start.1 = (bf16[768,1024]{1,0:T(8,128)(2,1)S(1)}, bf16[768,1024]{1,0:T(8,128)(2,1)}, u32[]{:S(2)}) copy-start(bf16[768,1024]{1,0:T(8,128)(2,1)} %copy-done) | copy-start | bytes 4718596
  139.2 14.9 %copy-start.3 = (f32[1,256,1024]{2,1,0:T(8,128)S(1)}, f32[1,256,1024]{2,1,0:T(8,128)}, u32[]{:S(2)}) copy-start(f32[1,256,1024]{2,1,0:T(8,128)} %param.11) | copy-start | bytes 3145732
  139.2 14.9 %copy-start.5 = (f32[1,256,1024]{2,1,0:T(8,128)S(1)}, f32[1,256,1024]{2,1,0:T(8,128)}, u32[]{:S(2)}) copy-start(f32[1,256,1024]{2,1,0:T(8,128)} %param.12) | copy-start | bytes 3145732
  139.3 14.9 %copy-start.7 = (f32[1,256,1024]{2,1,0:T(8,128)S(1)}, f32[1,256,1024]{2,1,0:T(8,128)}, u32[]{:S(2)}) copy-start(f32[1,256,1024]{2,1,0:T(8,128)} %param.13) | copy-start | bytes 3145732
  139.3 17.5 %collective-permute-start.19 = (bf16[128,1024]{1,0:T(8,128)(2,1)}, bf16[128,1024]{1,0:T(8,128)(2,1)S(1)}, u32[]{:S(2)}, u32[]{:S(2)}) collective-permute-start(bf16[128,1024]{1,0:T(8,128)(2,1)} %pick.4), channel_id=1, source_target_pairs={{0,8},{4,12},{8,0},{12,4},{1,9},{5,13},{9,1},{13,5},{2,10},{6,14},... | collective-permute-start | bytes 786440 | tf_op jit(solution)/shard_map/ppermute | solution.py:350
  (57 other events, 205.3 us)

commit v5 on v1

v5 whole, which is shorter than its diff:
```python
import functools
import math

import jax
import jax.numpy as jnp
from jax import lax
from jax.experimental import pallas as pl
from jax.experimental.pallas import tpu as pltpu
from jax.sharding import PartitionSpec as P

beta_one = 0.9
beta_two = 0.999
epsilon = 1e-08

MIB = 1 << 20
SMEM = pl.BlockSpec(memory_space=pltpu.SMEM)
VMEM = pl.BlockSpec(memory_space=pltpu.VMEM)
HBM = pl.BlockSpec(memory_space=pltpu.HBM)
ANY = pl.BlockSpec(memory_space=pl.ANY)
SMALL = pl.CostEstimate(flops=0, bytes_accessed=1024, transcendentals=0)


def call(kernel, name, out_shape, in_specs, out_specs, limit=8, scratch=(), aliases=None):
    return pl.pallas_call(
        kernel,
        out_shape=out_shape,
        in_specs=in_specs,
        out_specs=out_specs,
        scratch_shapes=scratch,
        input_output_aliases=aliases or {},
        compiler_params=pltpu.CompilerParams(vmem_limit_bytes=limit * MIB),
        cost_estimate=SMALL,
        name=name,
    )


def half_array(rows, depth):
    return jax.ShapeDtypeStruct((rows, depth), jnp.bfloat16)


def by_rows(ref, body, step=16):
    @pl.loop(0, ref.shape[0] // step)
    def _(i):
        body(pl.ds(pl.multiple_of(i * step, step), step))


def source_of(member, donor_ref):
    donor = donor_ref[member]
    return jnp.where(donor >= 0, donor, member)


def choices_kernel(where_ref, rates_ref, decays_ref, steps_ref, donor_ref, out_ref):
    member = where_ref[1]
    source = source_of(member, donor_ref)
    way = jnp.minimum(jnp.bitwise_xor(source, member), 2)
    partner_source = source_of(jnp.bitwise_xor(member, 2), donor_ref)
    flags = [partner_source == jnp.bitwise_xor(member, 1), way == 0, way == 1, way == 2]
    depth = out_ref.shape[1]
    for k, flag in enumerate(flags):
        out_ref[k:k + 1, :] = jnp.full((1, depth), jnp.where(flag, 1.0, 0.0))
    out_ref[4:5, :] = jnp.full((1, depth), rates_ref[source])
    out_ref[5:6, :] = jnp.full((1, depth), decays_ref[source])
    count = jnp.full((1, depth), (steps_ref[source] + 1).astype(jnp.float32))
    out_ref[6:7, :] = 1.0 / (1.0 - jnp.exp(count * math.log(beta_one)))
    out_ref[7:8, :] = 1.0 / (1.0 - jnp.exp(count * math.log(beta_two)))


def halves_kernel(parts, weight_ref, first_ref, second_ref, state_ref, *refs):
    own_refs, (full, sems) = refs[:-2], refs[-2:]
    rows = weight_ref.shape[0]
    copies = []
    for k, ref in enumerate((weight_ref, first_ref, second_ref)):
        for c, (start, size) in enumerate(parts):
            copies.append(pltpu.make_async_copy(
                ref.at[pl.ds(start, size), :], full.at[k, pl.ds(start, size), :], sems.at[k * len(parts) + c]
            ))
            copies[-1].start()
    for k in range(3):
        for c, (start, size) in enumerate(parts):
            copies[k * len(parts) + c].wait()
            rounded = full[k, start:start + size, :].astype(jnp.bfloat16)
            if k == 0:
                own_refs[c][...] = rounded
            state_ref[k * rows + start:k * rows + start + size, :] = rounded


def halves(parts, weight, first, second):
    rows, depth = weight.shape
    sizes = [3 * rows] + [size for _, size in parts]
    return call(
        functools.partial(halves_kernel, parts), "halves",
        [half_array(size, depth) for size in sizes], [HBM] * 3, [VMEM] * len(sizes), limit=56,
        scratch=[pltpu.VMEM((3, rows, depth), jnp.float32), pltpu.SemaphoreType.DMA((3 * len(parts),))],
    )(weight, first, second)


def pick_kernel(choices_ref, own_ref, mate_ref, after_ref, out_ref):
    def body(at):
        wants_mate = jnp.broadcast_to(choices_ref[0:1, :], (16, out_ref.shape[1])) > 0
        own, mate = own_ref[at, :].astype(jnp.float32), mate_ref[at, :].astype(jnp.float32)
        out_ref[at, :] = jnp.where(wants_mate, mate, own).astype(out_ref.dtype)

    by_rows(out_ref, body)


def pick(choices, own, mate, after):
    return call(pick_kernel, "pick", half_array(*own.shape), [VMEM, VMEM, VMEM, ANY], VMEM)(
        choices, own, mate, after
    )


def partial_kernel(n, scale, parts, order, where_ref, context_ref, cotangent_ref, *refs):
    outs, (context, cotangent, product, rounded, sems, out_sems) = refs[:-6], refs[-6:]
    width = product.shape[0]
    rows = width // n
    me = where_ref[0]
    even = lax.rem(me, 2) == 0
    tile = min(256, width)
    tokens = context.shape[0]
    loads = []
    for i, start in enumerate(range(0, tokens, tokens // 4)):
        at = pl.ds(start, tokens // 4)
        loads.append(pltpu.make_async_copy(cotangent_ref.at[at, :], cotangent.at[at, :], sems.at[i]))
    for i, start in enumerate(range(0, width, tile)):
        at = pl.ds(start, tile)
        loads.append(pltpu.make_async_copy(context_ref.at[:, at], context.at[:, at], sems.at[4 + i]))
    for load in loads:
        load.start()
    rounded[width:, :] = jnp.zeros((rows, rounded.shape[1]), rounded.dtype)
    for load in loads[:4]:
        load.wait()
    for i, start in enumerate(range(0, width, tile)):
        loads[4 + i].wait()
        block = scale * lax.dot_general(
            context[:, start:start + tile], cotangent[...],
            (((0,), (0,)), ((), ())), preferred_element_type=jnp.float32,
        )
        product[start:start + tile, :] = block
        rounded[start:start + tile, :] = block.astype(rounded.dtype)
    writes = []

    def write(source, first_row, size):
        at = len(writes)
        writes.append(pltpu.make_async_copy(
            source.at[pl.ds(pl.multiple_of(first_row, 16), size), :], outs[at], out_sems.at[at]
        ))
        writes[-1].start()

    for slot, swap in order:
        rightward = even if swap == 0 else jnp.logical_not(even)
        block = lax.rem(me + jnp.where(rightward, n + 1 - slot, slot - 1), n)
        place = jnp.where(rightward, me, n - 1 - me)
        first_row = jnp.where(place >= slot - 1, width, block * rows)
        for start, size in parts:
            write(rounded, first_row + start, size)
    for start, size in parts:
        write(product, me * rows + start, size)
    for copy in writes:
        copy.wait()


def partial_blocks(n, scale, parts, order, where, context_rows, cotangent):
    tokens, width = context_rows.shape
    depth = cotangent.shape[1]
    outs = (len(order) + 1) * len(parts)
    flat = call(
        functools.partial(partial_kernel, n, scale, parts, order), "partial_blocks",
        [half_array(size, depth) for _, size in parts] * len(order)
        + [jax.ShapeDtypeStruct((size, depth), jnp.float32) for _, size in parts],
        [SMEM, HBM, HBM], [HBM] * outs, limit=14,
        scratch=[
            pltpu.VMEM(context_rows.shape, context_rows.dtype),
            pltpu.VMEM(cotangent.shape, cotangent.dtype),
            pltpu.VMEM((width, depth), jnp.float32),
            pltpu.VMEM((width + width // n, depth), jnp.bfloat16),
            pltpu.SemaphoreType.DMA((4 + width // min(256, width),)),
            pltpu.SemaphoreType.DMA((outs,)),
        ],
    )(where, context_rows, cotangent)
    return [flat[k * len(parts):(k + 1) * len(parts)] for k in range(len(order) + 1)]


def sum_kernel(arrived_ref, term_ref, after_ref, out_ref):
    def body(at):
        total = arrived_ref[at, :].astype(jnp.float32) + term_ref[at, :].astype(jnp.float32)
        out_ref[at, :] = total.astype(out_ref.dtype)

    by_rows(out_ref, body)


def grad_kernel(own_ref, one_ref, other_ref, after_ref, out_ref):
    def body(at):
        arrived = one_ref[at, :].astype(jnp.float32) + other_ref[at, :].astype(jnp.float32)
        out_ref[at, :] = (own_ref[at, :] + arrived).astype(out_ref.dtype)

    by_rows(out_ref, body)


def summed(kernel, name, addends, after):
    return call(kernel, name, half_array(*addends[0].shape), [VMEM] * len(addends) + [ANY], VMEM)(
        *addends, after
    )


def columns_kernel(n, scale, parts, where_ref, cotangent_ref, after_ref, *refs):
    blocks, (out_ref, token_ref, full, result, out_sems) = refs[:-5], refs[-5:]
    token_ref[...] = jnp.zeros_like(token_ref)
    width = full.shape[0]
    rows = width // n
    me = where_ref[0]
    even = lax.rem(me, 2) == 0
    for k in range(2 * n - 1):
        slot, swap = (k + 1) // 2, (k + 1) % 2
        shard = me + (jnp.where(even, slot, -slot) if swap == 0 else jnp.where(even, -slot, slot))

        @pl.when(jnp.logical_and(shard >= 0, shard < n))
        def _():
            for c, (start, size) in enumerate(parts):
                first_row = pl.multiple_of(shard * rows + start, 16)
                full[pl.ds(first_row, size), :] = blocks[k * len(parts) + c][...]
    tile = min(256, width)
    writes = []
    for i, start in enumerate(range(0, width, tile)):
        result[:, start:start + tile] = (scale * lax.dot_general(
            cotangent_ref[...], full[start:start + tile, :],
            (((1,), (1,)), ((), ())), preferred_element_type=jnp.float32,
        )).astype(out_ref.dtype)
        at = pl.ds(start, tile)
        writes.append(pltpu.make_async_copy(result.at[:, at], out_ref.at[:, at], out_sems.at[i]))
        writes[-1].start()
    for write in writes:
        write.wait()


def columns(n, scale, parts, where, cotangent, after, blocks):
    tokens, depth = cotangent.shape
    width = n * sum(size for _, size in parts)
    return call(
        functools.partial(columns_kernel, n, scale, parts), "context_grad",
        [half_array(tokens, width), jax.ShapeDtypeStruct((8, 128), jnp.float32)],
        [SMEM, VMEM, ANY] + [VMEM] * len(blocks), [HBM, VMEM], limit=14,
        scratch=[
            pltpu.VMEM((width, depth), cotangent.dtype),
            pltpu.VMEM((tokens, width), cotangent.dtype),
            pltpu.SemaphoreType.DMA((width // min(256, width),)),
        ],
    )(where, cotangent, after, *blocks)


def state_kernel(parts, where_ref, donor_ref, *refs):
    own, (mate_ref, across_ref), refs = refs[:3], refs[3:5], refs[5:]
    outs, (taken, sems) = refs[:-2], refs[-2:]
    rows = own[0].shape[0]
    member = where_ref[1]
    way = jnp.bitwise_xor(source_of(member, donor_ref), member)

    @pl.when(way == 0)
    def _():
        copies = []
        for c, (start, size) in enumerate(parts):
            for k in range(3):
                copies.append(pltpu.make_async_copy(
                    own[k].at[pl.ds(start, size), :], outs[c].at[pl.ds(k * size, size), :], sems.at[c * 3 + k]
                ))
                copies[-1].start()
        for copy in copies:
            copy.wait()

    def widen(ref):
        copies = []
        for k in range(3):
            at = pl.ds(k * rows, rows)
            copies.append(pltpu.make_async_copy(ref.at[at, :], taken.at[at, :], sems.at[k]))
            copies[-1].start()
        for k in range(3):
            copies[k].wait()
            for c, (start, size) in enumerate(parts):
                first_row = k * rows + start
                outs[c][k * size:(k + 1) * size, :] = taken[first_row:first_row + size, :].astype(jnp.float32)

    pl.when(way == 1)(lambda: widen(mate_ref))
    pl.when(way > 1)(lambda: widen(across_ref))


def taken_state(parts, where, donor, own, donated):
    rows, depth = own[0].shape
    return call(
        functools.partial(state_kernel, parts), "taken_state",
        [jax.ShapeDtypeStruct((3 * size, depth), jnp.float32) for _, size in parts],
        [SMEM, SMEM] + [HBM] * 3 + [ANY] * 2, [VMEM] * len(parts),
        scratch=[pltpu.VMEM((3 * rows, depth), jnp.bfloat16), pltpu.SemaphoreType.DMA((3 * len(parts),))],
    )(where, donor, *own, *donated)


def adam_kernel(start, size, filled, choices_ref, state_ref, grad_ref, mate_ref, across_ref, *refs):
    refs = refs[3 if filled else 0:]
    outs, (stepped, sems) = refs[:3], refs[3:]
    depth = grad_ref.shape[1]
    pieces = 4 if size % 64 == 0 else 1
    piece = size // pieces
    writes = []
    for p in range(pieces):
        def body(i):
            at = pl.ds(pl.multiple_of(p * piece + i * 16, 16), 16)
            row = lambda k: jnp.broadcast_to(choices_ref[k:k + 1, :], (16, depth))
            load = lambda k: state_ref[pl.ds(pl.multiple_of(k * size + p * piece + i * 16, 16), 16), :]
            g = jnp.where(
                row(1) > 0, grad_ref[at, :].astype(jnp.float32),
                jnp.where(row(2) > 0, mate_ref[at, :].astype(jnp.float32), across_ref[at, :].astype(jnp.float32)),
            )
            w = load(0)
            first_step = beta_one * load(1) + (1.0 - beta_one) * g
            second_step = beta_two * load(2) + (1.0 - beta_two) * g * g
            ratio = (first_step * row(6)) / (jnp.sqrt(second_step * row(7)) + epsilon)
            stepped[0, at, :] = w - row(4) * (ratio + row(5) * w)
            stepped[1, at, :] = first_step
            stepped[2, at, :] = second_step

        pl.loop(0, piece // 16)(body)
        for k in range(3):
            writes.append(pltpu.make_async_copy(
                stepped.at[k, pl.ds(p * piece, piece), :],
                outs[k].at[pl.ds(start + p * piece, piece), :], sems.at[p * 3 + k],
            ))
            writes[-1].start()
    for write in writes:
        write.wait()


def adam_update(start, size, rows, choices, state, grads, filled):
    depth = state.shape[1]
    return call(
        functools.partial(adam_kernel, start, size, bool(filled)), "adam",
        [jax.ShapeDtypeStruct((rows, depth), jnp.float32)] * 3,
        [VMEM] * 5 + [HBM] * len(filled), [HBM] * 3,
        scratch=[pltpu.VMEM((3, size, depth), jnp.float32), pltpu.SemaphoreType.DMA((12,))],
        aliases={5 + k: k for k in range(len(filled))},
    )(choices, state, *grads, *filled)


def on_device(n, members, context, out_grad, weight, first, second, rates, decays, steps, donor):
    context_rows = context[0]
    cotangent = out_grad[0]
    scale = context_rows.shape[1] ** (-0.5)
    rows, depth = weight.shape[1:]
    chains = 2 if rows % 32 == 0 else 1
    parts = [(c * rows // chains, rows // chains) for c in range(chains)]
    where = jnp.stack([lax.axis_index("shard"), lax.axis_index("member")]).astype(jnp.int32)

    swap_across = [(m, m ^ 2) for m in range(members)]
    swap_mates = [(m, m ^ 1) for m in range(members)]
    swaps = []
    for swap in range(2):
        pairs = [(s, s + 1) for s in range(swap, n - 1, 2)]
        swaps.append(pairs + [(b, a) for a, b in pairs])

    state, *own = halves(parts, weight[0], first[0], second[0])
    choices = call(
        choices_kernel, "choices", jax.ShapeDtypeStruct((8, depth), jnp.float32), [SMEM] * 5, VMEM
    )(where, rates, decays, steps, donor)
    order = [(slot, swap) for slot in range(2, n + 1) for swap in range(2)]
    terms = partial_blocks(n, scale, parts, order, where, context_rows, cotangent)

    arrived = [[own, own]]
    sent = early = own[0]
    for slot in range(1, n + 1):
        now = [[], []]
        for c in range(len(parts)):
            for swap in range(2):
                block = arrived[-1][1 - swap][c]
                if slot > 1:
                    addends = (block, terms[2 * (slot - 2) + swap][c])
                    block = sent = summed(sum_kernel, "to_send", addends, sent)
                if slot == 2 and c == 0:
                    early = block
                now[swap].append(lax.ppermute(block, "shard", swaps[swap]))
        arrived.append(now)

    def from_members(held, after):
        mate = lax.ppermute(held, "member", swap_mates)
        return mate, lax.ppermute(pick(choices, held, mate, after), "member", swap_across)

    states = taken_state(
        parts, where, donor, (weight[0], first[0], second[0]), from_members(state, early)
    )
    blocks = list(own)
    for slot in range(1, n):
        blocks += arrived[slot][0] + arrived[slot][1]
    context_grad, sent = columns(n, scale, parts, where, cotangent, sent, blocks)

    grads = []
    for c in range(len(parts)):
        addends = (terms[-1][c], arrived[n][0][c], arrived[n][1][c])
        sent = summed(grad_kernel, "summed_grad", addends, sent)
        grads.append(sent)

    updated = ()
    for (start, size), held, grad in zip(parts, states, grads):
        updated = adam_update(
            start, size, rows, choices, held, (grad,) + from_members(grad, grad), updated
        )
    return (context_grad[None],) + tuple(array[None] for array in updated)


def solution(mesh):
    whole = P(("groups", "member"), "shard", None)
    n, members = mesh.shape["shard"], mesh.shape["member"]
    return jax.shard_map(
        functools.partial(on_device, n, members),
        mesh=mesh,
        in_specs=(whole,) * 5 + (P("groups"),) * 4,
        out_specs=(whole,) * 4,
        check_vma=False,
    )
```

time: 103 us -> 77 us (0.75)
  other arithmetic: 21.4 us -> 0.07 us
  Pallas kernels: 0 us -> 17.8 us
  waiting for transfers between devices: 29.6 us -> 15.7 us
  starting transfers between devices: 31.2 us -> 39.3 us
  local copies, waits for them, and re-layouts: 9.86 us -> 1.81 us
  matrix products: 4.79 us -> 0 us
  between operations: 4.09 us -> 1.03 us
    pallas_call x0 -> x24, Pallas kernels: none -> 17.8 us  [the longest x1 3.34 us: halves(): call(functools.partial(halves_kernel, parts), 'halves', [half_array(size,...]
    ppermute x12 -> x22, waiting for transfers between devices: 29.6 us -> 15.7 us  [the longest x3 9.33 us: from_members(): lax.ppermute(pick(choices, held, mate, after), 'member', swap_across)]
    convert_element_type x7 -> x0, other arithmetic: 11.5 us -> none  [the longest x2 4.53 us: on_device(): left = (left.astype(jnp.float32) + add_left).astype(half)]
    ppermute x12 -> x22, starting transfers between devices: 31.2 us -> 39.3 us  [the longest x16 29.6 us: on_device(): now[swap].append(lax.ppermute(block, 'shard', swaps[swap]))]
    unnamed x50 -> x24, local copies, waits for them, and re-layouts: 8.78 us -> 1.81 us
    dot_general x2 -> x0, matrix products: 4.79 us -> none  [the longest x1 2.52 us: on_device(): lax.dot_general(context_rows, cotangent, (((0,), (0,)), ((), ())), prefer...]
    broadcast_in_dim x1 -> x0, other arithmetic: 3.72 us -> none  [on_device(): return (context_grad,) + tuple((array[None] for array in updated))]
    select_n x2 -> x0, other arithmetic: 2.79 us -> none  [from_donor(): jnp.where(mate_source == across, far, own)]
  transfers between devices with their start and end apart: 12 -> 22, of which waited for: 7 -> 8; matrix products, arithmetic and copies ran while one was open for 26% -> 0% of each run, Pallas kernels for 0% -> 17%
where the time goes in v5:
time: 77 us; the launch traced here: 75.8 us
  starting transfers between devices  39.3 us (51%)
  Pallas kernels  17.8 us (23%)
  waiting for transfers between devices  15.7 us (20%)
  local copies, waits for them, and re-layouts  1.81 us (2%)
  between operations  1.03 us (1%)
    ppermute x16, starting transfers between devices, on_device(): now[swap].append(lax.ppermute(block, 'shard', swaps[swap]))  29.6 us
    ppermute x3, waiting for transfers between devices, from_members(): lax.ppermute(pick(choices, held, mate, after), 'member', swap_across)  9.33 us
    ppermute x3, starting transfers between devices, from_members(): mate = lax.ppermute(held, 'member', swap_mates)  7.6 us
    ppermute x16, waiting for transfers between devices, on_device(): now[swap].append(lax.ppermute(block, 'shard', swaps[swap]))  5.69 us
    pallas_call x1, Pallas kernels, halves(): call(functools.partial(halves_kernel, parts), 'halves', [half_array(size,...  3.34 us
    pallas_call x1, Pallas kernels, columns(): call(functools.partial(columns_kernel, n, scale, parts), 'context_grad',...  3.28 us
    pallas_call x1, Pallas kernels, partial_blocks(): call(functools.partial(partial_kernel, n, scale, parts, order), 'partial_...  3.21 us
    pallas_call x2, Pallas kernels, adam_update(): call(functools.partial(adam_kernel, start, size, bool(filled)), 'adam', [...  3.16 us
  transfers between devices with their start and end apart: 22, of which 8 were waited for; matrix products, arithmetic and copies ran while one was open for 0% of the time, Pallas kernels for 17%

profile of v5, /device:TPU:1, one launch (start us, length us, event | category | flops | bytes accessed | tf_op | source)
XLA Modules:
  0.0 75.8 jit_solution(4455506181609128093)
XLA Ops:
  0.6 3.3 %halves.1 = (bf16[768,1024]{1,0:T(8,128)(2,1)}, bf16[128,1024]{1,0:T(8,128)(2,1)}, bf16[128,1024]{1,0:T(8,128)(2,1)}) custom-call(f32[256,1024]{1,0:T(8,128)} %bitcast.13, f32[256,1024]{1,0:T(8,128)} %bitcast.15, f32[256,1024]{1,0:T(8,128)} %bitcast.17), custom_call_target="tpu_custom_call" | custom-call | bytes 1024 | tf_op jit(solution)/shard_map/halves/pallas_call | solution.py:90
  4.2 0.7 collective-permute-start.3
  4.8 5.3 %collective-permute-start.2 = (bf16[128,1024]{1,0:T(8,128)(2,1)}, bf16[128,1024]{1,0:T(8,128)(2,1)S(1)}, u32[]{:S(2)}, u32[]{:S(2)}) collective-permute-start(bf16[128,1024]{1,0:T(8,128)(2,1)} %get-tuple-element.34.after_ref.refs_0_), channel_id=1, source_target_pairs={{0,1},{2,3},{1,0},{3,2},{4,5},{6,7},{5,4},{7,6},{8,9},{10,11},{9,8... | collective-permute-start | bytes 786440 | tf_op jit(solution)/shard_map/ppermute | solution.py:376
  10.2 1.4 %collective-permute-start.1 = (bf16[128,1024]{1,0:T(8,128)(2,1)}, bf16[128,1024]{1,0:T(8,128)(2,1)}, u32[]{:S(2)}, u32[]{:S(2)}) collective-permute-start(bf16[128,1024]{1,0:T(8,128)(2,1)} %get-tuple-element.31.refs_1_), channel_id=1, source_target_pairs={{1,2},{2,1},{5,6},{6,5},{9,10},{10,9},{13,14},{14,13},{17,18},{18,... | collective-permute-start | bytes 786440 | tf_op jit(solution)/shard_map/ppermute | solution.py:376
  11.7 1.2 %copy-done.5 = bf16[1,512,1024]{2,1,0:T(8,128)(2,1)S(1)} copy-done((bf16[1,512,1024]{2,1,0:T(8,128)(2,1)S(1)}, bf16[1,512,1024]{2,1,0:T(8,128)(2,1)}, u32[]{:S(2)}) %copy-start.5) | copy-done | bytes 1048600
  12.9 3.2 %partial_blocks.1 = (bf16[128,1024]{1,0:T(8,128)(2,1)S(1)}, bf16[128,1024]{1,0:T(8,128)(2,1)S(1)}, bf16[128,1024]{1,0:T(8,128)(2,1)S(1)}, bf16[128,1024]{1,0:T(8...) custom-call(s32[2]{0:T(128)S(1)} %pad_add_fusion.where_ref, ...), custom_call_target="tpu_custom_call" | custom-call | bytes 1024 | tf_op jit(solution)/shard_map/partial_blocks/pallas_call | solution.py:166
  17.6 0.7 pick.3
  18.3 1.3 %collective-permute-start.13 = (bf16[768,1024]{1,0:T(8,128)(2,1)S(1)}, bf16[768,1024]{1,0:T(8,128)(2,1)S(1)}, u32[]{:S(2)}, u32[]{:S(2)}) collective-permute-start(bf16[768,1024]{1,0:T(8,128)(2,1)S(1)} %pick.3), channel_id=1, source_target_pairs={{0,8},{4,12},{8,0},{12,4},{1,9},{5,13},{9,1},{13,5},{2,10},{6,14},... | collective-permute-start | bytes 4718600 | tf_op jit(solution)/shard_map/ppermute | solution.py:381
  19.5 0.7 collective-permute-start.6
  20.2 4.7 %collective-permute-start.5 = (bf16[128,1024]{1,0:T(8,128)(2,1)S(1)}, bf16[128,1024]{1,0:T(8,128)(2,1)S(1)}, u32[]{:S(2)}, u32[]{:S(2)}) collective-permute-start(bf16[128,1024]{1,0:T(8,128)(2,1)S(1)} %to_send.12.after_ref), channel_id=1, source_target_pairs={{0,1},{2,3},{1,0},{3,2},{4,5},{6,7},{5,4},{7,6},{8,9},{10,11},{9,8... | collective-permute-start | bytes 786440 | tf_op jit(solution)/shard_map/ppermute | solution.py:376
  24.9 1.0 %to_send.14.after_ref = bf16[128,1024]{1,0:T(8,128)(2,1)S(1)} custom-call(bf16[128,1024]{1,0:T(8,128)(2,1)} %collective-permute-done.1.arrived_ref.refs_5_, bf16[128,1024]{1,0:T(8,128)(2,1)S(1)} %get-tuple-element.33.term_ref, bf16[128,1024]{1,0:T(8,128)(2,1)S(1)} %to_send.13.after_ref), custom_call_target="tpu_custom_call" | custom-call | bytes 1024 | tf_op jit(solution)/shard_map/to_send/pallas_call | solution.py:200
  26.1 0.7 collective-permute-start.4
  26.8 1.5 %collective-permute-start.8 = (bf16[128,1024]{1,0:T(8,128)(2,1)S(1)}, bf16[128,1024]{1,0:T(8,128)(2,1)S(1)}, u32[]{:S(2)}, u32[]{:S(2)}) collective-permute-start(bf16[128,1024]{1,0:T(8,128)(2,1)S(1)} %to_send.14.after_ref), channel_id=1, source_target_pairs={{0,1},{2,3},{1,0},{3,2},{4,5},{6,7},{5,4},{7,6},{8,9},{10,11},{9,8... | collective-permute-start | bytes 786440 | tf_op jit(solution)/shard_map/ppermute | solution.py:376
  28.4 1.5 %collective-permute-done.5.arrived_ref.refs_6_ = bf16[128,1024]{1,0:T(8,128)(2,1)S(1)} collective-permute-done((bf16[128,1024]{1,0:T(8,128)(2,1)S(1)}, bf16[128,1024]{1,0:T(8,128)(2,1)S(1)}, u32[]{:S(2)}, u32[]{:S(2)}) %collective-permute-start.5) | collective-permute-done | bytes 262176 | tf_op jit(solution)/shard_map/ppermute | solution.py:376
  29.9 0.7 collective-permute-start.11
  30.6 2.8 %collective-permute-start.10 = (bf16[128,1024]{1,0:T(8,128)(2,1)S(1)}, bf16[128,1024]{1,0:T(8,128)(2,1)S(1)}, u32[]{:S(2)}, u32[]{:S(2)}) collective-permute-start(bf16[128,1024]{1,0:T(8,128)(2,1)S(1)} %to_send.16.after_ref), channel_id=1, source_target_pairs={{0,1},{2,3},{1,0},{3,2},{4,5},{6,7},{5,4},{7,6},{8,9},{10,11},{9,8... | collective-permute-start | bytes 786440 | tf_op jit(solution)/shard_map/ppermute | solution.py:376
  33.5 1.9 %collective-permute-done.8.arrived_ref.refs_7_ = bf16[128,1024]{1,0:T(8,128)(2,1)S(1)} collective-permute-done((bf16[128,1024]{1,0:T(8,128)(2,1)S(1)}, bf16[128,1024]{1,0:T(8,128)(2,1)S(1)}, u32[]{:S(2)}, u32[]{:S(2)}) %collective-permute-start.8) | collective-permute-done | bytes 262176 | tf_op jit(solution)/shard_map/ppermute | solution.py:376
  35.6 0.7 collective-permute-start.9
  36.2 3.5 %collective-permute-start.7 = (bf16[128,1024]{1,0:T(8,128)(2,1)S(1)}, bf16[128,1024]{1,0:T(8,128)(2,1)S(1)}, u32[]{:S(2)}, u32[]{:S(2)}) collective-permute-start(bf16[128,1024]{1,0:T(8,128)(2,1)S(1)} %to_send.18.after_ref), channel_id=1, source_target_pairs={{0,1},{2,3},{1,0},{3,2},{4,5},{6,7},{5,4},{7,6},{8,9},{10,11},{9,8... | collective-permute-start | bytes 786440 | tf_op jit(solution)/shard_map/ppermute | solution.py:376
  41.0 0.7 collective-permute-start.17
  41.9 5.0 %collective-permute-start.14 = (bf16[128,1024]{1,0:T(8,128)(2,1)S(1)}, bf16[128,1024]{1,0:T(8,128)(2,1)S(1)}, u32[]{:S(2)}, u32[]{:S(2)}) collective-permute-start(bf16[128,1024]{1,0:T(8,128)(2,1)S(1)} %to_send.22.after_ref), channel_id=1, source_target_pairs={{0,1},{2,3},{1,0},{3,2},{4,5},{6,7},{5,4},{7,6},{8,9},{10,11},{9,8... | collective-permute-start | bytes 786440 | tf_op jit(solution)/shard_map/ppermute | solution.py:376
  46.9 0.7 collective-permute-start.15
  47.6 3.3 %context_grad.1 = (bf16[512,1024]{1,0:T(8,128)(2,1)}, f32[8,128]{1,0:T(8,128)S(1)}) custom-call(s32[2]{0:T(128)S(1)} %pad_add_fusion.where_ref, bf16[512,1024]{1,0:T(8,128)(2,1)S(1)} %bitcast.12, bf16[128,1024]{1,0:T(8,128)(2,1)S(1)} %to_send.23.after_ref, bf16[128,1024]{1,0:T(8,128)(2,1)S(1)} %copy-done.6, bf16[128,1024]{1,0:T(8,128)(2,1)S(1)} %copy-done.7, ...), custom_call_target="tpu_custom_call" | custom-call | bytes 1024 | tf_op jit(solution)/shard_map/context_grad/pallas_call | solution.py:238
  50.9 1.2 %collective-permute-done.16.one_ref = bf16[128,1024]{1,0:T(8,128)(2,1)S(1)} collective-permute-done((bf16[128,1024]{1,0:T(8,128)(2,1)S(1)}, bf16[128,1024]{1,0:T(8,128)(2,1)S(1)}, u32[]{:S(2)}, u32[]{:S(2)}) %collective-permute-start.16) | collective-permute-done | bytes 262176 | tf_op jit(solution)/shard_map/ppermute | solution.py:376
  52.3 4.9 %collective-permute-start.20 = (bf16[128,1024]{1,0:T(8,128)(2,1)S(1)}, bf16[128,1024]{1,0:T(8,128)(2,1)S(1)}, u32[]{:S(2)}, u32[]{:S(2)}) collective-permute-start(bf16[128,1024]{1,0:T(8,128)(2,1)S(1)} %summed_grad.2.after_ref.own_ref.grad_ref), channel_id=1, source_target_pairs={{0,4},{4,0},{8,12},{12,8},{1,5},{5,1},{9,13},{13,9},{2,6},{6,2},{1... | collective-permute-start | bytes 786440 | tf_op jit(solution)/shard_map/ppermute | solution.py:380
  57.9 2.5 %collective-permute-start.18 = (bf16[128,1024]{1,0:T(8,128)(2,1)S(1)}, bf16[128,1024]{1,0:T(8,128)(2,1)S(1)}, u32[]{:S(2)}, u32[]{:S(2)}) collective-permute-start(bf16[128,1024]{1,0:T(8,128)(2,1)S(1)} %summed_grad.3.own_ref.after_ref.grad_ref), channel_id=1, source_target_pairs={{0,4},{4,0},{8,12},{12,8},{1,5},{5,1},{9,13},{13,9},{2,6},{6,2},{1... | collective-permute-start | bytes 786440 | tf_op jit(solution)/shard_map/ppermute | solution.py:380
  60.9 0.7 collective-permute-done.18.mate_ref
  62.3 0.9 %taken_state.1 = (f32[384,1024]{1,0:T(8,128)S(1)}, f32[384,1024]{1,0:T(8,128)S(1)}) custom-call(s32[2]{0:T(128)S(1)} %pad_add_fusion.where_ref, s32[4]{0:T(128)S(1)} %copy-done.8, f32[256,1024]{1,0:T(8,128)S(1)} %bitcast.14, f32[256,1024]{1,0:T(8,128)S(1)} %bitcast.16, f32[256,1024]{1,0:T(8,128)S(1)} %bitcast.18, ...), custom_call_target="tpu_custom_call" | custom-call | bytes 1024 | tf_op jit(solution)/shard_map/taken_state/pallas_call | solution.py:287
  63.3 5.3 %collective-permute-done.21.across_ref = bf16[128,1024]{1,0:T(8,128)(2,1)S(1)} collective-permute-done((bf16[128,1024]{1,0:T(8,128)(2,1)S(1)}, bf16[128,1024]{1,0:T(8,128)(2,1)S(1)}, u32[]{:S(2)}, u32[]{:S(2)}) %collective-permute-start.21) | collective-permute-done | bytes 262176 | tf_op jit(solution)/shard_map/ppermute | solution.py:381
  68.6 1.6 %adam.2 = (f32[256,1024]{1,0:T(8,128)}, f32[256,1024]{1,0:T(8,128)}, f32[256,1024]{1,0:T(8,128)}) custom-call(f32[8,1024]{1,0:T(8,128)S(1)} %choices.1.choices_ref, f32[384,1024]{1,0:T(8,128)S(1)} %get-tuple-element.51.state_ref, bf16[128,1024]{1,0:T(8,128)(2,1)S(1)} %summed_grad.2.after_ref.own_ref.grad_ref, ...), custom_call_target="tpu_custom_call" | custom-call | bytes 1024 | tf_op jit(solution)/shard_map/adam/pallas_call | solution.py:332
  70.2 4.0 %collective-permute-done.19.across_ref = bf16[128,1024]{1,0:T(8,128)(2,1)S(1)} collective-permute-done((bf16[128,1024]{1,0:T(8,128)(2,1)S(1)}, bf16[128,1024]{1,0:T(8,128)(2,1)S(1)}, u32[]{:S(2)}, u32[]{:S(2)}) %collective-permute-start.19) | collective-permute-done | bytes 262176 | tf_op jit(solution)/shard_map/ppermute | solution.py:381
  74.2 1.6 %adam.3 = (f32[256,1024]{1,0:T(8,128)}, f32[256,1024]{1,0:T(8,128)}, f32[256,1024]{1,0:T(8,128)}) custom-call(f32[8,1024]{1,0:T(8,128)S(1)} %choices.1.choices_ref, f32[384,1024]{1,0:T(8,128)S(1)} %get-tuple-element.47.state_ref, ...), custom_call_target="tpu_custom_call", output_to_operand_aliasing={{0}: (5, {}), {1}: (6, {}), {2}: (7, {})} | custom-call | bytes 1024 | tf_op jit(solution)/shard_map/adam/pallas_call | solution.py:332
  (61 shorter events, 5.6 us)
Async XLA Ops:
  0.6 11.0 %copy-start = (bf16[1,512,1024]{2,1,0:T(8,128)(2,1)S(1)}, bf16[1,512,1024]{2,1,0:T(8,128)(2,1)}, u32[]{:S(2)}) copy-start(bf16[1,512,1024]{2,1,0:T(8,128)(2,1)} %param.10) | copy-start | bytes 3145732
  4.0 12.1 %copy-start.8 = (s32[4]{0:T(128)S(1)}, s32[4]{0:T(128)}, u32[]{:S(2)}) copy-start(s32[4]{0:T(128)} %donor_ref.3) | copy-start | bytes 52
  4.0 12.1 %copy-start.9 = (f32[4]{0:T(128)S(1)}, f32[4]{0:T(128)}, u32[]{:S(2)}) copy-start(f32[4]{0:T(128)} %rates_ref.1) | copy-start | bytes 52
  4.0 12.1 %copy-start.10 = (f32[4]{0:T(128)S(1)}, f32[4]{0:T(128)}, u32[]{:S(2)}) copy-start(f32[4]{0:T(128)} %decays_ref.1) | copy-start | bytes 52
  4.0 12.1 %copy-start.11 = (s32[4]{0:T(128)S(1)}, s32[4]{0:T(128)}, u32[]{:S(2)}) copy-start(s32[4]{0:T(128)} %steps_ref.1) | copy-start | bytes 52
  4.0 13.0 %collective-permute-start.12 = (bf16[768,1024]{1,0:T(8,128)(2,1)}, bf16[768,1024]{1,0:T(8,128)(2,1)S(1)}, u32[]{:S(2)}, u32[]{:S(2)}) collective-permute-start(bf16[768,1024]{1,0:T(8,128)(2,1)} %get-tuple-element.46.own_ref), channel_id=1, source_target_pairs={{0,4},{4,0},{8,12},{12,8},{1,5},{5,1},{9,13},{13,9},{2,6},{6,2},{1... | collective-permute-start | bytes 4718600 | tf_op jit(solution)/shard_map/ppermute | solution.py:380
  4.2 12.6 %collective-permute-start.3 = (bf16[128,1024]{1,0:T(8,128)(2,1)}, bf16[128,1024]{1,0:T(8,128)(2,1)S(1)}, u32[]{:S(2)}, u32[]{:S(2)}) collective-permute-start(bf16[128,1024]{1,0:T(8,128)(2,1)} %get-tuple-element.34.after_ref.refs_0_), channel_id=1, source_target_pairs={{1,2},{2,1},{5,6},{6,5},{9,10},{10,9},{13,14},{14,13},{17,18},{18,... | collective-permute-start | bytes 786440 | tf_op jit(solution)/shard_map/ppermute | solution.py:376
  4.8 12.1 %collective-permute-start.2 = (bf16[128,1024]{1,0:T(8,128)(2,1)}, bf16[128,1024]{1,0:T(8,128)(2,1)S(1)}, u32[]{:S(2)}, u32[]{:S(2)}) collective-permute-start(bf16[128,1024]{1,0:T(8,128)(2,1)} %get-tuple-element.34.after_ref.refs_0_), channel_id=1, source_target_pairs={{0,1},{2,3},{1,0},{3,2},{4,5},{6,7},{5,4},{7,6},{8,9},{10,11},{9,8... | collective-permute-start | bytes 786440 | tf_op jit(solution)/shard_map/ppermute | solution.py:376
  10.2 15.8 %collective-permute-start = (bf16[128,1024]{1,0:T(8,128)(2,1)}, bf16[128,1024]{1,0:T(8,128)(2,1)S(1)}, u32[]{:S(2)}, u32[]{:S(2)}) collective-permute-start(bf16[128,1024]{1,0:T(8,128)(2,1)} %get-tuple-element.31.refs_1_), channel_id=1, source_target_pairs={{0,1},{2,3},{1,0},{3,2},{4,5},{6,7},{5,4},{7,6},{8,9},{10,11},{9,8... | collective-permute-start | bytes 786440 | tf_op jit(solution)/shard_map/ppermute | solution.py:376
  10.2 14.7 %collective-permute-start.1 = (bf16[128,1024]{1,0:T(8,128)(2,1)}, bf16[128,1024]{1,0:T(8,128)(2,1)}, u32[]{:S(2)}, u32[]{:S(2)}) collective-permute-start(bf16[128,1024]{1,0:T(8,128)(2,1)} %get-tuple-element.31.refs_1_), channel_id=1, source_target_pairs={{1,2},{2,1},{5,6},{6,5},{9,10},{10,9},{13,14},{14,13},{17,18},{18,... | collective-permute-start | bytes 786440 | tf_op jit(solution)/shard_map/ppermute | solution.py:376
  12.9 3.9 %copy-start.6 = (bf16[128,1024]{1,0:T(8,128)(2,1)S(1)}, bf16[128,1024]{1,0:T(8,128)(2,1)}, u32[]{:S(2)}) copy-start(bf16[128,1024]{1,0:T(8,128)(2,1)} %get-tuple-element.34.after_ref.refs_0_) | copy-start | bytes 786436
  18.3 44.1 %collective-permute-start.13 = (bf16[768,1024]{1,0:T(8,128)(2,1)S(1)}, bf16[768,1024]{1,0:T(8,128)(2,1)S(1)}, u32[]{:S(2)}, u32[]{:S(2)}) collective-permute-start(bf16[768,1024]{1,0:T(8,128)(2,1)S(1)} %pick.3), channel_id=1, source_target_pairs={{0,8},{4,12},{8,0},{12,4},{1,9},{5,13},{9,1},{13,5},{2,10},{6,14},... | collective-permute-start | bytes 4718600 | tf_op jit(solution)/shard_map/ppermute | solution.py:381
  19.5 8.7 %collective-permute-start.6 = (bf16[128,1024]{1,0:T(8,128)(2,1)S(1)}, bf16[128,1024]{1,0:T(8,128)(2,1)S(1)}, u32[]{:S(2)}, u32[]{:S(2)}) collective-permute-start(bf16[128,1024]{1,0:T(8,128)(2,1)S(1)} %to_send.13.after_ref), channel_id=1, source_target_pairs={{1,2},{2,1},{5,6},{6,5},{9,10},{10,9},{13,14},{14,13},{17,18},{18,... | collective-permute-start | bytes 786440 | tf_op jit(solution)/shard_map/ppermute | solution.py:376
  20.2 9.6 %collective-permute-start.5 = (bf16[128,1024]{1,0:T(8,128)(2,1)S(1)}, bf16[128,1024]{1,0:T(8,128)(2,1)S(1)}, u32[]{:S(2)}, u32[]{:S(2)}) collective-permute-start(bf16[128,1024]{1,0:T(8,128)(2,1)S(1)} %to_send.12.after_ref), channel_id=1, source_target_pairs={{0,1},{2,3},{1,0},{3,2},{4,5},{6,7},{5,4},{7,6},{8,9},{10,11},{9,8... | collective-permute-start | bytes 786440 | tf_op jit(solution)/shard_map/ppermute | solution.py:376
  26.1 7.3 %collective-permute-start.4 = (bf16[128,1024]{1,0:T(8,128)(2,1)S(1)}, bf16[128,1024]{1,0:T(8,128)(2,1)S(1)}, u32[]{:S(2)}, u32[]{:S(2)}) collective-permute-start(bf16[128,1024]{1,0:T(8,128)(2,1)S(1)} %to_send.15.after_ref), channel_id=1, source_target_pairs={{1,2},{2,1},{5,6},{6,5},{9,10},{10,9},{13,14},{14,13},{17,18},{18,... | collective-permute-start | bytes 786440 | tf_op jit(solution)/shard_map/ppermute | solution.py:376
  26.8 8.7 %collective-permute-start.8 = (bf16[128,1024]{1,0:T(8,128)(2,1)S(1)}, bf16[128,1024]{1,0:T(8,128)(2,1)S(1)}, u32[]{:S(2)}, u32[]{:S(2)}) collective-permute-start(bf16[128,1024]{1,0:T(8,128)(2,1)S(1)} %to_send.14.after_ref), channel_id=1, source_target_pairs={{0,1},{2,3},{1,0},{3,2},{4,5},{6,7},{5,4},{7,6},{8,9},{10,11},{9,8... | collective-permute-start | bytes 786440 | tf_op jit(solution)/shard_map/ppermute | solution.py:376
  29.9 9.8 %collective-permute-start.11 = (bf16[128,1024]{1,0:T(8,128)(2,1)S(1)}, bf16[128,1024]{1,0:T(8,128)(2,1)S(1)}, u32[]{:S(2)}, u32[]{:S(2)}) collective-permute-start(bf16[128,1024]{1,0:T(8,128)(2,1)S(1)} %to_send.17.after_ref), channel_id=1, source_target_pairs={{1,2},{2,1},{5,6},{6,5},{9,10},{10,9},{13,14},{14,13},{17,18},{18,... | collective-permute-start | bytes 786440 | tf_op jit(solution)/shard_map/ppermute | solution.py:376
  30.6 10.3 %collective-permute-start.10 = (bf16[128,1024]{1,0:T(8,128)(2,1)S(1)}, bf16[128,1024]{1,0:T(8,128)(2,1)S(1)}, u32[]{:S(2)}, u32[]{:S(2)}) collective-permute-start(bf16[128,1024]{1,0:T(8,128)(2,1)S(1)} %to_send.16.after_ref), channel_id=1, source_target_pairs={{0,1},{2,3},{1,0},{3,2},{4,5},{6,7},{5,4},{7,6},{8,9},{10,11},{9,8... | collective-permute-start | bytes 786440 | tf_op jit(solution)/shard_map/ppermute | solution.py:376
  35.6 6.2 %collective-permute-start.9 = (bf16[128,1024]{1,0:T(8,128)(2,1)S(1)}, bf16[128,1024]{1,0:T(8,128)(2,1)S(1)}, u32[]{:S(2)}, u32[]{:S(2)}) collective-permute-start(bf16[128,1024]{1,0:T(8,128)(2,1)S(1)} %to_send.19.after_ref), channel_id=1, source_target_pairs={{1,2},{2,1},{5,6},{6,5},{9,10},{10,9},{13,14},{14,13},{17,18},{18,... | collective-permute-start | bytes 786440 | tf_op jit(solution)/shard_map/ppermute | solution.py:376
  36.2 10.6 %collective-permute-start.7 = (bf16[128,1024]{1,0:T(8,128)(2,1)S(1)}, bf16[128,1024]{1,0:T(8,128)(2,1)S(1)}, u32[]{:S(2)}, u32[]{:S(2)}) collective-permute-start(bf16[128,1024]{1,0:T(8,128)(2,1)S(1)} %to_send.18.after_ref), channel_id=1, source_target_pairs={{0,1},{2,3},{1,0},{3,2},{4,5},{6,7},{5,4},{7,6},{8,9},{10,11},{9,8... | collective-permute-start | bytes 786440 | tf_op jit(solution)/shard_map/ppermute | solution.py:376
  39.9 12.3 %collective-permute-start.16 = (bf16[128,1024]{1,0:T(8,128)(2,1)S(1)}, bf16[128,1024]{1,0:T(8,128)(2,1)S(1)}, u32[]{:S(2)}, u32[]{:S(2)}) collective-permute-start(bf16[128,1024]{1,0:T(8,128)(2,1)S(1)} %to_send.20.after_ref), channel_id=1, source_target_pairs={{0,1},{2,3},{1,0},{3,2},{4,5},{6,7},{5,4},{7,6},{8,9},{10,11},{9,8... | collective-permute-start | bytes 786440 | tf_op jit(solution)/shard_map/ppermute | solution.py:376
  40.9 6.7 %copy-start.7 = (bf16[128,1024]{1,0:T(8,128)(2,1)S(1)}, bf16[128,1024]{1,0:T(8,128)(2,1)}, u32[]{:S(2)}) copy-start(bf16[128,1024]{1,0:T(8,128)(2,1)} %get-tuple-element.31.refs_1_) | copy-start | bytes 786436
  41.0 11.1 %collective-permute-start.17 = (bf16[128,1024]{1,0:T(8,128)(2,1)S(1)}, bf16[128,1024]{1,0:T(8,128)(2,1)S(1)}, u32[]{:S(2)}, u32[]{:S(2)}) collective-permute-start(bf16[128,1024]{1,0:T(8,128)(2,1)S(1)} %to_send.21.after_ref), channel_id=1, source_target_pairs={{1,2},{2,1},{5,6},{6,5},{9,10},{10,9},{13,14},{14,13},{17,18},{18,... | collective-permute-start | bytes 786440 | tf_op jit(solution)/shard_map/ppermute | solution.py:376
  41.9 15.9 %collective-permute-start.14 = (bf16[128,1024]{1,0:T(8,128)(2,1)S(1)}, bf16[128,1024]{1,0:T(8,128)(2,1)S(1)}, u32[]{:S(2)}, u32[]{:S(2)}) collective-permute-start(bf16[128,1024]{1,0:T(8,128)(2,1)S(1)} %to_send.22.after_ref), channel_id=1, source_target_pairs={{0,1},{2,3},{1,0},{3,2},{4,5},{6,7},{5,4},{7,6},{8,9},{10,11},{9,8... | collective-permute-start | bytes 786440 | tf_op jit(solution)/shard_map/ppermute | solution.py:376
  46.9 10.9 %collective-permute-start.15 = (bf16[128,1024]{1,0:T(8,128)(2,1)S(1)}, bf16[128,1024]{1,0:T(8,128)(2,1)S(1)}, u32[]{:S(2)}, u32[]{:S(2)}) collective-permute-start(bf16[128,1024]{1,0:T(8,128)(2,1)S(1)} %to_send.23.after_ref), channel_id=1, source_target_pairs={{1,2},{2,1},{5,6},{6,5},{9,10},{10,9},{13,14},{14,13},{17,18},{18,... | collective-permute-start | bytes 786440 | tf_op jit(solution)/shard_map/ppermute | solution.py:376
  52.3 8.2 %collective-permute-start.20 = (bf16[128,1024]{1,0:T(8,128)(2,1)S(1)}, bf16[128,1024]{1,0:T(8,128)(2,1)S(1)}, u32[]{:S(2)}, u32[]{:S(2)}) collective-permute-start(bf16[128,1024]{1,0:T(8,128)(2,1)S(1)} %summed_grad.2.after_ref.own_ref.grad_ref), channel_id=1, source_target_pairs={{0,4},{4,0},{8,12},{12,8},{1,5},{5,1},{9,13},{13,9},{2,6},{6,2},{1... | collective-permute-start | bytes 786440 | tf_op jit(solution)/shard_map/ppermute | solution.py:380
  57.8 4.5 %copy-start.1 = (f32[1,256,1024]{2,1,0:T(8,128)S(1)}, f32[1,256,1024]{2,1,0:T(8,128)}, u32[]{:S(2)}) copy-start(f32[1,256,1024]{2,1,0:T(8,128)} %param.11) | copy-start | bytes 3145732
  57.8 4.5 %copy-start.2 = (f32[1,256,1024]{2,1,0:T(8,128)S(1)}, f32[1,256,1024]{2,1,0:T(8,128)}, u32[]{:S(2)}) copy-start(f32[1,256,1024]{2,1,0:T(8,128)} %param.12) | copy-start | bytes 3145732
  57.8 4.5 %copy-start.3 = (f32[1,256,1024]{2,1,0:T(8,128)S(1)}, f32[1,256,1024]{2,1,0:T(8,128)}, u32[]{:S(2)}) copy-start(f32[1,256,1024]{2,1,0:T(8,128)} %param.13) | copy-start | bytes 3145732
  57.9 3.7 %collective-permute-start.18 = (bf16[128,1024]{1,0:T(8,128)(2,1)S(1)}, bf16[128,1024]{1,0:T(8,128)(2,1)S(1)}, u32[]{:S(2)}, u32[]{:S(2)}) collective-permute-start(bf16[128,1024]{1,0:T(8,128)(2,1)S(1)} %summed_grad.3.own_ref.after_ref.grad_ref), channel_id=1, source_target_pairs={{0,4},{4,0},{8,12},{12,8},{1,5},{5,1},{9,13},{13,9},{2,6},{6,2},{1... | collective-permute-start | bytes 786440 | tf_op jit(solution)/shard_map/ppermute | solution.py:380
  60.6 8.0 %collective-permute-start.21 = (bf16[128,1024]{1,0:T(8,128)(2,1)S(1)}, bf16[128,1024]{1,0:T(8,128)(2,1)S(1)}, u32[]{:S(2)}, u32[]{:S(2)}) collective-permute-start(bf16[128,1024]{1,0:T(8,128)(2,1)S(1)} %pick.5), channel_id=1, source_target_pairs={{0,8},{4,12},{8,0},{12,4},{1,9},{5,13},{9,1},{13,5},{2,10},{6,14},... | collective-permute-start | bytes 786440 | tf_op jit(solution)/shard_map/ppermute | solution.py:381
  61.8 12.4 %collective-permute-start.19 = (bf16[128,1024]{1,0:T(8,128)(2,1)S(1)}, bf16[128,1024]{1,0:T(8,128)(2,1)S(1)}, u32[]{:S(2)}, u32[]{:S(2)}) collective-permute-start(bf16[128,1024]{1,0:T(8,128)(2,1)S(1)} %pick.4), channel_id=1, source_target_pairs={{0,8},{4,12},{8,0},{12,4},{1,9},{5,13},{9,1},{13,5},{2,10},{6,14},... | collective-permute-start | bytes 786440 | tf_op jit(solution)/shard_map/ppermute | solution.py:381
  (2 other events, 2.6 us)

commit v6 on v5

--- a/solution.py
+++ b/solution.py
@@ -17,7 +17,6 @@
 VMEM = pl.BlockSpec(memory_space=pltpu.VMEM)
 HBM = pl.BlockSpec(memory_space=pltpu.HBM)
 ANY = pl.BlockSpec(memory_space=pl.ANY)
-SMALL = pl.CostEstimate(flops=0, bytes_accessed=1024, transcendentals=0)
 
 
 def call(kernel, name, out_shape, in_specs, out_specs, limit=8, scratch=(), aliases=None):
@@ -29,13 +28,21 @@
         scratch_shapes=scratch,
         input_output_aliases=aliases or {},
         compiler_params=pltpu.CompilerParams(vmem_limit_bytes=limit * MIB),
-        cost_estimate=SMALL,
+        cost_estimate=pl.CostEstimate(flops=0, bytes_accessed=1024, transcendentals=0),
         name=name,
     )
 
 
 def half_array(rows, depth):
     return jax.ShapeDtypeStruct((rows, depth), jnp.bfloat16)
+
+
+def gate_kernel(value_ref, after_ref, out_ref):
+    pass
+
+
+def gate(value, after):
+    return call(gate_kernel, "gate", half_array(*value.shape), [ANY, ANY], ANY, aliases={0: 0})(value, after)
 
 
 def by_rows(ref, body, step=16):
@@ -52,7 +59,7 @@
 def choices_kernel(where_ref, rates_ref, decays_ref, steps_ref, donor_ref, out_ref):
     member = where_ref[1]
     source = source_of(member, donor_ref)
-    way = jnp.minimum(jnp.bitwise_xor(source, member), 2)
+    way = jnp.bitwise_xor(source, member)
     partner_source = source_of(jnp.bitwise_xor(member, 2), donor_ref)
     flags = [partner_source == jnp.bitwise_xor(member, 1), way == 0, way == 1, way == 2]
     depth = out_ref.shape[1]
@@ -197,9 +204,9 @@
 
 
 def summed(kernel, name, addends, after):
-    return call(kernel, name, half_array(*addends[0].shape), [VMEM] * len(addends) + [ANY], VMEM)(
-        *addends, after
-    )
+    return call(
+        kernel, name, half_array(*addends[0].shape), [VMEM] * len(addends) + [ANY], VMEM
+    )(*addends, after)
 
 
 def columns_kernel(n, scale, parts, where_ref, cotangent_ref, after_ref, *refs):
@@ -247,7 +254,7 @@
     )(where, cotangent, after, *blocks)
 
 
-def state_kernel(parts, where_ref, donor_ref, *refs):
+def state_kernel(parts, where_ref, donor_ref, after_ref, *refs):
     own, (mate_ref, across_ref), refs = refs[:3], refs[3:5], refs[5:]
     outs, (taken, sems) = refs[:-2], refs[-2:]
     rows = own[0].shape[0]
@@ -282,20 +289,20 @@
     pl.when(way > 1)(lambda: widen(across_ref))
 
 
-def taken_state(parts, where, donor, own, donated):
+def taken_state(parts, where, donor, own, donated, after):
     rows, depth = own[0].shape
     return call(
         functools.partial(state_kernel, parts), "taken_state",
         [jax.ShapeDtypeStruct((3 * size, depth), jnp.float32) for _, size in parts],
-        [SMEM, SMEM] + [HBM] * 3 + [ANY] * 2, [VMEM] * len(parts),
+        [SMEM, SMEM, ANY] + [HBM] * 3 + [ANY] * 2, [VMEM] * len(parts),
         scratch=[pltpu.VMEM((3 * rows, depth), jnp.bfloat16), pltpu.SemaphoreType.DMA((3 * len(parts),))],
-    )(where, donor, *own, *donated)
-
-
-def adam_kernel(start, size, filled, choices_ref, state_ref, grad_ref, mate_ref, across_ref, *refs):
+    )(where, donor, after, *own, *donated)
+
+
+def adam_kernel(start, size, filled, choices_ref, state_ref, own_ref, mate_ref, across_ref, far_ref, after_ref, *refs):
     refs = refs[3 if filled else 0:]
     outs, (stepped, sems) = refs[:3], refs[3:]
-    depth = grad_ref.shape[1]
+    depth = own_ref.shape[1]
     pieces = 4 if size % 64 == 0 else 1
     piece = size // pieces
     writes = []
@@ -304,10 +311,9 @@
             at = pl.ds(pl.multiple_of(p * piece + i * 16, 16), 16)
             row = lambda k: jnp.broadcast_to(choices_ref[k:k + 1, :], (16, depth))
             load = lambda k: state_ref[pl.ds(pl.multiple_of(k * size + p * piece + i * 16, 16), 16), :]
-            g = jnp.where(
-                row(1) > 0, grad_ref[at, :].astype(jnp.float32),
-                jnp.where(row(2) > 0, mate_ref[at, :].astype(jnp.float32), across_ref[at, :].astype(jnp.float32)),
-            )
+            g = far_ref[at, :].astype(jnp.float32)
+            for k, ref in ((1, own_ref), (2, mate_ref), (3, across_ref)):
+                g = jnp.where(row(k) > 0, ref[at, :].astype(jnp.float32), g)
             w = load(0)
             first_step = beta_one * load(1) + (1.0 - beta_one) * g
             second_step = beta_two * load(2) + (1.0 - beta_two) * g * g
@@ -327,15 +333,15 @@
         write.wait()
 
 
-def adam_update(start, size, rows, choices, state, grads, filled):
+def adam_update(start, size, rows, choices, state, grads, after, filled):
     depth = state.shape[1]
     return call(
         functools.partial(adam_kernel, start, size, bool(filled)), "adam",
         [jax.ShapeDtypeStruct((rows, depth), jnp.float32)] * 3,
-        [VMEM] * 5 + [HBM] * len(filled), [HBM] * 3,
+        [VMEM] * 6 + [ANY] + [HBM] * len(filled), [HBM] * 3,
         scratch=[pltpu.VMEM((3, size, depth), jnp.float32), pltpu.SemaphoreType.DMA((12,))],
-        aliases={5 + k: k for k in range(len(filled))},
-    )(choices, state, *grads, *filled)
+        aliases={7 + k: k for k in range(len(filled))},
+    )(choices, state, *grads, after, *filled)
 
 
 def on_device(n, members, context, out_grad, weight, first, second, rates, decays, steps, donor):
@@ -376,28 +382,29 @@
                 now[swap].append(lax.ppermute(block, "shard", swaps[swap]))
         arrived.append(now)
 
-    def from_members(held, after):
-        mate = lax.ppermute(held, "member", swap_mates)
-        return mate, lax.ppermute(pick(choices, held, mate, after), "member", swap_across)
-
-    states = taken_state(
-        parts, where, donor, (weight[0], first[0], second[0]), from_members(state, early)
-    )
-    blocks = list(own)
-    for slot in range(1, n):
-        blocks += arrived[slot][0] + arrived[slot][1]
-    context_grad, sent = columns(n, scale, parts, where, cotangent, sent, blocks)
+    mate = lax.ppermute(state, "member", swap_mates)
+    across = lax.ppermute(pick(choices, state, mate, early), "member", swap_across)
+    states = taken_state(parts, where, donor, (weight[0], first[0], second[0]), (mate, across), sent)
 
     grads = []
     for c in range(len(parts)):
         addends = (terms[-1][c], arrived[n][0][c], arrived[n][1][c])
         sent = summed(grad_kernel, "summed_grad", addends, sent)
         grads.append(sent)
+    blocks = list(own)
+    for slot in range(1, n):
+        blocks += arrived[slot][0] + arrived[slot][1]
+    context_grad, computed = columns(n, scale, parts, where, cotangent, sent, blocks)
 
     updated = ()
-    for (start, size), held, grad in zip(parts, states, grads):
+    for c, (start, size) in enumerate(parts):
+        mate = lax.ppermute(grads[c], "member", swap_mates)
+        across = lax.ppermute(grads[c], "member", swap_across)
+        if c == 0:
+            across = gate(across, computed)
+        far = lax.ppermute(across, "member", swap_mates)
         updated = adam_update(
-            start, size, rows, choices, held, (grad,) + from_members(grad, grad), updated
+            start, size, rows, choices, states[c], (grads[c], mate, across, far), computed, updated
         )
     return (context_grad[None],) + tuple(array[None] for array in updated)
 

time: 77 us -> 71.9 us (0.934)
  starting transfers between devices: 39.3 us -> 33.8 us
  waiting for transfers between devices: 15.7 us -> 16.9 us
    ppermute x16, waiting for transfers between devices: 5.69 us -> 15.1 us  [on_device(): now[swap].append(lax.ppermute(block, 'shard', swaps[swap]))]
    ppermute x6 -> x8, waiting for transfers between devices: 10.1 us -> 1.87 us  [the longest x2 1.85 us: on_device(): across = lax.ppermute(grads[c], 'member', swap_across)]
    ppermute x6 -> x8, starting transfers between devices: 9.76 us -> 6.55 us  [the longest x2 2.32 us: on_device(): mate = lax.ppermute(grads[c], 'member', swap_mates)]
    ppermute x16, starting transfers between devices: 29.6 us -> 27.3 us  [on_device(): now[swap].append(lax.ppermute(block, 'shard', swaps[swap]))]
  transfers between devices with their start and end apart: 22 -> 24, of which waited for: 8 -> 7; matrix products, arithmetic and copies ran while one was open for 0% -> 0% of each run, Pallas kernels for 17% -> 18%
where the time goes in v6:
time: 71.9 us; the launch traced here: 71.3 us
  starting transfers between devices  33.8 us (47%)
  Pallas kernels  17.6 us (24%)
  waiting for transfers between devices  16.9 us (24%)
  local copies, waits for them, and re-layouts  1.81 us (3%)
  between operations  1.08 us (2%)
    ppermute x16, starting transfers between devices, on_device(): now[swap].append(lax.ppermute(block, 'shard', swaps[swap]))  27.3 us
    ppermute x16, waiting for transfers between devices, on_device(): now[swap].append(lax.ppermute(block, 'shard', swaps[swap]))  15.1 us
    pallas_call x2, Pallas kernels, adam_update(): call(functools.partial(adam_kernel, start, size, bool(filled)), 'adam', [...  3.34 us
    pallas_call x1, Pallas kernels, halves(): call(functools.partial(halves_kernel, parts), 'halves', [half_array(size,...  3.33 us
    pallas_call x1, Pallas kernels, columns(): call(functools.partial(columns_kernel, n, scale, parts), 'context_grad',...  3.27 us
    pallas_call x1, Pallas kernels, partial_blocks(): call(functools.partial(partial_kernel, n, scale, parts, order), 'partial_...  3.21 us
    pallas_call x14, Pallas kernels, summed(): call(kernel, name, half_array(*addends[0].shape), [VMEM] * len(addends) +...  2.38 us
    ppermute x2, starting transfers between devices, on_device(): mate = lax.ppermute(grads[c], 'member', swap_mates)  2.32 us
  transfers between devices with their start and end apart: 24, of which 7 were waited for; matrix products, arithmetic and copies ran while one was open for 0% of the time, Pallas kernels for 18%

profile of v6, /device:TPU:1, one launch (start us, length us, event | category | flops | bytes accessed | tf_op | source)
XLA Modules:
  0.0 71.3 jit_solution(16537594919285391042)
XLA Ops:
  0.6 3.3 %halves.1 = (bf16[768,1024]{1,0:T(8,128)(2,1)}, bf16[128,1024]{1,0:T(8,128)(2,1)}, bf16[128,1024]{1,0:T(8,128)(2,1)}) custom-call(f32[256,1024]{1,0:T(8,128)} %bitcast.13, f32[256,1024]{1,0:T(8,128)} %bitcast.15, f32[256,1024]{1,0:T(8,128)} %bitcast.17), custom_call_target="tpu_custom_call" | custom-call | bytes 1024 | tf_op jit(solution)/shard_map/halves/pallas_call | solution.py:97
  4.1 0.7 collective-permute-start.2
  4.8 5.3 %collective-permute-start.1 = (bf16[128,1024]{1,0:T(8,128)(2,1)}, bf16[128,1024]{1,0:T(8,128)(2,1)S(1)}, u32[]{:S(2)}, u32[]{:S(2)}) collective-permute-start(bf16[128,1024]{1,0:T(8,128)(2,1)} %get-tuple-element.34.after_ref.refs_0_), channel_id=1, source_target_pairs={{0,1},{2,3},{1,0},{3,2},{4,5},{6,7},{5,4},{7,6},{8,9},{10,11},{9,8... | collective-permute-start | bytes 786440 | tf_op jit(solution)/shard_map/ppermute | solution.py:382
  10.2 0.7 collective-permute-start
  10.8 1.5 %collective-permute-start.4 = (bf16[128,1024]{1,0:T(8,128)(2,1)}, bf16[128,1024]{1,0:T(8,128)(2,1)}, u32[]{:S(2)}, u32[]{:S(2)}) collective-permute-start(bf16[128,1024]{1,0:T(8,128)(2,1)} %get-tuple-element.32.refs_1_), channel_id=1, source_target_pairs={{0,1},{2,3},{1,0},{3,2},{4,5},{6,7},{5,4},{7,6},{8,9},{10,11},{9,8... | collective-permute-start | bytes 786440 | tf_op jit(solution)/shard_map/ppermute | solution.py:382
  12.4 1.2 %copy-done.5 = bf16[1,512,1024]{2,1,0:T(8,128)(2,1)S(1)} copy-done((bf16[1,512,1024]{2,1,0:T(8,128)(2,1)S(1)}, bf16[1,512,1024]{2,1,0:T(8,128)(2,1)}, u32[]{:S(2)}) %copy-start.5) | copy-done | bytes 1048600
  13.6 3.2 %partial_blocks.1 = (bf16[128,1024]{1,0:T(8,128)(2,1)S(1)}, bf16[128,1024]{1,0:T(8,128)(2,1)S(1)}, bf16[128,1024]{1,0:T(8,128)(2,1)S(1)}, bf16[128,1024]{1,0:T(8...) custom-call(s32[2]{0:T(128)S(1)} %pad_add_fusion.where_ref, ...), custom_call_target="tpu_custom_call" | custom-call | bytes 1024 | tf_op jit(solution)/shard_map/partial_blocks/pallas_call | solution.py:173
  18.3 0.7 pick.1
  19.0 1.3 %collective-permute-start.17 = (bf16[768,1024]{1,0:T(8,128)(2,1)S(1)}, bf16[768,1024]{1,0:T(8,128)(2,1)S(1)}, u32[]{:S(2)}, u32[]{:S(2)}) collective-permute-start(bf16[768,1024]{1,0:T(8,128)(2,1)S(1)} %pick.1), channel_id=1, source_target_pairs={{0,8},{4,12},{8,0},{12,4},{1,9},{5,13},{9,1},{13,5},{2,10},{6,14},... | collective-permute-start | bytes 4718600 | tf_op jit(solution)/shard_map/ppermute | solution.py:386
  20.9 2.6 %collective-permute-start.6 = (bf16[128,1024]{1,0:T(8,128)(2,1)S(1)}, bf16[128,1024]{1,0:T(8,128)(2,1)S(1)}, u32[]{:S(2)}, u32[]{:S(2)}) collective-permute-start(bf16[128,1024]{1,0:T(8,128)(2,1)S(1)} %to_send.12.after_ref), channel_id=1, source_target_pairs={{0,1},{2,3},{1,0},{3,2},{4,5},{6,7},{5,4},{7,6},{8,9},{10,11},{9,8... | collective-permute-start | bytes 786440 | tf_op jit(solution)/shard_map/ppermute | solution.py:382
  23.7 1.0 %to_send.15.after_ref = bf16[128,1024]{1,0:T(8,128)(2,1)S(1)} custom-call(bf16[128,1024]{1,0:T(8,128)(2,1)} %collective-permute-done.4.arrived_ref.refs_3_, bf16[128,1024]{1,0:T(8,128)(2,1)S(1)} %get-tuple-element.38.term_ref, bf16[128,1024]{1,0:T(8,128)(2,1)S(1)} %to_send.14.after_ref), custom_call_target="tpu_custom_call" | custom-call | bytes 1024 | tf_op jit(solution)/shard_map/to_send/pallas_call | solution.py:207
  24.7 0.7 collective-permute-start.5
  25.4 1.7 %collective-permute-start.3 = (bf16[128,1024]{1,0:T(8,128)(2,1)S(1)}, bf16[128,1024]{1,0:T(8,128)(2,1)S(1)}, u32[]{:S(2)}, u32[]{:S(2)}) collective-permute-start(bf16[128,1024]{1,0:T(8,128)(2,1)S(1)} %to_send.14.after_ref), channel_id=1, source_target_pairs={{0,1},{2,3},{1,0},{3,2},{4,5},{6,7},{5,4},{7,6},{8,9},{10,11},{9,8... | collective-permute-start | bytes 786440 | tf_op jit(solution)/shard_map/ppermute | solution.py:382
  27.2 1.9 %collective-permute-done.6.arrived_ref.refs_6_ = bf16[128,1024]{1,0:T(8,128)(2,1)S(1)} collective-permute-done((bf16[128,1024]{1,0:T(8,128)(2,1)S(1)}, bf16[128,1024]{1,0:T(8,128)(2,1)S(1)}, u32[]{:S(2)}, u32[]{:S(2)}) %collective-permute-start.6) | collective-permute-done | bytes 262176 | tf_op jit(solution)/shard_map/ppermute | solution.py:382
  29.1 0.7 collective-permute-start.10
  29.8 2.8 %collective-permute-start.9 = (bf16[128,1024]{1,0:T(8,128)(2,1)S(1)}, bf16[128,1024]{1,0:T(8,128)(2,1)S(1)}, u32[]{:S(2)}, u32[]{:S(2)}) collective-permute-start(bf16[128,1024]{1,0:T(8,128)(2,1)S(1)} %to_send.16.after_ref), channel_id=1, source_target_pairs={{0,1},{2,3},{1,0},{3,2},{4,5},{6,7},{5,4},{7,6},{8,9},{10,11},{9,8... | collective-permute-start | bytes 786440 | tf_op jit(solution)/shard_map/ppermute | solution.py:382
  32.7 1.9 %collective-permute-done.3.arrived_ref.refs_7_ = bf16[128,1024]{1,0:T(8,128)(2,1)S(1)} collective-permute-done((bf16[128,1024]{1,0:T(8,128)(2,1)S(1)}, bf16[128,1024]{1,0:T(8,128)(2,1)S(1)}, u32[]{:S(2)}, u32[]{:S(2)}) %collective-permute-start.3) | collective-permute-done | bytes 262176 | tf_op jit(solution)/shard_map/ppermute | solution.py:382
  34.8 0.7 collective-permute-start.8
  35.4 3.2 %collective-permute-start.12 = (bf16[128,1024]{1,0:T(8,128)(2,1)S(1)}, bf16[128,1024]{1,0:T(8,128)(2,1)S(1)}, u32[]{:S(2)}, u32[]{:S(2)}) collective-permute-start(bf16[128,1024]{1,0:T(8,128)(2,1)S(1)} %to_send.18.after_ref), channel_id=1, source_target_pairs={{0,1},{2,3},{1,0},{3,2},{4,5},{6,7},{5,4},{7,6},{8,9},{10,11},{9,8... | collective-permute-start | bytes 786440 | tf_op jit(solution)/shard_map/ppermute | solution.py:382
  38.8 0.7 collective-permute-start.14
  40.2 0.7 collective-permute-start.15
  41.1 4.0 %collective-permute-start.11 = (bf16[128,1024]{1,0:T(8,128)(2,1)S(1)}, bf16[128,1024]{1,0:T(8,128)(2,1)S(1)}, u32[]{:S(2)}, u32[]{:S(2)}) collective-permute-start(bf16[128,1024]{1,0:T(8,128)(2,1)S(1)} %to_send.22.after_ref), channel_id=1, source_target_pairs={{0,1},{2,3},{1,0},{3,2},{4,5},{6,7},{5,4},{7,6},{8,9},{10,11},{9,8... | collective-permute-start | bytes 786440 | tf_op jit(solution)/shard_map/ppermute | solution.py:382
  45.9 0.7 collective-permute-start.13
  46.6 4.8 %collective-permute-done.14.one_ref = bf16[128,1024]{1,0:T(8,128)(2,1)S(1)} collective-permute-done((bf16[128,1024]{1,0:T(8,128)(2,1)S(1)}, bf16[128,1024]{1,0:T(8,128)(2,1)S(1)}, u32[]{:S(2)}, u32[]{:S(2)}) %collective-permute-start.14) | collective-permute-done | bytes 262176 | tf_op jit(solution)/shard_map/ppermute | solution.py:382
  51.9 5.1 %collective-permute-done.11.one_ref = bf16[128,1024]{1,0:T(8,128)(2,1)S(1)} collective-permute-done((bf16[128,1024]{1,0:T(8,128)(2,1)S(1)}, bf16[128,1024]{1,0:T(8,128)(2,1)S(1)}, u32[]{:S(2)}, u32[]{:S(2)}) %collective-permute-start.11) | collective-permute-done | bytes 262176 | tf_op jit(solution)/shard_map/ppermute | solution.py:382
  57.6 2.1 %collective-permute-start.21 = (bf16[128,1024]{1,0:T(8,128)(2,1)S(1)}, bf16[128,1024]{1,0:T(8,128)(2,1)S(1)}, u32[]{:S(2)}, u32[]{:S(2)}) collective-permute-start(bf16[128,1024]{1,0:T(8,128)(2,1)S(1)} %summed_grad.2.after_ref.own_ref), channel_id=1, source_target_pairs={{0,4},{4,0},{8,12},{12,8},{1,5},{5,1},{9,13},{13,9},{2,6},{6,2},{1... | collective-permute-start | bytes 786440 | tf_op jit(solution)/shard_map/ppermute | solution.py:401
  59.7 3.3 %context_grad.1 = (bf16[512,1024]{1,0:T(8,128)(2,1)}, f32[8,128]{1,0:T(8,128)S(1)}) custom-call(s32[2]{0:T(128)S(1)} %pad_add_fusion.where_ref, bf16[512,1024]{1,0:T(8,128)(2,1)S(1)} %bitcast.12, bf16[128,1024]{1,0:T(8,128)(2,1)S(1)} %summed_grad.3.after_ref.own_ref, bf16[128,1024]{1,0:T(8,128)(2,1)S(1)} %copy-done.6, bf16[128,1024]{1,0:T(8,128)(2,1)S(1)} %copy-done.7, ...), custom_call_target="tpu_custom_call" | custom-call | bytes 1024 | tf_op jit(solution)/shard_map/context_grad/pallas_call | solution.py:245
  63.6 1.9 %collective-permute-done.19.across_ref = bf16[128,1024]{1,0:T(8,128)(2,1)S(1)} collective-permute-done((bf16[128,1024]{1,0:T(8,128)(2,1)S(1)}, bf16[128,1024]{1,0:T(8,128)(2,1)S(1)}, u32[]{:S(2)}, u32[]{:S(2)}) %collective-permute-start.19) | collective-permute-done | bytes 262176 | tf_op jit(solution)/shard_map/ppermute | solution.py:402
  65.4 1.7 %collective-permute-start.20 = (bf16[128,1024]{1,0:T(8,128)(2,1)S(1)}, bf16[128,1024]{1,0:T(8,128)(2,1)S(1)}, u32[]{:S(2)}, u32[]{:S(2)}) collective-permute-start(bf16[128,1024]{1,0:T(8,128)(2,1)S(1)} %collective-permute-done.19.across_ref), channel_id=1, source_target_pairs={{0,4},{4,0},{8,12},{12,8},{1,5},{5,1},{9,13},{13,9},{2,6},{6,2},{1... | collective-permute-start | bytes 786440 | tf_op jit(solution)/shard_map/ppermute | solution.py:405
  67.1 0.8 %taken_state.1 = (f32[384,1024]{1,0:T(8,128)S(1)}, f32[384,1024]{1,0:T(8,128)S(1)}) custom-call(s32[2]{0:T(128)S(1)} %pad_add_fusion.where_ref, s32[4]{0:T(128)S(1)} %copy-done.8, bf16[128,1024]{1,0:T(8,128)(2,1)S(1)} %to_send.23.after_ref, f32[256,1024]{1,0:T(8,128)S(1)} %bitcast.14, f32[256,1024]{1,0:T(8,128)S(1)} %bitcast.16, f32[256,1024]{1,0:T(8,128)S(1)} %bitcast.18, ...), custom_call_target="tpu_custom_call" | custom-call | bytes 1024 | tf_op jit(solution)/shard_map/taken_state/pallas_call | solution.py:294
  68.0 1.7 %adam.2 = (f32[256,1024]{1,0:T(8,128)}, f32[256,1024]{1,0:T(8,128)}, f32[256,1024]{1,0:T(8,128)}) custom-call(f32[8,1024]{1,0:T(8,128)S(1)} %choices.1.choices_ref, f32[384,1024]{1,0:T(8,128)S(1)} %get-tuple-element.51.state_ref, bf16[128,1024]{1,0:T(8,128)(2,1)S(1)} %summed_grad.2.after_ref.own_ref, bf16[128,1024]{1,0:T(8,128)(2,1)S(1)} %collective-permute-done.21.mate_ref, ...), custom_call_target="tpu_custom_call" | custom-call | bytes 1024 | tf_op jit(solution)/shard_map/adam/pallas_call | solution.py:338
  69.7 1.7 %adam.3 = (f32[256,1024]{1,0:T(8,128)}, f32[256,1024]{1,0:T(8,128)}, f32[256,1024]{1,0:T(8,128)}) custom-call(f32[8,1024]{1,0:T(8,128)S(1)} %choices.1.choices_ref, f32[384,1024]{1,0:T(8,128)S(1)} %get-tuple-element.49.state_ref, bf16[128,1024]{1,0:T(8,128)(2,1)S(1)} %summed_grad.3.after_ref.own_ref, ...), custom_call_target="tpu_custom_call", output_to_operand_aliasing={{0}: (7, {}), {1}: (8, {}), {2}: (9, {})} | custom-call | bytes 1024 | tf_op jit(solution)/shard_map/adam/pallas_call | solution.py:338
  (64 shorter events, 6.1 us)
Async XLA Ops:
  0.6 11.8 %copy-start = (bf16[1,512,1024]{2,1,0:T(8,128)(2,1)S(1)}, bf16[1,512,1024]{2,1,0:T(8,128)(2,1)}, u32[]{:S(2)}) copy-start(bf16[1,512,1024]{2,1,0:T(8,128)(2,1)} %param.10) | copy-start | bytes 3145732
  4.0 12.9 %copy-start.8 = (s32[4]{0:T(128)S(1)}, s32[4]{0:T(128)}, u32[]{:S(2)}) copy-start(s32[4]{0:T(128)} %donor_ref.3) | copy-start | bytes 52
  4.0 12.9 %copy-start.9 = (f32[4]{0:T(128)S(1)}, f32[4]{0:T(128)}, u32[]{:S(2)}) copy-start(f32[4]{0:T(128)} %rates_ref.1) | copy-start | bytes 52
  4.0 12.9 %copy-start.10 = (f32[4]{0:T(128)S(1)}, f32[4]{0:T(128)}, u32[]{:S(2)}) copy-start(f32[4]{0:T(128)} %decays_ref.1) | copy-start | bytes 52
  4.0 12.9 %copy-start.11 = (s32[4]{0:T(128)S(1)}, s32[4]{0:T(128)}, u32[]{:S(2)}) copy-start(s32[4]{0:T(128)} %steps_ref.1) | copy-start | bytes 52
  4.0 13.7 %collective-permute-start.16 = (bf16[768,1024]{1,0:T(8,128)(2,1)}, bf16[768,1024]{1,0:T(8,128)(2,1)S(1)}, u32[]{:S(2)}, u32[]{:S(2)}) collective-permute-start(bf16[768,1024]{1,0:T(8,128)(2,1)} %get-tuple-element.48.own_ref), channel_id=1, source_target_pairs={{0,4},{4,0},{8,12},{12,8},{1,5},{5,1},{9,13},{13,9},{2,6},{6,2},{1... | collective-permute-start | bytes 4718600 | tf_op jit(solution)/shard_map/ppermute | solution.py:385
  4.1 13.4 %collective-permute-start.2 = (bf16[128,1024]{1,0:T(8,128)(2,1)}, bf16[128,1024]{1,0:T(8,128)(2,1)S(1)}, u32[]{:S(2)}, u32[]{:S(2)}) collective-permute-start(bf16[128,1024]{1,0:T(8,128)(2,1)} %get-tuple-element.34.after_ref.refs_0_), channel_id=1, source_target_pairs={{1,2},{2,1},{5,6},{6,5},{9,10},{10,9},{13,14},{14,13},{17,18},{18,... | collective-permute-start | bytes 786440 | tf_op jit(solution)/shard_map/ppermute | solution.py:382
  4.8 12.8 %collective-permute-start.1 = (bf16[128,1024]{1,0:T(8,128)(2,1)}, bf16[128,1024]{1,0:T(8,128)(2,1)S(1)}, u32[]{:S(2)}, u32[]{:S(2)}) collective-permute-start(bf16[128,1024]{1,0:T(8,128)(2,1)} %get-tuple-element.34.after_ref.refs_0_), channel_id=1, source_target_pairs={{0,1},{2,3},{1,0},{3,2},{4,5},{6,7},{5,4},{7,6},{8,9},{10,11},{9,8... | collective-permute-start | bytes 786440 | tf_op jit(solution)/shard_map/ppermute | solution.py:382
  10.2 13.4 %collective-permute-start = (bf16[128,1024]{1,0:T(8,128)(2,1)}, bf16[128,1024]{1,0:T(8,128)(2,1)S(1)}, u32[]{:S(2)}, u32[]{:S(2)}) collective-permute-start(bf16[128,1024]{1,0:T(8,128)(2,1)} %get-tuple-element.32.refs_1_), channel_id=1, source_target_pairs={{1,2},{2,1},{5,6},{6,5},{9,10},{10,9},{13,14},{14,13},{17,18},{18,... | collective-permute-start | bytes 786440 | tf_op jit(solution)/shard_map/ppermute | solution.py:382
  10.8 12.8 %collective-permute-start.4 = (bf16[128,1024]{1,0:T(8,128)(2,1)}, bf16[128,1024]{1,0:T(8,128)(2,1)}, u32[]{:S(2)}, u32[]{:S(2)}) collective-permute-start(bf16[128,1024]{1,0:T(8,128)(2,1)} %get-tuple-element.32.refs_1_), channel_id=1, source_target_pairs={{0,1},{2,3},{1,0},{3,2},{4,5},{6,7},{5,4},{7,6},{8,9},{10,11},{9,8... | collective-permute-start | bytes 786440 | tf_op jit(solution)/shard_map/ppermute | solution.py:382
  19.0 48.1 %collective-permute-start.17 = (bf16[768,1024]{1,0:T(8,128)(2,1)S(1)}, bf16[768,1024]{1,0:T(8,128)(2,1)S(1)}, u32[]{:S(2)}, u32[]{:S(2)}) collective-permute-start(bf16[768,1024]{1,0:T(8,128)(2,1)S(1)} %pick.1), channel_id=1, source_target_pairs={{0,8},{4,12},{8,0},{12,4},{1,9},{5,13},{9,1},{13,5},{2,10},{6,14},... | collective-permute-start | bytes 4718600 | tf_op jit(solution)/shard_map/ppermute | solution.py:386
  20.3 6.8 %collective-permute-start.7 = (bf16[128,1024]{1,0:T(8,128)(2,1)S(1)}, bf16[128,1024]{1,0:T(8,128)(2,1)S(1)}, u32[]{:S(2)}, u32[]{:S(2)}) collective-permute-start(bf16[128,1024]{1,0:T(8,128)(2,1)S(1)} %to_send.13.after_ref), channel_id=1, source_target_pairs={{1,2},{2,1},{5,6},{6,5},{9,10},{10,9},{13,14},{14,13},{17,18},{18,... | collective-permute-start | bytes 786440 | tf_op jit(solution)/shard_map/ppermute | solution.py:382
  20.9 8.1 %collective-permute-start.6 = (bf16[128,1024]{1,0:T(8,128)(2,1)S(1)}, bf16[128,1024]{1,0:T(8,128)(2,1)S(1)}, u32[]{:S(2)}, u32[]{:S(2)}) collective-permute-start(bf16[128,1024]{1,0:T(8,128)(2,1)S(1)} %to_send.12.after_ref), channel_id=1, source_target_pairs={{0,1},{2,3},{1,0},{3,2},{4,5},{6,7},{5,4},{7,6},{8,9},{10,11},{9,8... | collective-permute-start | bytes 786440 | tf_op jit(solution)/shard_map/ppermute | solution.py:382
  24.7 7.9 %collective-permute-start.5 = (bf16[128,1024]{1,0:T(8,128)(2,1)S(1)}, bf16[128,1024]{1,0:T(8,128)(2,1)S(1)}, u32[]{:S(2)}, u32[]{:S(2)}) collective-permute-start(bf16[128,1024]{1,0:T(8,128)(2,1)S(1)} %to_send.15.after_ref), channel_id=1, source_target_pairs={{1,2},{2,1},{5,6},{6,5},{9,10},{10,9},{13,14},{14,13},{17,18},{18,... | collective-permute-start | bytes 786440 | tf_op jit(solution)/shard_map/ppermute | solution.py:382
  25.4 9.3 %collective-permute-start.3 = (bf16[128,1024]{1,0:T(8,128)(2,1)S(1)}, bf16[128,1024]{1,0:T(8,128)(2,1)S(1)}, u32[]{:S(2)}, u32[]{:S(2)}) collective-permute-start(bf16[128,1024]{1,0:T(8,128)(2,1)S(1)} %to_send.14.after_ref), channel_id=1, source_target_pairs={{0,1},{2,3},{1,0},{3,2},{4,5},{6,7},{5,4},{7,6},{8,9},{10,11},{9,8... | collective-permute-start | bytes 786440 | tf_op jit(solution)/shard_map/ppermute | solution.py:382
  29.1 9.5 %collective-permute-start.10 = (bf16[128,1024]{1,0:T(8,128)(2,1)S(1)}, bf16[128,1024]{1,0:T(8,128)(2,1)S(1)}, u32[]{:S(2)}, u32[]{:S(2)}) collective-permute-start(bf16[128,1024]{1,0:T(8,128)(2,1)S(1)} %to_send.17.after_ref), channel_id=1, source_target_pairs={{1,2},{2,1},{5,6},{6,5},{9,10},{10,9},{13,14},{14,13},{17,18},{18,... | collective-permute-start | bytes 786440 | tf_op jit(solution)/shard_map/ppermute | solution.py:382
  29.8 10.3 %collective-permute-start.9 = (bf16[128,1024]{1,0:T(8,128)(2,1)S(1)}, bf16[128,1024]{1,0:T(8,128)(2,1)S(1)}, u32[]{:S(2)}, u32[]{:S(2)}) collective-permute-start(bf16[128,1024]{1,0:T(8,128)(2,1)S(1)} %to_send.16.after_ref), channel_id=1, source_target_pairs={{0,1},{2,3},{1,0},{3,2},{4,5},{6,7},{5,4},{7,6},{8,9},{10,11},{9,8... | collective-permute-start | bytes 786440 | tf_op jit(solution)/shard_map/ppermute | solution.py:382
  34.8 6.2 %collective-permute-start.8 = (bf16[128,1024]{1,0:T(8,128)(2,1)S(1)}, bf16[128,1024]{1,0:T(8,128)(2,1)S(1)}, u32[]{:S(2)}, u32[]{:S(2)}) collective-permute-start(bf16[128,1024]{1,0:T(8,128)(2,1)S(1)} %to_send.19.after_ref), channel_id=1, source_target_pairs={{1,2},{2,1},{5,6},{6,5},{9,10},{10,9},{13,14},{14,13},{17,18},{18,... | collective-permute-start | bytes 786440 | tf_op jit(solution)/shard_map/ppermute | solution.py:382
  35.4 10.3 %collective-permute-start.12 = (bf16[128,1024]{1,0:T(8,128)(2,1)S(1)}, bf16[128,1024]{1,0:T(8,128)(2,1)S(1)}, u32[]{:S(2)}, u32[]{:S(2)}) collective-permute-start(bf16[128,1024]{1,0:T(8,128)(2,1)S(1)} %to_send.18.after_ref), channel_id=1, source_target_pairs={{0,1},{2,3},{1,0},{3,2},{4,5},{6,7},{5,4},{7,6},{8,9},{10,11},{9,8... | collective-permute-start | bytes 786440 | tf_op jit(solution)/shard_map/ppermute | solution.py:382
  38.8 12.6 %collective-permute-start.14 = (bf16[128,1024]{1,0:T(8,128)(2,1)S(1)}, bf16[128,1024]{1,0:T(8,128)(2,1)S(1)}, u32[]{:S(2)}, u32[]{:S(2)}) collective-permute-start(bf16[128,1024]{1,0:T(8,128)(2,1)S(1)} %to_send.20.after_ref), channel_id=1, source_target_pairs={{0,1},{2,3},{1,0},{3,2},{4,5},{6,7},{5,4},{7,6},{8,9},{10,11},{9,8... | collective-permute-start | bytes 786440 | tf_op jit(solution)/shard_map/ppermute | solution.py:382
  40.2 11.1 %collective-permute-start.15 = (bf16[128,1024]{1,0:T(8,128)(2,1)S(1)}, bf16[128,1024]{1,0:T(8,128)(2,1)S(1)}, u32[]{:S(2)}, u32[]{:S(2)}) collective-permute-start(bf16[128,1024]{1,0:T(8,128)(2,1)S(1)} %to_send.21.after_ref), channel_id=1, source_target_pairs={{1,2},{2,1},{5,6},{6,5},{9,10},{10,9},{13,14},{14,13},{17,18},{18,... | collective-permute-start | bytes 786440 | tf_op jit(solution)/shard_map/ppermute | solution.py:382
  41.1 15.9 %collective-permute-start.11 = (bf16[128,1024]{1,0:T(8,128)(2,1)S(1)}, bf16[128,1024]{1,0:T(8,128)(2,1)S(1)}, u32[]{:S(2)}, u32[]{:S(2)}) collective-permute-start(bf16[128,1024]{1,0:T(8,128)(2,1)S(1)} %to_send.22.after_ref), channel_id=1, source_target_pairs={{0,1},{2,3},{1,0},{3,2},{4,5},{6,7},{5,4},{7,6},{8,9},{10,11},{9,8... | collective-permute-start | bytes 786440 | tf_op jit(solution)/shard_map/ppermute | solution.py:382
  45.9 11.1 %collective-permute-start.13 = (bf16[128,1024]{1,0:T(8,128)(2,1)S(1)}, bf16[128,1024]{1,0:T(8,128)(2,1)S(1)}, u32[]{:S(2)}, u32[]{:S(2)}) collective-permute-start(bf16[128,1024]{1,0:T(8,128)(2,1)S(1)} %to_send.23.after_ref), channel_id=1, source_target_pairs={{1,2},{2,1},{5,6},{6,5},{9,10},{10,9},{13,14},{14,13},{17,18},{18,... | collective-permute-start | bytes 786440 | tf_op jit(solution)/shard_map/ppermute | solution.py:382
  51.5 11.4 %collective-permute-start.22 = (bf16[128,1024]{1,0:T(8,128)(2,1)S(1)}, bf16[128,1024]{1,0:T(8,128)(2,1)S(1)}, u32[]{:S(2)}, u32[]{:S(2)}) collective-permute-start(bf16[128,1024]{1,0:T(8,128)(2,1)S(1)} %summed_grad.2.after_ref.own_ref), channel_id=1, source_target_pairs={{0,8},{4,12},{8,0},{12,4},{1,9},{5,13},{9,1},{13,5},{2,10},{6,14},... | collective-permute-start | bytes 786440 | tf_op jit(solution)/shard_map/ppermute | solution.py:402
  57.1 10.0 %copy-start.1 = (f32[1,256,1024]{2,1,0:T(8,128)S(1)}, f32[1,256,1024]{2,1,0:T(8,128)}, u32[]{:S(2)}) copy-start(f32[1,256,1024]{2,1,0:T(8,128)} %param.11) | copy-start | bytes 3145732
  57.1 10.0 %copy-start.2 = (f32[1,256,1024]{2,1,0:T(8,128)S(1)}, f32[1,256,1024]{2,1,0:T(8,128)}, u32[]{:S(2)}) copy-start(f32[1,256,1024]{2,1,0:T(8,128)} %param.12) | copy-start | bytes 3145732
  57.2 9.9 %copy-start.3 = (f32[1,256,1024]{2,1,0:T(8,128)S(1)}, f32[1,256,1024]{2,1,0:T(8,128)}, u32[]{:S(2)}) copy-start(f32[1,256,1024]{2,1,0:T(8,128)} %param.13) | copy-start | bytes 3145732
  57.2 8.2 %collective-permute-start.19 = (bf16[128,1024]{1,0:T(8,128)(2,1)S(1)}, bf16[128,1024]{1,0:T(8,128)(2,1)S(1)}, u32[]{:S(2)}, u32[]{:S(2)}) collective-permute-start(bf16[128,1024]{1,0:T(8,128)(2,1)S(1)} %summed_grad.3.after_ref.own_ref), channel_id=1, source_target_pairs={{0,8},{4,12},{8,0},{12,4},{1,9},{5,13},{9,1},{13,5},{2,10},{6,14},... | collective-permute-start | bytes 786440 | tf_op jit(solution)/shard_map/ppermute | solution.py:402
  57.6 10.4 %collective-permute-start.21 = (bf16[128,1024]{1,0:T(8,128)(2,1)S(1)}, bf16[128,1024]{1,0:T(8,128)(2,1)S(1)}, u32[]{:S(2)}, u32[]{:S(2)}) collective-permute-start(bf16[128,1024]{1,0:T(8,128)(2,1)S(1)} %summed_grad.2.after_ref.own_ref), channel_id=1, source_target_pairs={{0,4},{4,0},{8,12},{12,8},{1,5},{5,1},{9,13},{13,9},{2,6},{6,2},{1... | collective-permute-start | bytes 786440 | tf_op jit(solution)/shard_map/ppermute | solution.py:401
  63.0 5.0 %collective-permute-start.23 = (bf16[128,1024]{1,0:T(8,128)(2,1)S(1)}, bf16[128,1024]{1,0:T(8,128)(2,1)S(1)}, u32[]{:S(2)}, u32[]{:S(2)}) collective-permute-start(bf16[128,1024]{1,0:T(8,128)(2,1)S(1)} %gate.1.across_ref), channel_id=1, source_target_pairs={{0,4},{4,0},{8,12},{12,8},{1,5},{5,1},{9,13},{13,9},{2,6},{6,2},{1... | collective-permute-start | bytes 786440 | tf_op jit(solution)/shard_map/ppermute | solution.py:405
  63.3 6.3 %collective-permute-start.18 = (bf16[128,1024]{1,0:T(8,128)(2,1)S(1)}, bf16[128,1024]{1,0:T(8,128)(2,1)S(1)}, u32[]{:S(2)}, u32[]{:S(2)}) collective-permute-start(bf16[128,1024]{1,0:T(8,128)(2,1)S(1)} %summed_grad.3.after_ref.own_ref), channel_id=1, source_target_pairs={{0,4},{4,0},{8,12},{12,8},{1,5},{5,1},{9,13},{13,9},{2,6},{6,2},{1... | collective-permute-start | bytes 786440 | tf_op jit(solution)/shard_map/ppermute | solution.py:401
  65.4 4.3 %collective-permute-start.20 = (bf16[128,1024]{1,0:T(8,128)(2,1)S(1)}, bf16[128,1024]{1,0:T(8,128)(2,1)S(1)}, u32[]{:S(2)}, u32[]{:S(2)}) collective-permute-start(bf16[128,1024]{1,0:T(8,128)(2,1)S(1)} %collective-permute-done.19.across_ref), channel_id=1, source_target_pairs={{0,4},{4,0},{8,12},{12,8},{1,5},{5,1},{9,13},{13,9},{2,6},{6,2},{1... | collective-permute-start | bytes 786440 | tf_op jit(solution)/shard_map/ppermute | solution.py:405
  (4 other events, 14.8 us)

commit v7 on v6

--- a/solution.py
+++ b/solution.py
@@ -13,13 +13,14 @@
 epsilon = 1e-08
 
 MIB = 1 << 20
+SUM_FLOPS = 2 ** 30
 SMEM = pl.BlockSpec(memory_space=pltpu.SMEM)
 VMEM = pl.BlockSpec(memory_space=pltpu.VMEM)
 HBM = pl.BlockSpec(memory_space=pltpu.HBM)
 ANY = pl.BlockSpec(memory_space=pl.ANY)
 
 
-def call(kernel, name, out_shape, in_specs, out_specs, limit=8, scratch=(), aliases=None):
+def call(kernel, name, out_shape, in_specs, out_specs, limit=8, scratch=(), aliases=None, flops=0):
     return pl.pallas_call(
         kernel,
         out_shape=out_shape,
@@ -28,21 +29,13 @@
         scratch_shapes=scratch,
         input_output_aliases=aliases or {},
         compiler_params=pltpu.CompilerParams(vmem_limit_bytes=limit * MIB),
-        cost_estimate=pl.CostEstimate(flops=0, bytes_accessed=1024, transcendentals=0),
+        cost_estimate=pl.CostEstimate(flops=flops, bytes_accessed=1024, transcendentals=0),
         name=name,
     )
 
 
 def half_array(rows, depth):
     return jax.ShapeDtypeStruct((rows, depth), jnp.bfloat16)
-
-
-def gate_kernel(value_ref, after_ref, out_ref):
-    pass
-
-
-def gate(value, after):
-    return call(gate_kernel, "gate", half_array(*value.shape), [ANY, ANY], ANY, aliases={0: 0})(value, after)
 
 
 def by_rows(ref, body, step=16):
@@ -187,12 +180,21 @@
     return [flat[k * len(parts):(k + 1) * len(parts)] for k in range(len(order) + 1)]
 
 
-def sum_kernel(arrived_ref, term_ref, after_ref, out_ref):
+def send_kernel(arrived_ref, term_ref, arrived_too_ref, term_too_ref, after_ref, out_ref, out_too_ref):
     def body(at):
         total = arrived_ref[at, :].astype(jnp.float32) + term_ref[at, :].astype(jnp.float32)
         out_ref[at, :] = total.astype(out_ref.dtype)
+        total = arrived_too_ref[at, :].astype(jnp.float32) + term_too_ref[at, :].astype(jnp.float32)
+        out_too_ref[at, :] = total.astype(out_too_ref.dtype)
 
     by_rows(out_ref, body)
+
+
+def to_send(pairs, after):
+    like = half_array(*pairs[0][0].shape)
+    return call(send_kernel, "to_send", [like] * 2, [VMEM] * 4 + [ANY], [VMEM] * 2, flops=SUM_FLOPS)(
+        *pairs[0], *pairs[1], after
+    )
 
 
 def grad_kernel(own_ref, one_ref, other_ref, after_ref, out_ref):
@@ -203,15 +205,14 @@
     by_rows(out_ref, body)
 
 
-def summed(kernel, name, addends, after):
-    return call(
-        kernel, name, half_array(*addends[0].shape), [VMEM] * len(addends) + [ANY], VMEM
-    )(*addends, after)
-
-
-def columns_kernel(n, scale, parts, where_ref, cotangent_ref, after_ref, *refs):
-    blocks, (out_ref, token_ref, full, result, out_sems) = refs[:-5], refs[-5:]
-    token_ref[...] = jnp.zeros_like(token_ref)
+def summed_grad(own, one, other, after):
+    return call(grad_kernel, "summed_grad", half_array(*one.shape), [VMEM] * 3 + [ANY], VMEM)(
+        own, one, other, after
+    )
+
+
+def columns_kernel(n, scale, parts, where_ref, cotangent_ref, *refs):
+    blocks, (out_ref, full, result, out_sems) = refs[:-4], refs[-4:]
     width = full.shape[0]
     rows = width // n
     me = where_ref[0]
@@ -239,19 +240,60 @@
         write.wait()
 
 
-def columns(n, scale, parts, where, cotangent, after, blocks):
+def columns(n, scale, parts, where, cotangent, blocks):
     tokens, depth = cotangent.shape
     width = n * sum(size for _, size in parts)
     return call(
         functools.partial(columns_kernel, n, scale, parts), "context_grad",
-        [half_array(tokens, width), jax.ShapeDtypeStruct((8, 128), jnp.float32)],
-        [SMEM, VMEM, ANY] + [VMEM] * len(blocks), [HBM, VMEM], limit=14,
+        half_array(tokens, width), [SMEM, VMEM] + [VMEM] * len(blocks), HBM, limit=14,
         scratch=[
             pltpu.VMEM((width, depth), cotangent.dtype),
             pltpu.VMEM((tokens, width), cotangent.dtype),
             pltpu.SemaphoreType.DMA((width // min(256, width),)),
         ],
-    )(where, cotangent, after, *blocks)
+    )(where, cotangent, *blocks)
+
+
+def slot_columns_kernel(scale, parts, slot, filled, cotangent_ref, *refs):
+    groups = 3 if slot == 1 else 2
+    count = groups * len(parts)
+    blocks, (out_ref, token_ref, result, sems) = refs[:count], refs[count + filled:]
+    token_ref[...] = jnp.zeros_like(token_ref)
+    me, n = lax.axis_index("shard"), lax.axis_size("shard")
+    rows = sum(size for _, size in parts)
+    even = lax.rem(me, 2) == 0
+    for group in range(groups):
+        ahead = (jnp.where(even, slot, -slot), jnp.where(even, -slot, slot), 0)[group]
+        shard = me + ahead
+
+        @pl.when(jnp.logical_and(shard >= 0, shard < n))
+        def _():
+            writes = []
+            for c, (start, size) in enumerate(parts):
+                at = pl.ds(group * rows + start, size)
+                result[:, at] = (scale * lax.dot_general(
+                    cotangent_ref[...], blocks[group * len(parts) + c][...],
+                    (((1,), (1,)), ((), ())), preferred_element_type=jnp.float32,
+                )).astype(out_ref.dtype)
+                column = pl.multiple_of(shard * rows + start, 128)
+                writes.append(pltpu.make_async_copy(
+                    result.at[:, at], out_ref.at[:, pl.ds(column, size)], sems.at[group, c]
+                ))
+                writes[-1].start()
+            for write in writes:
+                write.wait()
+
+
+def slot_columns(scale, width, parts, slot, cotangent, blocks, filled):
+    tokens, depth = cotangent.shape
+    rows = sum(size for _, size in parts)
+    return call(
+        functools.partial(slot_columns_kernel, scale, parts, slot, len(filled)), "context_grad",
+        [half_array(tokens, width), jax.ShapeDtypeStruct((8, 128), jnp.float32)],
+        [VMEM] * (1 + len(blocks)) + [HBM] * len(filled), [HBM, VMEM],
+        scratch=[pltpu.VMEM((tokens, 3 * rows), cotangent.dtype), pltpu.SemaphoreType.DMA((3, len(parts)))],
+        aliases={1 + len(blocks): 0} if filled else None,
+    )(cotangent, *blocks, *filled)
 
 
 def state_kernel(parts, where_ref, donor_ref, after_ref, *refs):
@@ -299,7 +341,7 @@
     )(where, donor, after, *own, *donated)
 
 
-def adam_kernel(start, size, filled, choices_ref, state_ref, own_ref, mate_ref, across_ref, far_ref, after_ref, *refs):
+def adam_kernel(start, size, filled, choices_ref, state_ref, own_ref, mate_ref, across_ref, far_ref, *refs):
     refs = refs[3 if filled else 0:]
     outs, (stepped, sems) = refs[:3], refs[3:]
     depth = own_ref.shape[1]
@@ -333,15 +375,15 @@
         write.wait()
 
 
-def adam_update(start, size, rows, choices, state, grads, after, filled):
+def adam_update(start, size, rows, choices, state, grads, filled):
     depth = state.shape[1]
     return call(
         functools.partial(adam_kernel, start, size, bool(filled)), "adam",
         [jax.ShapeDtypeStruct((rows, depth), jnp.float32)] * 3,
-        [VMEM] * 6 + [ANY] + [HBM] * len(filled), [HBM] * 3,
+        [VMEM] * 6 + [HBM] * len(filled), [HBM] * 3,
         scratch=[pltpu.VMEM((3, size, depth), jnp.float32), pltpu.SemaphoreType.DMA((12,))],
-        aliases={7 + k: k for k in range(len(filled))},
-    )(choices, state, *grads, after, *filled)
+        aliases={6 + k: k for k in range(len(filled))},
+    )(choices, state, *grads, *filled)
 
 
 def on_device(n, members, context, out_grad, weight, first, second, rates, decays, steps, donor):
@@ -367,46 +409,46 @@
     order = [(slot, swap) for slot in range(2, n + 1) for swap in range(2)]
     terms = partial_blocks(n, scale, parts, order, where, context_rows, cotangent)
 
+    width = context_rows.shape[1]
+    by_slots = all(size % 128 == 0 for _, size in parts)
+    context_grad = ()
+
     arrived = [[own, own]]
-    sent = early = own[0]
+    sent = own[0]
     for slot in range(1, n + 1):
         now = [[], []]
         for c in range(len(parts)):
+            blocks = [arrived[-1][1][c], arrived[-1][0][c]]
+            if slot > 1:
+                blocks = to_send([(blocks[swap], terms[2 * (slot - 2) + swap][c]) for swap in range(2)], sent)
+                sent = blocks[0]
+            if slot == 2 and c == 0:
+                early = sent
             for swap in range(2):
-                block = arrived[-1][1 - swap][c]
-                if slot > 1:
-                    addends = (block, terms[2 * (slot - 2) + swap][c])
-                    block = sent = summed(sum_kernel, "to_send", addends, sent)
-                if slot == 2 and c == 0:
-                    early = block
-                now[swap].append(lax.ppermute(block, "shard", swaps[swap]))
+                now[swap].append(lax.ppermute(blocks[swap], "shard", swaps[swap]))
         arrived.append(now)
+        if by_slots and slot > 1:
+            blocks = arrived[slot - 1][0] + arrived[slot - 1][1] + (list(own) if slot == 2 else [])
+            *context_grad, sent = slot_columns(scale, width, parts, slot - 1, cotangent, blocks, context_grad)
+    if not by_slots:
+        blocks = [block for now in arrived[1:n] for swap in now for block in swap]
+        context_grad = [columns(n, scale, parts, where, cotangent, list(own) + blocks)]
 
     mate = lax.ppermute(state, "member", swap_mates)
     across = lax.ppermute(pick(choices, state, mate, early), "member", swap_across)
-    states = taken_state(parts, where, donor, (weight[0], first[0], second[0]), (mate, across), sent)
-
-    grads = []
-    for c in range(len(parts)):
-        addends = (terms[-1][c], arrived[n][0][c], arrived[n][1][c])
-        sent = summed(grad_kernel, "summed_grad", addends, sent)
-        grads.append(sent)
-    blocks = list(own)
-    for slot in range(1, n):
-        blocks += arrived[slot][0] + arrived[slot][1]
-    context_grad, computed = columns(n, scale, parts, where, cotangent, sent, blocks)
+    states = taken_state(parts, where, donor, (weight[0], first[0], second[0]), (mate, across), own[0])
 
     updated = ()
     for c, (start, size) in enumerate(parts):
-        mate = lax.ppermute(grads[c], "member", swap_mates)
-        across = lax.ppermute(grads[c], "member", swap_across)
-        if c == 0:
-            across = gate(across, computed)
-        far = lax.ppermute(across, "member", swap_mates)
-        updated = adam_update(
-            start, size, rows, choices, states[c], (grads[c], mate, across, far), computed, updated
-        )
-    return (context_grad[None],) + tuple(array[None] for array in updated)
+        grad = sent = summed_grad(terms[-1][c], arrived[n][0][c], arrived[n][1][c], sent)
+        mate = lax.ppermute(grad, "member", swap_mates)
+        if c == len(parts) - 1:
+            far = across = lax.ppermute(pick(choices, grad, mate, grad), "member", swap_across)
+        else:
+            across = lax.ppermute(grad, "member", swap_across)
+            far = lax.ppermute(across, "member", swap_mates)
+        updated = adam_update(start, size, rows, choices, states[c], (grad, mate, across, far), updated)
+    return (context_grad[0][None],) + tuple(array[None] for array in updated)
 
 
 def solution(mesh):

time: 71.9 us -> 76.4 us (1.063)
  Pallas kernels: 17.6 us -> 21.3 us
  starting transfers between devices: 33.8 us -> 36.2 us
  waiting for transfers between devices: 16.9 us -> 15.5 us
    pallas_call x16 -> x11, Pallas kernels: 5.65 us -> 9.14 us  [the longest x3 6.85 us: slot_columns(): call(functools.partial(slot_columns_kernel, scale, parts, slot, len(fille...]
    ppermute x20, starting transfers between devices: 30.3 us -> 32.3 us  [the longest x16 26.5 us: on_device(): now[swap].append(lax.ppermute(blocks[swap], 'shard', swaps[swap]))]
    ppermute x20, waiting for transfers between devices: 16.9 us -> 15.5 us  [the longest x16 9.29 us: on_device(): now[swap].append(lax.ppermute(blocks[swap], 'shard', swaps[swap]))]
    ppermute x2 -> x1, starting transfers between devices: 2.06 us -> 2.49 us  [on_device(): far = lax.ppermute(across, 'member', swap_mates)]
  transfers between devices with their start and end apart: 24 -> 23, of which waited for: 7 -> 6; matrix products, arithmetic and copies ran while one was open for 0% -> 0% of each run, Pallas kernels for 18% -> 22%
where the time goes in v7:
time: 76.4 us; the launch traced here: 75.3 us
  starting transfers between devices  36.2 us (47%)
  Pallas kernels  21.3 us (28%)
  waiting for transfers between devices  15.5 us (20%)
  local copies, waits for them, and re-layouts  1.28 us (2%)
  between operations  1.02 us (1%)
    ppermute x16, starting transfers between devices, on_device(): now[swap].append(lax.ppermute(blocks[swap], 'shard', swaps[swap]))  26.5 us
    ppermute x16, waiting for transfers between devices, on_device(): now[swap].append(lax.ppermute(blocks[swap], 'shard', swaps[swap]))  9.29 us
    pallas_call x3, Pallas kernels, slot_columns(): call(functools.partial(slot_columns_kernel, scale, parts, slot, len(fille...  6.85 us
    ppermute x1, waiting for transfers between devices, on_device(): lax.ppermute(pick(choices, grad, mate, grad), 'member', swap_across)  4.06 us
    ppermute x2, starting transfers between devices, on_device(): mate = lax.ppermute(grad, 'member', swap_mates)  3.93 us
    pallas_call x2, Pallas kernels, adam_update(): call(functools.partial(adam_kernel, start, size, bool(filled)), 'adam', [...  3.33 us
    pallas_call x1, Pallas kernels, halves(): call(functools.partial(halves_kernel, parts), 'halves', [half_array(size,...  3.31 us
    pallas_call x1, Pallas kernels, partial_blocks(): call(functools.partial(partial_kernel, n, scale, parts, order), 'partial_...  3.21 us
  transfers between devices with their start and end apart: 23, of which 6 were waited for; matrix products, arithmetic and copies ran while one was open for 0% of the time, Pallas kernels for 22%

profile of v7, /device:TPU:1, one launch (start us, length us, event | category | flops | bytes accessed | tf_op | source)
XLA Modules:
  0.0 75.3 jit_solution(2098792688615410892)
XLA Ops:
  0.7 3.3 %halves.1 = (bf16[768,1024]{1,0:T(8,128)(2,1)}, bf16[128,1024]{1,0:T(8,128)(2,1)}, bf16[128,1024]{1,0:T(8,128)(2,1)}) custom-call(f32[256,1024]{1,0:T(8,128)} %bitcast.15, f32[256,1024]{1,0:T(8,128)} %bitcast.17, f32[256,1024]{1,0:T(8,128)} %bitcast.19), custom_call_target="tpu_custom_call" | custom-call | bytes 1024 | tf_op jit(solution)/shard_map/halves/pallas_call | solution.py:90
  4.1 2.8 %collective-permute-start.1 = (bf16[128,1024]{1,0:T(8,128)(2,1)}, bf16[128,1024]{1,0:T(8,128)(2,1)S(1)}, u32[]{:S(2)}, u32[]{:S(2)}) collective-permute-start(bf16[128,1024]{1,0:T(8,128)(2,1)} %get-tuple-element.47.after_ref.refs_4_), channel_id=1, source_target_pairs={{0,1},{2,3},{1,0},{3,2},{4,5},{6,7},{5,4},{7,6},{8,9},{10,11},{9,8... | collective-permute-start | bytes 786440 | tf_op jit(solution)/shard_map/ppermute | solution.py:428
  7.6 1.4 %collective-permute-start.5 = (bf16[128,1024]{1,0:T(8,128)(2,1)}, bf16[128,1024]{1,0:T(8,128)(2,1)}, u32[]{:S(2)}, u32[]{:S(2)}) collective-permute-start(bf16[128,1024]{1,0:T(8,128)(2,1)} %get-tuple-element.54.refs_5_), channel_id=1, source_target_pairs={{1,2},{2,1},{5,6},{6,5},{9,10},{10,9},{13,14},{14,13},{17,18},{18,... | collective-permute-start | bytes 786440 | tf_op jit(solution)/shard_map/ppermute | solution.py:428
  9.0 4.4 %collective-permute-start.4 = (bf16[128,1024]{1,0:T(8,128)(2,1)}, bf16[128,1024]{1,0:T(8,128)(2,1)}, u32[]{:S(2)}, u32[]{:S(2)}) collective-permute-start(bf16[128,1024]{1,0:T(8,128)(2,1)} %get-tuple-element.54.refs_5_), channel_id=1, source_target_pairs={{0,1},{2,3},{1,0},{3,2},{4,5},{6,7},{5,4},{7,6},{8,9},{10,11},{9,8... | collective-permute-start | bytes 786440 | tf_op jit(solution)/shard_map/ppermute | solution.py:428
  13.5 1.2 %copy-done.6 = bf16[1,512,1024]{2,1,0:T(8,128)(2,1)S(1)} copy-done((bf16[1,512,1024]{2,1,0:T(8,128)(2,1)S(1)}, bf16[1,512,1024]{2,1,0:T(8,128)(2,1)}, u32[]{:S(2)}) %copy-start.6) | copy-done | bytes 1048600
  14.7 3.2 %partial_blocks.1 = (bf16[128,1024]{1,0:T(8,128)(2,1)S(1)}, bf16[128,1024]{1,0:T(8,128)(2,1)S(1)}, bf16[128,1024]{1,0:T(8,128)(2,1)S(1)}, bf16[128,1024]{1,0:T(8...) custom-call(s32[2]{0:T(128)S(1)} %pad_add_fusion.where_ref, ...), custom_call_target="tpu_custom_call" | custom-call | bytes 1024 | tf_op jit(solution)/shard_map/partial_blocks/pallas_call | solution.py:166
  18.8 0.8 %collective-permute-start.2 = (bf16[128,1024]{1,0:T(8,128)(2,1)S(1)}, bf16[128,1024]{1,0:T(8,128)(2,1)S(1)}, u32[]{:S(2)}, u32[]{:S(2)}) collective-permute-start(bf16[128,1024]{1,0:T(8,128)(2,1)S(1)} %get-tuple-element.50), channel_id=1, source_target_pairs={{1,2},{2,1},{5,6},{6,5},{9,10},{10,9},{13,14},{14,13},{17,18},{18,... | collective-permute-start | bytes 786440 | tf_op jit(solution)/shard_map/ppermute | solution.py:428
  19.6 2.8 %collective-permute-start.3 = (bf16[128,1024]{1,0:T(8,128)(2,1)S(1)}, bf16[128,1024]{1,0:T(8,128)(2,1)S(1)}, u32[]{:S(2)}, u32[]{:S(2)}) collective-permute-start(bf16[128,1024]{1,0:T(8,128)(2,1)S(1)} %get-tuple-element.52.after_ref), channel_id=1, source_target_pairs={{0,1},{2,3},{1,0},{3,2},{4,5},{6,7},{5,4},{7,6},{8,9},{10,11},{9,8... | collective-permute-start | bytes 786440 | tf_op jit(solution)/shard_map/ppermute | solution.py:428
  22.4 0.7 pick.2
  23.0 1.3 %collective-permute-start.13 = (bf16[768,1024]{1,0:T(8,128)(2,1)S(1)}, bf16[768,1024]{1,0:T(8,128)(2,1)S(1)}, u32[]{:S(2)}, u32[]{:S(2)}) collective-permute-start(bf16[768,1024]{1,0:T(8,128)(2,1)S(1)} %pick.2), channel_id=1, source_target_pairs={{0,8},{4,12},{8,0},{12,4},{1,9},{5,13},{9,1},{13,5},{2,10},{6,14},... | collective-permute-start | bytes 4718600 | tf_op jit(solution)/shard_map/ppermute | solution.py:438
  24.3 1.2 %to_send.8 = (bf16[128,1024]{1,0:T(8,128)(2,1)S(1)}, bf16[128,1024]{1,0:T(8,128)(2,1)S(1)}) custom-call(bf16[128,1024]{1,0:T(8,128)(2,1)} %collective-permute-done.5.refs_3_.arrived_ref, bf16[128,1024]{1,0:T(8,128)(2,1)S(1)} %get-tuple-element.57.term_ref, bf16[128,1024]{1,0:T(8,128)(2,1)} %collective-permute-done.4.refs_1_.arrived_too_ref, ...), custom_call_target="tpu_custom_call" | custom-call | flops 1073741824 | bytes 1024 | tf_op jit(solution)/shard_map/to_send/pallas_call | solution.py:195
  25.6 0.7 collective-permute-start.7
  26.3 1.8 %collective-permute-start.8 = (bf16[128,1024]{1,0:T(8,128)(2,1)S(1)}, bf16[128,1024]{1,0:T(8,128)(2,1)S(1)}, u32[]{:S(2)}, u32[]{:S(2)}) collective-permute-start(bf16[128,1024]{1,0:T(8,128)(2,1)S(1)} %get-tuple-element.61), channel_id=1, source_target_pairs={{0,1},{2,3},{1,0},{3,2},{4,5},{6,7},{5,4},{7,6},{8,9},{10,11},{9,8... | collective-permute-start | bytes 786440 | tf_op jit(solution)/shard_map/ppermute | solution.py:428
  28.1 3.9 %context_grad.3 = (bf16[512,1024]{1,0:T(8,128)(2,1)}, f32[8,128]{1,0:T(8,128)S(1)}) custom-call(bf16[512,1024]{1,0:T(8,128)(2,1)S(1)} %bitcast.12, bf16[128,1024]{1,0:T(8,128)(2,1)S(1)} %collective-permute-done.1.arrived_too_ref.refs_0_, bf16[128,1024]{1,0:T(8,128)(2,1)} %collective-permute-done.4.refs_1_.arrived_too_ref, ...), custom_call_target="tpu_custom_call" | custom-call | bytes 1024 | tf_op jit(solution)/shard_map/context_grad/pallas_call | solution.py:290
  32.9 3.7 %collective-permute-start.6 = (bf16[128,1024]{1,0:T(8,128)(2,1)S(1)}, bf16[128,1024]{1,0:T(8,128)(2,1)S(1)}, u32[]{:S(2)}, u32[]{:S(2)}) collective-permute-start(bf16[128,1024]{1,0:T(8,128)(2,1)S(1)} %get-tuple-element.56.after_ref), channel_id=1, source_target_pairs={{0,1},{2,3},{1,0},{3,2},{4,5},{6,7},{5,4},{7,6},{8,9},{10,11},{9,8... | collective-permute-start | bytes 786440 | tf_op jit(solution)/shard_map/ppermute | solution.py:428
  37.5 1.5 %context_grad.4 = (bf16[512,1024]{1,0:T(8,128)(2,1)}, f32[8,128]{1,0:T(8,128)S(1)}) custom-call(bf16[512,1024]{1,0:T(8,128)(2,1)S(1)} %bitcast.13, bf16[128,1024]{1,0:T(8,128)(2,1)S(1)} %collective-permute-done.3.arrived_too_ref.refs_0_, bf16[128,1024]{1,0:T(8,128)(2,1)S(1)} %collective-permute-done.8.arrived_too_ref.refs_1_, ...), custom_call_target="tpu_custom_call", output_to_operand_aliasing={{0}: (5, {})} | custom-call | bytes 1024 | tf_op jit(solution)/shard_map/context_grad/pallas_call | solution.py:290
  39.0 2.0 %collective-permute-done.6.refs_0_.arrived_too_ref = bf16[128,1024]{1,0:T(8,128)(2,1)S(1)} collective-permute-done((bf16[128,1024]{1,0:T(8,128)(2,1)S(1)}, bf16[128,1024]{1,0:T(8,128)(2,1)S(1)}, u32[]{:S(2)}, u32[]{:S(2)}) %collective-permute-start.6) | collective-permute-done | bytes 262176 | tf_op jit(solution)/shard_map/ppermute | solution.py:428
  41.2 0.7 collective-permute-start.17
  41.9 3.4 %collective-permute-start.16 = (bf16[128,1024]{1,0:T(8,128)(2,1)S(1)}, bf16[128,1024]{1,0:T(8,128)(2,1)S(1)}, u32[]{:S(2)}, u32[]{:S(2)}) collective-permute-start(bf16[128,1024]{1,0:T(8,128)(2,1)S(1)} %get-tuple-element.77.after_ref), channel_id=1, source_target_pairs={{0,1},{2,3},{1,0},{3,2},{4,5},{6,7},{5,4},{7,6},{8,9},{10,11},{9,8... | collective-permute-start | bytes 786440 | tf_op jit(solution)/shard_map/ppermute | solution.py:428
  45.3 1.4 %collective-permute-done.9.refs_1_.arrived_too_ref = bf16[128,1024]{1,0:T(8,128)(2,1)S(1)} collective-permute-done((bf16[128,1024]{1,0:T(8,128)(2,1)S(1)}, bf16[128,1024]{1,0:T(8,128)(2,1)S(1)}, u32[]{:S(2)}, u32[]{:S(2)}) %collective-permute-start.9) | collective-permute-done | bytes 262176 | tf_op jit(solution)/shard_map/ppermute | solution.py:428
  46.8 1.2 %collective-permute-start.14 = (bf16[128,1024]{1,0:T(8,128)(2,1)S(1)}, bf16[128,1024]{1,0:T(8,128)(2,1)S(1)}, u32[]{:S(2)}, u32[]{:S(2)}) collective-permute-start(bf16[128,1024]{1,0:T(8,128)(2,1)S(1)} %get-tuple-element.78), channel_id=1, source_target_pairs={{0,1},{2,3},{1,0},{3,2},{4,5},{6,7},{5,4},{7,6},{8,9},{10,11},{9,8... | collective-permute-start | bytes 786440 | tf_op jit(solution)/shard_map/ppermute | solution.py:428
  48.8 1.5 %context_grad.5 = (bf16[512,1024]{1,0:T(8,128)(2,1)}, f32[8,128]{1,0:T(8,128)S(1)}) custom-call(bf16[512,1024]{1,0:T(8,128)(2,1)S(1)} %bitcast.14, bf16[128,1024]{1,0:T(8,128)(2,1)S(1)} %collective-permute-done.6.refs_0_.arrived_too_ref, bf16[128,1024]{1,0:T(8,128)(2,1)S(1)} %collective-permute-done.9.refs_1_.arrived_too_ref, ...), custom_call_target="tpu_custom_call", output_to_operand_aliasing={{0}: (5, {})} | custom-call | bytes 1024 | tf_op jit(solution)/shard_map/context_grad/pallas_call | solution.py:290
  50.3 1.6 %collective-permute-done.16.one_ref = bf16[128,1024]{1,0:T(8,128)(2,1)S(1)} collective-permute-done((bf16[128,1024]{1,0:T(8,128)(2,1)S(1)}, bf16[128,1024]{1,0:T(8,128)(2,1)S(1)}, u32[]{:S(2)}, u32[]{:S(2)}) %collective-permute-start.16) | collective-permute-done | bytes 262176 | tf_op jit(solution)/shard_map/ppermute | solution.py:428
  52.6 4.2 %collective-permute-done.14.one_ref = bf16[128,1024]{1,0:T(8,128)(2,1)S(1)} collective-permute-done((bf16[128,1024]{1,0:T(8,128)(2,1)S(1)}, bf16[128,1024]{1,0:T(8,128)(2,1)S(1)}, u32[]{:S(2)}, u32[]{:S(2)}) %collective-permute-start.14) | collective-permute-done | bytes 262176 | tf_op jit(solution)/shard_map/ppermute | solution.py:428
  57.0 3.9 %collective-permute-start.18 = (bf16[128,1024]{1,0:T(8,128)(2,1)S(1)}, bf16[128,1024]{1,0:T(8,128)(2,1)S(1)}, u32[]{:S(2)}, u32[]{:S(2)}) collective-permute-start(bf16[128,1024]{1,0:T(8,128)(2,1)S(1)} %summed_grad.3.own_ref.after_ref), channel_id=1, source_target_pairs={{0,4},{4,0},{8,12},{12,8},{1,5},{5,1},{9,13},{13,9},{2,6},{6,2},{1... | collective-permute-start | bytes 786440 | tf_op jit(solution)/shard_map/ppermute | solution.py:444
  61.0 2.1 %collective-permute-done.21.across_ref = bf16[128,1024]{1,0:T(8,128)(2,1)S(1)} collective-permute-done((bf16[128,1024]{1,0:T(8,128)(2,1)S(1)}, bf16[128,1024]{1,0:T(8,128)(2,1)S(1)}, u32[]{:S(2)}, u32[]{:S(2)}) %collective-permute-start.21) | collective-permute-done | bytes 262176 | tf_op jit(solution)/shard_map/ppermute | solution.py:448
  63.1 2.5 %collective-permute-start.22 = (bf16[128,1024]{1,0:T(8,128)(2,1)S(1)}, bf16[128,1024]{1,0:T(8,128)(2,1)S(1)}, u32[]{:S(2)}, u32[]{:S(2)}) collective-permute-start(bf16[128,1024]{1,0:T(8,128)(2,1)S(1)} %collective-permute-done.21.across_ref), channel_id=1, source_target_pairs={{0,4},{4,0},{8,12},{12,8},{1,5},{5,1},{9,13},{13,9},{2,6},{6,2},{1... | collective-permute-start | bytes 786440 | tf_op jit(solution)/shard_map/ppermute | solution.py:449
  65.7 1.3 %collective-permute-start.19 = (bf16[128,1024]{1,0:T(8,128)(2,1)S(1)}, bf16[128,1024]{1,0:T(8,128)(2,1)S(1)}, u32[]{:S(2)}, u32[]{:S(2)}) collective-permute-start(bf16[128,1024]{1,0:T(8,128)(2,1)S(1)} %pick.3), channel_id=1, source_target_pairs={{0,8},{4,12},{8,0},{12,4},{1,9},{5,13},{9,1},{13,5},{2,10},{6,14},... | collective-permute-start | bytes 786440 | tf_op jit(solution)/shard_map/ppermute | solution.py:446
  67.0 0.9 %taken_state.1 = (f32[384,1024]{1,0:T(8,128)S(1)}, f32[384,1024]{1,0:T(8,128)S(1)}) custom-call(s32[2]{0:T(128)S(1)} %pad_add_fusion.where_ref, s32[4]{0:T(128)S(1)} %copy-done.8, bf16[128,1024]{1,0:T(8,128)(2,1)S(1)} %copy-done.5, f32[256,1024]{1,0:T(8,128)S(1)} %bitcast.16, f32[256,1024]{1,0:T(8,128)S(1)} %bitcast.18, f32[256,1024]{1,0:T(8,128)S(1)} %bitcast.20, ...), custom_call_target="tpu_custom_call" | custom-call | bytes 1024 | tf_op jit(solution)/shard_map/taken_state/pallas_call | solution.py:336
  67.9 1.7 %adam.2 = (f32[256,1024]{1,0:T(8,128)}, f32[256,1024]{1,0:T(8,128)}, f32[256,1024]{1,0:T(8,128)}) custom-call(f32[8,1024]{1,0:T(8,128)S(1)} %choices.1.choices_ref, f32[384,1024]{1,0:T(8,128)S(1)} %get-tuple-element.83.state_ref, bf16[128,1024]{1,0:T(8,128)(2,1)S(1)} %summed_grad.2.after_ref.own_ref, bf16[128,1024]{1,0:T(8,128)(2,1)S(1)} %collective-permute-done.20.mate_ref, ...), custom_call_target="tpu_custom_call" | custom-call | bytes 1024 | tf_op jit(solution)/shard_map/adam/pallas_call | solution.py:380
  69.6 4.1 %collective-permute-done.19.across_ref.far_ref = bf16[128,1024]{1,0:T(8,128)(2,1)S(1)} collective-permute-done((bf16[128,1024]{1,0:T(8,128)(2,1)S(1)}, bf16[128,1024]{1,0:T(8,128)(2,1)S(1)}, u32[]{:S(2)}, u32[]{:S(2)}) %collective-permute-start.19) | collective-permute-done | bytes 262176 | tf_op jit(solution)/shard_map/ppermute | solution.py:446
  73.7 1.7 %adam.3 = (f32[256,1024]{1,0:T(8,128)}, f32[256,1024]{1,0:T(8,128)}, f32[256,1024]{1,0:T(8,128)}) custom-call(f32[8,1024]{1,0:T(8,128)S(1)} %choices.1.choices_ref, f32[384,1024]{1,0:T(8,128)S(1)} %get-tuple-element.70.state_ref, bf16[128,1024]{1,0:T(8,128)(2,1)S(1)} %summed_grad.3.own_ref.after_ref, ...), custom_call_target="tpu_custom_call", output_to_operand_aliasing={{0}: (6, {}), {1}: (7, {}), {2}: (8, {})} | custom-call | bytes 1024 | tf_op jit(solution)/shard_map/adam/pallas_call | solution.py:380
  (58 shorter events, 5.5 us)
Async XLA Ops:
  0.6 12.8 %copy-start = (bf16[1,512,1024]{2,1,0:T(8,128)(2,1)S(1)}, bf16[1,512,1024]{2,1,0:T(8,128)(2,1)}, u32[]{:S(2)}) copy-start(bf16[1,512,1024]{2,1,0:T(8,128)(2,1)} %param.10) | copy-start | bytes 3145732
  0.6 17.3 %copy-start.8 = (s32[4]{0:T(128)S(1)}, s32[4]{0:T(128)}, u32[]{:S(2)}) copy-start(s32[4]{0:T(128)} %donor_ref.3) | copy-start | bytes 52
  0.7 17.3 %copy-start.9 = (f32[4]{0:T(128)S(1)}, f32[4]{0:T(128)}, u32[]{:S(2)}) copy-start(f32[4]{0:T(128)} %rates_ref.1) | copy-start | bytes 52
  0.7 17.3 %copy-start.10 = (f32[4]{0:T(128)S(1)}, f32[4]{0:T(128)}, u32[]{:S(2)}) copy-start(f32[4]{0:T(128)} %decays_ref.1) | copy-start | bytes 52
  0.7 17.3 %copy-start.11 = (s32[4]{0:T(128)S(1)}, s32[4]{0:T(128)}, u32[]{:S(2)}) copy-start(s32[4]{0:T(128)} %steps_ref.1) | copy-start | bytes 52
  4.0 14.6 %copy-start.5 = (bf16[128,1024]{1,0:T(8,128)(2,1)S(1)}, bf16[128,1024]{1,0:T(8,128)(2,1)}, u32[]{:S(2)}) copy-start(bf16[128,1024]{1,0:T(8,128)(2,1)} %get-tuple-element.47.after_ref.refs_4_) | copy-start | bytes 786436
  4.0 18.3 %collective-permute-start.12 = (bf16[768,1024]{1,0:T(8,128)(2,1)}, bf16[768,1024]{1,0:T(8,128)(2,1)S(1)}, u32[]{:S(2)}, u32[]{:S(2)}) collective-permute-start(bf16[768,1024]{1,0:T(8,128)(2,1)} %get-tuple-element.69.own_ref), channel_id=1, source_target_pairs={{0,4},{4,0},{8,12},{12,8},{1,5},{5,1},{9,13},{13,9},{2,6},{6,2},{1... | collective-permute-start | bytes 4718600 | tf_op jit(solution)/shard_map/ppermute | solution.py:437
  4.1 14.4 %collective-permute-start.1 = (bf16[128,1024]{1,0:T(8,128)(2,1)}, bf16[128,1024]{1,0:T(8,128)(2,1)S(1)}, u32[]{:S(2)}, u32[]{:S(2)}) collective-permute-start(bf16[128,1024]{1,0:T(8,128)(2,1)} %get-tuple-element.47.after_ref.refs_4_), channel_id=1, source_target_pairs={{0,1},{2,3},{1,0},{3,2},{4,5},{6,7},{5,4},{7,6},{8,9},{10,11},{9,8... | collective-permute-start | bytes 786440 | tf_op jit(solution)/shard_map/ppermute | solution.py:428
  6.9 11.7 %collective-permute-start = (bf16[128,1024]{1,0:T(8,128)(2,1)}, bf16[128,1024]{1,0:T(8,128)(2,1)S(1)}, u32[]{:S(2)}, u32[]{:S(2)}) collective-permute-start(bf16[128,1024]{1,0:T(8,128)(2,1)} %get-tuple-element.47.after_ref.refs_4_), channel_id=1, source_target_pairs={{1,2},{2,1},{5,6},{6,5},{9,10},{10,9},{13,14},{14,13},{17,18},{18,... | collective-permute-start | bytes 786440 | tf_op jit(solution)/shard_map/ppermute | solution.py:428
  7.6 16.8 %collective-permute-start.5 = (bf16[128,1024]{1,0:T(8,128)(2,1)}, bf16[128,1024]{1,0:T(8,128)(2,1)}, u32[]{:S(2)}, u32[]{:S(2)}) collective-permute-start(bf16[128,1024]{1,0:T(8,128)(2,1)} %get-tuple-element.54.refs_5_), channel_id=1, source_target_pairs={{1,2},{2,1},{5,6},{6,5},{9,10},{10,9},{13,14},{14,13},{17,18},{18,... | collective-permute-start | bytes 786440 | tf_op jit(solution)/shard_map/ppermute | solution.py:428
  9.0 15.4 %collective-permute-start.4 = (bf16[128,1024]{1,0:T(8,128)(2,1)}, bf16[128,1024]{1,0:T(8,128)(2,1)}, u32[]{:S(2)}, u32[]{:S(2)}) collective-permute-start(bf16[128,1024]{1,0:T(8,128)(2,1)} %get-tuple-element.54.refs_5_), channel_id=1, source_target_pairs={{0,1},{2,3},{1,0},{3,2},{4,5},{6,7},{5,4},{7,6},{8,9},{10,11},{9,8... | collective-permute-start | bytes 786440 | tf_op jit(solution)/shard_map/ppermute | solution.py:428
  18.8 13.2 %collective-permute-start.2 = (bf16[128,1024]{1,0:T(8,128)(2,1)S(1)}, bf16[128,1024]{1,0:T(8,128)(2,1)S(1)}, u32[]{:S(2)}, u32[]{:S(2)}) collective-permute-start(bf16[128,1024]{1,0:T(8,128)(2,1)S(1)} %get-tuple-element.50), channel_id=1, source_target_pairs={{1,2},{2,1},{5,6},{6,5},{9,10},{10,9},{13,14},{14,13},{17,18},{18,... | collective-permute-start | bytes 786440 | tf_op jit(solution)/shard_map/ppermute | solution.py:428
  19.6 12.4 %collective-permute-start.3 = (bf16[128,1024]{1,0:T(8,128)(2,1)S(1)}, bf16[128,1024]{1,0:T(8,128)(2,1)S(1)}, u32[]{:S(2)}, u32[]{:S(2)}) collective-permute-start(bf16[128,1024]{1,0:T(8,128)(2,1)S(1)} %get-tuple-element.52.after_ref), channel_id=1, source_target_pairs={{0,1},{2,3},{1,0},{3,2},{4,5},{6,7},{5,4},{7,6},{8,9},{10,11},{9,8... | collective-permute-start | bytes 786440 | tf_op jit(solution)/shard_map/ppermute | solution.py:428
  23.0 43.9 %collective-permute-start.13 = (bf16[768,1024]{1,0:T(8,128)(2,1)S(1)}, bf16[768,1024]{1,0:T(8,128)(2,1)S(1)}, u32[]{:S(2)}, u32[]{:S(2)}) collective-permute-start(bf16[768,1024]{1,0:T(8,128)(2,1)S(1)} %pick.2), channel_id=1, source_target_pairs={{0,8},{4,12},{8,0},{12,4},{1,9},{5,13},{9,1},{13,5},{2,10},{6,14},... | collective-permute-start | bytes 4718600 | tf_op jit(solution)/shard_map/ppermute | solution.py:438
  25.6 11.0 %collective-permute-start.7 = (bf16[128,1024]{1,0:T(8,128)(2,1)S(1)}, bf16[128,1024]{1,0:T(8,128)(2,1)S(1)}, u32[]{:S(2)}, u32[]{:S(2)}) collective-permute-start(bf16[128,1024]{1,0:T(8,128)(2,1)S(1)} %get-tuple-element.59), channel_id=1, source_target_pairs={{1,2},{2,1},{5,6},{6,5},{9,10},{10,9},{13,14},{14,13},{17,18},{18,... | collective-permute-start | bytes 786440 | tf_op jit(solution)/shard_map/ppermute | solution.py:428
  26.3 10.3 %collective-permute-start.8 = (bf16[128,1024]{1,0:T(8,128)(2,1)S(1)}, bf16[128,1024]{1,0:T(8,128)(2,1)S(1)}, u32[]{:S(2)}, u32[]{:S(2)}) collective-permute-start(bf16[128,1024]{1,0:T(8,128)(2,1)S(1)} %get-tuple-element.61), channel_id=1, source_target_pairs={{0,1},{2,3},{1,0},{3,2},{4,5},{6,7},{5,4},{7,6},{8,9},{10,11},{9,8... | collective-permute-start | bytes 786440 | tf_op jit(solution)/shard_map/ppermute | solution.py:428
  32.2 6.8 %collective-permute-start.10 = (bf16[128,1024]{1,0:T(8,128)(2,1)S(1)}, bf16[128,1024]{1,0:T(8,128)(2,1)S(1)}, u32[]{:S(2)}, u32[]{:S(2)}) collective-permute-start(bf16[128,1024]{1,0:T(8,128)(2,1)S(1)} %get-tuple-element.64), channel_id=1, source_target_pairs={{1,2},{2,1},{5,6},{6,5},{9,10},{10,9},{13,14},{14,13},{17,18},{18,... | collective-permute-start | bytes 786440 | tf_op jit(solution)/shard_map/ppermute | solution.py:428
  32.9 8.2 %collective-permute-start.6 = (bf16[128,1024]{1,0:T(8,128)(2,1)S(1)}, bf16[128,1024]{1,0:T(8,128)(2,1)S(1)}, u32[]{:S(2)}, u32[]{:S(2)}) collective-permute-start(bf16[128,1024]{1,0:T(8,128)(2,1)S(1)} %get-tuple-element.56.after_ref), channel_id=1, source_target_pairs={{0,1},{2,3},{1,0},{3,2},{4,5},{6,7},{5,4},{7,6},{8,9},{10,11},{9,8... | collective-permute-start | bytes 786440 | tf_op jit(solution)/shard_map/ppermute | solution.py:428
  36.7 9.9 %collective-permute-start.9 = (bf16[128,1024]{1,0:T(8,128)(2,1)S(1)}, bf16[128,1024]{1,0:T(8,128)(2,1)S(1)}, u32[]{:S(2)}, u32[]{:S(2)}) collective-permute-start(bf16[128,1024]{1,0:T(8,128)(2,1)S(1)} %get-tuple-element.63), channel_id=1, source_target_pairs={{0,1},{2,3},{1,0},{3,2},{4,5},{6,7},{5,4},{7,6},{8,9},{10,11},{9,8... | collective-permute-start | bytes 786440 | tf_op jit(solution)/shard_map/ppermute | solution.py:428
  36.8 9.8 %collective-permute-start.11 = (bf16[128,1024]{1,0:T(8,128)(2,1)S(1)}, bf16[128,1024]{1,0:T(8,128)(2,1)S(1)}, u32[]{:S(2)}, u32[]{:S(2)}) collective-permute-start(bf16[128,1024]{1,0:T(8,128)(2,1)S(1)} %get-tuple-element.65), channel_id=1, source_target_pairs={{1,2},{2,1},{5,6},{6,5},{9,10},{10,9},{13,14},{14,13},{17,18},{18,... | collective-permute-start | bytes 786440 | tf_op jit(solution)/shard_map/ppermute | solution.py:428
  41.2 9.0 %collective-permute-start.17 = (bf16[128,1024]{1,0:T(8,128)(2,1)S(1)}, bf16[128,1024]{1,0:T(8,128)(2,1)S(1)}, u32[]{:S(2)}, u32[]{:S(2)}) collective-permute-start(bf16[128,1024]{1,0:T(8,128)(2,1)S(1)} %get-tuple-element.81), channel_id=1, source_target_pairs={{1,2},{2,1},{5,6},{6,5},{9,10},{10,9},{13,14},{14,13},{17,18},{18,... | collective-permute-start | bytes 786440 | tf_op jit(solution)/shard_map/ppermute | solution.py:428
  41.9 10.0 %collective-permute-start.16 = (bf16[128,1024]{1,0:T(8,128)(2,1)S(1)}, bf16[128,1024]{1,0:T(8,128)(2,1)S(1)}, u32[]{:S(2)}, u32[]{:S(2)}) collective-permute-start(bf16[128,1024]{1,0:T(8,128)(2,1)S(1)} %get-tuple-element.77.after_ref), channel_id=1, source_target_pairs={{0,1},{2,3},{1,0},{3,2},{4,5},{6,7},{5,4},{7,6},{8,9},{10,11},{9,8... | collective-permute-start | bytes 786440 | tf_op jit(solution)/shard_map/ppermute | solution.py:428
  46.8 10.1 %collective-permute-start.14 = (bf16[128,1024]{1,0:T(8,128)(2,1)S(1)}, bf16[128,1024]{1,0:T(8,128)(2,1)S(1)}, u32[]{:S(2)}, u32[]{:S(2)}) collective-permute-start(bf16[128,1024]{1,0:T(8,128)(2,1)S(1)} %get-tuple-element.78), channel_id=1, source_target_pairs={{0,1},{2,3},{1,0},{3,2},{4,5},{6,7},{5,4},{7,6},{8,9},{10,11},{9,8... | collective-permute-start | bytes 786440 | tf_op jit(solution)/shard_map/ppermute | solution.py:428
  48.1 8.8 %collective-permute-start.15 = (bf16[128,1024]{1,0:T(8,128)(2,1)S(1)}, bf16[128,1024]{1,0:T(8,128)(2,1)S(1)}, u32[]{:S(2)}, u32[]{:S(2)}) collective-permute-start(bf16[128,1024]{1,0:T(8,128)(2,1)S(1)} %get-tuple-element.79), channel_id=1, source_target_pairs={{1,2},{2,1},{5,6},{6,5},{9,10},{10,9},{13,14},{14,13},{17,18},{18,... | collective-permute-start | bytes 786440 | tf_op jit(solution)/shard_map/ppermute | solution.py:428
  51.9 15.1 %copy-start.3 = (f32[1,256,1024]{2,1,0:T(8,128)S(1)}, f32[1,256,1024]{2,1,0:T(8,128)}, u32[]{:S(2)}) copy-start(f32[1,256,1024]{2,1,0:T(8,128)} %param.13) | copy-start | bytes 3145732
  52.0 15.0 %copy-start.1 = (f32[1,256,1024]{2,1,0:T(8,128)S(1)}, f32[1,256,1024]{2,1,0:T(8,128)}, u32[]{:S(2)}) copy-start(f32[1,256,1024]{2,1,0:T(8,128)} %param.11) | copy-start | bytes 3145732
  52.0 14.9 %copy-start.2 = (f32[1,256,1024]{2,1,0:T(8,128)S(1)}, f32[1,256,1024]{2,1,0:T(8,128)}, u32[]{:S(2)}) copy-start(f32[1,256,1024]{2,1,0:T(8,128)} %param.12) | copy-start | bytes 3145732
  52.0 11.0 %collective-permute-start.21 = (bf16[128,1024]{1,0:T(8,128)(2,1)S(1)}, bf16[128,1024]{1,0:T(8,128)(2,1)S(1)}, u32[]{:S(2)}, u32[]{:S(2)}) collective-permute-start(bf16[128,1024]{1,0:T(8,128)(2,1)S(1)} %summed_grad.2.after_ref.own_ref), channel_id=1, source_target_pairs={{0,8},{4,12},{8,0},{12,4},{1,9},{5,13},{9,1},{13,5},{2,10},{6,14},... | collective-permute-start | bytes 786440 | tf_op jit(solution)/shard_map/ppermute | solution.py:448
  57.0 8.5 %collective-permute-start.18 = (bf16[128,1024]{1,0:T(8,128)(2,1)S(1)}, bf16[128,1024]{1,0:T(8,128)(2,1)S(1)}, u32[]{:S(2)}, u32[]{:S(2)}) collective-permute-start(bf16[128,1024]{1,0:T(8,128)(2,1)S(1)} %summed_grad.3.own_ref.after_ref), channel_id=1, source_target_pairs={{0,4},{4,0},{8,12},{12,8},{1,5},{5,1},{9,13},{13,9},{2,6},{6,2},{1... | collective-permute-start | bytes 786440 | tf_op jit(solution)/shard_map/ppermute | solution.py:444
  60.9 7.0 %collective-permute-start.20 = (bf16[128,1024]{1,0:T(8,128)(2,1)S(1)}, bf16[128,1024]{1,0:T(8,128)(2,1)S(1)}, u32[]{:S(2)}, u32[]{:S(2)}) collective-permute-start(bf16[128,1024]{1,0:T(8,128)(2,1)S(1)} %summed_grad.2.after_ref.own_ref), channel_id=1, source_target_pairs={{0,4},{4,0},{8,12},{12,8},{1,5},{5,1},{9,13},{13,9},{2,6},{6,2},{1... | collective-permute-start | bytes 786440 | tf_op jit(solution)/shard_map/ppermute | solution.py:444
  63.1 4.9 %collective-permute-start.22 = (bf16[128,1024]{1,0:T(8,128)(2,1)S(1)}, bf16[128,1024]{1,0:T(8,128)(2,1)S(1)}, u32[]{:S(2)}, u32[]{:S(2)}) collective-permute-start(bf16[128,1024]{1,0:T(8,128)(2,1)S(1)} %collective-permute-done.21.across_ref), channel_id=1, source_target_pairs={{0,4},{4,0},{8,12},{12,8},{1,5},{5,1},{9,13},{13,9},{2,6},{6,2},{1... | collective-permute-start | bytes 786440 | tf_op jit(solution)/shard_map/ppermute | solution.py:449
  65.7 8.0 %collective-permute-start.19 = (bf16[128,1024]{1,0:T(8,128)(2,1)S(1)}, bf16[128,1024]{1,0:T(8,128)(2,1)S(1)}, u32[]{:S(2)}, u32[]{:S(2)}) collective-permute-start(bf16[128,1024]{1,0:T(8,128)(2,1)S(1)} %pick.3), channel_id=1, source_target_pairs={{0,8},{4,12},{8,0},{12,4},{1,9},{5,13},{9,1},{13,5},{2,10},{6,14},... | collective-permute-start | bytes 786440 | tf_op jit(solution)/shard_map/ppermute | solution.py:446
  (3 other events, 8.7 us)

commit v8 on v6

--- a/solution.py
+++ b/solution.py
@@ -13,13 +13,14 @@
 epsilon = 1e-08
 
 MIB = 1 << 20
+SUM_FLOPS = 3 * 2 ** 29
 SMEM = pl.BlockSpec(memory_space=pltpu.SMEM)
 VMEM = pl.BlockSpec(memory_space=pltpu.VMEM)
 HBM = pl.BlockSpec(memory_space=pltpu.HBM)
 ANY = pl.BlockSpec(memory_space=pl.ANY)
 
 
-def call(kernel, name, out_shape, in_specs, out_specs, limit=8, scratch=(), aliases=None):
+def call(kernel, name, out_shape, in_specs, out_specs, limit=8, scratch=(), aliases=None, flops=0):
     return pl.pallas_call(
         kernel,
         out_shape=out_shape,
@@ -28,7 +29,7 @@
         scratch_shapes=scratch,
         input_output_aliases=aliases or {},
         compiler_params=pltpu.CompilerParams(vmem_limit_bytes=limit * MIB),
-        cost_estimate=pl.CostEstimate(flops=0, bytes_accessed=1024, transcendentals=0),
+        cost_estimate=pl.CostEstimate(flops=flops, bytes_accessed=1024, transcendentals=0),
         name=name,
     )
 
@@ -187,12 +188,21 @@
     return [flat[k * len(parts):(k + 1) * len(parts)] for k in range(len(order) + 1)]
 
 
-def sum_kernel(arrived_ref, term_ref, after_ref, out_ref):
+def send_kernel(arrived_ref, term_ref, arrived_too_ref, term_too_ref, after_ref, out_ref, out_too_ref):
     def body(at):
         total = arrived_ref[at, :].astype(jnp.float32) + term_ref[at, :].astype(jnp.float32)
         out_ref[at, :] = total.astype(out_ref.dtype)
+        total = arrived_too_ref[at, :].astype(jnp.float32) + term_too_ref[at, :].astype(jnp.float32)
+        out_too_ref[at, :] = total.astype(out_too_ref.dtype)
 
     by_rows(out_ref, body)
+
+
+def to_send(pairs, after):
+    like = half_array(*pairs[0][0].shape)
+    return call(send_kernel, "to_send", [like] * 2, [VMEM] * 4 + [ANY], [VMEM] * 2, flops=SUM_FLOPS)(
+        *pairs[0], *pairs[1], after
+    )
 
 
 def grad_kernel(own_ref, one_ref, other_ref, after_ref, out_ref):
@@ -203,10 +213,10 @@
     by_rows(out_ref, body)
 
 
-def summed(kernel, name, addends, after):
-    return call(
-        kernel, name, half_array(*addends[0].shape), [VMEM] * len(addends) + [ANY], VMEM
-    )(*addends, after)
+def summed_grad(own, one, other, after):
+    return call(grad_kernel, "summed_grad", half_array(*one.shape), [VMEM] * 3 + [ANY], VMEM)(
+        own, one, other, after
+    )
 
 
 def columns_kernel(n, scale, parts, where_ref, cotangent_ref, after_ref, *refs):
@@ -301,9 +311,10 @@
 
 def adam_kernel(start, size, filled, choices_ref, state_ref, own_ref, mate_ref, across_ref, far_ref, after_ref, *refs):
     refs = refs[3 if filled else 0:]
-    outs, (stepped, sems) = refs[:3], refs[3:]
+    outs, (token_ref, stepped, sems) = refs[:3], refs[3:]
+    token_ref[...] = jnp.zeros_like(token_ref)
     depth = own_ref.shape[1]
-    pieces = 4 if size % 64 == 0 else 1
+    pieces = 4 if size % 64 == 0 else 3 if size % 48 == 0 else 1
     piece = size // pieces
     writes = []
     for p in range(pieces):
@@ -337,8 +348,8 @@
     depth = state.shape[1]
     return call(
         functools.partial(adam_kernel, start, size, bool(filled)), "adam",
-        [jax.ShapeDtypeStruct((rows, depth), jnp.float32)] * 3,
-        [VMEM] * 6 + [ANY] + [HBM] * len(filled), [HBM] * 3,
+        [jax.ShapeDtypeStruct((rows, depth), jnp.float32)] * 3 + [jax.ShapeDtypeStruct((8, 128), jnp.float32)],
+        [VMEM] * 6 + [ANY] + [HBM] * len(filled), [HBM] * 3 + [VMEM],
         scratch=[pltpu.VMEM((3, size, depth), jnp.float32), pltpu.SemaphoreType.DMA((12,))],
         aliases={7 + k: k for k in range(len(filled))},
     )(choices, state, *grads, after, *filled)
@@ -349,8 +360,8 @@
     cotangent = out_grad[0]
     scale = context_rows.shape[1] ** (-0.5)
     rows, depth = weight.shape[1:]
-    chains = 2 if rows % 32 == 0 else 1
-    parts = [(c * rows // chains, rows // chains) for c in range(chains)]
+    smaller = rows * 112 // 256 // 16 * 16
+    parts = [(0, smaller), (smaller, rows - smaller)] if smaller else [(0, rows)]
     where = jnp.stack([lax.axis_index("shard"), lax.axis_index("member")]).astype(jnp.int32)
 
     swap_across = [(m, m ^ 2) for m in range(members)]
@@ -368,18 +379,18 @@
     terms = partial_blocks(n, scale, parts, order, where, context_rows, cotangent)
 
     arrived = [[own, own]]
-    sent = early = own[0]
+    sent = own[0]
     for slot in range(1, n + 1):
         now = [[], []]
         for c in range(len(parts)):
+            blocks = [arrived[-1][1][c], arrived[-1][0][c]]
+            if slot > 1:
+                blocks = to_send([(blocks[swap], terms[2 * (slot - 2) + swap][c]) for swap in range(2)], sent)
+                sent = blocks[0]
+            if slot == 2 and c == 0:
+                early = sent
             for swap in range(2):
-                block = arrived[-1][1 - swap][c]
-                if slot > 1:
-                    addends = (block, terms[2 * (slot - 2) + swap][c])
-                    block = sent = summed(sum_kernel, "to_send", addends, sent)
-                if slot == 2 and c == 0:
-                    early = block
-                now[swap].append(lax.ppermute(block, "shard", swaps[swap]))
+                now[swap].append(lax.ppermute(blocks[swap], "shard", swaps[swap]))
         arrived.append(now)
 
     mate = lax.ppermute(state, "member", swap_mates)
@@ -388,8 +399,7 @@
 
     grads = []
     for c in range(len(parts)):
-        addends = (terms[-1][c], arrived[n][0][c], arrived[n][1][c])
-        sent = summed(grad_kernel, "summed_grad", addends, sent)
+        sent = summed_grad(terms[-1][c], arrived[n][0][c], arrived[n][1][c], sent)
         grads.append(sent)
     blocks = list(own)
     for slot in range(1, n):
@@ -399,11 +409,9 @@
     updated = ()
     for c, (start, size) in enumerate(parts):
         mate = lax.ppermute(grads[c], "member", swap_mates)
-        across = lax.ppermute(grads[c], "member", swap_across)
-        if c == 0:
-            across = gate(across, computed)
+        across = gate(lax.ppermute(grads[c], "member", swap_across), computed)
         far = lax.ppermute(across, "member", swap_mates)
-        updated = adam_update(
+        *updated, computed = adam_update(
             start, size, rows, choices, states[c], (grads[c], mate, across, far), computed, updated
         )
     return (context_grad[None],) + tuple(array[None] for array in updated)

time: 71.9 us -> 77.5 us (1.078)
  starting transfers between devices: 33.8 us -> 39.2 us
  Pallas kernels: 17.6 us -> 20.8 us
  waiting for transfers between devices: 16.9 us -> 14.3 us
    ppermute x18, waiting for transfers between devices: 16.9 us -> 13 us  [the longest x16 12.9 us: on_device(): now[swap].append(lax.ppermute(blocks[swap], 'shard', swaps[swap]))]
    ppermute x2, starting transfers between devices: 2.06 us -> 5.37 us  [on_device(): far = lax.ppermute(across, 'member', swap_mates)]
    pallas_call x1, Pallas kernels: 3.21 us -> 5.5 us  [partial_blocks(): call(functools.partial(partial_kernel, n, scale, parts, order), 'partial_...]
    ppermute x2, waiting for transfers between devices: 0.01 us -> 1.33 us  [on_device(): far = lax.ppermute(across, 'member', swap_mates)]
    ppermute x18, starting transfers between devices: 28 us -> 29.2 us  [the longest x16 24.7 us: on_device(): now[swap].append(lax.ppermute(blocks[swap], 'shard', swaps[swap]))]
    ppermute x2, starting transfers between devices: 2.32 us -> 3.28 us  [on_device(): mate = lax.ppermute(grads[c], 'member', swap_mates)]
    pallas_call x2, Pallas kernels: 3.34 us -> 4.29 us  [adam_update(): call(functools.partial(adam_kernel, start, size, bool(filled)), 'adam', [...]
    pallas_call x14 -> x8, Pallas kernels: 2.38 us -> 2.23 us  [the longest x6 1.99 us: to_send(): call(send_kernel, 'to_send', [like] * 2, [VMEM] * 4 + [ANY], [VMEM] * 2,...]
  transfers between devices with their start and end apart: 24 -> 24, of which waited for: 7 -> 9; matrix products, arithmetic and copies ran while one was open for 0% -> 0% of each run, Pallas kernels for 18% -> 20%
where the time goes in v8:
time: 77.5 us; the launch traced here: 76.7 us
  starting transfers between devices  39.2 us (51%)
  Pallas kernels  20.8 us (27%)
  waiting for transfers between devices  14.3 us (18%)
  local copies, waits for them, and re-layouts  1.28 us (2%)
  between operations  1.01 us (1%)
    ppermute x16, starting transfers between devices, on_device(): now[swap].append(lax.ppermute(blocks[swap], 'shard', swaps[swap]))  24.7 us
    ppermute x16, waiting for transfers between devices, on_device(): now[swap].append(lax.ppermute(blocks[swap], 'shard', swaps[swap]))  12.9 us
    pallas_call x1, Pallas kernels, partial_blocks(): call(functools.partial(partial_kernel, n, scale, parts, order), 'partial_...  5.5 us
    ppermute x2, starting transfers between devices, on_device(): far = lax.ppermute(across, 'member', swap_mates)  5.37 us
    ppermute x2, starting transfers between devices, on_device(): across = gate(lax.ppermute(grads[c], 'member', swap_across), computed)  4.46 us
    pallas_call x2, Pallas kernels, adam_update(): call(functools.partial(adam_kernel, start, size, bool(filled)), 'adam', [...  4.29 us
    pallas_call x1, Pallas kernels, halves(): call(functools.partial(halves_kernel, parts), 'halves', [half_array(size,...  3.33 us
    ppermute x2, starting transfers between devices, on_device(): mate = lax.ppermute(grads[c], 'member', swap_mates)  3.28 us
  transfers between devices with their start and end apart: 24, of which 9 were waited for; matrix products, arithmetic and copies ran while one was open for 0% of the time, Pallas kernels for 20%

profile of v8, /device:TPU:1, one launch (start us, length us, event | category | flops | bytes accessed | tf_op | source)
XLA Modules:
  0.0 76.7 jit_solution(4358481123492570164)
XLA Ops:
  0.6 3.3 %halves.1 = (bf16[768,1024]{1,0:T(8,128)(2,1)}, bf16[112,1024]{1,0:T(8,128)(2,1)}, bf16[144,1024]{1,0:T(8,128)(2,1)}) custom-call(f32[256,1024]{1,0:T(8,128)} %bitcast.11, f32[256,1024]{1,0:T(8,128)} %bitcast.13, f32[256,1024]{1,0:T(8,128)} %bitcast.15), custom_call_target="tpu_custom_call" | custom-call | bytes 1024 | tf_op jit(solution)/shard_map/halves/pallas_call | solution.py:98
  4.8 5.3 %collective-permute-start.3 = (bf16[112,1024]{1,0:T(8,128)(2,1)}, bf16[112,1024]{1,0:T(8,128)(2,1)}, u32[]{:S(2)}, u32[]{:S(2)}) collective-permute-start(bf16[112,1024]{1,0:T(8,128)(2,1)} %get-tuple-element.48.after_ref.refs_0_), channel_id=1, source_target_pairs={{0,1},{2,3},{1,0},{3,2},{4,5},{6,7},{5,4},{7,6},{8,9},{10,11},{9,8... | collective-permute-start | bytes 688136 | tf_op jit(solution)/shard_map/ppermute | solution.py:393
  10.8 1.5 %collective-permute-start.1 = (bf16[144,1024]{1,0:T(8,128)(2,1)}, bf16[144,1024]{1,0:T(8,128)(2,1)S(1)}, u32[]{:S(2)}, u32[]{:S(2)}) collective-permute-start(bf16[144,1024]{1,0:T(8,128)(2,1)} %get-tuple-element.45.refs_1_), channel_id=1, source_target_pairs={{0,1},{2,3},{1,0},{3,2},{4,5},{6,7},{5,4},{7,6},{8,9},{10,11},{9,8... | collective-permute-start | bytes 884744 | tf_op jit(solution)/shard_map/ppermute | solution.py:393
  12.4 1.2 %copy-done.5 = bf16[1,512,1024]{2,1,0:T(8,128)(2,1)S(1)} copy-done((bf16[1,512,1024]{2,1,0:T(8,128)(2,1)S(1)}, bf16[1,512,1024]{2,1,0:T(8,128)(2,1)}, u32[]{:S(2)}) %copy-start.5) | copy-done | bytes 1048600
  13.6 5.5 %partial_blocks.1 = (bf16[112,1024]{1,0:T(8,128)(2,1)S(1)}, bf16[144,1024]{1,0:T(8,128)(2,1)S(1)}, bf16[112,1024]{1,0:T(8,128)(2,1)S(1)}, bf16[144,1024]{1,0:T(8...) custom-call(s32[2]{0:T(128)S(1)} %pad_add_fusion.where_ref, ...), custom_call_target="tpu_custom_call" | custom-call | bytes 1024 | tf_op jit(solution)/shard_map/partial_blocks/pallas_call | solution.py:174
  19.8 1.2 %to_send.6 = (bf16[112,1024]{1,0:T(8,128)(2,1)S(1)}, bf16[112,1024]{1,0:T(8,128)(2,1)S(1)}) custom-call(bf16[112,1024]{1,0:T(8,128)(2,1)S(1)} %collective-permute-done.2.arrived_ref.refs_4_, bf16[112,1024]{1,0:T(8,128)(2,1)S(1)} %get-tuple-element.49.term_ref, bf16[112,1024]{1,0:T(8,128)(2,1)} %collective-permute-done.3.arrived_too_ref.refs_2_, ...), custom_call_target="tpu_custom_call" | custom-call | flops 1610612736 | bytes 1024 | tf_op jit(solution)/shard_map/to_send/pallas_call | solution.py:203
  21.7 2.6 %collective-permute-start.7 = (bf16[112,1024]{1,0:T(8,128)(2,1)S(1)}, bf16[112,1024]{1,0:T(8,128)(2,1)S(1)}, u32[]{:S(2)}, u32[]{:S(2)}) collective-permute-start(bf16[112,1024]{1,0:T(8,128)(2,1)S(1)} %get-tuple-element.51.after_ref), channel_id=1, source_target_pairs={{0,1},{2,3},{1,0},{3,2},{4,5},{6,7},{5,4},{7,6},{8,9},{10,11},{9,8... | collective-permute-start | bytes 688136 | tf_op jit(solution)/shard_map/ppermute | solution.py:393
  24.3 0.7 pick.1
  25.0 1.3 %collective-permute-start.17 = (bf16[768,1024]{1,0:T(8,128)(2,1)S(1)}, bf16[768,1024]{1,0:T(8,128)(2,1)S(1)}, u32[]{:S(2)}, u32[]{:S(2)}) collective-permute-start(bf16[768,1024]{1,0:T(8,128)(2,1)S(1)} %pick.1), channel_id=1, source_target_pairs={{0,8},{4,12},{8,0},{12,4},{1,9},{5,13},{9,1},{13,5},{2,10},{6,14},... | collective-permute-start | bytes 4718600 | tf_op jit(solution)/shard_map/ppermute | solution.py:397
  26.5 0.7 collective-permute-start.4
  27.2 1.5 %collective-permute-start.5 = (bf16[144,1024]{1,0:T(8,128)(2,1)S(1)}, bf16[144,1024]{1,0:T(8,128)(2,1)S(1)}, u32[]{:S(2)}, u32[]{:S(2)}) collective-permute-start(bf16[144,1024]{1,0:T(8,128)(2,1)S(1)} %get-tuple-element.54.after_ref), channel_id=1, source_target_pairs={{0,1},{2,3},{1,0},{3,2},{4,5},{6,7},{5,4},{7,6},{8,9},{10,11},{9,8... | collective-permute-start | bytes 884744 | tf_op jit(solution)/shard_map/ppermute | solution.py:393
  28.7 0.7 collective-permute-done.7.arrived_too_ref.refs_6_
  30.3 2.7 %collective-permute-start.11 = (bf16[112,1024]{1,0:T(8,128)(2,1)S(1)}, bf16[112,1024]{1,0:T(8,128)(2,1)S(1)}, u32[]{:S(2)}, u32[]{:S(2)}) collective-permute-start(bf16[112,1024]{1,0:T(8,128)(2,1)S(1)} %get-tuple-element.59.after_ref), channel_id=1, source_target_pairs={{0,1},{2,3},{1,0},{3,2},{4,5},{6,7},{5,4},{7,6},{8,9},{10,11},{9,8... | collective-permute-start | bytes 688136 | tf_op jit(solution)/shard_map/ppermute | solution.py:393
  32.9 2.5 %collective-permute-done.5.arrived_too_ref.refs_7_ = bf16[144,1024]{1,0:T(8,128)(2,1)S(1)} collective-permute-done((bf16[144,1024]{1,0:T(8,128)(2,1)S(1)}, bf16[144,1024]{1,0:T(8,128)(2,1)S(1)}, u32[]{:S(2)}, u32[]{:S(2)}) %collective-permute-start.5) | collective-permute-done | bytes 294944 | tf_op jit(solution)/shard_map/ppermute | solution.py:393
  35.6 0.7 collective-permute-start.8
  36.3 2.9 %collective-permute-start.9 = (bf16[144,1024]{1,0:T(8,128)(2,1)S(1)}, bf16[144,1024]{1,0:T(8,128)(2,1)S(1)}, u32[]{:S(2)}, u32[]{:S(2)}) collective-permute-start(bf16[144,1024]{1,0:T(8,128)(2,1)S(1)} %get-tuple-element.62.after_ref), channel_id=1, source_target_pairs={{0,1},{2,3},{1,0},{3,2},{4,5},{6,7},{5,4},{7,6},{8,9},{10,11},{9,8... | collective-permute-start | bytes 884744 | tf_op jit(solution)/shard_map/ppermute | solution.py:393
  39.2 1.1 %collective-permute-done.11.arrived_too_ref.refs_10_ = bf16[112,1024]{1,0:T(8,128)(2,1)S(1)} collective-permute-done((bf16[112,1024]{1,0:T(8,128)(2,1)S(1)}, bf16[112,1024]{1,0:T(8,128)(2,1)S(1)}, u32[]{:S(2)}, u32[]{:S(2)}) %collective-permute-start.11) | collective-permute-done | bytes 229408 | tf_op jit(solution)/shard_map/ppermute | solution.py:393
  40.4 1.2 %collective-permute-start.14 = (bf16[112,1024]{1,0:T(8,128)(2,1)S(1)}, bf16[112,1024]{1,0:T(8,128)(2,1)S(1)}, u32[]{:S(2)}, u32[]{:S(2)}) collective-permute-start(bf16[112,1024]{1,0:T(8,128)(2,1)S(1)} %get-tuple-element.67.after_ref), channel_id=1, source_target_pairs={{0,1},{2,3},{1,0},{3,2},{4,5},{6,7},{5,4},{7,6},{8,9},{10,11},{9,8... | collective-permute-start | bytes 688136 | tf_op jit(solution)/shard_map/ppermute | solution.py:393
  42.4 2.5 %collective-permute-done.9.arrived_too_ref.refs_11_ = bf16[144,1024]{1,0:T(8,128)(2,1)S(1)} collective-permute-done((bf16[144,1024]{1,0:T(8,128)(2,1)S(1)}, bf16[144,1024]{1,0:T(8,128)(2,1)S(1)}, u32[]{:S(2)}, u32[]{:S(2)}) %collective-permute-start.9) | collective-permute-done | bytes 294944 | tf_op jit(solution)/shard_map/ppermute | solution.py:393
  45.1 1.5 %collective-permute-start.12 = (bf16[144,1024]{1,0:T(8,128)(2,1)S(1)}, bf16[144,1024]{1,0:T(8,128)(2,1)S(1)}, u32[]{:S(2)}, u32[]{:S(2)}) collective-permute-start(bf16[144,1024]{1,0:T(8,128)(2,1)S(1)} %get-tuple-element.68.after_ref), channel_id=1, source_target_pairs={{0,1},{2,3},{1,0},{3,2},{4,5},{6,7},{5,4},{7,6},{8,9},{10,11},{9,8... | collective-permute-start | bytes 884744 | tf_op jit(solution)/shard_map/ppermute | solution.py:393
  47.3 2.1 %collective-permute-done.14.one_ref = bf16[112,1024]{1,0:T(8,128)(2,1)S(1)} collective-permute-done((bf16[112,1024]{1,0:T(8,128)(2,1)S(1)}, bf16[112,1024]{1,0:T(8,128)(2,1)S(1)}, u32[]{:S(2)}, u32[]{:S(2)}) %collective-permute-start.14) | collective-permute-done | bytes 229408 | tf_op jit(solution)/shard_map/ppermute | solution.py:393
  49.5 2.2 %collective-permute-start.21 = (bf16[112,1024]{1,0:T(8,128)(2,1)S(1)}, bf16[112,1024]{1,0:T(8,128)(2,1)S(1)}, u32[]{:S(2)}, u32[]{:S(2)}) collective-permute-start(bf16[112,1024]{1,0:T(8,128)(2,1)S(1)} %summed_grad.2.after_ref.own_ref), channel_id=1, source_target_pairs={{0,8},{4,12},{8,0},{12,4},{1,9},{5,13},{9,1},{13,5},{2,10},{6,14},... | collective-permute-start | bytes 688136 | tf_op jit(solution)/shard_map/ppermute | solution.py:412
  51.7 4.0 %collective-permute-done.12.one_ref = bf16[144,1024]{1,0:T(8,128)(2,1)S(1)} collective-permute-done((bf16[144,1024]{1,0:T(8,128)(2,1)S(1)}, bf16[144,1024]{1,0:T(8,128)(2,1)S(1)}, u32[]{:S(2)}, u32[]{:S(2)}) %collective-permute-start.12) | collective-permute-done | bytes 294944 | tf_op jit(solution)/shard_map/ppermute | solution.py:393
  55.9 2.2 %collective-permute-start.19 = (bf16[144,1024]{1,0:T(8,128)(2,1)S(1)}, bf16[144,1024]{1,0:T(8,128)(2,1)S(1)}, u32[]{:S(2)}, u32[]{:S(2)}) collective-permute-start(bf16[144,1024]{1,0:T(8,128)(2,1)S(1)} %summed_grad.3.after_ref.own_ref), channel_id=1, source_target_pairs={{0,8},{4,12},{8,0},{12,4},{1,9},{5,13},{9,1},{13,5},{2,10},{6,14},... | collective-permute-start | bytes 884744 | tf_op jit(solution)/shard_map/ppermute | solution.py:412
  58.1 3.3 %collective-permute-start.20 = (bf16[112,1024]{1,0:T(8,128)(2,1)S(1)}, bf16[112,1024]{1,0:T(8,128)(2,1)S(1)}, u32[]{:S(2)}, u32[]{:S(2)}) collective-permute-start(bf16[112,1024]{1,0:T(8,128)(2,1)S(1)} %summed_grad.2.after_ref.own_ref), channel_id=1, source_target_pairs={{0,4},{4,0},{8,12},{12,8},{1,5},{5,1},{9,13},{13,9},{2,6},{6,2},{1... | collective-permute-start | bytes 688136 | tf_op jit(solution)/shard_map/ppermute | solution.py:411
  61.4 3.3 %context_grad.1 = (bf16[512,1024]{1,0:T(8,128)(2,1)}, f32[8,128]{1,0:T(8,128)S(1)}) custom-call(s32[2]{0:T(128)S(1)} %pad_add_fusion.where_ref, bf16[512,1024]{1,0:T(8,128)(2,1)S(1)} %bitcast.18, bf16[144,1024]{1,0:T(8,128)(2,1)S(1)} %summed_grad.3.after_ref.own_ref, bf16[112,1024]{1,0:T(8,128)(2,1)S(1)} %copy-done.7, bf16[144,1024]{1,0:T(8,128)(2,1)S(1)} %copy-done.6, ...), custom_call_target="tpu_custom_call" | custom-call | bytes 1024 | tf_op jit(solution)/shard_map/context_grad/pallas_call | solution.py:255
  64.7 3.7 %collective-permute-start.22 = (bf16[112,1024]{1,0:T(8,128)(2,1)S(1)}, bf16[112,1024]{1,0:T(8,128)(2,1)S(1)}, u32[]{:S(2)}, u32[]{:S(2)}) collective-permute-start(bf16[112,1024]{1,0:T(8,128)(2,1)S(1)} %gate.2.across_ref), channel_id=1, source_target_pairs={{0,4},{4,0},{8,12},{12,8},{1,5},{5,1},{9,13},{13,9},{2,6},{6,2},{1... | collective-permute-start | bytes 688136 | tf_op jit(solution)/shard_map/ppermute | solution.py:413
  68.5 0.9 %taken_state.1 = (f32[336,1024]{1,0:T(8,128)S(1)}, f32[432,1024]{1,0:T(8,128)S(1)}) custom-call(s32[2]{0:T(128)S(1)} %pad_add_fusion.where_ref, s32[4]{0:T(128)S(1)} %copy-done.8, bf16[144,1024]{1,0:T(8,128)(2,1)S(1)} %get-tuple-element.68.after_ref, f32[256,1024]{1,0:T(8,128)S(1)} %bitcast.12, f32[256,1024]{1,0:T(8,128)S(1)} %bitcast.14, ...), custom_call_target="tpu_custom_call" | custom-call | bytes 1024 | tf_op jit(solution)/shard_map/taken_state/pallas_call | solution.py:304
  69.6 1.9 %adam.2 = (f32[256,1024]{1,0:T(8,128)}, f32[256,1024]{1,0:T(8,128)}, f32[256,1024]{1,0:T(8,128)}, f32[8,128]{1,0:T(8,128)S(1)}) custom-call(f32[8,1024]{1,0:T(8,128)S(1)} %choices.1.choices_ref, f32[336,1024]{1,0:T(8,128)S(1)} %get-tuple-element.75.state_ref, bf16[112,1024]{1,0:T(8,128)(2,1)S(1)} %summed_grad.2.after_ref.own_ref, ...), custom_call_target="tpu_custom_call" | custom-call | bytes 1024 | tf_op jit(solution)/shard_map/adam/pallas_call | solution.py:349
  71.5 1.6 %collective-permute-start.23 = (bf16[144,1024]{1,0:T(8,128)(2,1)S(1)}, bf16[144,1024]{1,0:T(8,128)(2,1)S(1)}, u32[]{:S(2)}, u32[]{:S(2)}) collective-permute-start(bf16[144,1024]{1,0:T(8,128)(2,1)S(1)} %gate.3.across_ref), channel_id=1, source_target_pairs={{0,4},{4,0},{8,12},{12,8},{1,5},{5,1},{9,13},{13,9},{2,6},{6,2},{1... | collective-permute-start | bytes 884744 | tf_op jit(solution)/shard_map/ppermute | solution.py:413
  73.1 1.2 %collective-permute-done.23.far_ref = bf16[144,1024]{1,0:T(8,128)(2,1)S(1)} collective-permute-done((bf16[144,1024]{1,0:T(8,128)(2,1)S(1)}, bf16[144,1024]{1,0:T(8,128)(2,1)S(1)}, u32[]{:S(2)}, u32[]{:S(2)}) %collective-permute-start.23) | collective-permute-done | bytes 294944 | tf_op jit(solution)/shard_map/ppermute | solution.py:413
  74.3 2.4 %adam.3 = (f32[256,1024]{1,0:T(8,128)}, f32[256,1024]{1,0:T(8,128)}, f32[256,1024]{1,0:T(8,128)}, f32[8,128]{1,0:T(8,128)}) custom-call(f32[8,1024]{1,0:T(8,128)S(1)} %choices.1.choices_ref, f32[432,1024]{1,0:T(8,128)S(1)} %get-tuple-element.74.state_ref, ...), custom_call_target="tpu_custom_call", output_to_operand_aliasing={{0}: (7, {}), {1}: (8, {}), {2}: (9, {})} | custom-call | bytes 1024 | tf_op jit(solution)/shard_map/adam/pallas_call | solution.py:349
  (59 shorter events, 6.1 us)
Async XLA Ops:
  4.0 15.2 %copy-start.8 = (s32[4]{0:T(128)S(1)}, s32[4]{0:T(128)}, u32[]{:S(2)}) copy-start(s32[4]{0:T(128)} %donor_ref.3) | copy-start | bytes 52
  4.0 15.2 %copy-start.9 = (f32[4]{0:T(128)S(1)}, f32[4]{0:T(128)}, u32[]{:S(2)}) copy-start(f32[4]{0:T(128)} %rates_ref.1) | copy-start | bytes 52
  4.0 15.2 %copy-start.10 = (f32[4]{0:T(128)S(1)}, f32[4]{0:T(128)}, u32[]{:S(2)}) copy-start(f32[4]{0:T(128)} %decays_ref.1) | copy-start | bytes 52
  4.0 15.2 %copy-start.11 = (s32[4]{0:T(128)S(1)}, s32[4]{0:T(128)}, u32[]{:S(2)}) copy-start(s32[4]{0:T(128)} %steps_ref.1) | copy-start | bytes 52
  4.0 20.3 %collective-permute-start.16 = (bf16[768,1024]{1,0:T(8,128)(2,1)}, bf16[768,1024]{1,0:T(8,128)(2,1)S(1)}, u32[]{:S(2)}, u32[]{:S(2)}) collective-permute-start(bf16[768,1024]{1,0:T(8,128)(2,1)} %get-tuple-element.73.own_ref), channel_id=1, source_target_pairs={{0,4},{4,0},{8,12},{12,8},{1,5},{5,1},{9,13},{13,9},{2,6},{6,2},{1... | collective-permute-start | bytes 4718600 | tf_op jit(solution)/shard_map/ppermute | solution.py:396
  4.1 15.6 %collective-permute-start.2 = (bf16[112,1024]{1,0:T(8,128)(2,1)}, bf16[112,1024]{1,0:T(8,128)(2,1)S(1)}, u32[]{:S(2)}, u32[]{:S(2)}) collective-permute-start(bf16[112,1024]{1,0:T(8,128)(2,1)} %get-tuple-element.48.after_ref.refs_0_), channel_id=1, source_target_pairs={{1,2},{2,1},{5,6},{6,5},{9,10},{10,9},{13,14},{14,13},{17,18},{18,... | collective-permute-start | bytes 688136 | tf_op jit(solution)/shard_map/ppermute | solution.py:393
  4.8 15.0 %collective-permute-start.3 = (bf16[112,1024]{1,0:T(8,128)(2,1)}, bf16[112,1024]{1,0:T(8,128)(2,1)}, u32[]{:S(2)}, u32[]{:S(2)}) collective-permute-start(bf16[112,1024]{1,0:T(8,128)(2,1)} %get-tuple-element.48.after_ref.refs_0_), channel_id=1, source_target_pairs={{0,1},{2,3},{1,0},{3,2},{4,5},{6,7},{5,4},{7,6},{8,9},{10,11},{9,8... | collective-permute-start | bytes 688136 | tf_op jit(solution)/shard_map/ppermute | solution.py:393
  10.2 16.1 %collective-permute-start = (bf16[144,1024]{1,0:T(8,128)(2,1)}, bf16[144,1024]{1,0:T(8,128)(2,1)S(1)}, u32[]{:S(2)}, u32[]{:S(2)}) collective-permute-start(bf16[144,1024]{1,0:T(8,128)(2,1)} %get-tuple-element.45.refs_1_), channel_id=1, source_target_pairs={{1,2},{2,1},{5,6},{6,5},{9,10},{10,9},{13,14},{14,13},{17,18},{18,... | collective-permute-start | bytes 884744 | tf_op jit(solution)/shard_map/ppermute | solution.py:393
  10.8 15.5 %collective-permute-start.1 = (bf16[144,1024]{1,0:T(8,128)(2,1)}, bf16[144,1024]{1,0:T(8,128)(2,1)S(1)}, u32[]{:S(2)}, u32[]{:S(2)}) collective-permute-start(bf16[144,1024]{1,0:T(8,128)(2,1)} %get-tuple-element.45.refs_1_), channel_id=1, source_target_pairs={{0,1},{2,3},{1,0},{3,2},{4,5},{6,7},{5,4},{7,6},{8,9},{10,11},{9,8... | collective-permute-start | bytes 884744 | tf_op jit(solution)/shard_map/ppermute | solution.py:393
  21.0 7.7 %collective-permute-start.6 = (bf16[112,1024]{1,0:T(8,128)(2,1)S(1)}, bf16[112,1024]{1,0:T(8,128)(2,1)S(1)}, u32[]{:S(2)}, u32[]{:S(2)}) collective-permute-start(bf16[112,1024]{1,0:T(8,128)(2,1)S(1)} %get-tuple-element.56), channel_id=1, source_target_pairs={{1,2},{2,1},{5,6},{6,5},{9,10},{10,9},{13,14},{14,13},{17,18},{18,... | collective-permute-start | bytes 688136 | tf_op jit(solution)/shard_map/ppermute | solution.py:393
  21.7 7.7 %collective-permute-start.7 = (bf16[112,1024]{1,0:T(8,128)(2,1)S(1)}, bf16[112,1024]{1,0:T(8,128)(2,1)S(1)}, u32[]{:S(2)}, u32[]{:S(2)}) collective-permute-start(bf16[112,1024]{1,0:T(8,128)(2,1)S(1)} %get-tuple-element.51.after_ref), channel_id=1, source_target_pairs={{0,1},{2,3},{1,0},{3,2},{4,5},{6,7},{5,4},{7,6},{8,9},{10,11},{9,8... | collective-permute-start | bytes 688136 | tf_op jit(solution)/shard_map/ppermute | solution.py:393
  25.0 43.5 %collective-permute-start.17 = (bf16[768,1024]{1,0:T(8,128)(2,1)S(1)}, bf16[768,1024]{1,0:T(8,128)(2,1)S(1)}, u32[]{:S(2)}, u32[]{:S(2)}) collective-permute-start(bf16[768,1024]{1,0:T(8,128)(2,1)S(1)} %pick.1), channel_id=1, source_target_pairs={{0,8},{4,12},{8,0},{12,4},{1,9},{5,13},{9,1},{13,5},{2,10},{6,14},... | collective-permute-start | bytes 4718600 | tf_op jit(solution)/shard_map/ppermute | solution.py:397
  26.5 6.5 %collective-permute-start.4 = (bf16[144,1024]{1,0:T(8,128)(2,1)S(1)}, bf16[144,1024]{1,0:T(8,128)(2,1)S(1)}, u32[]{:S(2)}, u32[]{:S(2)}) collective-permute-start(bf16[144,1024]{1,0:T(8,128)(2,1)S(1)} %get-tuple-element.52), channel_id=1, source_target_pairs={{1,2},{2,1},{5,6},{6,5},{9,10},{10,9},{13,14},{14,13},{17,18},{18,... | collective-permute-start | bytes 884744 | tf_op jit(solution)/shard_map/ppermute | solution.py:393
  27.2 8.2 %collective-permute-start.5 = (bf16[144,1024]{1,0:T(8,128)(2,1)S(1)}, bf16[144,1024]{1,0:T(8,128)(2,1)S(1)}, u32[]{:S(2)}, u32[]{:S(2)}) collective-permute-start(bf16[144,1024]{1,0:T(8,128)(2,1)S(1)} %get-tuple-element.54.after_ref), channel_id=1, source_target_pairs={{0,1},{2,3},{1,0},{3,2},{4,5},{6,7},{5,4},{7,6},{8,9},{10,11},{9,8... | collective-permute-start | bytes 884744 | tf_op jit(solution)/shard_map/ppermute | solution.py:393
  29.6 9.6 %collective-permute-start.10 = (bf16[112,1024]{1,0:T(8,128)(2,1)S(1)}, bf16[112,1024]{1,0:T(8,128)(2,1)S(1)}, u32[]{:S(2)}, u32[]{:S(2)}) collective-permute-start(bf16[112,1024]{1,0:T(8,128)(2,1)S(1)} %get-tuple-element.64), channel_id=1, source_target_pairs={{1,2},{2,1},{5,6},{6,5},{9,10},{10,9},{13,14},{14,13},{17,18},{18,... | collective-permute-start | bytes 688136 | tf_op jit(solution)/shard_map/ppermute | solution.py:393
  30.3 10.1 %collective-permute-start.11 = (bf16[112,1024]{1,0:T(8,128)(2,1)S(1)}, bf16[112,1024]{1,0:T(8,128)(2,1)S(1)}, u32[]{:S(2)}, u32[]{:S(2)}) collective-permute-start(bf16[112,1024]{1,0:T(8,128)(2,1)S(1)} %get-tuple-element.59.after_ref), channel_id=1, source_target_pairs={{0,1},{2,3},{1,0},{3,2},{4,5},{6,7},{5,4},{7,6},{8,9},{10,11},{9,8... | collective-permute-start | bytes 688136 | tf_op jit(solution)/shard_map/ppermute | solution.py:393
  35.6 6.8 %collective-permute-start.8 = (bf16[144,1024]{1,0:T(8,128)(2,1)S(1)}, bf16[144,1024]{1,0:T(8,128)(2,1)S(1)}, u32[]{:S(2)}, u32[]{:S(2)}) collective-permute-start(bf16[144,1024]{1,0:T(8,128)(2,1)S(1)} %get-tuple-element.60), channel_id=1, source_target_pairs={{1,2},{2,1},{5,6},{6,5},{9,10},{10,9},{13,14},{14,13},{17,18},{18,... | collective-permute-start | bytes 884744 | tf_op jit(solution)/shard_map/ppermute | solution.py:393
  36.3 8.6 %collective-permute-start.9 = (bf16[144,1024]{1,0:T(8,128)(2,1)S(1)}, bf16[144,1024]{1,0:T(8,128)(2,1)S(1)}, u32[]{:S(2)}, u32[]{:S(2)}) collective-permute-start(bf16[144,1024]{1,0:T(8,128)(2,1)S(1)} %get-tuple-element.62.after_ref), channel_id=1, source_target_pairs={{0,1},{2,3},{1,0},{3,2},{4,5},{6,7},{5,4},{7,6},{8,9},{10,11},{9,8... | collective-permute-start | bytes 884744 | tf_op jit(solution)/shard_map/ppermute | solution.py:393
  40.4 8.9 %collective-permute-start.14 = (bf16[112,1024]{1,0:T(8,128)(2,1)S(1)}, bf16[112,1024]{1,0:T(8,128)(2,1)S(1)}, u32[]{:S(2)}, u32[]{:S(2)}) collective-permute-start(bf16[112,1024]{1,0:T(8,128)(2,1)S(1)} %get-tuple-element.67.after_ref), channel_id=1, source_target_pairs={{0,1},{2,3},{1,0},{3,2},{4,5},{6,7},{5,4},{7,6},{8,9},{10,11},{9,8... | collective-permute-start | bytes 688136 | tf_op jit(solution)/shard_map/ppermute | solution.py:393
  41.7 7.7 %collective-permute-start.15 = (bf16[112,1024]{1,0:T(8,128)(2,1)S(1)}, bf16[112,1024]{1,0:T(8,128)(2,1)S(1)}, u32[]{:S(2)}, u32[]{:S(2)}) collective-permute-start(bf16[112,1024]{1,0:T(8,128)(2,1)S(1)} %get-tuple-element.71), channel_id=1, source_target_pairs={{1,2},{2,1},{5,6},{6,5},{9,10},{10,9},{13,14},{14,13},{17,18},{18,... | collective-permute-start | bytes 688136 | tf_op jit(solution)/shard_map/ppermute | solution.py:393
  45.1 10.7 %collective-permute-start.12 = (bf16[144,1024]{1,0:T(8,128)(2,1)S(1)}, bf16[144,1024]{1,0:T(8,128)(2,1)S(1)}, u32[]{:S(2)}, u32[]{:S(2)}) collective-permute-start(bf16[144,1024]{1,0:T(8,128)(2,1)S(1)} %get-tuple-element.68.after_ref), channel_id=1, source_target_pairs={{0,1},{2,3},{1,0},{3,2},{4,5},{6,7},{5,4},{7,6},{8,9},{10,11},{9,8... | collective-permute-start | bytes 884744 | tf_op jit(solution)/shard_map/ppermute | solution.py:393
  46.6 9.1 %collective-permute-start.13 = (bf16[144,1024]{1,0:T(8,128)(2,1)S(1)}, bf16[144,1024]{1,0:T(8,128)(2,1)S(1)}, u32[]{:S(2)}, u32[]{:S(2)}) collective-permute-start(bf16[144,1024]{1,0:T(8,128)(2,1)S(1)} %get-tuple-element.69), channel_id=1, source_target_pairs={{1,2},{2,1},{5,6},{6,5},{9,10},{10,9},{13,14},{14,13},{17,18},{18,... | collective-permute-start | bytes 884744 | tf_op jit(solution)/shard_map/ppermute | solution.py:393
  49.4 12.0 %copy-start.6 = (bf16[144,1024]{1,0:T(8,128)(2,1)S(1)}, bf16[144,1024]{1,0:T(8,128)(2,1)}, u32[]{:S(2)}) copy-start(bf16[144,1024]{1,0:T(8,128)(2,1)} %get-tuple-element.45.refs_1_) | copy-start | bytes 884740
  49.5 15.2 %collective-permute-start.21 = (bf16[112,1024]{1,0:T(8,128)(2,1)S(1)}, bf16[112,1024]{1,0:T(8,128)(2,1)S(1)}, u32[]{:S(2)}, u32[]{:S(2)}) collective-permute-start(bf16[112,1024]{1,0:T(8,128)(2,1)S(1)} %summed_grad.2.after_ref.own_ref), channel_id=1, source_target_pairs={{0,8},{4,12},{8,0},{12,4},{1,9},{5,13},{9,1},{13,5},{2,10},{6,14},... | collective-permute-start | bytes 688136 | tf_op jit(solution)/shard_map/ppermute | solution.py:412
  55.9 12.6 %copy-start = (f32[1,256,1024]{2,1,0:T(8,128)S(1)}, f32[1,256,1024]{2,1,0:T(8,128)}, u32[]{:S(2)}) copy-start(f32[1,256,1024]{2,1,0:T(8,128)} %param.11) | copy-start | bytes 3145732
  55.9 12.6 %copy-start.1 = (f32[1,256,1024]{2,1,0:T(8,128)S(1)}, f32[1,256,1024]{2,1,0:T(8,128)}, u32[]{:S(2)}) copy-start(f32[1,256,1024]{2,1,0:T(8,128)} %param.12) | copy-start | bytes 3145732
  55.9 12.6 %copy-start.2 = (f32[1,256,1024]{2,1,0:T(8,128)S(1)}, f32[1,256,1024]{2,1,0:T(8,128)}, u32[]{:S(2)}) copy-start(f32[1,256,1024]{2,1,0:T(8,128)} %param.13) | copy-start | bytes 3145732
  55.9 15.6 %collective-permute-start.19 = (bf16[144,1024]{1,0:T(8,128)(2,1)S(1)}, bf16[144,1024]{1,0:T(8,128)(2,1)S(1)}, u32[]{:S(2)}, u32[]{:S(2)}) collective-permute-start(bf16[144,1024]{1,0:T(8,128)(2,1)S(1)} %summed_grad.3.after_ref.own_ref), channel_id=1, source_target_pairs={{0,8},{4,12},{8,0},{12,4},{1,9},{5,13},{9,1},{13,5},{2,10},{6,14},... | collective-permute-start | bytes 884744 | tf_op jit(solution)/shard_map/ppermute | solution.py:412
  58.1 11.3 %collective-permute-start.20 = (bf16[112,1024]{1,0:T(8,128)(2,1)S(1)}, bf16[112,1024]{1,0:T(8,128)(2,1)S(1)}, u32[]{:S(2)}, u32[]{:S(2)}) collective-permute-start(bf16[112,1024]{1,0:T(8,128)(2,1)S(1)} %summed_grad.2.after_ref.own_ref), channel_id=1, source_target_pairs={{0,4},{4,0},{8,12},{12,8},{1,5},{5,1},{9,13},{13,9},{2,6},{6,2},{1... | collective-permute-start | bytes 688136 | tf_op jit(solution)/shard_map/ppermute | solution.py:411
  64.7 4.9 %collective-permute-start.22 = (bf16[112,1024]{1,0:T(8,128)(2,1)S(1)}, bf16[112,1024]{1,0:T(8,128)(2,1)S(1)}, u32[]{:S(2)}, u32[]{:S(2)}) collective-permute-start(bf16[112,1024]{1,0:T(8,128)(2,1)S(1)} %gate.2.across_ref), channel_id=1, source_target_pairs={{0,4},{4,0},{8,12},{12,8},{1,5},{5,1},{9,13},{13,9},{2,6},{6,2},{1... | collective-permute-start | bytes 688136 | tf_op jit(solution)/shard_map/ppermute | solution.py:413
  68.5 4.7 %collective-permute-start.18 = (bf16[144,1024]{1,0:T(8,128)(2,1)S(1)}, bf16[144,1024]{1,0:T(8,128)(2,1)S(1)}, u32[]{:S(2)}, u32[]{:S(2)}) collective-permute-start(bf16[144,1024]{1,0:T(8,128)(2,1)S(1)} %summed_grad.3.after_ref.own_ref), channel_id=1, source_target_pairs={{0,4},{4,0},{8,12},{12,8},{1,5},{5,1},{9,13},{13,9},{2,6},{6,2},{1... | collective-permute-start | bytes 884744 | tf_op jit(solution)/shard_map/ppermute | solution.py:411
  71.5 2.8 %collective-permute-start.23 = (bf16[144,1024]{1,0:T(8,128)(2,1)S(1)}, bf16[144,1024]{1,0:T(8,128)(2,1)S(1)}, u32[]{:S(2)}, u32[]{:S(2)}) collective-permute-start(bf16[144,1024]{1,0:T(8,128)(2,1)S(1)} %gate.3.across_ref), channel_id=1, source_target_pairs={{0,4},{4,0},{8,12},{12,8},{1,5},{5,1},{9,13},{13,9},{2,6},{6,2},{1... | collective-permute-start | bytes 884744 | tf_op jit(solution)/shard_map/ppermute | solution.py:413
  (4 other events, 23.7 us)

commit v9 on v8

--- a/solution.py
+++ b/solution.py
@@ -13,7 +13,7 @@
 epsilon = 1e-08
 
 MIB = 1 << 20
-SUM_FLOPS = 3 * 2 ** 29
+SUM_FLOPS = 2 ** 30
 SMEM = pl.BlockSpec(memory_space=pltpu.SMEM)
 VMEM = pl.BlockSpec(memory_space=pltpu.VMEM)
 HBM = pl.BlockSpec(memory_space=pltpu.HBM)
@@ -205,18 +205,34 @@
     )
 
 
-def grad_kernel(own_ref, one_ref, other_ref, after_ref, out_ref):
+def grad_kernel(cuts, own_ref, one_ref, other_ref, after_ref, *refs):
     def body(at):
         arrived = one_ref[at, :].astype(jnp.float32) + other_ref[at, :].astype(jnp.float32)
-        out_ref[at, :] = (own_ref[at, :] + arrived).astype(out_ref.dtype)
-
-    by_rows(out_ref, body)
-
-
-def summed_grad(own, one, other, after):
-    return call(grad_kernel, "summed_grad", half_array(*one.shape), [VMEM] * 3 + [ANY], VMEM)(
-        own, one, other, after
-    )
+        return (own_ref[at, :] + arrived).astype(jnp.bfloat16)
+
+    first = 0
+    carried = refs[0] if len(refs) > len(cuts) else None
+    for out_ref, size in zip(refs[len(refs) - len(cuts):], cuts):
+        top = 0
+        if carried is not None:
+            top = carried.shape[0]
+            out_ref[0:top, :] = carried[...]
+
+        @pl.loop(0, (size - top) // 16)
+        def _(i):
+            out_ref[pl.ds(pl.multiple_of(top + i * 16, 16), 16), :] = body(
+                pl.ds(pl.multiple_of(first + i * 16, 16), 16)
+            )
+
+        first, carried = first + size - top, None
+
+
+def summed_grad(own, one, other, after, cuts, carried=()):
+    depth = one.shape[1]
+    return call(
+        functools.partial(grad_kernel, cuts), "summed_grad", [half_array(size, depth) for size in cuts],
+        [VMEM] * 3 + [ANY] + [VMEM] * len(carried), [VMEM] * len(cuts),
+    )(own, one, other, after, *carried)
 
 
 def columns_kernel(n, scale, parts, where_ref, cotangent_ref, after_ref, *refs):
@@ -360,8 +376,10 @@
     cotangent = out_grad[0]
     scale = context_rows.shape[1] ** (-0.5)
     rows, depth = weight.shape[1:]
-    smaller = rows * 112 // 256 // 16 * 16
-    parts = [(0, smaller), (smaller, rows - smaller)] if smaller else [(0, rows)]
+    chains = 2 if rows % 32 == 0 else 1
+    parts = [(c * rows // chains, rows // chains) for c in range(chains)]
+    lower = rows * 112 // 256 // 16 * 16
+    steps_of = [(0, lower), (lower, rows - lower)] if chains == 2 and lower else [(0, rows)]
     where = jnp.stack([lax.axis_index("shard"), lax.axis_index("member")]).astype(jnp.int32)
 
     swap_across = [(m, m ^ 2) for m in range(members)]
@@ -387,27 +405,29 @@
             if slot > 1:
                 blocks = to_send([(blocks[swap], terms[2 * (slot - 2) + swap][c]) for swap in range(2)], sent)
                 sent = blocks[0]
-            if slot == 2 and c == 0:
-                early = sent
             for swap in range(2):
                 now[swap].append(lax.ppermute(blocks[swap], "shard", swaps[swap]))
         arrived.append(now)
 
     mate = lax.ppermute(state, "member", swap_mates)
-    across = lax.ppermute(pick(choices, state, mate, early), "member", swap_across)
-    states = taken_state(parts, where, donor, (weight[0], first[0], second[0]), (mate, across), sent)
-
-    grads = []
-    for c in range(len(parts)):
-        sent = summed_grad(terms[-1][c], arrived[n][0][c], arrived[n][1][c], sent)
-        grads.append(sent)
+    across = lax.ppermute(pick(choices, state, mate, own[0]), "member", swap_across)
+    states = taken_state(steps_of, where, donor, (weight[0], first[0], second[0]), (mate, across), sent)
+
+    grads, carried = [], ()
+    for c, (_, size) in enumerate(parts):
+        last = c == len(parts) - 1
+        cuts = [steps_of[c][1]] if last else [steps_of[c][1], size - steps_of[c][1]]
+        cuts = [cut for cut in cuts if cut]
+        sums = summed_grad(terms[-1][c], arrived[n][0][c], arrived[n][1][c], sent, cuts, carried)
+        grads.append(sums[0])
+        sent, carried = sums[0], tuple(sums[1:])
     blocks = list(own)
     for slot in range(1, n):
         blocks += arrived[slot][0] + arrived[slot][1]
     context_grad, computed = columns(n, scale, parts, where, cotangent, sent, blocks)
 
     updated = ()
-    for c, (start, size) in enumerate(parts):
+    for c, (start, size) in enumerate(steps_of):
         mate = lax.ppermute(grads[c], "member", swap_mates)
         across = gate(lax.ppermute(grads[c], "member", swap_across), computed)
         far = lax.ppermute(across, "member", swap_mates)

time: 77.5 us -> 72.9 us (0.941)
  starting transfers between devices: 39.2 us -> 32.2 us
  waiting for transfers between devices: 14.3 us -> 19.3 us
  Pallas kernels: 20.8 us -> 17 us
  local copies, waits for them, and re-layouts: 1.28 us -> 2.49 us
    ppermute x16, waiting for transfers between devices: 12.9 us -> 18 us  [on_device(): now[swap].append(lax.ppermute(blocks[swap], 'shard', swaps[swap]))]
    ppermute x2, starting transfers between devices: 5.37 us -> 2.22 us  [on_device(): far = lax.ppermute(across, 'member', swap_mates)]
    ppermute x2, starting transfers between devices: 4.46 us -> 1.58 us  [on_device(): across = gate(lax.ppermute(grads[c], 'member', swap_across), computed)]
    pallas_call x1, Pallas kernels: 5.5 us -> 3.21 us  [partial_blocks(): call(functools.partial(partial_kernel, n, scale, parts, order), 'partial_...]
    unnamed x24 -> x26, local copies, waits for them, and re-layouts: 1.28 us -> 2.49 us
    pallas_call x6, Pallas kernels: 1.99 us -> 0.94 us  [to_send(): call(send_kernel, 'to_send', [like] * 2, [VMEM] * 4 + [ANY], [VMEM] * 2,...]
  transfers between devices with their start and end apart: 24 -> 24, of which waited for: 9 -> 8; matrix products, arithmetic and copies ran while one was open for 0% -> 0% of each run, Pallas kernels for 20% -> 16%
where the time goes in v9:
time: 72.9 us; the launch traced here: 72.2 us
  starting transfers between devices  32.2 us (44%)
  waiting for transfers between devices  19.3 us (26%)
  Pallas kernels  17 us (23%)
  local copies, waits for them, and re-layouts  2.49 us (3%)
  between operations  1.01 us (1%)
    ppermute x16, starting transfers between devices, on_device(): now[swap].append(lax.ppermute(blocks[swap], 'shard', swaps[swap]))  24.4 us
    ppermute x16, waiting for transfers between devices, on_device(): now[swap].append(lax.ppermute(blocks[swap], 'shard', swaps[swap]))  18 us
    pallas_call x2, Pallas kernels, adam_update(): call(functools.partial(adam_kernel, start, size, bool(filled)), 'adam', [...  4.29 us
    pallas_call x1, Pallas kernels, halves(): call(functools.partial(halves_kernel, parts), 'halves', [half_array(size,...  3.26 us
    pallas_call x1, Pallas kernels, partial_blocks(): call(functools.partial(partial_kernel, n, scale, parts, order), 'partial_...  3.21 us
    pallas_call x1, Pallas kernels, columns(): call(functools.partial(columns_kernel, n, scale, parts), 'context_grad',...  2.86 us
    ppermute x2, starting transfers between devices, on_device(): mate = lax.ppermute(grads[c], 'member', swap_mates)  2.61 us
    unnamed x26, local copies, waits for them, and re-layouts  2.49 us
  transfers between devices with their start and end apart: 24, of which 8 were waited for; matrix products, arithmetic and copies ran while one was open for 0% of the time, Pallas kernels for 16%

profile of v9, /device:TPU:1, one launch (start us, length us, event | category | flops | bytes accessed | tf_op | source)
XLA Modules:
  0.0 72.2 jit_solution(9049616934813339213)
XLA Ops:
  0.7 3.3 %halves.1 = (bf16[768,1024]{1,0:T(8,128)(2,1)}, bf16[128,1024]{1,0:T(8,128)(2,1)}, bf16[128,1024]{1,0:T(8,128)(2,1)}) custom-call(f32[256,1024]{1,0:T(8,128)} %bitcast.11, f32[256,1024]{1,0:T(8,128)} %bitcast.13, f32[256,1024]{1,0:T(8,128)} %bitcast.15), custom_call_target="tpu_custom_call" | custom-call | bytes 1024 | tf_op jit(solution)/shard_map/halves/pallas_call | solution.py:98
  4.7 5.3 %collective-permute-start.3 = (bf16[128,1024]{1,0:T(8,128)(2,1)}, bf16[128,1024]{1,0:T(8,128)(2,1)S(1)}, u32[]{:S(2)}, u32[]{:S(2)}) collective-permute-start(bf16[128,1024]{1,0:T(8,128)(2,1)} %get-tuple-element.50.after_ref.refs_0_), channel_id=1, source_target_pairs={{0,1},{2,3},{1,0},{3,2},{4,5},{6,7},{5,4},{7,6},{8,9},{10,11},{9,8... | collective-permute-start | bytes 786440 | tf_op jit(solution)/shard_map/ppermute | solution.py:409
  10.8 1.5 %collective-permute-start.1 = (bf16[128,1024]{1,0:T(8,128)(2,1)}, bf16[128,1024]{1,0:T(8,128)(2,1)S(1)}, u32[]{:S(2)}, u32[]{:S(2)}) collective-permute-start(bf16[128,1024]{1,0:T(8,128)(2,1)} %get-tuple-element.47.refs_1_), channel_id=1, source_target_pairs={{0,1},{2,3},{1,0},{3,2},{4,5},{6,7},{5,4},{7,6},{8,9},{10,11},{9,8... | collective-permute-start | bytes 786440 | tf_op jit(solution)/shard_map/ppermute | solution.py:409
  13.0 1.5 %copy-done.4 = bf16[768,1024]{1,0:T(8,128)(2,1)S(1)} copy-done((bf16[768,1024]{1,0:T(8,128)(2,1)S(1)}, bf16[768,1024]{1,0:T(8,128)(2,1)}, u32[]{:S(2)}) %copy-start.4) | copy-done | bytes 1572888
  14.5 0.9 %copy-done.6 = bf16[128,1024]{1,0:T(8,128)(2,1)S(1)} copy-done((bf16[128,1024]{1,0:T(8,128)(2,1)S(1)}, bf16[128,1024]{1,0:T(8,128)(2,1)}, u32[]{:S(2)}) %copy-start.6) | copy-done | bytes 262168
  15.4 0.7 pick.1
  16.1 1.3 %collective-permute-start.17 = (bf16[768,1024]{1,0:T(8,128)(2,1)S(1)}, bf16[768,1024]{1,0:T(8,128)(2,1)S(1)}, u32[]{:S(2)}, u32[]{:S(2)}) collective-permute-start(bf16[768,1024]{1,0:T(8,128)(2,1)S(1)} %pick.1), channel_id=1, source_target_pairs={{0,8},{4,12},{8,0},{12,4},{1,9},{5,13},{9,1},{13,5},{2,10},{6,14},... | collective-permute-start | bytes 4718600 | tf_op jit(solution)/shard_map/ppermute | solution.py:413
  17.4 3.2 %partial_blocks.1 = (bf16[128,1024]{1,0:T(8,128)(2,1)S(1)}, bf16[128,1024]{1,0:T(8,128)(2,1)S(1)}, bf16[128,1024]{1,0:T(8,128)(2,1)S(1)}, bf16[128,1024]{1,0:T(8...) custom-call(s32[2]{0:T(128)S(1)} %pad_add_fusion.where_ref, ...), custom_call_target="tpu_custom_call" | custom-call | bytes 1024 | tf_op jit(solution)/shard_map/partial_blocks/pallas_call | solution.py:174
  20.8 0.7 collective-permute-start.6
  21.5 2.6 %collective-permute-start.7 = (bf16[128,1024]{1,0:T(8,128)(2,1)S(1)}, bf16[128,1024]{1,0:T(8,128)(2,1)S(1)}, u32[]{:S(2)}, u32[]{:S(2)}) collective-permute-start(bf16[128,1024]{1,0:T(8,128)(2,1)S(1)} %get-tuple-element.53.after_ref), channel_id=1, source_target_pairs={{0,1},{2,3},{1,0},{3,2},{4,5},{6,7},{5,4},{7,6},{8,9},{10,11},{9,8... | collective-permute-start | bytes 786440 | tf_op jit(solution)/shard_map/ppermute | solution.py:409
  24.3 0.7 collective-permute-start.4
  25.0 1.5 %collective-permute-start.5 = (bf16[128,1024]{1,0:T(8,128)(2,1)S(1)}, bf16[128,1024]{1,0:T(8,128)(2,1)S(1)}, u32[]{:S(2)}, u32[]{:S(2)}) collective-permute-start(bf16[128,1024]{1,0:T(8,128)(2,1)S(1)} %get-tuple-element.56.after_ref), channel_id=1, source_target_pairs={{0,1},{2,3},{1,0},{3,2},{4,5},{6,7},{5,4},{7,6},{8,9},{10,11},{9,8... | collective-permute-start | bytes 786440 | tf_op jit(solution)/shard_map/ppermute | solution.py:409
  26.5 3.1 %collective-permute-done.7.arrived_too_ref.refs_6_ = bf16[128,1024]{1,0:T(8,128)(2,1)S(1)} collective-permute-done((bf16[128,1024]{1,0:T(8,128)(2,1)S(1)}, bf16[128,1024]{1,0:T(8,128)(2,1)S(1)}, u32[]{:S(2)}, u32[]{:S(2)}) %collective-permute-start.7) | collective-permute-done | bytes 262176 | tf_op jit(solution)/shard_map/ppermute | solution.py:409
  30.4 2.7 %collective-permute-start.11 = (bf16[128,1024]{1,0:T(8,128)(2,1)S(1)}, bf16[128,1024]{1,0:T(8,128)(2,1)S(1)}, u32[]{:S(2)}, u32[]{:S(2)}) collective-permute-start(bf16[128,1024]{1,0:T(8,128)(2,1)S(1)} %get-tuple-element.61.after_ref), channel_id=1, source_target_pairs={{0,1},{2,3},{1,0},{3,2},{4,5},{6,7},{5,4},{7,6},{8,9},{10,11},{9,8... | collective-permute-start | bytes 786440 | tf_op jit(solution)/shard_map/ppermute | solution.py:409
  33.1 2.1 %collective-permute-done.5.arrived_too_ref.refs_7_ = bf16[128,1024]{1,0:T(8,128)(2,1)S(1)} collective-permute-done((bf16[128,1024]{1,0:T(8,128)(2,1)S(1)}, bf16[128,1024]{1,0:T(8,128)(2,1)S(1)}, u32[]{:S(2)}, u32[]{:S(2)}) %collective-permute-start.5) | collective-permute-done | bytes 262176 | tf_op jit(solution)/shard_map/ppermute | solution.py:409
  36.1 2.7 %collective-permute-start.9 = (bf16[128,1024]{1,0:T(8,128)(2,1)S(1)}, bf16[128,1024]{1,0:T(8,128)(2,1)S(1)}, u32[]{:S(2)}, u32[]{:S(2)}) collective-permute-start(bf16[128,1024]{1,0:T(8,128)(2,1)S(1)} %get-tuple-element.64.after_ref), channel_id=1, source_target_pairs={{0,1},{2,3},{1,0},{3,2},{4,5},{6,7},{5,4},{7,6},{8,9},{10,11},{9,8... | collective-permute-start | bytes 786440 | tf_op jit(solution)/shard_map/ppermute | solution.py:409
  38.7 1.2 %collective-permute-done.11.arrived_too_ref.refs_10_ = bf16[128,1024]{1,0:T(8,128)(2,1)S(1)} collective-permute-done((bf16[128,1024]{1,0:T(8,128)(2,1)S(1)}, bf16[128,1024]{1,0:T(8,128)(2,1)S(1)}, u32[]{:S(2)}, u32[]{:S(2)}) %collective-permute-start.11) | collective-permute-done | bytes 262176 | tf_op jit(solution)/shard_map/ppermute | solution.py:409
  40.1 1.2 %collective-permute-start.14 = (bf16[128,1024]{1,0:T(8,128)(2,1)S(1)}, bf16[128,1024]{1,0:T(8,128)(2,1)S(1)}, u32[]{:S(2)}, u32[]{:S(2)}) collective-permute-start(bf16[128,1024]{1,0:T(8,128)(2,1)S(1)} %get-tuple-element.69.after_ref), channel_id=1, source_target_pairs={{0,1},{2,3},{1,0},{3,2},{4,5},{6,7},{5,4},{7,6},{8,9},{10,11},{9,8... | collective-permute-start | bytes 786440 | tf_op jit(solution)/shard_map/ppermute | solution.py:409
  42.0 3.6 %collective-permute-done.9.arrived_too_ref.refs_11_ = bf16[128,1024]{1,0:T(8,128)(2,1)S(1)} collective-permute-done((bf16[128,1024]{1,0:T(8,128)(2,1)S(1)}, bf16[128,1024]{1,0:T(8,128)(2,1)S(1)}, u32[]{:S(2)}, u32[]{:S(2)}) %collective-permute-start.9) | collective-permute-done | bytes 262176 | tf_op jit(solution)/shard_map/ppermute | solution.py:409
  45.8 1.5 %collective-permute-start.12 = (bf16[128,1024]{1,0:T(8,128)(2,1)S(1)}, bf16[128,1024]{1,0:T(8,128)(2,1)S(1)}, u32[]{:S(2)}, u32[]{:S(2)}) collective-permute-start(bf16[128,1024]{1,0:T(8,128)(2,1)S(1)} %get-tuple-element.70.after_ref), channel_id=1, source_target_pairs={{0,1},{2,3},{1,0},{3,2},{4,5},{6,7},{5,4},{7,6},{8,9},{10,11},{9,8... | collective-permute-start | bytes 786440 | tf_op jit(solution)/shard_map/ppermute | solution.py:409
  48.0 3.3 %collective-permute-done.14.one_ref = bf16[128,1024]{1,0:T(8,128)(2,1)S(1)} collective-permute-done((bf16[128,1024]{1,0:T(8,128)(2,1)S(1)}, bf16[128,1024]{1,0:T(8,128)(2,1)S(1)}, u32[]{:S(2)}, u32[]{:S(2)}) %collective-permute-start.14) | collective-permute-done | bytes 262176 | tf_op jit(solution)/shard_map/ppermute | solution.py:409
  51.4 0.8 %collective-permute-start.21 = (bf16[112,1024]{1,0:T(8,128)(2,1)S(1)}, bf16[112,1024]{1,0:T(8,128)(2,1)S(1)}, u32[]{:S(2)}, u32[]{:S(2)}) collective-permute-start(bf16[112,1024]{1,0:T(8,128)(2,1)S(1)} %get-tuple-element.74.after_ref.own_ref), channel_id=1, source_target_pairs={{0,8},{4,12},{8,0},{12,4},{1,9},{5,13},{9,1},{13,5},{2,10},{6,14},... | collective-permute-start | bytes 688136 | tf_op jit(solution)/shard_map/ppermute | solution.py:432
  52.2 4.7 %collective-permute-done.12.one_ref = bf16[128,1024]{1,0:T(8,128)(2,1)S(1)} collective-permute-done((bf16[128,1024]{1,0:T(8,128)(2,1)S(1)}, bf16[128,1024]{1,0:T(8,128)(2,1)S(1)}, u32[]{:S(2)}, u32[]{:S(2)}) %collective-permute-start.12) | collective-permute-done | bytes 262176 | tf_op jit(solution)/shard_map/ppermute | solution.py:409
  57.0 0.8 %collective-permute-start.19 = (bf16[144,1024]{1,0:T(8,128)(2,1)S(1)}, bf16[144,1024]{1,0:T(8,128)(2,1)S(1)}, u32[]{:S(2)}, u32[]{:S(2)}) collective-permute-start(bf16[144,1024]{1,0:T(8,128)(2,1)S(1)} %summed_grad.3.after_ref.own_ref), channel_id=1, source_target_pairs={{0,8},{4,12},{8,0},{12,4},{1,9},{5,13},{9,1},{13,5},{2,10},{6,14},... | collective-permute-start | bytes 884744 | tf_op jit(solution)/shard_map/ppermute | solution.py:432
  57.8 2.6 %collective-permute-start.20 = (bf16[112,1024]{1,0:T(8,128)(2,1)S(1)}, bf16[112,1024]{1,0:T(8,128)(2,1)S(1)}, u32[]{:S(2)}, u32[]{:S(2)}) collective-permute-start(bf16[112,1024]{1,0:T(8,128)(2,1)S(1)} %get-tuple-element.74.after_ref.own_ref), channel_id=1, source_target_pairs={{0,4},{4,0},{8,12},{12,8},{1,5},{5,1},{9,13},{13,9},{2,6},{6,2},{1... | collective-permute-start | bytes 688136 | tf_op jit(solution)/shard_map/ppermute | solution.py:431
  60.4 2.9 %context_grad.1 = (bf16[512,1024]{1,0:T(8,128)(2,1)}, f32[8,128]{1,0:T(8,128)S(1)}) custom-call(s32[2]{0:T(128)S(1)} %pad_add_fusion.where_ref, bf16[512,1024]{1,0:T(8,128)(2,1)S(1)} %bitcast.18, bf16[144,1024]{1,0:T(8,128)(2,1)S(1)} %summed_grad.3.after_ref.own_ref, bf16[128,1024]{1,0:T(8,128)(2,1)S(1)} %copy-done.7, bf16[128,1024]{1,0:T(8,128)(2,1)S(1)} %copy-done.8, ...), custom_call_target="tpu_custom_call" | custom-call | bytes 1024 | tf_op jit(solution)/shard_map/context_grad/pallas_call | solution.py:271
  63.3 1.1 %collective-permute-start.22 = (bf16[112,1024]{1,0:T(8,128)(2,1)S(1)}, bf16[112,1024]{1,0:T(8,128)(2,1)S(1)}, u32[]{:S(2)}, u32[]{:S(2)}) collective-permute-start(bf16[112,1024]{1,0:T(8,128)(2,1)S(1)} %gate.2.across_ref), channel_id=1, source_target_pairs={{0,4},{4,0},{8,12},{12,8},{1,5},{5,1},{9,13},{13,9},{2,6},{6,2},{1... | collective-permute-start | bytes 688136 | tf_op jit(solution)/shard_map/ppermute | solution.py:433
  64.4 0.9 %taken_state.1 = (f32[336,1024]{1,0:T(8,128)S(1)}, f32[432,1024]{1,0:T(8,128)S(1)}) custom-call(s32[2]{0:T(128)S(1)} %pad_add_fusion.where_ref, s32[4]{0:T(128)S(1)} %copy-done.9, bf16[128,1024]{1,0:T(8,128)(2,1)S(1)} %get-tuple-element.70.after_ref, f32[256,1024]{1,0:T(8,128)S(1)} %bitcast.12, f32[256,1024]{1,0:T(8,128)S(1)} %bitcast.14, ...), custom_call_target="tpu_custom_call" | custom-call | bytes 1024 | tf_op jit(solution)/shard_map/taken_state/pallas_call | solution.py:320
  65.5 1.9 %adam.2 = (f32[256,1024]{1,0:T(8,128)}, f32[256,1024]{1,0:T(8,128)}, f32[256,1024]{1,0:T(8,128)}, f32[8,128]{1,0:T(8,128)S(1)}) custom-call(f32[8,1024]{1,0:T(8,128)S(1)} %choices.1.choices_ref, f32[336,1024]{1,0:T(8,128)S(1)} %get-tuple-element.79.state_ref, bf16[112,1024]{1,0:T(8,128)(2,1)S(1)} %get-tuple-element.74.after_ref.own_ref, ...), custom_call_target="tpu_custom_call" | custom-call | bytes 1024 | tf_op jit(solution)/shard_map/adam/pallas_call | solution.py:365
  67.4 1.2 %collective-permute-start.23 = (bf16[144,1024]{1,0:T(8,128)(2,1)S(1)}, bf16[144,1024]{1,0:T(8,128)(2,1)S(1)}, u32[]{:S(2)}, u32[]{:S(2)}) collective-permute-start(bf16[144,1024]{1,0:T(8,128)(2,1)S(1)} %gate.3.across_ref), channel_id=1, source_target_pairs={{0,4},{4,0},{8,12},{12,8},{1,5},{5,1},{9,13},{13,9},{2,6},{6,2},{1... | collective-permute-start | bytes 884744 | tf_op jit(solution)/shard_map/ppermute | solution.py:433
  68.6 1.2 %collective-permute-done.23.far_ref = bf16[144,1024]{1,0:T(8,128)(2,1)S(1)} collective-permute-done((bf16[144,1024]{1,0:T(8,128)(2,1)S(1)}, bf16[144,1024]{1,0:T(8,128)(2,1)S(1)}, u32[]{:S(2)}, u32[]{:S(2)}) %collective-permute-start.23) | collective-permute-done | bytes 294944 | tf_op jit(solution)/shard_map/ppermute | solution.py:433
  69.8 2.4 %adam.3 = (f32[256,1024]{1,0:T(8,128)}, f32[256,1024]{1,0:T(8,128)}, f32[256,1024]{1,0:T(8,128)}, f32[8,128]{1,0:T(8,128)}) custom-call(f32[8,1024]{1,0:T(8,128)S(1)} %choices.1.choices_ref, f32[432,1024]{1,0:T(8,128)S(1)} %get-tuple-element.78.state_ref, ...), custom_call_target="tpu_custom_call", output_to_operand_aliasing={{0}: (7, {}), {1}: (8, {}), {2}: (9, {})} | custom-call | bytes 1024 | tf_op jit(solution)/shard_map/adam/pallas_call | solution.py:365
  (61 shorter events, 6.2 us)
Async XLA Ops:
  0.6 11.7 %copy-start.9 = (s32[4]{0:T(128)S(1)}, s32[4]{0:T(128)}, u32[]{:S(2)}) copy-start(s32[4]{0:T(128)} %donor_ref.3) | copy-start | bytes 52
  0.6 11.7 %copy-start.10 = (f32[4]{0:T(128)S(1)}, f32[4]{0:T(128)}, u32[]{:S(2)}) copy-start(f32[4]{0:T(128)} %rates_ref.1) | copy-start | bytes 52
  0.7 11.7 %copy-start.11 = (f32[4]{0:T(128)S(1)}, f32[4]{0:T(128)}, u32[]{:S(2)}) copy-start(f32[4]{0:T(128)} %decays_ref.1) | copy-start | bytes 52
  0.7 11.7 %copy-start.12 = (s32[4]{0:T(128)S(1)}, s32[4]{0:T(128)}, u32[]{:S(2)}) copy-start(s32[4]{0:T(128)} %steps_ref.1) | copy-start | bytes 52
  3.9 9.0 %collective-permute-start.16 = (bf16[768,1024]{1,0:T(8,128)(2,1)}, bf16[768,1024]{1,0:T(8,128)(2,1)S(1)}, u32[]{:S(2)}, u32[]{:S(2)}) collective-permute-start(bf16[768,1024]{1,0:T(8,128)(2,1)} %get-tuple-element.77.own_ref), channel_id=1, source_target_pairs={{0,4},{4,0},{8,12},{12,8},{1,5},{5,1},{9,13},{13,9},{2,6},{6,2},{1... | collective-permute-start | bytes 4718600 | tf_op jit(solution)/shard_map/ppermute | solution.py:412
  4.1 16.5 %collective-permute-start.2 = (bf16[128,1024]{1,0:T(8,128)(2,1)}, bf16[128,1024]{1,0:T(8,128)(2,1)S(1)}, u32[]{:S(2)}, u32[]{:S(2)}) collective-permute-start(bf16[128,1024]{1,0:T(8,128)(2,1)} %get-tuple-element.50.after_ref.refs_0_), channel_id=1, source_target_pairs={{1,2},{2,1},{5,6},{6,5},{9,10},{10,9},{13,14},{14,13},{17,18},{18,... | collective-permute-start | bytes 786440 | tf_op jit(solution)/shard_map/ppermute | solution.py:409
  4.7 15.9 %collective-permute-start.3 = (bf16[128,1024]{1,0:T(8,128)(2,1)}, bf16[128,1024]{1,0:T(8,128)(2,1)S(1)}, u32[]{:S(2)}, u32[]{:S(2)}) collective-permute-start(bf16[128,1024]{1,0:T(8,128)(2,1)} %get-tuple-element.50.after_ref.refs_0_), channel_id=1, source_target_pairs={{0,1},{2,3},{1,0},{3,2},{4,5},{6,7},{5,4},{7,6},{8,9},{10,11},{9,8... | collective-permute-start | bytes 786440 | tf_op jit(solution)/shard_map/ppermute | solution.py:409
  10.1 14.0 %collective-permute-start = (bf16[128,1024]{1,0:T(8,128)(2,1)}, bf16[128,1024]{1,0:T(8,128)(2,1)S(1)}, u32[]{:S(2)}, u32[]{:S(2)}) collective-permute-start(bf16[128,1024]{1,0:T(8,128)(2,1)} %get-tuple-element.47.refs_1_), channel_id=1, source_target_pairs={{1,2},{2,1},{5,6},{6,5},{9,10},{10,9},{13,14},{14,13},{17,18},{18,... | collective-permute-start | bytes 786440 | tf_op jit(solution)/shard_map/ppermute | solution.py:409
  10.8 13.4 %collective-permute-start.1 = (bf16[128,1024]{1,0:T(8,128)(2,1)}, bf16[128,1024]{1,0:T(8,128)(2,1)S(1)}, u32[]{:S(2)}, u32[]{:S(2)}) collective-permute-start(bf16[128,1024]{1,0:T(8,128)(2,1)} %get-tuple-element.47.refs_1_), channel_id=1, source_target_pairs={{0,1},{2,3},{1,0},{3,2},{4,5},{6,7},{5,4},{7,6},{8,9},{10,11},{9,8... | collective-permute-start | bytes 786440 | tf_op jit(solution)/shard_map/ppermute | solution.py:409
  16.1 48.3 %collective-permute-start.17 = (bf16[768,1024]{1,0:T(8,128)(2,1)S(1)}, bf16[768,1024]{1,0:T(8,128)(2,1)S(1)}, u32[]{:S(2)}, u32[]{:S(2)}) collective-permute-start(bf16[768,1024]{1,0:T(8,128)(2,1)S(1)} %pick.1), channel_id=1, source_target_pairs={{0,8},{4,12},{8,0},{12,4},{1,9},{5,13},{9,1},{13,5},{2,10},{6,14},... | collective-permute-start | bytes 4718600 | tf_op jit(solution)/shard_map/ppermute | solution.py:413
  20.8 5.7 %collective-permute-start.6 = (bf16[128,1024]{1,0:T(8,128)(2,1)S(1)}, bf16[128,1024]{1,0:T(8,128)(2,1)S(1)}, u32[]{:S(2)}, u32[]{:S(2)}) collective-permute-start(bf16[128,1024]{1,0:T(8,128)(2,1)S(1)} %get-tuple-element.58), channel_id=1, source_target_pairs={{1,2},{2,1},{5,6},{6,5},{9,10},{10,9},{13,14},{14,13},{17,18},{18,... | collective-permute-start | bytes 786440 | tf_op jit(solution)/shard_map/ppermute | solution.py:409
  21.5 8.1 %collective-permute-start.7 = (bf16[128,1024]{1,0:T(8,128)(2,1)S(1)}, bf16[128,1024]{1,0:T(8,128)(2,1)S(1)}, u32[]{:S(2)}, u32[]{:S(2)}) collective-permute-start(bf16[128,1024]{1,0:T(8,128)(2,1)S(1)} %get-tuple-element.53.after_ref), channel_id=1, source_target_pairs={{0,1},{2,3},{1,0},{3,2},{4,5},{6,7},{5,4},{7,6},{8,9},{10,11},{9,8... | collective-permute-start | bytes 786440 | tf_op jit(solution)/shard_map/ppermute | solution.py:409
  24.3 8.8 %collective-permute-start.4 = (bf16[128,1024]{1,0:T(8,128)(2,1)S(1)}, bf16[128,1024]{1,0:T(8,128)(2,1)S(1)}, u32[]{:S(2)}, u32[]{:S(2)}) collective-permute-start(bf16[128,1024]{1,0:T(8,128)(2,1)S(1)} %get-tuple-element.54), channel_id=1, source_target_pairs={{1,2},{2,1},{5,6},{6,5},{9,10},{10,9},{13,14},{14,13},{17,18},{18,... | collective-permute-start | bytes 786440 | tf_op jit(solution)/shard_map/ppermute | solution.py:409
  25.0 10.3 %collective-permute-start.5 = (bf16[128,1024]{1,0:T(8,128)(2,1)S(1)}, bf16[128,1024]{1,0:T(8,128)(2,1)S(1)}, u32[]{:S(2)}, u32[]{:S(2)}) collective-permute-start(bf16[128,1024]{1,0:T(8,128)(2,1)S(1)} %get-tuple-element.56.after_ref), channel_id=1, source_target_pairs={{0,1},{2,3},{1,0},{3,2},{4,5},{6,7},{5,4},{7,6},{8,9},{10,11},{9,8... | collective-permute-start | bytes 786440 | tf_op jit(solution)/shard_map/ppermute | solution.py:409
  29.8 9.0 %collective-permute-start.10 = (bf16[128,1024]{1,0:T(8,128)(2,1)S(1)}, bf16[128,1024]{1,0:T(8,128)(2,1)S(1)}, u32[]{:S(2)}, u32[]{:S(2)}) collective-permute-start(bf16[128,1024]{1,0:T(8,128)(2,1)S(1)} %get-tuple-element.66), channel_id=1, source_target_pairs={{1,2},{2,1},{5,6},{6,5},{9,10},{10,9},{13,14},{14,13},{17,18},{18,... | collective-permute-start | bytes 786440 | tf_op jit(solution)/shard_map/ppermute | solution.py:409
  30.4 9.5 %collective-permute-start.11 = (bf16[128,1024]{1,0:T(8,128)(2,1)S(1)}, bf16[128,1024]{1,0:T(8,128)(2,1)S(1)}, u32[]{:S(2)}, u32[]{:S(2)}) collective-permute-start(bf16[128,1024]{1,0:T(8,128)(2,1)S(1)} %get-tuple-element.61.after_ref), channel_id=1, source_target_pairs={{0,1},{2,3},{1,0},{3,2},{4,5},{6,7},{5,4},{7,6},{8,9},{10,11},{9,8... | collective-permute-start | bytes 786440 | tf_op jit(solution)/shard_map/ppermute | solution.py:409
  35.4 6.6 %collective-permute-start.8 = (bf16[128,1024]{1,0:T(8,128)(2,1)S(1)}, bf16[128,1024]{1,0:T(8,128)(2,1)S(1)}, u32[]{:S(2)}, u32[]{:S(2)}) collective-permute-start(bf16[128,1024]{1,0:T(8,128)(2,1)S(1)} %get-tuple-element.62), channel_id=1, source_target_pairs={{1,2},{2,1},{5,6},{6,5},{9,10},{10,9},{13,14},{14,13},{17,18},{18,... | collective-permute-start | bytes 786440 | tf_op jit(solution)/shard_map/ppermute | solution.py:409
  36.1 9.6 %collective-permute-start.9 = (bf16[128,1024]{1,0:T(8,128)(2,1)S(1)}, bf16[128,1024]{1,0:T(8,128)(2,1)S(1)}, u32[]{:S(2)}, u32[]{:S(2)}) collective-permute-start(bf16[128,1024]{1,0:T(8,128)(2,1)S(1)} %get-tuple-element.64.after_ref), channel_id=1, source_target_pairs={{0,1},{2,3},{1,0},{3,2},{4,5},{6,7},{5,4},{7,6},{8,9},{10,11},{9,8... | collective-permute-start | bytes 786440 | tf_op jit(solution)/shard_map/ppermute | solution.py:409
  40.1 11.2 %collective-permute-start.14 = (bf16[128,1024]{1,0:T(8,128)(2,1)S(1)}, bf16[128,1024]{1,0:T(8,128)(2,1)S(1)}, u32[]{:S(2)}, u32[]{:S(2)}) collective-permute-start(bf16[128,1024]{1,0:T(8,128)(2,1)S(1)} %get-tuple-element.69.after_ref), channel_id=1, source_target_pairs={{0,1},{2,3},{1,0},{3,2},{4,5},{6,7},{5,4},{7,6},{8,9},{10,11},{9,8... | collective-permute-start | bytes 786440 | tf_op jit(solution)/shard_map/ppermute | solution.py:409
  41.3 9.9 %collective-permute-start.15 = (bf16[128,1024]{1,0:T(8,128)(2,1)S(1)}, bf16[128,1024]{1,0:T(8,128)(2,1)S(1)}, u32[]{:S(2)}, u32[]{:S(2)}) collective-permute-start(bf16[128,1024]{1,0:T(8,128)(2,1)S(1)} %get-tuple-element.73), channel_id=1, source_target_pairs={{1,2},{2,1},{5,6},{6,5},{9,10},{10,9},{13,14},{14,13},{17,18},{18,... | collective-permute-start | bytes 786440 | tf_op jit(solution)/shard_map/ppermute | solution.py:409
  45.8 14.6 %copy-start.8 = (bf16[128,1024]{1,0:T(8,128)(2,1)S(1)}, bf16[128,1024]{1,0:T(8,128)(2,1)}, u32[]{:S(2)}) copy-start(bf16[128,1024]{1,0:T(8,128)(2,1)} %get-tuple-element.47.refs_1_) | copy-start | bytes 786436
  45.8 11.1 %collective-permute-start.12 = (bf16[128,1024]{1,0:T(8,128)(2,1)S(1)}, bf16[128,1024]{1,0:T(8,128)(2,1)S(1)}, u32[]{:S(2)}, u32[]{:S(2)}) collective-permute-start(bf16[128,1024]{1,0:T(8,128)(2,1)S(1)} %get-tuple-element.70.after_ref), channel_id=1, source_target_pairs={{0,1},{2,3},{1,0},{3,2},{4,5},{6,7},{5,4},{7,6},{8,9},{10,11},{9,8... | collective-permute-start | bytes 786440 | tf_op jit(solution)/shard_map/ppermute | solution.py:409
  47.3 9.6 %collective-permute-start.13 = (bf16[128,1024]{1,0:T(8,128)(2,1)S(1)}, bf16[128,1024]{1,0:T(8,128)(2,1)S(1)}, u32[]{:S(2)}, u32[]{:S(2)}) collective-permute-start(bf16[128,1024]{1,0:T(8,128)(2,1)S(1)} %get-tuple-element.71), channel_id=1, source_target_pairs={{1,2},{2,1},{5,6},{6,5},{9,10},{10,9},{13,14},{14,13},{17,18},{18,... | collective-permute-start | bytes 786440 | tf_op jit(solution)/shard_map/ppermute | solution.py:409
  51.4 11.9 %collective-permute-start.21 = (bf16[112,1024]{1,0:T(8,128)(2,1)S(1)}, bf16[112,1024]{1,0:T(8,128)(2,1)S(1)}, u32[]{:S(2)}, u32[]{:S(2)}) collective-permute-start(bf16[112,1024]{1,0:T(8,128)(2,1)S(1)} %get-tuple-element.74.after_ref.own_ref), channel_id=1, source_target_pairs={{0,8},{4,12},{8,0},{12,4},{1,9},{5,13},{9,1},{13,5},{2,10},{6,14},... | collective-permute-start | bytes 688136 | tf_op jit(solution)/shard_map/ppermute | solution.py:432
  57.0 7.4 %copy-start = (f32[1,256,1024]{2,1,0:T(8,128)S(1)}, f32[1,256,1024]{2,1,0:T(8,128)}, u32[]{:S(2)}) copy-start(f32[1,256,1024]{2,1,0:T(8,128)} %param.11) | copy-start | bytes 3145732
  57.0 7.4 %copy-start.1 = (f32[1,256,1024]{2,1,0:T(8,128)S(1)}, f32[1,256,1024]{2,1,0:T(8,128)}, u32[]{:S(2)}) copy-start(f32[1,256,1024]{2,1,0:T(8,128)} %param.12) | copy-start | bytes 3145732
  57.0 7.4 %copy-start.2 = (f32[1,256,1024]{2,1,0:T(8,128)S(1)}, f32[1,256,1024]{2,1,0:T(8,128)}, u32[]{:S(2)}) copy-start(f32[1,256,1024]{2,1,0:T(8,128)} %param.13) | copy-start | bytes 3145732
  57.0 10.4 %collective-permute-start.19 = (bf16[144,1024]{1,0:T(8,128)(2,1)S(1)}, bf16[144,1024]{1,0:T(8,128)(2,1)S(1)}, u32[]{:S(2)}, u32[]{:S(2)}) collective-permute-start(bf16[144,1024]{1,0:T(8,128)(2,1)S(1)} %summed_grad.3.after_ref.own_ref), channel_id=1, source_target_pairs={{0,8},{4,12},{8,0},{12,4},{1,9},{5,13},{9,1},{13,5},{2,10},{6,14},... | collective-permute-start | bytes 884744 | tf_op jit(solution)/shard_map/ppermute | solution.py:432
  57.8 7.5 %collective-permute-start.20 = (bf16[112,1024]{1,0:T(8,128)(2,1)S(1)}, bf16[112,1024]{1,0:T(8,128)(2,1)S(1)}, u32[]{:S(2)}, u32[]{:S(2)}) collective-permute-start(bf16[112,1024]{1,0:T(8,128)(2,1)S(1)} %get-tuple-element.74.after_ref.own_ref), channel_id=1, source_target_pairs={{0,4},{4,0},{8,12},{12,8},{1,5},{5,1},{9,13},{13,9},{2,6},{6,2},{1... | collective-permute-start | bytes 688136 | tf_op jit(solution)/shard_map/ppermute | solution.py:431
  63.3 2.2 %collective-permute-start.22 = (bf16[112,1024]{1,0:T(8,128)(2,1)S(1)}, bf16[112,1024]{1,0:T(8,128)(2,1)S(1)}, u32[]{:S(2)}, u32[]{:S(2)}) collective-permute-start(bf16[112,1024]{1,0:T(8,128)(2,1)S(1)} %gate.2.across_ref), channel_id=1, source_target_pairs={{0,4},{4,0},{8,12},{12,8},{1,5},{5,1},{9,13},{13,9},{2,6},{6,2},{1... | collective-permute-start | bytes 688136 | tf_op jit(solution)/shard_map/ppermute | solution.py:433
  64.4 4.2 %collective-permute-start.18 = (bf16[144,1024]{1,0:T(8,128)(2,1)S(1)}, bf16[144,1024]{1,0:T(8,128)(2,1)S(1)}, u32[]{:S(2)}, u32[]{:S(2)}) collective-permute-start(bf16[144,1024]{1,0:T(8,128)(2,1)S(1)} %summed_grad.3.after_ref.own_ref), channel_id=1, source_target_pairs={{0,4},{4,0},{8,12},{12,8},{1,5},{5,1},{9,13},{13,9},{2,6},{6,2},{1... | collective-permute-start | bytes 884744 | tf_op jit(solution)/shard_map/ppermute | solution.py:431
  67.4 2.4 %collective-permute-start.23 = (bf16[144,1024]{1,0:T(8,128)(2,1)S(1)}, bf16[144,1024]{1,0:T(8,128)(2,1)S(1)}, u32[]{:S(2)}, u32[]{:S(2)}) collective-permute-start(bf16[144,1024]{1,0:T(8,128)(2,1)S(1)} %gate.3.across_ref), channel_id=1, source_target_pairs={{0,4},{4,0},{8,12},{12,8},{1,5},{5,1},{9,13},{13,9},{2,6},{6,2},{1... | collective-permute-start | bytes 884744 | tf_op jit(solution)/shard_map/ppermute | solution.py:433
  (5 other events, 13.4 us)

commit v10 on v9

--- a/solution.py
+++ b/solution.py
@@ -13,7 +13,7 @@
 epsilon = 1e-08
 
 MIB = 1 << 20
-SUM_FLOPS = 2 ** 30
+SUM_FLOPS = 5 * 2 ** 28
 SMEM = pl.BlockSpec(memory_space=pltpu.SMEM)
 VMEM = pl.BlockSpec(memory_space=pltpu.VMEM)
 HBM = pl.BlockSpec(memory_space=pltpu.HBM)
@@ -330,14 +330,15 @@
     outs, (token_ref, stepped, sems) = refs[:3], refs[3:]
     token_ref[...] = jnp.zeros_like(token_ref)
     depth = own_ref.shape[1]
-    pieces = 4 if size % 64 == 0 else 3 if size % 48 == 0 else 1
-    piece = size // pieces
     writes = []
-    for p in range(pieces):
+    piece = 32
+    for top in range(0, size, piece):
+        height = min(piece, size - top)
+
         def body(i):
-            at = pl.ds(pl.multiple_of(p * piece + i * 16, 16), 16)
+            at = pl.ds(pl.multiple_of(top + i * 16, 16), 16)
             row = lambda k: jnp.broadcast_to(choices_ref[k:k + 1, :], (16, depth))
-            load = lambda k: state_ref[pl.ds(pl.multiple_of(k * size + p * piece + i * 16, 16), 16), :]
+            load = lambda k: state_ref[pl.ds(pl.multiple_of(k * size + top + i * 16, 16), 16), :]
             g = far_ref[at, :].astype(jnp.float32)
             for k, ref in ((1, own_ref), (2, mate_ref), (3, across_ref)):
                 g = jnp.where(row(k) > 0, ref[at, :].astype(jnp.float32), g)
@@ -349,11 +350,11 @@
             stepped[1, at, :] = first_step
             stepped[2, at, :] = second_step
 
-        pl.loop(0, piece // 16)(body)
+        pl.loop(0, height // 16)(body)
         for k in range(3):
             writes.append(pltpu.make_async_copy(
-                stepped.at[k, pl.ds(p * piece, piece), :],
-                outs[k].at[pl.ds(start + p * piece, piece), :], sems.at[p * 3 + k],
+                stepped.at[k, pl.ds(top, height), :],
+                outs[k].at[pl.ds(start + top, height), :], sems.at[len(writes)],
             ))
             writes[-1].start()
     for write in writes:
@@ -366,7 +367,7 @@
         functools.partial(adam_kernel, start, size, bool(filled)), "adam",
         [jax.ShapeDtypeStruct((rows, depth), jnp.float32)] * 3 + [jax.ShapeDtypeStruct((8, 128), jnp.float32)],
         [VMEM] * 6 + [ANY] + [HBM] * len(filled), [HBM] * 3 + [VMEM],
-        scratch=[pltpu.VMEM((3, size, depth), jnp.float32), pltpu.SemaphoreType.DMA((12,))],
+        scratch=[pltpu.VMEM((3, size, depth), jnp.float32), pltpu.SemaphoreType.DMA((3 * (-(-size // 32)),))],
         aliases={7 + k: k for k in range(len(filled))},
     )(choices, state, *grads, after, *filled)
 
@@ -410,7 +411,7 @@
         arrived.append(now)
 
     mate = lax.ppermute(state, "member", swap_mates)
-    across = lax.ppermute(pick(choices, state, mate, own[0]), "member", swap_across)
+    across = lax.ppermute(pick(choices, state, mate, terms[0][0]), "member", swap_across)
     states = taken_state(steps_of, where, donor, (weight[0], first[0], second[0]), (mate, across), sent)
 
     grads, carried = [], ()

time: 72.9 us -> 71.1 us (0.975)
  starting transfers between devices: 32.2 us -> 31 us
  local copies, waits for them, and re-layouts: 2.49 us -> 1.39 us
  Pallas kernels: 17 us -> 18 us
    ppermute x2, starting transfers between devices: 1.58 us -> 0.14 us  [on_device(): across = gate(lax.ppermute(grads[c], 'member', swap_across), computed)]
    unnamed x26 -> x24, local copies, waits for them, and re-layouts: 2.49 us -> 1.39 us
    pallas_call x6, Pallas kernels: 0.94 us -> 1.89 us  [to_send(): call(send_kernel, 'to_send', [like] * 2, [VMEM] * 4 + [ANY], [VMEM] * 2,...]
  transfers between devices with their start and end apart: 24 -> 24, of which waited for: 8 -> 7; matrix products, arithmetic and copies ran while one was open for 0% -> 0% of each run, Pallas kernels for 16% -> 18%
where the time goes in v10:
time: 71.1 us; the launch traced here: 70.4 us
  starting transfers between devices  31 us (44%)
  waiting for transfers between devices  18.9 us (27%)
  Pallas kernels  18 us (25%)
  local copies, waits for them, and re-layouts  1.39 us (2%)
  between operations  1.04 us (1%)
    ppermute x16, starting transfers between devices, on_device(): now[swap].append(lax.ppermute(blocks[swap], 'shard', swaps[swap]))  25.1 us
    ppermute x16, waiting for transfers between devices, on_device(): now[swap].append(lax.ppermute(blocks[swap], 'shard', swaps[swap]))  17.7 us
    pallas_call x2, Pallas kernels, adam_update(): call(functools.partial(adam_kernel, start, size, bool(filled)), 'adam', [...  3.85 us
    pallas_call x1, Pallas kernels, halves(): call(functools.partial(halves_kernel, parts), 'halves', [half_array(size,...  3.32 us
    pallas_call x1, Pallas kernels, columns(): call(functools.partial(columns_kernel, n, scale, parts), 'context_grad',...  3.27 us
    pallas_call x1, Pallas kernels, partial_blocks(): call(functools.partial(partial_kernel, n, scale, parts, order), 'partial_...  3.21 us
    ppermute x2, starting transfers between devices, on_device(): mate = lax.ppermute(grads[c], 'member', swap_mates)  2.68 us
    pallas_call x6, Pallas kernels, to_send(): call(send_kernel, 'to_send', [like] * 2, [VMEM] * 4 + [ANY], [VMEM] * 2,...  1.89 us
  transfers between devices with their start and end apart: 24, of which 7 were waited for; matrix products, arithmetic and copies ran while one was open for 0% of the time, Pallas kernels for 18%

profile of v10, /device:TPU:1, one launch (start us, length us, event | category | flops | bytes accessed | tf_op | source)
XLA Modules:
  0.0 70.4 jit_solution(8283274128247064419)
XLA Ops:
  0.6 3.3 %halves.1 = (bf16[768,1024]{1,0:T(8,128)(2,1)}, bf16[128,1024]{1,0:T(8,128)(2,1)}, bf16[128,1024]{1,0:T(8,128)(2,1)}) custom-call(f32[256,1024]{1,0:T(8,128)} %bitcast.11, f32[256,1024]{1,0:T(8,128)} %bitcast.13, f32[256,1024]{1,0:T(8,128)} %bitcast.15), custom_call_target="tpu_custom_call" | custom-call | bytes 1024 | tf_op jit(solution)/shard_map/halves/pallas_call | solution.py:98
  4.1 0.7 collective-permute-start.2
  4.8 5.3 %collective-permute-start.3 = (bf16[128,1024]{1,0:T(8,128)(2,1)}, bf16[128,1024]{1,0:T(8,128)(2,1)S(1)}, u32[]{:S(2)}, u32[]{:S(2)}) collective-permute-start(bf16[128,1024]{1,0:T(8,128)(2,1)} %get-tuple-element.50.after_ref.refs_0_), channel_id=1, source_target_pairs={{0,1},{2,3},{1,0},{3,2},{4,5},{6,7},{5,4},{7,6},{8,9},{10,11},{9,8... | collective-permute-start | bytes 786440 | tf_op jit(solution)/shard_map/ppermute | solution.py:410
  10.8 1.5 %collective-permute-start.1 = (bf16[128,1024]{1,0:T(8,128)(2,1)}, bf16[128,1024]{1,0:T(8,128)(2,1)}, u32[]{:S(2)}, u32[]{:S(2)}) collective-permute-start(bf16[128,1024]{1,0:T(8,128)(2,1)} %get-tuple-element.47.refs_1_), channel_id=1, source_target_pairs={{0,1},{2,3},{1,0},{3,2},{4,5},{6,7},{5,4},{7,6},{8,9},{10,11},{9,8... | collective-permute-start | bytes 786440 | tf_op jit(solution)/shard_map/ppermute | solution.py:410
  12.4 1.3 %copy-done.5 = bf16[1,512,1024]{2,1,0:T(8,128)(2,1)S(1)} copy-done((bf16[1,512,1024]{2,1,0:T(8,128)(2,1)S(1)}, bf16[1,512,1024]{2,1,0:T(8,128)(2,1)}, u32[]{:S(2)}) %copy-start.5) | copy-done | bytes 1048600
  13.7 3.2 %partial_blocks.1 = (bf16[128,1024]{1,0:T(8,128)(2,1)S(1)}, bf16[128,1024]{1,0:T(8,128)(2,1)S(1)}, bf16[128,1024]{1,0:T(8,128)(2,1)S(1)}, bf16[128,1024]{1,0:T(8...) custom-call(s32[2]{0:T(128)S(1)} %pad_add_fusion.where_ref, ...), custom_call_target="tpu_custom_call" | custom-call | bytes 1024 | tf_op jit(solution)/shard_map/partial_blocks/pallas_call | solution.py:174
  17.6 0.7 pick.1
  18.3 1.3 %collective-permute-start.17 = (bf16[768,1024]{1,0:T(8,128)(2,1)S(1)}, bf16[768,1024]{1,0:T(8,128)(2,1)S(1)}, u32[]{:S(2)}, u32[]{:S(2)}) collective-permute-start(bf16[768,1024]{1,0:T(8,128)(2,1)S(1)} %pick.1), channel_id=1, source_target_pairs={{0,8},{4,12},{8,0},{12,4},{1,9},{5,13},{9,1},{13,5},{2,10},{6,14},... | collective-permute-start | bytes 4718600 | tf_op jit(solution)/shard_map/ppermute | solution.py:414
  19.8 0.7 collective-permute-start.6
  20.5 2.6 %collective-permute-start.7 = (bf16[128,1024]{1,0:T(8,128)(2,1)S(1)}, bf16[128,1024]{1,0:T(8,128)(2,1)S(1)}, u32[]{:S(2)}, u32[]{:S(2)}) collective-permute-start(bf16[128,1024]{1,0:T(8,128)(2,1)S(1)} %get-tuple-element.53.after_ref), channel_id=1, source_target_pairs={{0,1},{2,3},{1,0},{3,2},{4,5},{6,7},{5,4},{7,6},{8,9},{10,11},{9,8... | collective-permute-start | bytes 786440 | tf_op jit(solution)/shard_map/ppermute | solution.py:410
  23.1 1.1 %to_send.7 = (bf16[128,1024]{1,0:T(8,128)(2,1)S(1)}, bf16[128,1024]{1,0:T(8,128)(2,1)S(1)}) custom-call(bf16[128,1024]{1,0:T(8,128)(2,1)S(1)} %collective-permute-done.arrived_ref.refs_5_, bf16[128,1024]{1,0:T(8,128)(2,1)S(1)} %get-tuple-element.48.term_ref, bf16[128,1024]{1,0:T(8,128)(2,1)} %collective-permute-done.1.arrived_too_ref.refs_3_, ...), custom_call_target="tpu_custom_call" | custom-call | flops 1342177280 | bytes 1024 | tf_op jit(solution)/shard_map/to_send/pallas_call | solution.py:203
  24.2 0.7 collective-permute-start.4
  24.9 2.1 %collective-permute-start.5 = (bf16[128,1024]{1,0:T(8,128)(2,1)S(1)}, bf16[128,1024]{1,0:T(8,128)(2,1)S(1)}, u32[]{:S(2)}, u32[]{:S(2)}) collective-permute-start(bf16[128,1024]{1,0:T(8,128)(2,1)S(1)} %get-tuple-element.56.after_ref), channel_id=1, source_target_pairs={{0,1},{2,3},{1,0},{3,2},{4,5},{6,7},{5,4},{7,6},{8,9},{10,11},{9,8... | collective-permute-start | bytes 786440 | tf_op jit(solution)/shard_map/ppermute | solution.py:410
  27.0 1.6 %collective-permute-done.7.arrived_too_ref.refs_6_ = bf16[128,1024]{1,0:T(8,128)(2,1)S(1)} collective-permute-done((bf16[128,1024]{1,0:T(8,128)(2,1)S(1)}, bf16[128,1024]{1,0:T(8,128)(2,1)S(1)}, u32[]{:S(2)}, u32[]{:S(2)}) %collective-permute-start.7) | collective-permute-done | bytes 262176 | tf_op jit(solution)/shard_map/ppermute | solution.py:410
  28.7 0.7 collective-permute-start.10
  29.4 2.7 %collective-permute-start.11 = (bf16[128,1024]{1,0:T(8,128)(2,1)S(1)}, bf16[128,1024]{1,0:T(8,128)(2,1)S(1)}, u32[]{:S(2)}, u32[]{:S(2)}) collective-permute-start(bf16[128,1024]{1,0:T(8,128)(2,1)S(1)} %get-tuple-element.61.after_ref), channel_id=1, source_target_pairs={{0,1},{2,3},{1,0},{3,2},{4,5},{6,7},{5,4},{7,6},{8,9},{10,11},{9,8... | collective-permute-start | bytes 786440 | tf_op jit(solution)/shard_map/ppermute | solution.py:410
  32.1 2.1 %collective-permute-done.5.arrived_too_ref.refs_7_ = bf16[128,1024]{1,0:T(8,128)(2,1)S(1)} collective-permute-done((bf16[128,1024]{1,0:T(8,128)(2,1)S(1)}, bf16[128,1024]{1,0:T(8,128)(2,1)S(1)}, u32[]{:S(2)}, u32[]{:S(2)}) %collective-permute-start.5) | collective-permute-done | bytes 262176 | tf_op jit(solution)/shard_map/ppermute | solution.py:410
  34.3 0.7 collective-permute-start.8
  35.0 3.0 %collective-permute-start.9 = (bf16[128,1024]{1,0:T(8,128)(2,1)S(1)}, bf16[128,1024]{1,0:T(8,128)(2,1)S(1)}, u32[]{:S(2)}, u32[]{:S(2)}) collective-permute-start(bf16[128,1024]{1,0:T(8,128)(2,1)S(1)} %get-tuple-element.64.after_ref), channel_id=1, source_target_pairs={{0,1},{2,3},{1,0},{3,2},{4,5},{6,7},{5,4},{7,6},{8,9},{10,11},{9,8... | collective-permute-start | bytes 786440 | tf_op jit(solution)/shard_map/ppermute | solution.py:410
  38.1 1.6 %collective-permute-done.11.arrived_too_ref.refs_10_ = bf16[128,1024]{1,0:T(8,128)(2,1)S(1)} collective-permute-done((bf16[128,1024]{1,0:T(8,128)(2,1)S(1)}, bf16[128,1024]{1,0:T(8,128)(2,1)S(1)}, u32[]{:S(2)}, u32[]{:S(2)}) %collective-permute-start.11) | collective-permute-done | bytes 262176 | tf_op jit(solution)/shard_map/ppermute | solution.py:410
  39.8 1.2 %collective-permute-start.14 = (bf16[128,1024]{1,0:T(8,128)(2,1)S(1)}, bf16[128,1024]{1,0:T(8,128)(2,1)S(1)}, u32[]{:S(2)}, u32[]{:S(2)}) collective-permute-start(bf16[128,1024]{1,0:T(8,128)(2,1)S(1)} %get-tuple-element.69.after_ref), channel_id=1, source_target_pairs={{0,1},{2,3},{1,0},{3,2},{4,5},{6,7},{5,4},{7,6},{8,9},{10,11},{9,8... | collective-permute-start | bytes 786440 | tf_op jit(solution)/shard_map/ppermute | solution.py:410
  41.7 3.5 %collective-permute-done.9.arrived_too_ref.refs_11_ = bf16[128,1024]{1,0:T(8,128)(2,1)S(1)} collective-permute-done((bf16[128,1024]{1,0:T(8,128)(2,1)S(1)}, bf16[128,1024]{1,0:T(8,128)(2,1)S(1)}, u32[]{:S(2)}, u32[]{:S(2)}) %collective-permute-start.9) | collective-permute-done | bytes 262176 | tf_op jit(solution)/shard_map/ppermute | solution.py:410
  45.4 1.2 %collective-permute-start.12 = (bf16[128,1024]{1,0:T(8,128)(2,1)S(1)}, bf16[128,1024]{1,0:T(8,128)(2,1)S(1)}, u32[]{:S(2)}, u32[]{:S(2)}) collective-permute-start(bf16[128,1024]{1,0:T(8,128)(2,1)S(1)} %get-tuple-element.70.after_ref), channel_id=1, source_target_pairs={{0,1},{2,3},{1,0},{3,2},{4,5},{6,7},{5,4},{7,6},{8,9},{10,11},{9,8... | collective-permute-start | bytes 786440 | tf_op jit(solution)/shard_map/ppermute | solution.py:410
  47.3 3.5 %collective-permute-done.14.one_ref = bf16[128,1024]{1,0:T(8,128)(2,1)S(1)} collective-permute-done((bf16[128,1024]{1,0:T(8,128)(2,1)S(1)}, bf16[128,1024]{1,0:T(8,128)(2,1)S(1)}, u32[]{:S(2)}, u32[]{:S(2)}) %collective-permute-start.14) | collective-permute-done | bytes 262176 | tf_op jit(solution)/shard_map/ppermute | solution.py:410
  51.1 5.4 %collective-permute-done.12.one_ref = bf16[128,1024]{1,0:T(8,128)(2,1)S(1)} collective-permute-done((bf16[128,1024]{1,0:T(8,128)(2,1)S(1)}, bf16[128,1024]{1,0:T(8,128)(2,1)S(1)}, u32[]{:S(2)}, u32[]{:S(2)}) %collective-permute-start.12) | collective-permute-done | bytes 262176 | tf_op jit(solution)/shard_map/ppermute | solution.py:410
  56.7 2.5 %collective-permute-start.20 = (bf16[112,1024]{1,0:T(8,128)(2,1)S(1)}, bf16[112,1024]{1,0:T(8,128)(2,1)S(1)}, u32[]{:S(2)}, u32[]{:S(2)}) collective-permute-start(bf16[112,1024]{1,0:T(8,128)(2,1)S(1)} %get-tuple-element.74.after_ref.own_ref), channel_id=1, source_target_pairs={{0,4},{4,0},{8,12},{12,8},{1,5},{5,1},{9,13},{13,9},{2,6},{6,2},{1... | collective-permute-start | bytes 688136 | tf_op jit(solution)/shard_map/ppermute | solution.py:432
  59.2 3.3 %context_grad.1 = (bf16[512,1024]{1,0:T(8,128)(2,1)}, f32[8,128]{1,0:T(8,128)S(1)}) custom-call(s32[2]{0:T(128)S(1)} %pad_add_fusion.where_ref, bf16[512,1024]{1,0:T(8,128)(2,1)S(1)} %bitcast.18, bf16[144,1024]{1,0:T(8,128)(2,1)S(1)} %summed_grad.3.after_ref.own_ref, bf16[128,1024]{1,0:T(8,128)(2,1)S(1)} %copy-done.6, bf16[128,1024]{1,0:T(8,128)(2,1)S(1)} %copy-done.7, ...), custom_call_target="tpu_custom_call" | custom-call | bytes 1024 | tf_op jit(solution)/shard_map/context_grad/pallas_call | solution.py:271
  63.1 0.9 %taken_state.1 = (f32[336,1024]{1,0:T(8,128)S(1)}, f32[432,1024]{1,0:T(8,128)S(1)}) custom-call(s32[2]{0:T(128)S(1)} %pad_add_fusion.where_ref, s32[4]{0:T(128)S(1)} %copy-done.8, bf16[128,1024]{1,0:T(8,128)(2,1)S(1)} %get-tuple-element.70.after_ref, f32[256,1024]{1,0:T(8,128)S(1)} %bitcast.12, f32[256,1024]{1,0:T(8,128)S(1)} %bitcast.14, ...), custom_call_target="tpu_custom_call" | custom-call | bytes 1024 | tf_op jit(solution)/shard_map/taken_state/pallas_call | solution.py:320
  64.1 1.5 %adam.2 = (f32[256,1024]{1,0:T(8,128)}, f32[256,1024]{1,0:T(8,128)}, f32[256,1024]{1,0:T(8,128)}, f32[8,128]{1,0:T(8,128)S(1)}) custom-call(f32[8,1024]{1,0:T(8,128)S(1)} %choices.1.choices_ref, f32[336,1024]{1,0:T(8,128)S(1)} %get-tuple-element.79.state_ref, bf16[112,1024]{1,0:T(8,128)(2,1)S(1)} %get-tuple-element.74.after_ref.own_ref, ...), custom_call_target="tpu_custom_call" | custom-call | bytes 1024 | tf_op jit(solution)/shard_map/adam/pallas_call | solution.py:366
  65.6 1.3 %collective-permute-start.23 = (bf16[144,1024]{1,0:T(8,128)(2,1)S(1)}, bf16[144,1024]{1,0:T(8,128)(2,1)S(1)}, u32[]{:S(2)}, u32[]{:S(2)}) collective-permute-start(bf16[144,1024]{1,0:T(8,128)(2,1)S(1)} %gate.3.across_ref), channel_id=1, source_target_pairs={{0,4},{4,0},{8,12},{12,8},{1,5},{5,1},{9,13},{13,9},{2,6},{6,2},{1... | collective-permute-start | bytes 884744 | tf_op jit(solution)/shard_map/ppermute | solution.py:434
  66.9 1.2 %collective-permute-done.23.far_ref = bf16[144,1024]{1,0:T(8,128)(2,1)S(1)} collective-permute-done((bf16[144,1024]{1,0:T(8,128)(2,1)S(1)}, bf16[144,1024]{1,0:T(8,128)(2,1)S(1)}, u32[]{:S(2)}, u32[]{:S(2)}) %collective-permute-start.23) | collective-permute-done | bytes 294944 | tf_op jit(solution)/shard_map/ppermute | solution.py:434
  68.1 2.3 %adam.3 = (f32[256,1024]{1,0:T(8,128)}, f32[256,1024]{1,0:T(8,128)}, f32[256,1024]{1,0:T(8,128)}, f32[8,128]{1,0:T(8,128)}) custom-call(f32[8,1024]{1,0:T(8,128)S(1)} %choices.1.choices_ref, f32[432,1024]{1,0:T(8,128)S(1)} %get-tuple-element.78.state_ref, ...), custom_call_target="tpu_custom_call", output_to_operand_aliasing={{0}: (7, {}), {1}: (8, {}), {2}: (9, {})} | custom-call | bytes 1024 | tf_op jit(solution)/shard_map/adam/pallas_call | solution.py:366
  (59 shorter events, 4.6 us)
Async XLA Ops:
  0.6 11.8 %copy-start.3 = (bf16[1,512,1024]{2,1,0:T(8,128)(2,1)S(1)}, bf16[1,512,1024]{2,1,0:T(8,128)(2,1)}, u32[]{:S(2)}) copy-start(bf16[1,512,1024]{2,1,0:T(8,128)(2,1)} %param.10) | copy-start | bytes 3145732
  4.0 13.0 %copy-start.8 = (s32[4]{0:T(128)S(1)}, s32[4]{0:T(128)}, u32[]{:S(2)}) copy-start(s32[4]{0:T(128)} %donor_ref.3) | copy-start | bytes 52
  4.0 13.0 %copy-start.9 = (f32[4]{0:T(128)S(1)}, f32[4]{0:T(128)}, u32[]{:S(2)}) copy-start(f32[4]{0:T(128)} %rates_ref.1) | copy-start | bytes 52
  4.0 13.0 %copy-start.10 = (f32[4]{0:T(128)S(1)}, f32[4]{0:T(128)}, u32[]{:S(2)}) copy-start(f32[4]{0:T(128)} %decays_ref.1) | copy-start | bytes 52
  4.0 13.0 %copy-start.11 = (s32[4]{0:T(128)S(1)}, s32[4]{0:T(128)}, u32[]{:S(2)}) copy-start(s32[4]{0:T(128)} %steps_ref.1) | copy-start | bytes 52
  4.0 13.6 %collective-permute-start.16 = (bf16[768,1024]{1,0:T(8,128)(2,1)}, bf16[768,1024]{1,0:T(8,128)(2,1)S(1)}, u32[]{:S(2)}, u32[]{:S(2)}) collective-permute-start(bf16[768,1024]{1,0:T(8,128)(2,1)} %get-tuple-element.77.own_ref), channel_id=1, source_target_pairs={{0,4},{4,0},{8,12},{12,8},{1,5},{5,1},{9,13},{13,9},{2,6},{6,2},{1... | collective-permute-start | bytes 4718600 | tf_op jit(solution)/shard_map/ppermute | solution.py:413
  4.1 15.4 %collective-permute-start.2 = (bf16[128,1024]{1,0:T(8,128)(2,1)}, bf16[128,1024]{1,0:T(8,128)(2,1)S(1)}, u32[]{:S(2)}, u32[]{:S(2)}) collective-permute-start(bf16[128,1024]{1,0:T(8,128)(2,1)} %get-tuple-element.50.after_ref.refs_0_), channel_id=1, source_target_pairs={{1,2},{2,1},{5,6},{6,5},{9,10},{10,9},{13,14},{14,13},{17,18},{18,... | collective-permute-start | bytes 786440 | tf_op jit(solution)/shard_map/ppermute | solution.py:410
  4.8 14.8 %collective-permute-start.3 = (bf16[128,1024]{1,0:T(8,128)(2,1)}, bf16[128,1024]{1,0:T(8,128)(2,1)S(1)}, u32[]{:S(2)}, u32[]{:S(2)}) collective-permute-start(bf16[128,1024]{1,0:T(8,128)(2,1)} %get-tuple-element.50.after_ref.refs_0_), channel_id=1, source_target_pairs={{0,1},{2,3},{1,0},{3,2},{4,5},{6,7},{5,4},{7,6},{8,9},{10,11},{9,8... | collective-permute-start | bytes 786440 | tf_op jit(solution)/shard_map/ppermute | solution.py:410
  10.1 12.9 %collective-permute-start = (bf16[128,1024]{1,0:T(8,128)(2,1)}, bf16[128,1024]{1,0:T(8,128)(2,1)S(1)}, u32[]{:S(2)}, u32[]{:S(2)}) collective-permute-start(bf16[128,1024]{1,0:T(8,128)(2,1)} %get-tuple-element.47.refs_1_), channel_id=1, source_target_pairs={{1,2},{2,1},{5,6},{6,5},{9,10},{10,9},{13,14},{14,13},{17,18},{18,... | collective-permute-start | bytes 786440 | tf_op jit(solution)/shard_map/ppermute | solution.py:410
  10.8 12.3 %collective-permute-start.1 = (bf16[128,1024]{1,0:T(8,128)(2,1)}, bf16[128,1024]{1,0:T(8,128)(2,1)}, u32[]{:S(2)}, u32[]{:S(2)}) collective-permute-start(bf16[128,1024]{1,0:T(8,128)(2,1)} %get-tuple-element.47.refs_1_), channel_id=1, source_target_pairs={{0,1},{2,3},{1,0},{3,2},{4,5},{6,7},{5,4},{7,6},{8,9},{10,11},{9,8... | collective-permute-start | bytes 786440 | tf_op jit(solution)/shard_map/ppermute | solution.py:410
  18.3 44.8 %collective-permute-start.17 = (bf16[768,1024]{1,0:T(8,128)(2,1)S(1)}, bf16[768,1024]{1,0:T(8,128)(2,1)S(1)}, u32[]{:S(2)}, u32[]{:S(2)}) collective-permute-start(bf16[768,1024]{1,0:T(8,128)(2,1)S(1)} %pick.1), channel_id=1, source_target_pairs={{0,8},{4,12},{8,0},{12,4},{1,9},{5,13},{9,1},{13,5},{2,10},{6,14},... | collective-permute-start | bytes 4718600 | tf_op jit(solution)/shard_map/ppermute | solution.py:414
  19.8 7.2 %collective-permute-start.6 = (bf16[128,1024]{1,0:T(8,128)(2,1)S(1)}, bf16[128,1024]{1,0:T(8,128)(2,1)S(1)}, u32[]{:S(2)}, u32[]{:S(2)}) collective-permute-start(bf16[128,1024]{1,0:T(8,128)(2,1)S(1)} %get-tuple-element.58), channel_id=1, source_target_pairs={{1,2},{2,1},{5,6},{6,5},{9,10},{10,9},{13,14},{14,13},{17,18},{18,... | collective-permute-start | bytes 786440 | tf_op jit(solution)/shard_map/ppermute | solution.py:410
  20.5 8.1 %collective-permute-start.7 = (bf16[128,1024]{1,0:T(8,128)(2,1)S(1)}, bf16[128,1024]{1,0:T(8,128)(2,1)S(1)}, u32[]{:S(2)}, u32[]{:S(2)}) collective-permute-start(bf16[128,1024]{1,0:T(8,128)(2,1)S(1)} %get-tuple-element.53.after_ref), channel_id=1, source_target_pairs={{0,1},{2,3},{1,0},{3,2},{4,5},{6,7},{5,4},{7,6},{8,9},{10,11},{9,8... | collective-permute-start | bytes 786440 | tf_op jit(solution)/shard_map/ppermute | solution.py:410
  24.2 7.9 %collective-permute-start.4 = (bf16[128,1024]{1,0:T(8,128)(2,1)S(1)}, bf16[128,1024]{1,0:T(8,128)(2,1)S(1)}, u32[]{:S(2)}, u32[]{:S(2)}) collective-permute-start(bf16[128,1024]{1,0:T(8,128)(2,1)S(1)} %get-tuple-element.54), channel_id=1, source_target_pairs={{1,2},{2,1},{5,6},{6,5},{9,10},{10,9},{13,14},{14,13},{17,18},{18,... | collective-permute-start | bytes 786440 | tf_op jit(solution)/shard_map/ppermute | solution.py:410
  24.9 9.3 %collective-permute-start.5 = (bf16[128,1024]{1,0:T(8,128)(2,1)S(1)}, bf16[128,1024]{1,0:T(8,128)(2,1)S(1)}, u32[]{:S(2)}, u32[]{:S(2)}) collective-permute-start(bf16[128,1024]{1,0:T(8,128)(2,1)S(1)} %get-tuple-element.56.after_ref), channel_id=1, source_target_pairs={{0,1},{2,3},{1,0},{3,2},{4,5},{6,7},{5,4},{7,6},{8,9},{10,11},{9,8... | collective-permute-start | bytes 786440 | tf_op jit(solution)/shard_map/ppermute | solution.py:410
  28.7 9.3 %collective-permute-start.10 = (bf16[128,1024]{1,0:T(8,128)(2,1)S(1)}, bf16[128,1024]{1,0:T(8,128)(2,1)S(1)}, u32[]{:S(2)}, u32[]{:S(2)}) collective-permute-start(bf16[128,1024]{1,0:T(8,128)(2,1)S(1)} %get-tuple-element.66), channel_id=1, source_target_pairs={{1,2},{2,1},{5,6},{6,5},{9,10},{10,9},{13,14},{14,13},{17,18},{18,... | collective-permute-start | bytes 786440 | tf_op jit(solution)/shard_map/ppermute | solution.py:410
  29.4 10.2 %collective-permute-start.11 = (bf16[128,1024]{1,0:T(8,128)(2,1)S(1)}, bf16[128,1024]{1,0:T(8,128)(2,1)S(1)}, u32[]{:S(2)}, u32[]{:S(2)}) collective-permute-start(bf16[128,1024]{1,0:T(8,128)(2,1)S(1)} %get-tuple-element.61.after_ref), channel_id=1, source_target_pairs={{0,1},{2,3},{1,0},{3,2},{4,5},{6,7},{5,4},{7,6},{8,9},{10,11},{9,8... | collective-permute-start | bytes 786440 | tf_op jit(solution)/shard_map/ppermute | solution.py:410
  34.3 7.4 %collective-permute-start.8 = (bf16[128,1024]{1,0:T(8,128)(2,1)S(1)}, bf16[128,1024]{1,0:T(8,128)(2,1)S(1)}, u32[]{:S(2)}, u32[]{:S(2)}) collective-permute-start(bf16[128,1024]{1,0:T(8,128)(2,1)S(1)} %get-tuple-element.62), channel_id=1, source_target_pairs={{1,2},{2,1},{5,6},{6,5},{9,10},{10,9},{13,14},{14,13},{17,18},{18,... | collective-permute-start | bytes 786440 | tf_op jit(solution)/shard_map/ppermute | solution.py:410
  35.0 10.2 %collective-permute-start.9 = (bf16[128,1024]{1,0:T(8,128)(2,1)S(1)}, bf16[128,1024]{1,0:T(8,128)(2,1)S(1)}, u32[]{:S(2)}, u32[]{:S(2)}) collective-permute-start(bf16[128,1024]{1,0:T(8,128)(2,1)S(1)} %get-tuple-element.64.after_ref), channel_id=1, source_target_pairs={{0,1},{2,3},{1,0},{3,2},{4,5},{6,7},{5,4},{7,6},{8,9},{10,11},{9,8... | collective-permute-start | bytes 786440 | tf_op jit(solution)/shard_map/ppermute | solution.py:410
  39.8 11.1 %collective-permute-start.14 = (bf16[128,1024]{1,0:T(8,128)(2,1)S(1)}, bf16[128,1024]{1,0:T(8,128)(2,1)S(1)}, u32[]{:S(2)}, u32[]{:S(2)}) collective-permute-start(bf16[128,1024]{1,0:T(8,128)(2,1)S(1)} %get-tuple-element.69.after_ref), channel_id=1, source_target_pairs={{0,1},{2,3},{1,0},{3,2},{4,5},{6,7},{5,4},{7,6},{8,9},{10,11},{9,8... | collective-permute-start | bytes 786440 | tf_op jit(solution)/shard_map/ppermute | solution.py:410
  41.0 9.8 %collective-permute-start.15 = (bf16[128,1024]{1,0:T(8,128)(2,1)S(1)}, bf16[128,1024]{1,0:T(8,128)(2,1)S(1)}, u32[]{:S(2)}, u32[]{:S(2)}) collective-permute-start(bf16[128,1024]{1,0:T(8,128)(2,1)S(1)} %get-tuple-element.73), channel_id=1, source_target_pairs={{1,2},{2,1},{5,6},{6,5},{9,10},{10,9},{13,14},{14,13},{17,18},{18,... | collective-permute-start | bytes 786440 | tf_op jit(solution)/shard_map/ppermute | solution.py:410
  45.4 13.8 %copy-start.7 = (bf16[128,1024]{1,0:T(8,128)(2,1)S(1)}, bf16[128,1024]{1,0:T(8,128)(2,1)}, u32[]{:S(2)}) copy-start(bf16[128,1024]{1,0:T(8,128)(2,1)} %get-tuple-element.47.refs_1_) | copy-start | bytes 786436
  45.4 11.1 %collective-permute-start.12 = (bf16[128,1024]{1,0:T(8,128)(2,1)S(1)}, bf16[128,1024]{1,0:T(8,128)(2,1)S(1)}, u32[]{:S(2)}, u32[]{:S(2)}) collective-permute-start(bf16[128,1024]{1,0:T(8,128)(2,1)S(1)} %get-tuple-element.70.after_ref), channel_id=1, source_target_pairs={{0,1},{2,3},{1,0},{3,2},{4,5},{6,7},{5,4},{7,6},{8,9},{10,11},{9,8... | collective-permute-start | bytes 786440 | tf_op jit(solution)/shard_map/ppermute | solution.py:410
  46.7 9.8 %collective-permute-start.13 = (bf16[128,1024]{1,0:T(8,128)(2,1)S(1)}, bf16[128,1024]{1,0:T(8,128)(2,1)S(1)}, u32[]{:S(2)}, u32[]{:S(2)}) collective-permute-start(bf16[128,1024]{1,0:T(8,128)(2,1)S(1)} %get-tuple-element.71), channel_id=1, source_target_pairs={{1,2},{2,1},{5,6},{6,5},{9,10},{10,9},{13,14},{14,13},{17,18},{18,... | collective-permute-start | bytes 786440 | tf_op jit(solution)/shard_map/ppermute | solution.py:410
  51.0 11.5 %collective-permute-start.21 = (bf16[112,1024]{1,0:T(8,128)(2,1)S(1)}, bf16[112,1024]{1,0:T(8,128)(2,1)S(1)}, u32[]{:S(2)}, u32[]{:S(2)}) collective-permute-start(bf16[112,1024]{1,0:T(8,128)(2,1)S(1)} %get-tuple-element.74.after_ref.own_ref), channel_id=1, source_target_pairs={{0,8},{4,12},{8,0},{12,4},{1,9},{5,13},{9,1},{13,5},{2,10},{6,14},... | collective-permute-start | bytes 688136 | tf_op jit(solution)/shard_map/ppermute | solution.py:433
  56.6 6.5 %copy-start = (f32[1,256,1024]{2,1,0:T(8,128)S(1)}, f32[1,256,1024]{2,1,0:T(8,128)}, u32[]{:S(2)}) copy-start(f32[1,256,1024]{2,1,0:T(8,128)} %param.11) | copy-start | bytes 3145732
  56.6 6.5 %copy-start.1 = (f32[1,256,1024]{2,1,0:T(8,128)S(1)}, f32[1,256,1024]{2,1,0:T(8,128)}, u32[]{:S(2)}) copy-start(f32[1,256,1024]{2,1,0:T(8,128)} %param.12) | copy-start | bytes 3145732
  56.6 8.9 %collective-permute-start.19 = (bf16[144,1024]{1,0:T(8,128)(2,1)S(1)}, bf16[144,1024]{1,0:T(8,128)(2,1)S(1)}, u32[]{:S(2)}, u32[]{:S(2)}) collective-permute-start(bf16[144,1024]{1,0:T(8,128)(2,1)S(1)} %summed_grad.3.after_ref.own_ref), channel_id=1, source_target_pairs={{0,8},{4,12},{8,0},{12,4},{1,9},{5,13},{9,1},{13,5},{2,10},{6,14},... | collective-permute-start | bytes 884744 | tf_op jit(solution)/shard_map/ppermute | solution.py:433
  56.7 7.3 %collective-permute-start.20 = (bf16[112,1024]{1,0:T(8,128)(2,1)S(1)}, bf16[112,1024]{1,0:T(8,128)(2,1)S(1)}, u32[]{:S(2)}, u32[]{:S(2)}) collective-permute-start(bf16[112,1024]{1,0:T(8,128)(2,1)S(1)} %get-tuple-element.74.after_ref.own_ref), channel_id=1, source_target_pairs={{0,4},{4,0},{8,12},{12,8},{1,5},{5,1},{9,13},{13,9},{2,6},{6,2},{1... | collective-permute-start | bytes 688136 | tf_op jit(solution)/shard_map/ppermute | solution.py:432
  62.5 1.6 %collective-permute-start.22 = (bf16[112,1024]{1,0:T(8,128)(2,1)S(1)}, bf16[112,1024]{1,0:T(8,128)(2,1)S(1)}, u32[]{:S(2)}, u32[]{:S(2)}) collective-permute-start(bf16[112,1024]{1,0:T(8,128)(2,1)S(1)} %gate.2.across_ref), channel_id=1, source_target_pairs={{0,4},{4,0},{8,12},{12,8},{1,5},{5,1},{9,13},{13,9},{2,6},{6,2},{1... | collective-permute-start | bytes 688136 | tf_op jit(solution)/shard_map/ppermute | solution.py:434
  62.9 4.0 %collective-permute-start.18 = (bf16[144,1024]{1,0:T(8,128)(2,1)S(1)}, bf16[144,1024]{1,0:T(8,128)(2,1)S(1)}, u32[]{:S(2)}, u32[]{:S(2)}) collective-permute-start(bf16[144,1024]{1,0:T(8,128)(2,1)S(1)} %summed_grad.3.after_ref.own_ref), channel_id=1, source_target_pairs={{0,4},{4,0},{8,12},{12,8},{1,5},{5,1},{9,13},{13,9},{2,6},{6,2},{1... | collective-permute-start | bytes 884744 | tf_op jit(solution)/shard_map/ppermute | solution.py:432
  65.6 2.5 %collective-permute-start.23 = (bf16[144,1024]{1,0:T(8,128)(2,1)S(1)}, bf16[144,1024]{1,0:T(8,128)(2,1)S(1)}, u32[]{:S(2)}, u32[]{:S(2)}) collective-permute-start(bf16[144,1024]{1,0:T(8,128)(2,1)S(1)} %gate.3.across_ref), channel_id=1, source_target_pairs={{0,4},{4,0},{8,12},{12,8},{1,5},{5,1},{9,13},{13,9},{2,6},{6,2},{1... | collective-permute-start | bytes 884744 | tf_op jit(solution)/shard_map/ppermute | solution.py:434
  (4 other events, 15.1 us)

commit v11 on v10

--- a/solution.py
+++ b/solution.py
@@ -57,7 +57,7 @@
     return jnp.where(donor >= 0, donor, member)
 
 
-def choices_kernel(where_ref, rates_ref, decays_ref, steps_ref, donor_ref, out_ref):
+def make_choices(where_ref, rates_ref, decays_ref, steps_ref, donor_ref, out_ref):
     member = where_ref[1]
     source = source_of(member, donor_ref)
     way = jnp.bitwise_xor(source, member)
@@ -73,8 +73,8 @@
     out_ref[7:8, :] = 1.0 / (1.0 - jnp.exp(count * math.log(beta_two)))
 
 
-def halves_kernel(parts, weight_ref, first_ref, second_ref, state_ref, *refs):
-    own_refs, (full, sems) = refs[:-2], refs[-2:]
+def halves_kernel(parts, weight_ref, first_ref, second_ref, *refs):
+    tables, (state_ref, choices_ref), own_refs, (full, sems) = refs[:5], refs[5:7], refs[7:-2], refs[-2:]
     rows = weight_ref.shape[0]
     copies = []
     for k, ref in enumerate((weight_ref, first_ref, second_ref)):
@@ -83,6 +83,7 @@
                 ref.at[pl.ds(start, size), :], full.at[k, pl.ds(start, size), :], sems.at[k * len(parts) + c]
             ))
             copies[-1].start()
+    make_choices(*tables, choices_ref)
     for k in range(3):
         for c, (start, size) in enumerate(parts):
             copies[k * len(parts) + c].wait()
@@ -92,14 +93,15 @@
             state_ref[k * rows + start:k * rows + start + size, :] = rounded
 
 
-def halves(parts, weight, first, second):
-    rows, depth = weight.shape
-    sizes = [3 * rows] + [size for _, size in parts]
+def halves(parts, arrays, tables):
+    rows, depth = arrays[0].shape
+    shapes = [half_array(3 * rows, depth), jax.ShapeDtypeStruct((8, depth), jnp.float32)]
+    shapes += [half_array(size, depth) for _, size in parts]
     return call(
         functools.partial(halves_kernel, parts), "halves",
-        [half_array(size, depth) for size in sizes], [HBM] * 3, [VMEM] * len(sizes), limit=56,
+        shapes, [HBM] * 3 + [SMEM] * 5, [VMEM] * len(shapes), limit=56,
         scratch=[pltpu.VMEM((3, rows, depth), jnp.float32), pltpu.SemaphoreType.DMA((3 * len(parts),))],
-    )(weight, first, second)
+    )(*arrays, *tables)
 
 
 def pick_kernel(choices_ref, own_ref, mate_ref, after_ref, out_ref):
@@ -118,29 +120,16 @@
 
 
 def partial_kernel(n, scale, parts, order, where_ref, context_ref, cotangent_ref, *refs):
-    outs, (context, cotangent, product, rounded, sems, out_sems) = refs[:-6], refs[-6:]
+    outs, (product, rounded, out_sems) = refs[:-3], refs[-3:]
     width = product.shape[0]
     rows = width // n
     me = where_ref[0]
     even = lax.rem(me, 2) == 0
     tile = min(256, width)
-    tokens = context.shape[0]
-    loads = []
-    for i, start in enumerate(range(0, tokens, tokens // 4)):
-        at = pl.ds(start, tokens // 4)
-        loads.append(pltpu.make_async_copy(cotangent_ref.at[at, :], cotangent.at[at, :], sems.at[i]))
-    for i, start in enumerate(range(0, width, tile)):
-        at = pl.ds(start, tile)
-        loads.append(pltpu.make_async_copy(context_ref.at[:, at], context.at[:, at], sems.at[4 + i]))
-    for load in loads:
-        load.start()
     rounded[width:, :] = jnp.zeros((rows, rounded.shape[1]), rounded.dtype)
-    for load in loads[:4]:
-        load.wait()
-    for i, start in enumerate(range(0, width, tile)):
-        loads[4 + i].wait()
+    for start in range(0, width, tile):
         block = scale * lax.dot_general(
-            context[:, start:start + tile], cotangent[...],
+            context_ref[:, start:start + tile], cotangent_ref[...],
             (((0,), (0,)), ((), ())), preferred_element_type=jnp.float32,
         )
         product[start:start + tile, :] = block
@@ -175,13 +164,10 @@
         functools.partial(partial_kernel, n, scale, parts, order), "partial_blocks",
         [half_array(size, depth) for _, size in parts] * len(order)
         + [jax.ShapeDtypeStruct((size, depth), jnp.float32) for _, size in parts],
-        [SMEM, HBM, HBM], [HBM] * outs, limit=14,
+        [SMEM, VMEM, VMEM], [HBM] * outs, limit=14,
         scratch=[
-            pltpu.VMEM(context_rows.shape, context_rows.dtype),
-            pltpu.VMEM(cotangent.shape, cotangent.dtype),
             pltpu.VMEM((width, depth), jnp.float32),
             pltpu.VMEM((width + width // n, depth), jnp.bfloat16),
-            pltpu.SemaphoreType.DMA((4 + width // min(256, width),)),
             pltpu.SemaphoreType.DMA((outs,)),
         ],
     )(where, context_rows, cotangent)
@@ -390,10 +376,8 @@
         pairs = [(s, s + 1) for s in range(swap, n - 1, 2)]
         swaps.append(pairs + [(b, a) for a, b in pairs])
 
-    state, *own = halves(parts, weight[0], first[0], second[0])
-    choices = call(
-        choices_kernel, "choices", jax.ShapeDtypeStruct((8, depth), jnp.float32), [SMEM] * 5, VMEM
-    )(where, rates, decays, steps, donor)
+    arrays = (weight[0], first[0], second[0])
+    state, choices, *own = halves(parts, arrays, (where, rates, decays, steps, donor))
     order = [(slot, swap) for slot in range(2, n + 1) for swap in range(2)]
     terms = partial_blocks(n, scale, parts, order, where, context_rows, cotangent)
 
@@ -412,7 +396,7 @@
 
     mate = lax.ppermute(state, "member", swap_mates)
     across = lax.ppermute(pick(choices, state, mate, terms[0][0]), "member", swap_across)
-    states = taken_state(steps_of, where, donor, (weight[0], first[0], second[0]), (mate, across), sent)
+    states = taken_state(steps_of, where, donor, arrays, (mate, across), sent)
 
     grads, carried = [], ()
     for c, (_, size) in enumerate(parts):

time: 71.1 us -> 71.2 us (level)
  Pallas kernels: 18 us -> 15.9 us
  starting transfers between devices: 31 us -> 32.8 us
  local copies, waits for them, and re-layouts: 1.39 us -> 0.06 us
  waiting for transfers between devices: 18.9 us -> 20.2 us
    ppermute x2, starting transfers between devices: 0.14 us -> 2.55 us  [on_device(): across = gate(lax.ppermute(grads[c], 'member', swap_across), computed)]
    unnamed x24 -> x22, local copies, waits for them, and re-layouts: 1.39 us -> 0.06 us
    ppermute x16, waiting for transfers between devices: 17.7 us -> 18.9 us  [on_device(): now[swap].append(lax.ppermute(blocks[swap], 'shard', swaps[swap]))]
    pallas_call x6, Pallas kernels: 1.89 us -> 0.94 us  [to_send(): call(send_kernel, 'to_send', [like] * 2, [VMEM] * 4 + [ANY], [VMEM] * 2,...]
    pallas_call x1, Pallas kernels: 3.21 us -> 2.32 us  [partial_blocks(): call(functools.partial(partial_kernel, n, scale, parts, order), 'partial_...]
    pallas_call x2 -> x1, Pallas kernels: 3.91 us -> 4.08 us  [halves(): call(functools.partial(halves_kernel, parts), 'halves', shapes, [HBM] * 3...]
  transfers between devices with their start and end apart: 24 -> 24, of which waited for: 7 -> 8; matrix products, arithmetic and copies ran while one was open for 0% -> 0% of each run, Pallas kernels for 18% -> 13%
where the time goes in v11:
time: 71.2 us; the launch traced here: 70.6 us
  starting transfers between devices  32.8 us (46%)
  waiting for transfers between devices  20.2 us (28%)
  Pallas kernels  15.9 us (22%)
  between operations  1 us (1%)
    ppermute x16, starting transfers between devices, on_device(): now[swap].append(lax.ppermute(blocks[swap], 'shard', swaps[swap]))  25.4 us
    ppermute x16, waiting for transfers between devices, on_device(): now[swap].append(lax.ppermute(blocks[swap], 'shard', swaps[swap]))  18.9 us
    pallas_call x1, Pallas kernels, halves(): call(functools.partial(halves_kernel, parts), 'halves', shapes, [HBM] * 3...  4.08 us
    pallas_call x2, Pallas kernels, adam_update(): call(functools.partial(adam_kernel, start, size, bool(filled)), 'adam', [...  3.86 us
    pallas_call x1, Pallas kernels, columns(): call(functools.partial(columns_kernel, n, scale, parts), 'context_grad',...  2.86 us
    ppermute x2, starting transfers between devices, on_device(): across = gate(lax.ppermute(grads[c], 'member', swap_across), computed)  2.55 us
    ppermute x2, starting transfers between devices, on_device(): mate = lax.ppermute(grads[c], 'member', swap_mates)  2.45 us
    pallas_call x1, Pallas kernels, partial_blocks(): call(functools.partial(partial_kernel, n, scale, parts, order), 'partial_...  2.32 us
  transfers between devices with their start and end apart: 24, of which 8 were waited for; matrix products, arithmetic and copies ran while one was open for 0% of the time, Pallas kernels for 13%

profile of v11, /device:TPU:1, one launch (start us, length us, event | category | flops | bytes accessed | tf_op | source)
XLA Modules:
  0.0 70.6 jit_solution(10573976559177060918)
XLA Ops:
  1.2 4.1 %halves.1 = (bf16[768,1024]{1,0:T(8,128)(2,1)}, f32[8,1024]{1,0:T(8,128)}, bf16[128,1024]{1,0:T(8,128)(2,1)}, bf16[128,1024]{1,0:T(8,128)(2,1)}) custom-call(f32[256,1024]{1,0:T(8,128)} %bitcast.11, f32[256,1024]{1,0:T(8,128)} %bitcast.13, f32[256,1024]{1,0:T(8,128)} %bitcast.15, s32[2]{0:T(128)} %pad_add_fusion.where_ref.refs_0_, f32[4]{0:T(128)} %refs_1_.1, ...), custom_call_target="tpu_custom_call" | custom-call | bytes 1024 | tf_op jit(solution)/shard_map/halves/pallas_call | solution.py:100
  5.5 0.8 %collective-permute-start.2 = (bf16[128,1024]{1,0:T(8,128)(2,1)}, bf16[128,1024]{1,0:T(8,128)(2,1)S(1)}, u32[]{:S(2)}, u32[]{:S(2)}) collective-permute-start(bf16[128,1024]{1,0:T(8,128)(2,1)} %get-tuple-element.51.after_ref.refs_0_), channel_id=1, source_target_pairs={{1,2},{2,1},{5,6},{6,5},{9,10},{10,9},{13,14},{14,13},{17,18},{18,... | collective-permute-start | bytes 786440 | tf_op jit(solution)/shard_map/ppermute | solution.py:394
  6.3 5.2 %collective-permute-start.3 = (bf16[128,1024]{1,0:T(8,128)(2,1)}, bf16[128,1024]{1,0:T(8,128)(2,1)S(1)}, u32[]{:S(2)}, u32[]{:S(2)}) collective-permute-start(bf16[128,1024]{1,0:T(8,128)(2,1)} %get-tuple-element.51.after_ref.refs_0_), channel_id=1, source_target_pairs={{0,1},{2,3},{1,0},{3,2},{4,5},{6,7},{5,4},{7,6},{8,9},{10,11},{9,8... | collective-permute-start | bytes 786440 | tf_op jit(solution)/shard_map/ppermute | solution.py:394
  12.1 1.5 %collective-permute-start.1 = (bf16[128,1024]{1,0:T(8,128)(2,1)}, bf16[128,1024]{1,0:T(8,128)(2,1)S(1)}, u32[]{:S(2)}, u32[]{:S(2)}) collective-permute-start(bf16[128,1024]{1,0:T(8,128)(2,1)} %get-tuple-element.48.refs_1_), channel_id=1, source_target_pairs={{0,1},{2,3},{1,0},{3,2},{4,5},{6,7},{5,4},{7,6},{8,9},{10,11},{9,8... | collective-permute-start | bytes 786440 | tf_op jit(solution)/shard_map/ppermute | solution.py:394
  13.6 2.3 %partial_blocks.1 = (bf16[128,1024]{1,0:T(8,128)(2,1)S(1)}, bf16[128,1024]{1,0:T(8,128)(2,1)S(1)}, bf16[128,1024]{1,0:T(8,128)(2,1)S(1)}, bf16[128,1024]{1,0:T(8...) custom-call(s32[2]{0:T(128)S(1)} %copy-done.9, ...), custom_call_target="tpu_custom_call" | custom-call | bytes 1024 | tf_op jit(solution)/shard_map/partial_blocks/pallas_call | solution.py:163
  16.0 0.7 pick.1
  16.7 1.3 %collective-permute-start.17 = (bf16[768,1024]{1,0:T(8,128)(2,1)S(1)}, bf16[768,1024]{1,0:T(8,128)(2,1)S(1)}, u32[]{:S(2)}, u32[]{:S(2)}) collective-permute-start(bf16[768,1024]{1,0:T(8,128)(2,1)S(1)} %pick.1), channel_id=1, source_target_pairs={{0,8},{4,12},{8,0},{12,4},{1,9},{5,13},{9,1},{13,5},{2,10},{6,14},... | collective-permute-start | bytes 4718600 | tf_op jit(solution)/shard_map/ppermute | solution.py:398
  18.2 0.7 collective-permute-start.6
  18.8 2.7 %collective-permute-start.7 = (bf16[128,1024]{1,0:T(8,128)(2,1)S(1)}, bf16[128,1024]{1,0:T(8,128)(2,1)S(1)}, u32[]{:S(2)}, u32[]{:S(2)}) collective-permute-start(bf16[128,1024]{1,0:T(8,128)(2,1)S(1)} %get-tuple-element.54.after_ref), channel_id=1, source_target_pairs={{0,1},{2,3},{1,0},{3,2},{4,5},{6,7},{5,4},{7,6},{8,9},{10,11},{9,8... | collective-permute-start | bytes 786440 | tf_op jit(solution)/shard_map/ppermute | solution.py:394
  21.5 2.1 %collective-permute-done.1.arrived_too_ref.refs_3_ = bf16[128,1024]{1,0:T(8,128)(2,1)S(1)} collective-permute-done((bf16[128,1024]{1,0:T(8,128)(2,1)}, bf16[128,1024]{1,0:T(8,128)(2,1)S(1)}, u32[]{:S(2)}, u32[]{:S(2)}) %collective-permute-start.1) | collective-permute-done | bytes 262176 | tf_op jit(solution)/shard_map/ppermute | solution.py:394
  23.8 0.7 collective-permute-start.4
  24.4 2.7 %collective-permute-start.5 = (bf16[128,1024]{1,0:T(8,128)(2,1)S(1)}, bf16[128,1024]{1,0:T(8,128)(2,1)S(1)}, u32[]{:S(2)}, u32[]{:S(2)}) collective-permute-start(bf16[128,1024]{1,0:T(8,128)(2,1)S(1)} %get-tuple-element.57.after_ref), channel_id=1, source_target_pairs={{0,1},{2,3},{1,0},{3,2},{4,5},{6,7},{5,4},{7,6},{8,9},{10,11},{9,8... | collective-permute-start | bytes 786440 | tf_op jit(solution)/shard_map/ppermute | solution.py:394
  27.1 1.4 %collective-permute-done.7.arrived_too_ref.refs_6_ = bf16[128,1024]{1,0:T(8,128)(2,1)S(1)} collective-permute-done((bf16[128,1024]{1,0:T(8,128)(2,1)S(1)}, bf16[128,1024]{1,0:T(8,128)(2,1)S(1)}, u32[]{:S(2)}, u32[]{:S(2)}) %collective-permute-start.7) | collective-permute-done | bytes 262176 | tf_op jit(solution)/shard_map/ppermute | solution.py:394
  29.4 2.7 %collective-permute-start.11 = (bf16[128,1024]{1,0:T(8,128)(2,1)S(1)}, bf16[128,1024]{1,0:T(8,128)(2,1)S(1)}, u32[]{:S(2)}, u32[]{:S(2)}) collective-permute-start(bf16[128,1024]{1,0:T(8,128)(2,1)S(1)} %get-tuple-element.62.after_ref), channel_id=1, source_target_pairs={{0,1},{2,3},{1,0},{3,2},{4,5},{6,7},{5,4},{7,6},{8,9},{10,11},{9,8... | collective-permute-start | bytes 786440 | tf_op jit(solution)/shard_map/ppermute | solution.py:394
  32.1 2.1 %collective-permute-done.5.arrived_too_ref.refs_7_ = bf16[128,1024]{1,0:T(8,128)(2,1)S(1)} collective-permute-done((bf16[128,1024]{1,0:T(8,128)(2,1)S(1)}, bf16[128,1024]{1,0:T(8,128)(2,1)S(1)}, u32[]{:S(2)}, u32[]{:S(2)}) %collective-permute-start.5) | collective-permute-done | bytes 262176 | tf_op jit(solution)/shard_map/ppermute | solution.py:394
  34.3 0.7 collective-permute-start.8
  35.0 2.7 %collective-permute-start.9 = (bf16[128,1024]{1,0:T(8,128)(2,1)S(1)}, bf16[128,1024]{1,0:T(8,128)(2,1)S(1)}, u32[]{:S(2)}, u32[]{:S(2)}) collective-permute-start(bf16[128,1024]{1,0:T(8,128)(2,1)S(1)} %get-tuple-element.65.after_ref), channel_id=1, source_target_pairs={{0,1},{2,3},{1,0},{3,2},{4,5},{6,7},{5,4},{7,6},{8,9},{10,11},{9,8... | collective-permute-start | bytes 786440 | tf_op jit(solution)/shard_map/ppermute | solution.py:394
  37.7 2.0 %collective-permute-done.11.arrived_too_ref.refs_10_ = bf16[128,1024]{1,0:T(8,128)(2,1)S(1)} collective-permute-done((bf16[128,1024]{1,0:T(8,128)(2,1)S(1)}, bf16[128,1024]{1,0:T(8,128)(2,1)S(1)}, u32[]{:S(2)}, u32[]{:S(2)}) %collective-permute-start.11) | collective-permute-done | bytes 262176 | tf_op jit(solution)/shard_map/ppermute | solution.py:394
  39.9 1.2 %collective-permute-start.14 = (bf16[128,1024]{1,0:T(8,128)(2,1)S(1)}, bf16[128,1024]{1,0:T(8,128)(2,1)S(1)}, u32[]{:S(2)}, u32[]{:S(2)}) collective-permute-start(bf16[128,1024]{1,0:T(8,128)(2,1)S(1)} %get-tuple-element.70.after_ref), channel_id=1, source_target_pairs={{0,1},{2,3},{1,0},{3,2},{4,5},{6,7},{5,4},{7,6},{8,9},{10,11},{9,8... | collective-permute-start | bytes 786440 | tf_op jit(solution)/shard_map/ppermute | solution.py:394
  41.8 3.5 %collective-permute-done.9.arrived_too_ref.refs_11_ = bf16[128,1024]{1,0:T(8,128)(2,1)S(1)} collective-permute-done((bf16[128,1024]{1,0:T(8,128)(2,1)S(1)}, bf16[128,1024]{1,0:T(8,128)(2,1)S(1)}, u32[]{:S(2)}, u32[]{:S(2)}) %collective-permute-start.9) | collective-permute-done | bytes 262176 | tf_op jit(solution)/shard_map/ppermute | solution.py:394
  45.5 1.2 %collective-permute-start.12 = (bf16[128,1024]{1,0:T(8,128)(2,1)S(1)}, bf16[128,1024]{1,0:T(8,128)(2,1)S(1)}, u32[]{:S(2)}, u32[]{:S(2)}) collective-permute-start(bf16[128,1024]{1,0:T(8,128)(2,1)S(1)} %get-tuple-element.71.after_ref), channel_id=1, source_target_pairs={{0,1},{2,3},{1,0},{3,2},{4,5},{6,7},{5,4},{7,6},{8,9},{10,11},{9,8... | collective-permute-start | bytes 786440 | tf_op jit(solution)/shard_map/ppermute | solution.py:394
  47.4 3.5 %collective-permute-done.14.one_ref = bf16[128,1024]{1,0:T(8,128)(2,1)S(1)} collective-permute-done((bf16[128,1024]{1,0:T(8,128)(2,1)S(1)}, bf16[128,1024]{1,0:T(8,128)(2,1)S(1)}, u32[]{:S(2)}, u32[]{:S(2)}) %collective-permute-start.14) | collective-permute-done | bytes 262176 | tf_op jit(solution)/shard_map/ppermute | solution.py:394
  51.1 1.3 %collective-permute-start.21 = (bf16[112,1024]{1,0:T(8,128)(2,1)S(1)}, bf16[112,1024]{1,0:T(8,128)(2,1)S(1)}, u32[]{:S(2)}, u32[]{:S(2)}) collective-permute-start(bf16[112,1024]{1,0:T(8,128)(2,1)S(1)} %get-tuple-element.75.after_ref.own_ref), channel_id=1, source_target_pairs={{0,8},{4,12},{8,0},{12,4},{1,9},{5,13},{9,1},{13,5},{2,10},{6,14},... | collective-permute-start | bytes 688136 | tf_op jit(solution)/shard_map/ppermute | solution.py:417
  52.4 4.2 %collective-permute-done.12.one_ref = bf16[128,1024]{1,0:T(8,128)(2,1)S(1)} collective-permute-done((bf16[128,1024]{1,0:T(8,128)(2,1)S(1)}, bf16[128,1024]{1,0:T(8,128)(2,1)S(1)}, u32[]{:S(2)}, u32[]{:S(2)}) %collective-permute-start.12) | collective-permute-done | bytes 262176 | tf_op jit(solution)/shard_map/ppermute | solution.py:394
  56.8 1.3 %collective-permute-start.19 = (bf16[144,1024]{1,0:T(8,128)(2,1)S(1)}, bf16[144,1024]{1,0:T(8,128)(2,1)S(1)}, u32[]{:S(2)}, u32[]{:S(2)}) collective-permute-start(bf16[144,1024]{1,0:T(8,128)(2,1)S(1)} %summed_grad.3.after_ref.own_ref), channel_id=1, source_target_pairs={{0,8},{4,12},{8,0},{12,4},{1,9},{5,13},{9,1},{13,5},{2,10},{6,14},... | collective-permute-start | bytes 884744 | tf_op jit(solution)/shard_map/ppermute | solution.py:417
  58.1 2.0 %collective-permute-start.20 = (bf16[112,1024]{1,0:T(8,128)(2,1)S(1)}, bf16[112,1024]{1,0:T(8,128)(2,1)S(1)}, u32[]{:S(2)}, u32[]{:S(2)}) collective-permute-start(bf16[112,1024]{1,0:T(8,128)(2,1)S(1)} %get-tuple-element.75.after_ref.own_ref), channel_id=1, source_target_pairs={{0,4},{4,0},{8,12},{12,8},{1,5},{5,1},{9,13},{13,9},{2,6},{6,2},{1... | collective-permute-start | bytes 688136 | tf_op jit(solution)/shard_map/ppermute | solution.py:416
  60.0 2.9 %context_grad.1 = (bf16[512,1024]{1,0:T(8,128)(2,1)}, f32[8,128]{1,0:T(8,128)S(1)}) custom-call(s32[2]{0:T(128)S(1)} %copy-done.9, bf16[512,1024]{1,0:T(8,128)(2,1)S(1)} %bitcast.18, bf16[144,1024]{1,0:T(8,128)(2,1)S(1)} %summed_grad.3.after_ref.own_ref, bf16[128,1024]{1,0:T(8,128)(2,1)S(1)} %copy-done.7, bf16[128,1024]{1,0:T(8,128)(2,1)S(1)} %copy-done.8, ...), custom_call_target="tpu_custom_call" | custom-call | bytes 1024 | tf_op jit(solution)/shard_map/context_grad/pallas_call | solution.py:257
  63.5 0.9 %taken_state.1 = (f32[336,1024]{1,0:T(8,128)S(1)}, f32[432,1024]{1,0:T(8,128)S(1)}) custom-call(s32[2]{0:T(128)S(1)} %copy-done.9, s32[4]{0:T(128)S(1)} %copy-done.10, bf16[128,1024]{1,0:T(8,128)(2,1)S(1)} %get-tuple-element.71.after_ref, f32[256,1024]{1,0:T(8,128)S(1)} %bitcast.12, f32[256,1024]{1,0:T(8,128)S(1)} %bitcast.14, f32[256,1024]{1,0:T(8,128)S(1)} %bitcast.16, ...), custom_call_target="tpu_custom_call" | custom-call | bytes 1024 | tf_op jit(solution)/shard_map/taken_state/pallas_call | solution.py:306
  64.5 1.5 %adam.2 = (f32[256,1024]{1,0:T(8,128)}, f32[256,1024]{1,0:T(8,128)}, f32[256,1024]{1,0:T(8,128)}, f32[8,128]{1,0:T(8,128)S(1)}) custom-call(f32[8,1024]{1,0:T(8,128)S(1)} %copy-done.6, f32[336,1024]{1,0:T(8,128)S(1)} %get-tuple-element.81.state_ref, bf16[112,1024]{1,0:T(8,128)(2,1)S(1)} %get-tuple-element.75.after_ref.own_ref, ...), custom_call_target="tpu_custom_call" | custom-call | bytes 1024 | tf_op jit(solution)/shard_map/adam/pallas_call | solution.py:352
  66.0 1.0 %collective-permute-start.23 = (bf16[144,1024]{1,0:T(8,128)(2,1)S(1)}, bf16[144,1024]{1,0:T(8,128)(2,1)S(1)}, u32[]{:S(2)}, u32[]{:S(2)}) collective-permute-start(bf16[144,1024]{1,0:T(8,128)(2,1)S(1)} %gate.3.across_ref), channel_id=1, source_target_pairs={{0,4},{4,0},{8,12},{12,8},{1,5},{5,1},{9,13},{13,9},{2,6},{6,2},{1... | collective-permute-start | bytes 884744 | tf_op jit(solution)/shard_map/ppermute | solution.py:418
  67.0 1.2 %collective-permute-done.23.far_ref = bf16[144,1024]{1,0:T(8,128)(2,1)S(1)} collective-permute-done((bf16[144,1024]{1,0:T(8,128)(2,1)S(1)}, bf16[144,1024]{1,0:T(8,128)(2,1)S(1)}, u32[]{:S(2)}, u32[]{:S(2)}) %collective-permute-start.23) | collective-permute-done | bytes 294944 | tf_op jit(solution)/shard_map/ppermute | solution.py:418
  68.2 2.3 %adam.3 = (f32[256,1024]{1,0:T(8,128)}, f32[256,1024]{1,0:T(8,128)}, f32[256,1024]{1,0:T(8,128)}, f32[8,128]{1,0:T(8,128)}) custom-call(f32[8,1024]{1,0:T(8,128)S(1)} %copy-done.6, f32[432,1024]{1,0:T(8,128)S(1)} %get-tuple-element.80.state_ref, ...), custom_call_target="tpu_custom_call", output_to_operand_aliasing={{0}: (7, {}), {1}: (8, {}), {2}: (9, {})} | custom-call | bytes 1024 | tf_op jit(solution)/shard_map/adam/pallas_call | solution.py:352
  (56 shorter events, 5.2 us)
Async XLA Ops:
  1.2 12.4 %copy-start.3 = (bf16[1,512,1024]{2,1,0:T(8,128)(2,1)S(1)}, bf16[1,512,1024]{2,1,0:T(8,128)(2,1)}, u32[]{:S(2)}) copy-start(bf16[1,512,1024]{2,1,0:T(8,128)(2,1)} %param.10) | copy-start | bytes 3145732
  1.2 12.4 %copy-start.5 = (bf16[1,512,1024]{2,1,0:T(8,128)(2,1)S(1)}, bf16[1,512,1024]{2,1,0:T(8,128)(2,1)}, u32[]{:S(2)}) copy-start(bf16[1,512,1024]{2,1,0:T(8,128)(2,1)} %param.9) | copy-start | bytes 3145732
  1.2 12.4 %copy-start.9 = (s32[2]{0:T(128)S(1)}, s32[2]{0:T(128)}, u32[]{:S(2)}) copy-start(s32[2]{0:T(128)} %pad_add_fusion.where_ref.refs_0_) | copy-start | bytes 28
  5.3 10.7 %copy-start.4 = (bf16[768,1024]{1,0:T(8,128)(2,1)S(1)}, bf16[768,1024]{1,0:T(8,128)(2,1)}, u32[]{:S(2)}) copy-start(bf16[768,1024]{1,0:T(8,128)(2,1)} %get-tuple-element.79.own_ref) | copy-start | bytes 4718596
  5.3 10.7 %copy-start.6 = (f32[8,1024]{1,0:T(8,128)S(1)}, f32[8,1024]{1,0:T(8,128)}, u32[]{:S(2)}) copy-start(f32[8,1024]{1,0:T(8,128)} %get-tuple-element.78.choices_ref) | copy-start | bytes 98308
  5.3 10.6 %collective-permute-start.16 = (bf16[768,1024]{1,0:T(8,128)(2,1)}, bf16[768,1024]{1,0:T(8,128)(2,1)S(1)}, u32[]{:S(2)}, u32[]{:S(2)}) collective-permute-start(bf16[768,1024]{1,0:T(8,128)(2,1)} %get-tuple-element.79.own_ref), channel_id=1, source_target_pairs={{0,4},{4,0},{8,12},{12,8},{1,5},{5,1},{9,13},{13,9},{2,6},{6,2},{1... | collective-permute-start | bytes 4718600 | tf_op jit(solution)/shard_map/ppermute | solution.py:397
  5.5 12.5 %collective-permute-start.2 = (bf16[128,1024]{1,0:T(8,128)(2,1)}, bf16[128,1024]{1,0:T(8,128)(2,1)S(1)}, u32[]{:S(2)}, u32[]{:S(2)}) collective-permute-start(bf16[128,1024]{1,0:T(8,128)(2,1)} %get-tuple-element.51.after_ref.refs_0_), channel_id=1, source_target_pairs={{1,2},{2,1},{5,6},{6,5},{9,10},{10,9},{13,14},{14,13},{17,18},{18,... | collective-permute-start | bytes 786440 | tf_op jit(solution)/shard_map/ppermute | solution.py:394
  6.3 11.7 %collective-permute-start.3 = (bf16[128,1024]{1,0:T(8,128)(2,1)}, bf16[128,1024]{1,0:T(8,128)(2,1)S(1)}, u32[]{:S(2)}, u32[]{:S(2)}) collective-permute-start(bf16[128,1024]{1,0:T(8,128)(2,1)} %get-tuple-element.51.after_ref.refs_0_), channel_id=1, source_target_pairs={{0,1},{2,3},{1,0},{3,2},{4,5},{6,7},{5,4},{7,6},{8,9},{10,11},{9,8... | collective-permute-start | bytes 786440 | tf_op jit(solution)/shard_map/ppermute | solution.py:394
  11.5 10.0 %collective-permute-start = (bf16[128,1024]{1,0:T(8,128)(2,1)}, bf16[128,1024]{1,0:T(8,128)(2,1)S(1)}, u32[]{:S(2)}, u32[]{:S(2)}) collective-permute-start(bf16[128,1024]{1,0:T(8,128)(2,1)} %get-tuple-element.48.refs_1_), channel_id=1, source_target_pairs={{1,2},{2,1},{5,6},{6,5},{9,10},{10,9},{13,14},{14,13},{17,18},{18,... | collective-permute-start | bytes 786440 | tf_op jit(solution)/shard_map/ppermute | solution.py:394
  12.1 11.5 %collective-permute-start.1 = (bf16[128,1024]{1,0:T(8,128)(2,1)}, bf16[128,1024]{1,0:T(8,128)(2,1)S(1)}, u32[]{:S(2)}, u32[]{:S(2)}) collective-permute-start(bf16[128,1024]{1,0:T(8,128)(2,1)} %get-tuple-element.48.refs_1_), channel_id=1, source_target_pairs={{0,1},{2,3},{1,0},{3,2},{4,5},{6,7},{5,4},{7,6},{8,9},{10,11},{9,8... | collective-permute-start | bytes 786440 | tf_op jit(solution)/shard_map/ppermute | solution.py:394
  16.7 46.8 %collective-permute-start.17 = (bf16[768,1024]{1,0:T(8,128)(2,1)S(1)}, bf16[768,1024]{1,0:T(8,128)(2,1)S(1)}, u32[]{:S(2)}, u32[]{:S(2)}) collective-permute-start(bf16[768,1024]{1,0:T(8,128)(2,1)S(1)} %pick.1), channel_id=1, source_target_pairs={{0,8},{4,12},{8,0},{12,4},{1,9},{5,13},{9,1},{13,5},{2,10},{6,14},... | collective-permute-start | bytes 4718600 | tf_op jit(solution)/shard_map/ppermute | solution.py:398
  18.2 9.0 %collective-permute-start.6 = (bf16[128,1024]{1,0:T(8,128)(2,1)S(1)}, bf16[128,1024]{1,0:T(8,128)(2,1)S(1)}, u32[]{:S(2)}, u32[]{:S(2)}) collective-permute-start(bf16[128,1024]{1,0:T(8,128)(2,1)S(1)} %get-tuple-element.59), channel_id=1, source_target_pairs={{1,2},{2,1},{5,6},{6,5},{9,10},{10,9},{13,14},{14,13},{17,18},{18,... | collective-permute-start | bytes 786440 | tf_op jit(solution)/shard_map/ppermute | solution.py:394
  18.8 9.7 %collective-permute-start.7 = (bf16[128,1024]{1,0:T(8,128)(2,1)S(1)}, bf16[128,1024]{1,0:T(8,128)(2,1)S(1)}, u32[]{:S(2)}, u32[]{:S(2)}) collective-permute-start(bf16[128,1024]{1,0:T(8,128)(2,1)S(1)} %get-tuple-element.54.after_ref), channel_id=1, source_target_pairs={{0,1},{2,3},{1,0},{3,2},{4,5},{6,7},{5,4},{7,6},{8,9},{10,11},{9,8... | collective-permute-start | bytes 786440 | tf_op jit(solution)/shard_map/ppermute | solution.py:394
  23.8 8.3 %collective-permute-start.4 = (bf16[128,1024]{1,0:T(8,128)(2,1)S(1)}, bf16[128,1024]{1,0:T(8,128)(2,1)S(1)}, u32[]{:S(2)}, u32[]{:S(2)}) collective-permute-start(bf16[128,1024]{1,0:T(8,128)(2,1)S(1)} %get-tuple-element.55), channel_id=1, source_target_pairs={{1,2},{2,1},{5,6},{6,5},{9,10},{10,9},{13,14},{14,13},{17,18},{18,... | collective-permute-start | bytes 786440 | tf_op jit(solution)/shard_map/ppermute | solution.py:394
  24.4 9.7 %collective-permute-start.5 = (bf16[128,1024]{1,0:T(8,128)(2,1)S(1)}, bf16[128,1024]{1,0:T(8,128)(2,1)S(1)}, u32[]{:S(2)}, u32[]{:S(2)}) collective-permute-start(bf16[128,1024]{1,0:T(8,128)(2,1)S(1)} %get-tuple-element.57.after_ref), channel_id=1, source_target_pairs={{0,1},{2,3},{1,0},{3,2},{4,5},{6,7},{5,4},{7,6},{8,9},{10,11},{9,8... | collective-permute-start | bytes 786440 | tf_op jit(solution)/shard_map/ppermute | solution.py:394
  28.7 9.0 %collective-permute-start.10 = (bf16[128,1024]{1,0:T(8,128)(2,1)S(1)}, bf16[128,1024]{1,0:T(8,128)(2,1)S(1)}, u32[]{:S(2)}, u32[]{:S(2)}) collective-permute-start(bf16[128,1024]{1,0:T(8,128)(2,1)S(1)} %get-tuple-element.67), channel_id=1, source_target_pairs={{1,2},{2,1},{5,6},{6,5},{9,10},{10,9},{13,14},{14,13},{17,18},{18,... | collective-permute-start | bytes 786440 | tf_op jit(solution)/shard_map/ppermute | solution.py:394
  29.4 10.3 %collective-permute-start.11 = (bf16[128,1024]{1,0:T(8,128)(2,1)S(1)}, bf16[128,1024]{1,0:T(8,128)(2,1)S(1)}, u32[]{:S(2)}, u32[]{:S(2)}) collective-permute-start(bf16[128,1024]{1,0:T(8,128)(2,1)S(1)} %get-tuple-element.62.after_ref), channel_id=1, source_target_pairs={{0,1},{2,3},{1,0},{3,2},{4,5},{6,7},{5,4},{7,6},{8,9},{10,11},{9,8... | collective-permute-start | bytes 786440 | tf_op jit(solution)/shard_map/ppermute | solution.py:394
  34.3 7.5 %collective-permute-start.8 = (bf16[128,1024]{1,0:T(8,128)(2,1)S(1)}, bf16[128,1024]{1,0:T(8,128)(2,1)S(1)}, u32[]{:S(2)}, u32[]{:S(2)}) collective-permute-start(bf16[128,1024]{1,0:T(8,128)(2,1)S(1)} %get-tuple-element.63), channel_id=1, source_target_pairs={{1,2},{2,1},{5,6},{6,5},{9,10},{10,9},{13,14},{14,13},{17,18},{18,... | collective-permute-start | bytes 786440 | tf_op jit(solution)/shard_map/ppermute | solution.py:394
  35.0 10.3 %collective-permute-start.9 = (bf16[128,1024]{1,0:T(8,128)(2,1)S(1)}, bf16[128,1024]{1,0:T(8,128)(2,1)S(1)}, u32[]{:S(2)}, u32[]{:S(2)}) collective-permute-start(bf16[128,1024]{1,0:T(8,128)(2,1)S(1)} %get-tuple-element.65.after_ref), channel_id=1, source_target_pairs={{0,1},{2,3},{1,0},{3,2},{4,5},{6,7},{5,4},{7,6},{8,9},{10,11},{9,8... | collective-permute-start | bytes 786440 | tf_op jit(solution)/shard_map/ppermute | solution.py:394
  39.9 11.1 %collective-permute-start.14 = (bf16[128,1024]{1,0:T(8,128)(2,1)S(1)}, bf16[128,1024]{1,0:T(8,128)(2,1)S(1)}, u32[]{:S(2)}, u32[]{:S(2)}) collective-permute-start(bf16[128,1024]{1,0:T(8,128)(2,1)S(1)} %get-tuple-element.70.after_ref), channel_id=1, source_target_pairs={{0,1},{2,3},{1,0},{3,2},{4,5},{6,7},{5,4},{7,6},{8,9},{10,11},{9,8... | collective-permute-start | bytes 786440 | tf_op jit(solution)/shard_map/ppermute | solution.py:394
  41.1 9.8 %collective-permute-start.15 = (bf16[128,1024]{1,0:T(8,128)(2,1)S(1)}, bf16[128,1024]{1,0:T(8,128)(2,1)S(1)}, u32[]{:S(2)}, u32[]{:S(2)}) collective-permute-start(bf16[128,1024]{1,0:T(8,128)(2,1)S(1)} %get-tuple-element.74), channel_id=1, source_target_pairs={{1,2},{2,1},{5,6},{6,5},{9,10},{10,9},{13,14},{14,13},{17,18},{18,... | collective-permute-start | bytes 786440 | tf_op jit(solution)/shard_map/ppermute | solution.py:394
  45.5 14.5 %copy-start.8 = (bf16[128,1024]{1,0:T(8,128)(2,1)S(1)}, bf16[128,1024]{1,0:T(8,128)(2,1)}, u32[]{:S(2)}) copy-start(bf16[128,1024]{1,0:T(8,128)(2,1)} %get-tuple-element.48.refs_1_) | copy-start | bytes 786436
  45.5 11.1 %collective-permute-start.12 = (bf16[128,1024]{1,0:T(8,128)(2,1)S(1)}, bf16[128,1024]{1,0:T(8,128)(2,1)S(1)}, u32[]{:S(2)}, u32[]{:S(2)}) collective-permute-start(bf16[128,1024]{1,0:T(8,128)(2,1)S(1)} %get-tuple-element.71.after_ref), channel_id=1, source_target_pairs={{0,1},{2,3},{1,0},{3,2},{4,5},{6,7},{5,4},{7,6},{8,9},{10,11},{9,8... | collective-permute-start | bytes 786440 | tf_op jit(solution)/shard_map/ppermute | solution.py:394
  46.8 9.8 %collective-permute-start.13 = (bf16[128,1024]{1,0:T(8,128)(2,1)S(1)}, bf16[128,1024]{1,0:T(8,128)(2,1)S(1)}, u32[]{:S(2)}, u32[]{:S(2)}) collective-permute-start(bf16[128,1024]{1,0:T(8,128)(2,1)S(1)} %get-tuple-element.72), channel_id=1, source_target_pairs={{1,2},{2,1},{5,6},{6,5},{9,10},{10,9},{13,14},{14,13},{17,18},{18,... | collective-permute-start | bytes 786440 | tf_op jit(solution)/shard_map/ppermute | solution.py:394
  51.1 11.8 %collective-permute-start.21 = (bf16[112,1024]{1,0:T(8,128)(2,1)S(1)}, bf16[112,1024]{1,0:T(8,128)(2,1)S(1)}, u32[]{:S(2)}, u32[]{:S(2)}) collective-permute-start(bf16[112,1024]{1,0:T(8,128)(2,1)S(1)} %get-tuple-element.75.after_ref.own_ref), channel_id=1, source_target_pairs={{0,8},{4,12},{8,0},{12,4},{1,9},{5,13},{9,1},{13,5},{2,10},{6,14},... | collective-permute-start | bytes 688136 | tf_op jit(solution)/shard_map/ppermute | solution.py:417
  56.7 6.7 %copy-start = (f32[1,256,1024]{2,1,0:T(8,128)S(1)}, f32[1,256,1024]{2,1,0:T(8,128)}, u32[]{:S(2)}) copy-start(f32[1,256,1024]{2,1,0:T(8,128)} %param.11) | copy-start | bytes 3145732
  56.7 6.7 %copy-start.1 = (f32[1,256,1024]{2,1,0:T(8,128)S(1)}, f32[1,256,1024]{2,1,0:T(8,128)}, u32[]{:S(2)}) copy-start(f32[1,256,1024]{2,1,0:T(8,128)} %param.12) | copy-start | bytes 3145732
  56.8 9.2 %collective-permute-start.19 = (bf16[144,1024]{1,0:T(8,128)(2,1)S(1)}, bf16[144,1024]{1,0:T(8,128)(2,1)S(1)}, u32[]{:S(2)}, u32[]{:S(2)}) collective-permute-start(bf16[144,1024]{1,0:T(8,128)(2,1)S(1)} %summed_grad.3.after_ref.own_ref), channel_id=1, source_target_pairs={{0,8},{4,12},{8,0},{12,4},{1,9},{5,13},{9,1},{13,5},{2,10},{6,14},... | collective-permute-start | bytes 884744 | tf_op jit(solution)/shard_map/ppermute | solution.py:417
  58.1 6.4 %collective-permute-start.20 = (bf16[112,1024]{1,0:T(8,128)(2,1)S(1)}, bf16[112,1024]{1,0:T(8,128)(2,1)S(1)}, u32[]{:S(2)}, u32[]{:S(2)}) collective-permute-start(bf16[112,1024]{1,0:T(8,128)(2,1)S(1)} %get-tuple-element.75.after_ref.own_ref), channel_id=1, source_target_pairs={{0,4},{4,0},{8,12},{12,8},{1,5},{5,1},{9,13},{13,9},{2,6},{6,2},{1... | collective-permute-start | bytes 688136 | tf_op jit(solution)/shard_map/ppermute | solution.py:416
  62.9 1.6 %collective-permute-start.22 = (bf16[112,1024]{1,0:T(8,128)(2,1)S(1)}, bf16[112,1024]{1,0:T(8,128)(2,1)S(1)}, u32[]{:S(2)}, u32[]{:S(2)}) collective-permute-start(bf16[112,1024]{1,0:T(8,128)(2,1)S(1)} %gate.2.across_ref), channel_id=1, source_target_pairs={{0,4},{4,0},{8,12},{12,8},{1,5},{5,1},{9,13},{13,9},{2,6},{6,2},{1... | collective-permute-start | bytes 688136 | tf_op jit(solution)/shard_map/ppermute | solution.py:418
  63.0 4.0 %collective-permute-start.18 = (bf16[144,1024]{1,0:T(8,128)(2,1)S(1)}, bf16[144,1024]{1,0:T(8,128)(2,1)S(1)}, u32[]{:S(2)}, u32[]{:S(2)}) collective-permute-start(bf16[144,1024]{1,0:T(8,128)(2,1)S(1)} %summed_grad.3.after_ref.own_ref), channel_id=1, source_target_pairs={{0,4},{4,0},{8,12},{12,8},{1,5},{5,1},{9,13},{13,9},{2,6},{6,2},{1... | collective-permute-start | bytes 884744 | tf_op jit(solution)/shard_map/ppermute | solution.py:416
  66.0 2.2 %collective-permute-start.23 = (bf16[144,1024]{1,0:T(8,128)(2,1)S(1)}, bf16[144,1024]{1,0:T(8,128)(2,1)S(1)}, u32[]{:S(2)}, u32[]{:S(2)}) collective-permute-start(bf16[144,1024]{1,0:T(8,128)(2,1)S(1)} %gate.3.across_ref), channel_id=1, source_target_pairs={{0,4},{4,0},{8,12},{12,8},{1,5},{5,1},{9,13},{13,9},{2,6},{6,2},{1... | collective-permute-start | bytes 884744 | tf_op jit(solution)/shard_map/ppermute | solution.py:418
  (3 other events, 15.5 us)

commit v12 on v11

--- a/solution.py
+++ b/solution.py
@@ -74,7 +74,7 @@
 
 
 def halves_kernel(parts, weight_ref, first_ref, second_ref, *refs):
-    tables, (state_ref, choices_ref), own_refs, (full, sems) = refs[:5], refs[5:7], refs[7:-2], refs[-2:]
+    state_ref, own_refs, (full, sems) = refs[0], refs[1:-2], refs[-2:]
     rows = weight_ref.shape[0]
     copies = []
     for k, ref in enumerate((weight_ref, first_ref, second_ref)):
@@ -83,7 +83,6 @@
                 ref.at[pl.ds(start, size), :], full.at[k, pl.ds(start, size), :], sems.at[k * len(parts) + c]
             ))
             copies[-1].start()
-    make_choices(*tables, choices_ref)
     for k in range(3):
         for c, (start, size) in enumerate(parts):
             copies[k * len(parts) + c].wait()
@@ -93,15 +92,14 @@
             state_ref[k * rows + start:k * rows + start + size, :] = rounded
 
 
-def halves(parts, arrays, tables):
+def halves(parts, arrays):
     rows, depth = arrays[0].shape
-    shapes = [half_array(3 * rows, depth), jax.ShapeDtypeStruct((8, depth), jnp.float32)]
-    shapes += [half_array(size, depth) for _, size in parts]
+    shapes = [half_array(3 * rows, depth)] + [half_array(size, depth) for _, size in parts]
     return call(
         functools.partial(halves_kernel, parts), "halves",
-        shapes, [HBM] * 3 + [SMEM] * 5, [VMEM] * len(shapes), limit=56,
+        shapes, [HBM] * 3, [VMEM] * len(shapes), limit=56,
         scratch=[pltpu.VMEM((3, rows, depth), jnp.float32), pltpu.SemaphoreType.DMA((3 * len(parts),))],
-    )(*arrays, *tables)
+    )(*arrays)
 
 
 def pick_kernel(choices_ref, own_ref, mate_ref, after_ref, out_ref):
@@ -119,8 +117,8 @@
     )
 
 
-def partial_kernel(n, scale, parts, order, where_ref, context_ref, cotangent_ref, *refs):
-    outs, (product, rounded, out_sems) = refs[:-3], refs[-3:]
+def partial_kernel(n, scale, parts, order, context_ref, cotangent_ref, where_ref, *refs):
+    tables, choices_ref, outs, (product, rounded, out_sems) = refs[:4], refs[4], refs[5:-3], refs[-3:]
     width = product.shape[0]
     rows = width // n
     me = where_ref[0]
@@ -152,26 +150,28 @@
             write(rounded, first_row + start, size)
     for start, size in parts:
         write(product, me * rows + start, size)
+    make_choices(where_ref, *tables, choices_ref)
     for copy in writes:
         copy.wait()
 
 
-def partial_blocks(n, scale, parts, order, where, context_rows, cotangent):
+def partial_blocks(n, scale, parts, order, context_rows, cotangent, tables):
     tokens, width = context_rows.shape
     depth = cotangent.shape[1]
     outs = (len(order) + 1) * len(parts)
-    flat = call(
+    choices, *flat = call(
         functools.partial(partial_kernel, n, scale, parts, order), "partial_blocks",
-        [half_array(size, depth) for _, size in parts] * len(order)
+        [jax.ShapeDtypeStruct((8, depth), jnp.float32)]
+        + [half_array(size, depth) for _, size in parts] * len(order)
         + [jax.ShapeDtypeStruct((size, depth), jnp.float32) for _, size in parts],
-        [SMEM, VMEM, VMEM], [HBM] * outs, limit=14,
+        [VMEM] * 2 + [SMEM] * 5, [VMEM] + [HBM] * outs, limit=14,
         scratch=[
             pltpu.VMEM((width, depth), jnp.float32),
             pltpu.VMEM((width + width // n, depth), jnp.bfloat16),
             pltpu.SemaphoreType.DMA((outs,)),
         ],
-    )(where, context_rows, cotangent)
-    return [flat[k * len(parts):(k + 1) * len(parts)] for k in range(len(order) + 1)]
+    )(context_rows, cotangent, *tables)
+    return choices, [flat[k * len(parts):(k + 1) * len(parts)] for k in range(len(order) + 1)]
 
 
 def send_kernel(arrived_ref, term_ref, arrived_too_ref, term_too_ref, after_ref, out_ref, out_too_ref):
@@ -377,9 +377,10 @@
         swaps.append(pairs + [(b, a) for a, b in pairs])
 
     arrays = (weight[0], first[0], second[0])
-    state, choices, *own = halves(parts, arrays, (where, rates, decays, steps, donor))
+    state, *own = halves(parts, arrays)
     order = [(slot, swap) for slot in range(2, n + 1) for swap in range(2)]
-    terms = partial_blocks(n, scale, parts, order, where, context_rows, cotangent)
+    tables = (where, rates, decays, steps, donor)
+    choices, terms = partial_blocks(n, scale, parts, order, context_rows, cotangent, tables)
 
     arrived = [[own, own]]
     sent = own[0]

time: 71.2 us -> 70.3 us (0.987)
  waiting for transfers between devices: 20.2 us -> 15 us
  starting transfers between devices: 32.8 us -> 35.1 us
  local copies, waits for them, and re-layouts: 0.06 us -> 1.38 us
    ppermute x16, waiting for transfers between devices: 18.9 us -> 13.7 us  [on_device(): now[swap].append(lax.ppermute(blocks[swap], 'shard', swaps[swap]))]
    unnamed x22 -> x24, local copies, waits for them, and re-layouts: 0.06 us -> 1.38 us
    ppermute x2, starting transfers between devices: 2.45 us -> 3.55 us  [on_device(): mate = lax.ppermute(grads[c], 'member', swap_mates)]
    pallas_call x6, Pallas kernels: 0.94 us -> 1.89 us  [to_send(): call(send_kernel, 'to_send', [like] * 2, [VMEM] * 4 + [ANY], [VMEM] * 2,...]
    pallas_call x1, Pallas kernels: 4.08 us -> 3.31 us  [halves(): call(functools.partial(halves_kernel, parts), 'halves', shapes, [HBM] * 3...]
    ppermute x16, starting transfers between devices: 25.4 us -> 26.1 us  [on_device(): now[swap].append(lax.ppermute(blocks[swap], 'shard', swaps[swap]))]
  transfers between devices with their start and end apart: 24 -> 24, of which waited for: 8 -> 9; matrix products, arithmetic and copies ran while one was open for 0% -> 0% of each run, Pallas kernels for 13% -> 16%
where the time goes in v12:
time: 70.3 us; the launch traced here: 69.2 us
  starting transfers between devices  35.1 us (50%)
  Pallas kernels  16.6 us (24%)
  waiting for transfers between devices  15 us (21%)
  local copies, waits for them, and re-layouts  1.38 us (2%)
  between operations  1 us (1%)
    ppermute x16, starting transfers between devices, on_device(): now[swap].append(lax.ppermute(blocks[swap], 'shard', swaps[swap]))  26.1 us
    ppermute x16, waiting for transfers between devices, on_device(): now[swap].append(lax.ppermute(blocks[swap], 'shard', swaps[swap]))  13.7 us
    pallas_call x2, Pallas kernels, adam_update(): call(functools.partial(adam_kernel, start, size, bool(filled)), 'adam', [...  3.86 us
    ppermute x2, starting transfers between devices, on_device(): mate = lax.ppermute(grads[c], 'member', swap_mates)  3.55 us
    pallas_call x1, Pallas kernels, halves(): call(functools.partial(halves_kernel, parts), 'halves', shapes, [HBM] * 3...  3.31 us
    pallas_call x1, Pallas kernels, columns(): call(functools.partial(columns_kernel, n, scale, parts), 'context_grad',...  3.27 us
    ppermute x2, starting transfers between devices, on_device(): across = gate(lax.ppermute(grads[c], 'member', swap_across), computed)  3.1 us
    pallas_call x1, Pallas kernels, partial_blocks(): call(functools.partial(partial_kernel, n, scale, parts, order), 'partial_...  2.38 us
  transfers between devices with their start and end apart: 24, of which 9 were waited for; matrix products, arithmetic and copies ran while one was open for 0% of the time, Pallas kernels for 16%

profile of v12, /device:TPU:1, one launch (start us, length us, event | category | flops | bytes accessed | tf_op | source)
XLA Modules:
  0.0 69.2 jit_solution(17151970114383559312)
XLA Ops:
  0.7 3.3 %halves.1 = (bf16[768,1024]{1,0:T(8,128)(2,1)}, bf16[128,1024]{1,0:T(8,128)(2,1)}, bf16[128,1024]{1,0:T(8,128)(2,1)}) custom-call(f32[256,1024]{1,0:T(8,128)} %bitcast.11, f32[256,1024]{1,0:T(8,128)} %bitcast.13, f32[256,1024]{1,0:T(8,128)} %bitcast.15), custom_call_target="tpu_custom_call" | custom-call | bytes 1024 | tf_op jit(solution)/shard_map/halves/pallas_call | solution.py:98
  4.8 5.3 %collective-permute-start.3 = (bf16[128,1024]{1,0:T(8,128)(2,1)}, bf16[128,1024]{1,0:T(8,128)(2,1)S(1)}, u32[]{:S(2)}, u32[]{:S(2)}) collective-permute-start(bf16[128,1024]{1,0:T(8,128)(2,1)} %get-tuple-element.51.after_ref.refs_0_), channel_id=1, source_target_pairs={{0,1},{2,3},{1,0},{3,2},{4,5},{6,7},{5,4},{7,6},{8,9},{10,11},{9,8... | collective-permute-start | bytes 786440 | tf_op jit(solution)/shard_map/ppermute | solution.py:395
  10.8 1.5 %collective-permute-start.1 = (bf16[128,1024]{1,0:T(8,128)(2,1)}, bf16[128,1024]{1,0:T(8,128)(2,1)}, u32[]{:S(2)}, u32[]{:S(2)}) collective-permute-start(bf16[128,1024]{1,0:T(8,128)(2,1)} %get-tuple-element.48.refs_1_), channel_id=1, source_target_pairs={{0,1},{2,3},{1,0},{3,2},{4,5},{6,7},{5,4},{7,6},{8,9},{10,11},{9,8... | collective-permute-start | bytes 786440 | tf_op jit(solution)/shard_map/ppermute | solution.py:395
  12.4 1.3 %copy-done.5 = bf16[1,512,1024]{2,1,0:T(8,128)(2,1)S(1)} copy-done((bf16[1,512,1024]{2,1,0:T(8,128)(2,1)S(1)}, bf16[1,512,1024]{2,1,0:T(8,128)(2,1)}, u32[]{:S(2)}) %copy-start.5) | copy-done | bytes 1048600
  13.7 2.4 %partial_blocks.1 = (f32[8,1024]{1,0:T(8,128)S(1)}, bf16[128,1024]{1,0:T(8,128)(2,1)S(1)}, bf16[128,1024]{1,0:T(8,128)(2,1)S(1)}, bf16[128,1024]{1,0:T(8,128)(2,...) custom-call(bf16[512,1024]{1,0:T(8,128)(2,1)S(1)} %bitcast.19, ...), custom_call_target="tpu_custom_call" | custom-call | bytes 1024 | tf_op jit(solution)/shard_map/partial_blocks/pallas_call | solution.py:162
  16.1 0.7 pick.1
  16.8 1.3 %collective-permute-start.17 = (bf16[768,1024]{1,0:T(8,128)(2,1)S(1)}, bf16[768,1024]{1,0:T(8,128)(2,1)S(1)}, u32[]{:S(2)}, u32[]{:S(2)}) collective-permute-start(bf16[768,1024]{1,0:T(8,128)(2,1)S(1)} %pick.1), channel_id=1, source_target_pairs={{0,8},{4,12},{8,0},{12,4},{1,9},{5,13},{9,1},{13,5},{2,10},{6,14},... | collective-permute-start | bytes 4718600 | tf_op jit(solution)/shard_map/ppermute | solution.py:399
  18.3 0.7 collective-permute-start.6
  19.0 2.6 %collective-permute-start.7 = (bf16[128,1024]{1,0:T(8,128)(2,1)S(1)}, bf16[128,1024]{1,0:T(8,128)(2,1)S(1)}, u32[]{:S(2)}, u32[]{:S(2)}) collective-permute-start(bf16[128,1024]{1,0:T(8,128)(2,1)S(1)} %get-tuple-element.54.after_ref), channel_id=1, source_target_pairs={{0,1},{2,3},{1,0},{3,2},{4,5},{6,7},{5,4},{7,6},{8,9},{10,11},{9,8... | collective-permute-start | bytes 786440 | tf_op jit(solution)/shard_map/ppermute | solution.py:395
  21.6 0.9 %collective-permute-done.1.arrived_too_ref.refs_3_ = bf16[128,1024]{1,0:T(8,128)(2,1)} collective-permute-done((bf16[128,1024]{1,0:T(8,128)(2,1)}, bf16[128,1024]{1,0:T(8,128)(2,1)}, u32[]{:S(2)}, u32[]{:S(2)}) %collective-permute-start.1) | collective-permute-done | bytes 262176 | tf_op jit(solution)/shard_map/ppermute | solution.py:395
  22.5 1.1 %to_send.7 = (bf16[128,1024]{1,0:T(8,128)(2,1)S(1)}, bf16[128,1024]{1,0:T(8,128)(2,1)S(1)}) custom-call(bf16[128,1024]{1,0:T(8,128)(2,1)S(1)} %collective-permute-done.arrived_ref.refs_5_, bf16[128,1024]{1,0:T(8,128)(2,1)S(1)} %get-tuple-element.49.term_ref, bf16[128,1024]{1,0:T(8,128)(2,1)} %collective-permute-done.1.arrived_too_ref.refs_3_, ...), custom_call_target="tpu_custom_call" | custom-call | flops 1342177280 | bytes 1024 | tf_op jit(solution)/shard_map/to_send/pallas_call | solution.py:189
  23.6 0.7 collective-permute-start.4
  24.3 2.7 %collective-permute-start.5 = (bf16[128,1024]{1,0:T(8,128)(2,1)S(1)}, bf16[128,1024]{1,0:T(8,128)(2,1)S(1)}, u32[]{:S(2)}, u32[]{:S(2)}) collective-permute-start(bf16[128,1024]{1,0:T(8,128)(2,1)S(1)} %get-tuple-element.57.after_ref), channel_id=1, source_target_pairs={{0,1},{2,3},{1,0},{3,2},{4,5},{6,7},{5,4},{7,6},{8,9},{10,11},{9,8... | collective-permute-start | bytes 786440 | tf_op jit(solution)/shard_map/ppermute | solution.py:395
  27.3 0.7 collective-permute-start.10
  27.9 2.7 %collective-permute-start.11 = (bf16[128,1024]{1,0:T(8,128)(2,1)S(1)}, bf16[128,1024]{1,0:T(8,128)(2,1)S(1)}, u32[]{:S(2)}, u32[]{:S(2)}) collective-permute-start(bf16[128,1024]{1,0:T(8,128)(2,1)S(1)} %get-tuple-element.62.after_ref), channel_id=1, source_target_pairs={{0,1},{2,3},{1,0},{3,2},{4,5},{6,7},{5,4},{7,6},{8,9},{10,11},{9,8... | collective-permute-start | bytes 786440 | tf_op jit(solution)/shard_map/ppermute | solution.py:395
  30.6 2.1 %collective-permute-done.5.arrived_too_ref.refs_7_ = bf16[128,1024]{1,0:T(8,128)(2,1)S(1)} collective-permute-done((bf16[128,1024]{1,0:T(8,128)(2,1)S(1)}, bf16[128,1024]{1,0:T(8,128)(2,1)S(1)}, u32[]{:S(2)}, u32[]{:S(2)}) %collective-permute-start.5) | collective-permute-done | bytes 262176 | tf_op jit(solution)/shard_map/ppermute | solution.py:395
  32.9 0.7 collective-permute-start.8
  33.6 3.2 %collective-permute-start.9 = (bf16[128,1024]{1,0:T(8,128)(2,1)S(1)}, bf16[128,1024]{1,0:T(8,128)(2,1)S(1)}, u32[]{:S(2)}, u32[]{:S(2)}) collective-permute-start(bf16[128,1024]{1,0:T(8,128)(2,1)S(1)} %get-tuple-element.65.after_ref), channel_id=1, source_target_pairs={{0,1},{2,3},{1,0},{3,2},{4,5},{6,7},{5,4},{7,6},{8,9},{10,11},{9,8... | collective-permute-start | bytes 786440 | tf_op jit(solution)/shard_map/ppermute | solution.py:395
  36.8 1.6 %collective-permute-done.11.arrived_too_ref.refs_10_ = bf16[128,1024]{1,0:T(8,128)(2,1)S(1)} collective-permute-done((bf16[128,1024]{1,0:T(8,128)(2,1)S(1)}, bf16[128,1024]{1,0:T(8,128)(2,1)S(1)}, u32[]{:S(2)}, u32[]{:S(2)}) %collective-permute-start.11) | collective-permute-done | bytes 262176 | tf_op jit(solution)/shard_map/ppermute | solution.py:395
  38.5 1.2 %collective-permute-start.14 = (bf16[128,1024]{1,0:T(8,128)(2,1)S(1)}, bf16[128,1024]{1,0:T(8,128)(2,1)S(1)}, u32[]{:S(2)}, u32[]{:S(2)}) collective-permute-start(bf16[128,1024]{1,0:T(8,128)(2,1)S(1)} %get-tuple-element.70.after_ref), channel_id=1, source_target_pairs={{0,1},{2,3},{1,0},{3,2},{4,5},{6,7},{5,4},{7,6},{8,9},{10,11},{9,8... | collective-permute-start | bytes 786440 | tf_op jit(solution)/shard_map/ppermute | solution.py:395
  40.4 2.1 %collective-permute-done.9.arrived_too_ref.refs_11_ = bf16[128,1024]{1,0:T(8,128)(2,1)S(1)} collective-permute-done((bf16[128,1024]{1,0:T(8,128)(2,1)S(1)}, bf16[128,1024]{1,0:T(8,128)(2,1)S(1)}, u32[]{:S(2)}, u32[]{:S(2)}) %collective-permute-start.9) | collective-permute-done | bytes 262176 | tf_op jit(solution)/shard_map/ppermute | solution.py:395
  42.7 1.5 %collective-permute-start.12 = (bf16[128,1024]{1,0:T(8,128)(2,1)S(1)}, bf16[128,1024]{1,0:T(8,128)(2,1)S(1)}, u32[]{:S(2)}, u32[]{:S(2)}) collective-permute-start(bf16[128,1024]{1,0:T(8,128)(2,1)S(1)} %get-tuple-element.71.after_ref), channel_id=1, source_target_pairs={{0,1},{2,3},{1,0},{3,2},{4,5},{6,7},{5,4},{7,6},{8,9},{10,11},{9,8... | collective-permute-start | bytes 786440 | tf_op jit(solution)/shard_map/ppermute | solution.py:395
  44.9 3.0 %collective-permute-done.14.one_ref = bf16[128,1024]{1,0:T(8,128)(2,1)S(1)} collective-permute-done((bf16[128,1024]{1,0:T(8,128)(2,1)S(1)}, bf16[128,1024]{1,0:T(8,128)(2,1)S(1)}, u32[]{:S(2)}, u32[]{:S(2)}) %collective-permute-start.14) | collective-permute-done | bytes 262176 | tf_op jit(solution)/shard_map/ppermute | solution.py:395
  48.0 1.5 %collective-permute-start.21 = (bf16[112,1024]{1,0:T(8,128)(2,1)S(1)}, bf16[112,1024]{1,0:T(8,128)(2,1)S(1)}, u32[]{:S(2)}, u32[]{:S(2)}) collective-permute-start(bf16[112,1024]{1,0:T(8,128)(2,1)S(1)} %get-tuple-element.75.after_ref.own_ref), channel_id=1, source_target_pairs={{0,8},{4,12},{8,0},{12,4},{1,9},{5,13},{9,1},{13,5},{2,10},{6,14},... | collective-permute-start | bytes 688136 | tf_op jit(solution)/shard_map/ppermute | solution.py:418
  49.5 3.9 %collective-permute-done.12.one_ref = bf16[128,1024]{1,0:T(8,128)(2,1)S(1)} collective-permute-done((bf16[128,1024]{1,0:T(8,128)(2,1)S(1)}, bf16[128,1024]{1,0:T(8,128)(2,1)S(1)}, u32[]{:S(2)}, u32[]{:S(2)}) %collective-permute-start.12) | collective-permute-done | bytes 262176 | tf_op jit(solution)/shard_map/ppermute | solution.py:395
  53.6 1.5 %collective-permute-start.19 = (bf16[144,1024]{1,0:T(8,128)(2,1)S(1)}, bf16[144,1024]{1,0:T(8,128)(2,1)S(1)}, u32[]{:S(2)}, u32[]{:S(2)}) collective-permute-start(bf16[144,1024]{1,0:T(8,128)(2,1)S(1)} %summed_grad.3.after_ref.own_ref), channel_id=1, source_target_pairs={{0,8},{4,12},{8,0},{12,4},{1,9},{5,13},{9,1},{13,5},{2,10},{6,14},... | collective-permute-start | bytes 884744 | tf_op jit(solution)/shard_map/ppermute | solution.py:418
  55.2 3.5 %collective-permute-start.20 = (bf16[112,1024]{1,0:T(8,128)(2,1)S(1)}, bf16[112,1024]{1,0:T(8,128)(2,1)S(1)}, u32[]{:S(2)}, u32[]{:S(2)}) collective-permute-start(bf16[112,1024]{1,0:T(8,128)(2,1)S(1)} %get-tuple-element.75.after_ref.own_ref), channel_id=1, source_target_pairs={{0,4},{4,0},{8,12},{12,8},{1,5},{5,1},{9,13},{13,9},{2,6},{6,2},{1... | collective-permute-start | bytes 688136 | tf_op jit(solution)/shard_map/ppermute | solution.py:417
  58.7 3.3 %context_grad.1 = (bf16[512,1024]{1,0:T(8,128)(2,1)}, f32[8,128]{1,0:T(8,128)S(1)}) custom-call(s32[2]{0:T(128)S(1)} %pad_add_fusion.where_ref, bf16[512,1024]{1,0:T(8,128)(2,1)S(1)} %bitcast.18, bf16[144,1024]{1,0:T(8,128)(2,1)S(1)} %summed_grad.3.after_ref.own_ref, bf16[128,1024]{1,0:T(8,128)(2,1)S(1)} %copy-done.6, bf16[128,1024]{1,0:T(8,128)(2,1)S(1)} %copy-done.7, ...), custom_call_target="tpu_custom_call" | custom-call | bytes 1024 | tf_op jit(solution)/shard_map/context_grad/pallas_call | solution.py:257
  62.6 0.9 %taken_state.1 = (f32[336,1024]{1,0:T(8,128)S(1)}, f32[432,1024]{1,0:T(8,128)S(1)}) custom-call(s32[2]{0:T(128)S(1)} %pad_add_fusion.where_ref, s32[4]{0:T(128)S(1)} %copy-done.8, bf16[128,1024]{1,0:T(8,128)(2,1)S(1)} %get-tuple-element.71.after_ref, f32[256,1024]{1,0:T(8,128)S(1)} %bitcast.12, f32[256,1024]{1,0:T(8,128)S(1)} %bitcast.14, ...), custom_call_target="tpu_custom_call" | custom-call | bytes 1024 | tf_op jit(solution)/shard_map/taken_state/pallas_call | solution.py:306
  63.6 1.5 %adam.2 = (f32[256,1024]{1,0:T(8,128)}, f32[256,1024]{1,0:T(8,128)}, f32[256,1024]{1,0:T(8,128)}, f32[8,128]{1,0:T(8,128)S(1)}) custom-call(f32[8,1024]{1,0:T(8,128)S(1)} %get-tuple-element.78.choices_ref, f32[336,1024]{1,0:T(8,128)S(1)} %get-tuple-element.81.state_ref, bf16[112,1024]{1,0:T(8,128)(2,1)S(1)} %get-tuple-element.75.after_ref.own_ref, ...), custom_call_target="tpu_custom_call" | custom-call | bytes 1024 | tf_op jit(solution)/shard_map/adam/pallas_call | solution.py:352
  65.6 1.2 %collective-permute-done.23.far_ref = bf16[144,1024]{1,0:T(8,128)(2,1)S(1)} collective-permute-done((bf16[144,1024]{1,0:T(8,128)(2,1)S(1)}, bf16[144,1024]{1,0:T(8,128)(2,1)S(1)}, u32[]{:S(2)}, u32[]{:S(2)}) %collective-permute-start.23) | collective-permute-done | bytes 294944 | tf_op jit(solution)/shard_map/ppermute | solution.py:419
  66.8 2.3 %adam.3 = (f32[256,1024]{1,0:T(8,128)}, f32[256,1024]{1,0:T(8,128)}, f32[256,1024]{1,0:T(8,128)}, f32[8,128]{1,0:T(8,128)}) custom-call(f32[8,1024]{1,0:T(8,128)S(1)} %get-tuple-element.78.choices_ref, f32[432,1024]{1,0:T(8,128)S(1)} %get-tuple-element.80.state_ref, ...), custom_call_target="tpu_custom_call", output_to_operand_aliasing={{0}: (7, {}), {1}: (8, {}), {2}: (9, {})} | custom-call | bytes 1024 | tf_op jit(solution)/shard_map/adam/pallas_call | solution.py:352
  (58 shorter events, 5.2 us)
Async XLA Ops:
  0.6 11.7 %copy-start.3 = (bf16[1,512,1024]{2,1,0:T(8,128)(2,1)S(1)}, bf16[1,512,1024]{2,1,0:T(8,128)(2,1)}, u32[]{:S(2)}) copy-start(bf16[1,512,1024]{2,1,0:T(8,128)(2,1)} %param.10) | copy-start | bytes 3145732
  0.6 11.7 %copy-start.8 = (s32[4]{0:T(128)S(1)}, s32[4]{0:T(128)}, u32[]{:S(2)}) copy-start(s32[4]{0:T(128)} %donor_ref.1) | copy-start | bytes 52
  0.7 11.7 %copy-start.9 = (f32[4]{0:T(128)S(1)}, f32[4]{0:T(128)}, u32[]{:S(2)}) copy-start(f32[4]{0:T(128)} %refs_0_.1) | copy-start | bytes 52
  0.7 11.7 %copy-start.10 = (f32[4]{0:T(128)S(1)}, f32[4]{0:T(128)}, u32[]{:S(2)}) copy-start(f32[4]{0:T(128)} %refs_1_.1) | copy-start | bytes 52
  0.7 11.7 %copy-start.11 = (s32[4]{0:T(128)S(1)}, s32[4]{0:T(128)}, u32[]{:S(2)}) copy-start(s32[4]{0:T(128)} %refs_2_.1) | copy-start | bytes 52
  4.0 12.1 %collective-permute-start.16 = (bf16[768,1024]{1,0:T(8,128)(2,1)}, bf16[768,1024]{1,0:T(8,128)(2,1)S(1)}, u32[]{:S(2)}, u32[]{:S(2)}) collective-permute-start(bf16[768,1024]{1,0:T(8,128)(2,1)} %get-tuple-element.79.own_ref), channel_id=1, source_target_pairs={{0,4},{4,0},{8,12},{12,8},{1,5},{5,1},{9,13},{13,9},{2,6},{6,2},{1... | collective-permute-start | bytes 4718600 | tf_op jit(solution)/shard_map/ppermute | solution.py:398
  4.1 14.0 %collective-permute-start.2 = (bf16[128,1024]{1,0:T(8,128)(2,1)}, bf16[128,1024]{1,0:T(8,128)(2,1)S(1)}, u32[]{:S(2)}, u32[]{:S(2)}) collective-permute-start(bf16[128,1024]{1,0:T(8,128)(2,1)} %get-tuple-element.51.after_ref.refs_0_), channel_id=1, source_target_pairs={{1,2},{2,1},{5,6},{6,5},{9,10},{10,9},{13,14},{14,13},{17,18},{18,... | collective-permute-start | bytes 786440 | tf_op jit(solution)/shard_map/ppermute | solution.py:395
  4.8 13.3 %collective-permute-start.3 = (bf16[128,1024]{1,0:T(8,128)(2,1)}, bf16[128,1024]{1,0:T(8,128)(2,1)S(1)}, u32[]{:S(2)}, u32[]{:S(2)}) collective-permute-start(bf16[128,1024]{1,0:T(8,128)(2,1)} %get-tuple-element.51.after_ref.refs_0_), channel_id=1, source_target_pairs={{0,1},{2,3},{1,0},{3,2},{4,5},{6,7},{5,4},{7,6},{8,9},{10,11},{9,8... | collective-permute-start | bytes 786440 | tf_op jit(solution)/shard_map/ppermute | solution.py:395
  10.1 11.5 %collective-permute-start = (bf16[128,1024]{1,0:T(8,128)(2,1)}, bf16[128,1024]{1,0:T(8,128)(2,1)S(1)}, u32[]{:S(2)}, u32[]{:S(2)}) collective-permute-start(bf16[128,1024]{1,0:T(8,128)(2,1)} %get-tuple-element.48.refs_1_), channel_id=1, source_target_pairs={{1,2},{2,1},{5,6},{6,5},{9,10},{10,9},{13,14},{14,13},{17,18},{18,... | collective-permute-start | bytes 786440 | tf_op jit(solution)/shard_map/ppermute | solution.py:395
  10.8 11.7 %collective-permute-start.1 = (bf16[128,1024]{1,0:T(8,128)(2,1)}, bf16[128,1024]{1,0:T(8,128)(2,1)}, u32[]{:S(2)}, u32[]{:S(2)}) collective-permute-start(bf16[128,1024]{1,0:T(8,128)(2,1)} %get-tuple-element.48.refs_1_), channel_id=1, source_target_pairs={{0,1},{2,3},{1,0},{3,2},{4,5},{6,7},{5,4},{7,6},{8,9},{10,11},{9,8... | collective-permute-start | bytes 786440 | tf_op jit(solution)/shard_map/ppermute | solution.py:395
  16.8 45.7 %collective-permute-start.17 = (bf16[768,1024]{1,0:T(8,128)(2,1)S(1)}, bf16[768,1024]{1,0:T(8,128)(2,1)S(1)}, u32[]{:S(2)}, u32[]{:S(2)}) collective-permute-start(bf16[768,1024]{1,0:T(8,128)(2,1)S(1)} %pick.1), channel_id=1, source_target_pairs={{0,8},{4,12},{8,0},{12,4},{1,9},{5,13},{9,1},{13,5},{2,10},{6,14},... | collective-permute-start | bytes 4718600 | tf_op jit(solution)/shard_map/ppermute | solution.py:399
  18.3 8.7 %collective-permute-start.6 = (bf16[128,1024]{1,0:T(8,128)(2,1)S(1)}, bf16[128,1024]{1,0:T(8,128)(2,1)S(1)}, u32[]{:S(2)}, u32[]{:S(2)}) collective-permute-start(bf16[128,1024]{1,0:T(8,128)(2,1)S(1)} %get-tuple-element.59), channel_id=1, source_target_pairs={{1,2},{2,1},{5,6},{6,5},{9,10},{10,9},{13,14},{14,13},{17,18},{18,... | collective-permute-start | bytes 786440 | tf_op jit(solution)/shard_map/ppermute | solution.py:395
  19.0 8.1 %collective-permute-start.7 = (bf16[128,1024]{1,0:T(8,128)(2,1)S(1)}, bf16[128,1024]{1,0:T(8,128)(2,1)S(1)}, u32[]{:S(2)}, u32[]{:S(2)}) collective-permute-start(bf16[128,1024]{1,0:T(8,128)(2,1)S(1)} %get-tuple-element.54.after_ref), channel_id=1, source_target_pairs={{0,1},{2,3},{1,0},{3,2},{4,5},{6,7},{5,4},{7,6},{8,9},{10,11},{9,8... | collective-permute-start | bytes 786440 | tf_op jit(solution)/shard_map/ppermute | solution.py:395
  23.6 7.0 %collective-permute-start.4 = (bf16[128,1024]{1,0:T(8,128)(2,1)S(1)}, bf16[128,1024]{1,0:T(8,128)(2,1)S(1)}, u32[]{:S(2)}, u32[]{:S(2)}) collective-permute-start(bf16[128,1024]{1,0:T(8,128)(2,1)S(1)} %get-tuple-element.55), channel_id=1, source_target_pairs={{1,2},{2,1},{5,6},{6,5},{9,10},{10,9},{13,14},{14,13},{17,18},{18,... | collective-permute-start | bytes 786440 | tf_op jit(solution)/shard_map/ppermute | solution.py:395
  24.3 8.4 %collective-permute-start.5 = (bf16[128,1024]{1,0:T(8,128)(2,1)S(1)}, bf16[128,1024]{1,0:T(8,128)(2,1)S(1)}, u32[]{:S(2)}, u32[]{:S(2)}) collective-permute-start(bf16[128,1024]{1,0:T(8,128)(2,1)S(1)} %get-tuple-element.57.after_ref), channel_id=1, source_target_pairs={{0,1},{2,3},{1,0},{3,2},{4,5},{6,7},{5,4},{7,6},{8,9},{10,11},{9,8... | collective-permute-start | bytes 786440 | tf_op jit(solution)/shard_map/ppermute | solution.py:395
  27.3 9.5 %collective-permute-start.10 = (bf16[128,1024]{1,0:T(8,128)(2,1)S(1)}, bf16[128,1024]{1,0:T(8,128)(2,1)S(1)}, u32[]{:S(2)}, u32[]{:S(2)}) collective-permute-start(bf16[128,1024]{1,0:T(8,128)(2,1)S(1)} %get-tuple-element.67), channel_id=1, source_target_pairs={{1,2},{2,1},{5,6},{6,5},{9,10},{10,9},{13,14},{14,13},{17,18},{18,... | collective-permute-start | bytes 786440 | tf_op jit(solution)/shard_map/ppermute | solution.py:395
  27.9 10.4 %collective-permute-start.11 = (bf16[128,1024]{1,0:T(8,128)(2,1)S(1)}, bf16[128,1024]{1,0:T(8,128)(2,1)S(1)}, u32[]{:S(2)}, u32[]{:S(2)}) collective-permute-start(bf16[128,1024]{1,0:T(8,128)(2,1)S(1)} %get-tuple-element.62.after_ref), channel_id=1, source_target_pairs={{0,1},{2,3},{1,0},{3,2},{4,5},{6,7},{5,4},{7,6},{8,9},{10,11},{9,8... | collective-permute-start | bytes 786440 | tf_op jit(solution)/shard_map/ppermute | solution.py:395
  32.9 7.5 %collective-permute-start.8 = (bf16[128,1024]{1,0:T(8,128)(2,1)S(1)}, bf16[128,1024]{1,0:T(8,128)(2,1)S(1)}, u32[]{:S(2)}, u32[]{:S(2)}) collective-permute-start(bf16[128,1024]{1,0:T(8,128)(2,1)S(1)} %get-tuple-element.63), channel_id=1, source_target_pairs={{1,2},{2,1},{5,6},{6,5},{9,10},{10,9},{13,14},{14,13},{17,18},{18,... | collective-permute-start | bytes 786440 | tf_op jit(solution)/shard_map/ppermute | solution.py:395
  33.6 8.9 %collective-permute-start.9 = (bf16[128,1024]{1,0:T(8,128)(2,1)S(1)}, bf16[128,1024]{1,0:T(8,128)(2,1)S(1)}, u32[]{:S(2)}, u32[]{:S(2)}) collective-permute-start(bf16[128,1024]{1,0:T(8,128)(2,1)S(1)} %get-tuple-element.65.after_ref), channel_id=1, source_target_pairs={{0,1},{2,3},{1,0},{3,2},{4,5},{6,7},{5,4},{7,6},{8,9},{10,11},{9,8... | collective-permute-start | bytes 786440 | tf_op jit(solution)/shard_map/ppermute | solution.py:395
  38.5 9.3 %collective-permute-start.14 = (bf16[128,1024]{1,0:T(8,128)(2,1)S(1)}, bf16[128,1024]{1,0:T(8,128)(2,1)S(1)}, u32[]{:S(2)}, u32[]{:S(2)}) collective-permute-start(bf16[128,1024]{1,0:T(8,128)(2,1)S(1)} %get-tuple-element.70.after_ref), channel_id=1, source_target_pairs={{0,1},{2,3},{1,0},{3,2},{4,5},{6,7},{5,4},{7,6},{8,9},{10,11},{9,8... | collective-permute-start | bytes 786440 | tf_op jit(solution)/shard_map/ppermute | solution.py:395
  39.8 8.1 %collective-permute-start.15 = (bf16[128,1024]{1,0:T(8,128)(2,1)S(1)}, bf16[128,1024]{1,0:T(8,128)(2,1)S(1)}, u32[]{:S(2)}, u32[]{:S(2)}) collective-permute-start(bf16[128,1024]{1,0:T(8,128)(2,1)S(1)} %get-tuple-element.74), channel_id=1, source_target_pairs={{1,2},{2,1},{5,6},{6,5},{9,10},{10,9},{13,14},{14,13},{17,18},{18,... | collective-permute-start | bytes 786440 | tf_op jit(solution)/shard_map/ppermute | solution.py:395
  42.7 16.0 %copy-start.7 = (bf16[128,1024]{1,0:T(8,128)(2,1)S(1)}, bf16[128,1024]{1,0:T(8,128)(2,1)}, u32[]{:S(2)}) copy-start(bf16[128,1024]{1,0:T(8,128)(2,1)} %get-tuple-element.48.refs_1_) | copy-start | bytes 786436
  42.7 10.8 %collective-permute-start.12 = (bf16[128,1024]{1,0:T(8,128)(2,1)S(1)}, bf16[128,1024]{1,0:T(8,128)(2,1)S(1)}, u32[]{:S(2)}, u32[]{:S(2)}) collective-permute-start(bf16[128,1024]{1,0:T(8,128)(2,1)S(1)} %get-tuple-element.71.after_ref), channel_id=1, source_target_pairs={{0,1},{2,3},{1,0},{3,2},{4,5},{6,7},{5,4},{7,6},{8,9},{10,11},{9,8... | collective-permute-start | bytes 786440 | tf_op jit(solution)/shard_map/ppermute | solution.py:395
  44.2 9.3 %collective-permute-start.13 = (bf16[128,1024]{1,0:T(8,128)(2,1)S(1)}, bf16[128,1024]{1,0:T(8,128)(2,1)S(1)}, u32[]{:S(2)}, u32[]{:S(2)}) collective-permute-start(bf16[128,1024]{1,0:T(8,128)(2,1)S(1)} %get-tuple-element.72), channel_id=1, source_target_pairs={{1,2},{2,1},{5,6},{6,5},{9,10},{10,9},{13,14},{14,13},{17,18},{18,... | collective-permute-start | bytes 786440 | tf_op jit(solution)/shard_map/ppermute | solution.py:395
  48.0 14.0 %collective-permute-start.21 = (bf16[112,1024]{1,0:T(8,128)(2,1)S(1)}, bf16[112,1024]{1,0:T(8,128)(2,1)S(1)}, u32[]{:S(2)}, u32[]{:S(2)}) collective-permute-start(bf16[112,1024]{1,0:T(8,128)(2,1)S(1)} %get-tuple-element.75.after_ref.own_ref), channel_id=1, source_target_pairs={{0,8},{4,12},{8,0},{12,4},{1,9},{5,13},{9,1},{13,5},{2,10},{6,14},... | collective-permute-start | bytes 688136 | tf_op jit(solution)/shard_map/ppermute | solution.py:418
  53.6 8.9 %copy-start = (f32[1,256,1024]{2,1,0:T(8,128)S(1)}, f32[1,256,1024]{2,1,0:T(8,128)}, u32[]{:S(2)}) copy-start(f32[1,256,1024]{2,1,0:T(8,128)} %param.11) | copy-start | bytes 3145732
  53.6 8.9 %copy-start.1 = (f32[1,256,1024]{2,1,0:T(8,128)S(1)}, f32[1,256,1024]{2,1,0:T(8,128)}, u32[]{:S(2)}) copy-start(f32[1,256,1024]{2,1,0:T(8,128)} %param.12) | copy-start | bytes 3145732
  53.6 11.5 %collective-permute-start.19 = (bf16[144,1024]{1,0:T(8,128)(2,1)S(1)}, bf16[144,1024]{1,0:T(8,128)(2,1)S(1)}, u32[]{:S(2)}, u32[]{:S(2)}) collective-permute-start(bf16[144,1024]{1,0:T(8,128)(2,1)S(1)} %summed_grad.3.after_ref.own_ref), channel_id=1, source_target_pairs={{0,8},{4,12},{8,0},{12,4},{1,9},{5,13},{9,1},{13,5},{2,10},{6,14},... | collective-permute-start | bytes 884744 | tf_op jit(solution)/shard_map/ppermute | solution.py:418
  55.2 8.3 %collective-permute-start.20 = (bf16[112,1024]{1,0:T(8,128)(2,1)S(1)}, bf16[112,1024]{1,0:T(8,128)(2,1)S(1)}, u32[]{:S(2)}, u32[]{:S(2)}) collective-permute-start(bf16[112,1024]{1,0:T(8,128)(2,1)S(1)} %get-tuple-element.75.after_ref.own_ref), channel_id=1, source_target_pairs={{0,4},{4,0},{8,12},{12,8},{1,5},{5,1},{9,13},{13,9},{2,6},{6,2},{1... | collective-permute-start | bytes 688136 | tf_op jit(solution)/shard_map/ppermute | solution.py:417
  62.0 1.6 %collective-permute-start.22 = (bf16[112,1024]{1,0:T(8,128)(2,1)S(1)}, bf16[112,1024]{1,0:T(8,128)(2,1)S(1)}, u32[]{:S(2)}, u32[]{:S(2)}) collective-permute-start(bf16[112,1024]{1,0:T(8,128)(2,1)S(1)} %gate.2.across_ref), channel_id=1, source_target_pairs={{0,4},{4,0},{8,12},{12,8},{1,5},{5,1},{9,13},{13,9},{2,6},{6,2},{1... | collective-permute-start | bytes 688136 | tf_op jit(solution)/shard_map/ppermute | solution.py:419
  62.5 3.2 %collective-permute-start.18 = (bf16[144,1024]{1,0:T(8,128)(2,1)S(1)}, bf16[144,1024]{1,0:T(8,128)(2,1)S(1)}, u32[]{:S(2)}, u32[]{:S(2)}) collective-permute-start(bf16[144,1024]{1,0:T(8,128)(2,1)S(1)} %summed_grad.3.after_ref.own_ref), channel_id=1, source_target_pairs={{0,4},{4,0},{8,12},{12,8},{1,5},{5,1},{9,13},{13,9},{2,6},{6,2},{1... | collective-permute-start | bytes 884744 | tf_op jit(solution)/shard_map/ppermute | solution.py:417
  65.1 1.7 %collective-permute-start.23 = (bf16[144,1024]{1,0:T(8,128)(2,1)S(1)}, bf16[144,1024]{1,0:T(8,128)(2,1)S(1)}, u32[]{:S(2)}, u32[]{:S(2)}) collective-permute-start(bf16[144,1024]{1,0:T(8,128)(2,1)S(1)} %gate.3.across_ref), channel_id=1, source_target_pairs={{0,4},{4,0},{8,12},{12,8},{1,5},{5,1},{9,13},{13,9},{2,6},{6,2},{1... | collective-permute-start | bytes 884744 | tf_op jit(solution)/shard_map/ppermute | solution.py:419
  (4 other events, 16.1 us)

commit v13 on v12

--- a/solution.py
+++ b/solution.py
@@ -38,12 +38,17 @@
     return jax.ShapeDtypeStruct((rows, depth), jnp.bfloat16)
 
 
-def gate_kernel(value_ref, after_ref, out_ref):
-    pass
-
-
-def gate(value, after):
-    return call(gate_kernel, "gate", half_array(*value.shape), [ANY, ANY], ANY, aliases={0: 0})(value, after)
+def gate_kernel(value_ref, after_ref, *out_refs):
+    size = out_refs[0].shape[0]
+    for k, out_ref in enumerate(out_refs):
+        out_ref[...] = value_ref[k * size:(k + 1) * size, :]
+
+
+def gate(value, after, count):
+    rows, depth = value.shape
+    return call(gate_kernel, "gate", [half_array(rows // count, depth)] * count, [VMEM, ANY], [VMEM] * count)(
+        value, after
+    )
 
 
 def by_rows(ref, body, step=16):
@@ -311,13 +316,13 @@
     )(where, donor, after, *own, *donated)
 
 
-def adam_kernel(start, size, filled, choices_ref, state_ref, own_ref, mate_ref, across_ref, far_ref, after_ref, *refs):
-    refs = refs[3 if filled else 0:]
+def adam_kernel(start, size, hops, filled, choices_ref, state_ref, own_ref, mate_ref, across_ref, after_ref, *refs):
+    far_refs, refs = refs[:hops], refs[hops + (3 if filled else 0):]
     outs, (token_ref, stepped, sems) = refs[:3], refs[3:]
     token_ref[...] = jnp.zeros_like(token_ref)
     depth = own_ref.shape[1]
     writes = []
-    piece = 32
+    piece, hop = 32, size // hops
     for top in range(0, size, piece):
         height = min(piece, size - top)
 
@@ -325,7 +330,8 @@
             at = pl.ds(pl.multiple_of(top + i * 16, 16), 16)
             row = lambda k: jnp.broadcast_to(choices_ref[k:k + 1, :], (16, depth))
             load = lambda k: state_ref[pl.ds(pl.multiple_of(k * size + top + i * 16, 16), 16), :]
-            g = far_ref[at, :].astype(jnp.float32)
+            near = pl.ds(pl.multiple_of(top % hop + i * 16, 16), 16)
+            g = far_refs[top // hop][near, :].astype(jnp.float32)
             for k, ref in ((1, own_ref), (2, mate_ref), (3, across_ref)):
                 g = jnp.where(row(k) > 0, ref[at, :].astype(jnp.float32), g)
             w = load(0)
@@ -347,15 +353,15 @@
         write.wait()
 
 
-def adam_update(start, size, rows, choices, state, grads, after, filled):
+def adam_update(start, size, rows, choices, state, grads, far, after, filled):
     depth = state.shape[1]
     return call(
-        functools.partial(adam_kernel, start, size, bool(filled)), "adam",
+        functools.partial(adam_kernel, start, size, len(far), bool(filled)), "adam",
         [jax.ShapeDtypeStruct((rows, depth), jnp.float32)] * 3 + [jax.ShapeDtypeStruct((8, 128), jnp.float32)],
-        [VMEM] * 6 + [ANY] + [HBM] * len(filled), [HBM] * 3 + [VMEM],
+        [VMEM] * 5 + [ANY] + [VMEM] * len(far) + [HBM] * len(filled), [HBM] * 3 + [VMEM],
         scratch=[pltpu.VMEM((3, size, depth), jnp.float32), pltpu.SemaphoreType.DMA((3 * (-(-size // 32)),))],
-        aliases={7 + k: k for k in range(len(filled))},
-    )(choices, state, *grads, after, *filled)
+        aliases={6 + len(far) + k: k for k in range(len(filled))},
+    )(choices, state, *grads, after, *far, *filled)
 
 
 def on_device(n, members, context, out_grad, weight, first, second, rates, decays, steps, donor):
@@ -365,7 +371,7 @@
     rows, depth = weight.shape[1:]
     chains = 2 if rows % 32 == 0 else 1
     parts = [(c * rows // chains, rows // chains) for c in range(chains)]
-    lower = rows * 112 // 256 // 16 * 16
+    lower = rows // 2 // 16 * 16
     steps_of = [(0, lower), (lower, rows - lower)] if chains == 2 and lower else [(0, rows)]
     where = jnp.stack([lax.axis_index("shard"), lax.axis_index("member")]).astype(jnp.int32)
 
@@ -415,10 +421,11 @@
     updated = ()
     for c, (start, size) in enumerate(steps_of):
         mate = lax.ppermute(grads[c], "member", swap_mates)
-        across = gate(lax.ppermute(grads[c], "member", swap_across), computed)
-        far = lax.ppermute(across, "member", swap_mates)
+        across = lax.ppermute(grads[c], "member", swap_across)
+        pieces = gate(across, computed, 2 if c == 0 and size % 64 == 0 else 1)
+        far = [lax.ppermute(piece, "member", swap_mates) for piece in pieces]
         *updated, computed = adam_update(
-            start, size, rows, choices, states[c], (grads[c], mate, across, far), computed, updated
+            start, size, rows, choices, states[c], (grads[c], mate, across), far, computed, updated
         )
     return (context_grad[None],) + tuple(array[None] for array in updated)
 

time: 70.3 us -> 70.5 us (level)
  starting transfers between devices: 35.1 us -> 39.7 us
  waiting for transfers between devices: 15 us -> 11 us
    ppermute x16, waiting for transfers between devices: 13.7 us -> 9.78 us  [on_device(): now[swap].append(lax.ppermute(blocks[swap], 'shard', swaps[swap]))]
    ppermute x2, starting transfers between devices: 3.55 us -> 6.69 us  [on_device(): mate = lax.ppermute(grads[c], 'member', swap_mates)]
    ppermute x4 -> x5, starting transfers between devices: 4.08 us -> 5.46 us  [the longest x3 3.55 us: on_device(): far = [lax.ppermute(piece, 'member', swap_mates) for piece in pieces]]
  transfers between devices with their start and end apart: 24 -> 25, of which waited for: 9 -> 7; matrix products, arithmetic and copies ran while one was open for 0% -> 0% of each run, Pallas kernels for 16% -> 16%
where the time goes in v13:
time: 70.5 us; the launch traced here: 69.9 us
  starting transfers between devices  39.7 us (56%)
  Pallas kernels  16.8 us (24%)
  waiting for transfers between devices  11 us (16%)
  local copies, waits for them, and re-layouts  1.37 us (2%)
  between operations  1 us (1%)
    ppermute x16, starting transfers between devices, on_device(): now[swap].append(lax.ppermute(blocks[swap], 'shard', swaps[swap]))  26.1 us
    ppermute x16, waiting for transfers between devices, on_device(): now[swap].append(lax.ppermute(blocks[swap], 'shard', swaps[swap]))  9.78 us
    ppermute x2, starting transfers between devices, on_device(): mate = lax.ppermute(grads[c], 'member', swap_mates)  6.69 us
    pallas_call x2, Pallas kernels, adam_update(): call(functools.partial(adam_kernel, start, size, len(far), bool(filled)),...  3.92 us
    ppermute x3, starting transfers between devices, on_device(): far = [lax.ppermute(piece, 'member', swap_mates) for piece in pieces]  3.55 us
    pallas_call x1, Pallas kernels, columns(): call(functools.partial(columns_kernel, n, scale, parts), 'context_grad',...  3.47 us
    pallas_call x1, Pallas kernels, halves(): call(functools.partial(halves_kernel, parts), 'halves', shapes, [HBM] * 3...  3.33 us
    pallas_call x1, Pallas kernels, partial_blocks(): call(functools.partial(partial_kernel, n, scale, parts, order), 'partial_...  2.38 us
  transfers between devices with their start and end apart: 25, of which 7 were waited for; matrix products, arithmetic and copies ran while one was open for 0% of the time, Pallas kernels for 16%

profile of v13, /device:TPU:1, one launch (start us, length us, event | category | flops | bytes accessed | tf_op | source)
XLA Modules:
  0.0 69.9 jit_solution(12037284294567238378)
XLA Ops:
  0.7 3.3 %halves.1 = (bf16[768,1024]{1,0:T(8,128)(2,1)}, bf16[128,1024]{1,0:T(8,128)(2,1)}, bf16[128,1024]{1,0:T(8,128)(2,1)}) custom-call(f32[256,1024]{1,0:T(8,128)} %bitcast.13, f32[256,1024]{1,0:T(8,128)} %bitcast.15, f32[256,1024]{1,0:T(8,128)} %bitcast.17), custom_call_target="tpu_custom_call" | custom-call | bytes 1024 | tf_op jit(solution)/shard_map/halves/pallas_call | solution.py:103
  4.8 5.3 %collective-permute-start.3 = (bf16[128,1024]{1,0:T(8,128)(2,1)}, bf16[128,1024]{1,0:T(8,128)(2,1)S(1)}, u32[]{:S(2)}, u32[]{:S(2)}) collective-permute-start(bf16[128,1024]{1,0:T(8,128)(2,1)} %get-tuple-element.51.after_ref.refs_0_), channel_id=1, source_target_pairs={{0,1},{2,3},{1,0},{3,2},{4,5},{6,7},{5,4},{7,6},{8,9},{10,11},{9,8... | collective-permute-start | bytes 786440 | tf_op jit(solution)/shard_map/ppermute | solution.py:401
  10.8 1.5 %collective-permute-start.1 = (bf16[128,1024]{1,0:T(8,128)(2,1)}, bf16[128,1024]{1,0:T(8,128)(2,1)}, u32[]{:S(2)}, u32[]{:S(2)}) collective-permute-start(bf16[128,1024]{1,0:T(8,128)(2,1)} %get-tuple-element.48.refs_1_), channel_id=1, source_target_pairs={{0,1},{2,3},{1,0},{3,2},{4,5},{6,7},{5,4},{7,6},{8,9},{10,11},{9,8... | collective-permute-start | bytes 786440 | tf_op jit(solution)/shard_map/ppermute | solution.py:401
  12.4 1.3 %copy-done.5 = bf16[1,512,1024]{2,1,0:T(8,128)(2,1)S(1)} copy-done((bf16[1,512,1024]{2,1,0:T(8,128)(2,1)S(1)}, bf16[1,512,1024]{2,1,0:T(8,128)(2,1)}, u32[]{:S(2)}) %copy-start.5) | copy-done | bytes 1048600
  13.7 2.4 %partial_blocks.1 = (f32[8,1024]{1,0:T(8,128)S(1)}, bf16[128,1024]{1,0:T(8,128)(2,1)S(1)}, bf16[128,1024]{1,0:T(8,128)(2,1)S(1)}, bf16[128,1024]{1,0:T(8,128)(2,...) custom-call(bf16[512,1024]{1,0:T(8,128)(2,1)S(1)} %bitcast.19, ...), custom_call_target="tpu_custom_call" | custom-call | bytes 1024 | tf_op jit(solution)/shard_map/partial_blocks/pallas_call | solution.py:167
  16.2 0.7 pick.1
  16.9 1.3 %collective-permute-start.17 = (bf16[768,1024]{1,0:T(8,128)(2,1)S(1)}, bf16[768,1024]{1,0:T(8,128)(2,1)S(1)}, u32[]{:S(2)}, u32[]{:S(2)}) collective-permute-start(bf16[768,1024]{1,0:T(8,128)(2,1)S(1)} %pick.1), channel_id=1, source_target_pairs={{0,8},{4,12},{8,0},{12,4},{1,9},{5,13},{9,1},{13,5},{2,10},{6,14},... | collective-permute-start | bytes 4718600 | tf_op jit(solution)/shard_map/ppermute | solution.py:405
  18.3 0.7 collective-permute-start.6
  19.0 2.6 %collective-permute-start.7 = (bf16[128,1024]{1,0:T(8,128)(2,1)S(1)}, bf16[128,1024]{1,0:T(8,128)(2,1)S(1)}, u32[]{:S(2)}, u32[]{:S(2)}) collective-permute-start(bf16[128,1024]{1,0:T(8,128)(2,1)S(1)} %get-tuple-element.54.after_ref), channel_id=1, source_target_pairs={{0,1},{2,3},{1,0},{3,2},{4,5},{6,7},{5,4},{7,6},{8,9},{10,11},{9,8... | collective-permute-start | bytes 786440 | tf_op jit(solution)/shard_map/ppermute | solution.py:401
  21.6 0.9 %collective-permute-done.1.arrived_too_ref.refs_3_ = bf16[128,1024]{1,0:T(8,128)(2,1)} collective-permute-done((bf16[128,1024]{1,0:T(8,128)(2,1)}, bf16[128,1024]{1,0:T(8,128)(2,1)}, u32[]{:S(2)}, u32[]{:S(2)}) %collective-permute-start.1) | collective-permute-done | bytes 262176 | tf_op jit(solution)/shard_map/ppermute | solution.py:401
  22.5 1.1 %to_send.7 = (bf16[128,1024]{1,0:T(8,128)(2,1)S(1)}, bf16[128,1024]{1,0:T(8,128)(2,1)S(1)}) custom-call(bf16[128,1024]{1,0:T(8,128)(2,1)S(1)} %collective-permute-done.arrived_ref.refs_5_, bf16[128,1024]{1,0:T(8,128)(2,1)S(1)} %get-tuple-element.49.term_ref, bf16[128,1024]{1,0:T(8,128)(2,1)} %collective-permute-done.1.arrived_too_ref.refs_3_, ...), custom_call_target="tpu_custom_call" | custom-call | flops 1342177280 | bytes 1024 | tf_op jit(solution)/shard_map/to_send/pallas_call | solution.py:194
  23.6 0.7 collective-permute-start.4
  24.3 2.7 %collective-permute-start.5 = (bf16[128,1024]{1,0:T(8,128)(2,1)S(1)}, bf16[128,1024]{1,0:T(8,128)(2,1)S(1)}, u32[]{:S(2)}, u32[]{:S(2)}) collective-permute-start(bf16[128,1024]{1,0:T(8,128)(2,1)S(1)} %get-tuple-element.57.after_ref), channel_id=1, source_target_pairs={{0,1},{2,3},{1,0},{3,2},{4,5},{6,7},{5,4},{7,6},{8,9},{10,11},{9,8... | collective-permute-start | bytes 786440 | tf_op jit(solution)/shard_map/ppermute | solution.py:401
  27.3 0.7 collective-permute-start.10
  28.0 2.7 %collective-permute-start.11 = (bf16[128,1024]{1,0:T(8,128)(2,1)S(1)}, bf16[128,1024]{1,0:T(8,128)(2,1)S(1)}, u32[]{:S(2)}, u32[]{:S(2)}) collective-permute-start(bf16[128,1024]{1,0:T(8,128)(2,1)S(1)} %get-tuple-element.62.after_ref), channel_id=1, source_target_pairs={{0,1},{2,3},{1,0},{3,2},{4,5},{6,7},{5,4},{7,6},{8,9},{10,11},{9,8... | collective-permute-start | bytes 786440 | tf_op jit(solution)/shard_map/ppermute | solution.py:401
  30.6 2.1 %collective-permute-done.5.arrived_too_ref.refs_7_ = bf16[128,1024]{1,0:T(8,128)(2,1)S(1)} collective-permute-done((bf16[128,1024]{1,0:T(8,128)(2,1)S(1)}, bf16[128,1024]{1,0:T(8,128)(2,1)S(1)}, u32[]{:S(2)}, u32[]{:S(2)}) %collective-permute-start.5) | collective-permute-done | bytes 262176 | tf_op jit(solution)/shard_map/ppermute | solution.py:401
  32.9 0.7 collective-permute-start.8
  33.6 3.2 %collective-permute-start.9 = (bf16[128,1024]{1,0:T(8,128)(2,1)S(1)}, bf16[128,1024]{1,0:T(8,128)(2,1)S(1)}, u32[]{:S(2)}, u32[]{:S(2)}) collective-permute-start(bf16[128,1024]{1,0:T(8,128)(2,1)S(1)} %get-tuple-element.65.after_ref), channel_id=1, source_target_pairs={{0,1},{2,3},{1,0},{3,2},{4,5},{6,7},{5,4},{7,6},{8,9},{10,11},{9,8... | collective-permute-start | bytes 786440 | tf_op jit(solution)/shard_map/ppermute | solution.py:401
  36.8 1.6 %collective-permute-done.11.arrived_too_ref.refs_10_ = bf16[128,1024]{1,0:T(8,128)(2,1)S(1)} collective-permute-done((bf16[128,1024]{1,0:T(8,128)(2,1)S(1)}, bf16[128,1024]{1,0:T(8,128)(2,1)S(1)}, u32[]{:S(2)}, u32[]{:S(2)}) %collective-permute-start.11) | collective-permute-done | bytes 262176 | tf_op jit(solution)/shard_map/ppermute | solution.py:401
  38.5 1.2 %collective-permute-start.14 = (bf16[128,1024]{1,0:T(8,128)(2,1)S(1)}, bf16[128,1024]{1,0:T(8,128)(2,1)S(1)}, u32[]{:S(2)}, u32[]{:S(2)}) collective-permute-start(bf16[128,1024]{1,0:T(8,128)(2,1)S(1)} %get-tuple-element.70.after_ref), channel_id=1, source_target_pairs={{0,1},{2,3},{1,0},{3,2},{4,5},{6,7},{5,4},{7,6},{8,9},{10,11},{9,8... | collective-permute-start | bytes 786440 | tf_op jit(solution)/shard_map/ppermute | solution.py:401
  40.4 2.1 %collective-permute-done.9.arrived_too_ref.refs_11_ = bf16[128,1024]{1,0:T(8,128)(2,1)S(1)} collective-permute-done((bf16[128,1024]{1,0:T(8,128)(2,1)S(1)}, bf16[128,1024]{1,0:T(8,128)(2,1)S(1)}, u32[]{:S(2)}, u32[]{:S(2)}) %collective-permute-start.9) | collective-permute-done | bytes 262176 | tf_op jit(solution)/shard_map/ppermute | solution.py:401
  42.7 1.5 %collective-permute-start.12 = (bf16[128,1024]{1,0:T(8,128)(2,1)S(1)}, bf16[128,1024]{1,0:T(8,128)(2,1)S(1)}, u32[]{:S(2)}, u32[]{:S(2)}) collective-permute-start(bf16[128,1024]{1,0:T(8,128)(2,1)S(1)} %get-tuple-element.71.after_ref), channel_id=1, source_target_pairs={{0,1},{2,3},{1,0},{3,2},{4,5},{6,7},{5,4},{7,6},{8,9},{10,11},{9,8... | collective-permute-start | bytes 786440 | tf_op jit(solution)/shard_map/ppermute | solution.py:401
  44.9 3.0 %collective-permute-done.14.one_ref = bf16[128,1024]{1,0:T(8,128)(2,1)S(1)} collective-permute-done((bf16[128,1024]{1,0:T(8,128)(2,1)S(1)}, bf16[128,1024]{1,0:T(8,128)(2,1)S(1)}, u32[]{:S(2)}, u32[]{:S(2)}) %collective-permute-start.14) | collective-permute-done | bytes 262176 | tf_op jit(solution)/shard_map/ppermute | solution.py:401
  48.0 1.6 %collective-permute-start.21 = (bf16[128,1024]{1,0:T(8,128)(2,1)S(1)}, bf16[128,1024]{1,0:T(8,128)(2,1)S(1)}, u32[]{:S(2)}, u32[]{:S(2)}) collective-permute-start(bf16[128,1024]{1,0:T(8,128)(2,1)S(1)} %summed_grad.2.after_ref.own_ref), channel_id=1, source_target_pairs={{0,8},{4,12},{8,0},{12,4},{1,9},{5,13},{9,1},{13,5},{2,10},{6,14},... | collective-permute-start | bytes 786440 | tf_op jit(solution)/shard_map/ppermute | solution.py:424
  49.6 6.3 %collective-permute-start.20 = (bf16[128,1024]{1,0:T(8,128)(2,1)S(1)}, bf16[128,1024]{1,0:T(8,128)(2,1)S(1)}, u32[]{:S(2)}, u32[]{:S(2)}) collective-permute-start(bf16[128,1024]{1,0:T(8,128)(2,1)S(1)} %summed_grad.2.after_ref.own_ref), channel_id=1, source_target_pairs={{0,4},{4,0},{8,12},{12,8},{1,5},{5,1},{9,13},{13,9},{2,6},{6,2},{1... | collective-permute-start | bytes 786440 | tf_op jit(solution)/shard_map/ppermute | solution.py:423
  56.3 3.5 %context_grad.1 = (bf16[512,1024]{1,0:T(8,128)(2,1)}, f32[8,128]{1,0:T(8,128)S(1)}) custom-call(s32[2]{0:T(128)S(1)} %pad_add_fusion.where_ref, bf16[512,1024]{1,0:T(8,128)(2,1)S(1)} %bitcast.12, bf16[128,1024]{1,0:T(8,128)(2,1)S(1)} %summed_grad.3.after_ref.own_ref, bf16[128,1024]{1,0:T(8,128)(2,1)S(1)} %copy-done.6, bf16[128,1024]{1,0:T(8,128)(2,1)S(1)} %copy-done.7, ...), custom_call_target="tpu_custom_call" | custom-call | bytes 1024 | tf_op jit(solution)/shard_map/context_grad/pallas_call | solution.py:262
  59.9 2.5 %collective-permute-start.22 = (bf16[64,1024]{1,0:T(8,128)(2,1)S(1)}, bf16[64,1024]{1,0:T(8,128)(2,1)S(1)}, u32[]{:S(2)}, u32[]{:S(2)}) collective-permute-start(bf16[64,1024]{1,0:T(8,128)(2,1)S(1)} %get-tuple-element.81), channel_id=1, source_target_pairs={{0,4},{4,0},{8,12},{12,8},{1,5},{5,1},{9,13},{13,9},{2,6},{6,2},{1... | collective-permute-start | bytes 393224 | tf_op jit(solution)/shard_map/ppermute | solution.py:426
  62.9 0.8 %taken_state.1 = (f32[384,1024]{1,0:T(8,128)S(1)}, f32[384,1024]{1,0:T(8,128)S(1)}) custom-call(s32[2]{0:T(128)S(1)} %pad_add_fusion.where_ref, s32[4]{0:T(128)S(1)} %copy-done.8, bf16[128,1024]{1,0:T(8,128)(2,1)S(1)} %get-tuple-element.71.after_ref, f32[256,1024]{1,0:T(8,128)S(1)} %bitcast.14, f32[256,1024]{1,0:T(8,128)S(1)} %bitcast.16, ...), custom_call_target="tpu_custom_call" | custom-call | bytes 1024 | tf_op jit(solution)/shard_map/taken_state/pallas_call | solution.py:311
  63.8 1.7 %adam.2 = (f32[256,1024]{1,0:T(8,128)}, f32[256,1024]{1,0:T(8,128)}, f32[256,1024]{1,0:T(8,128)}, f32[8,128]{1,0:T(8,128)S(1)}) custom-call(f32[8,1024]{1,0:T(8,128)S(1)} %get-tuple-element.76.choices_ref, f32[384,1024]{1,0:T(8,128)S(1)} %get-tuple-element.79.state_ref, bf16[128,1024]{1,0:T(8,128)(2,1)S(1)} %summed_grad.2.after_ref.own_ref, ...), custom_call_target="tpu_custom_call" | custom-call | bytes 1024 | tf_op jit(solution)/shard_map/adam/pallas_call | solution.py:358
  65.5 1.0 %collective-permute-start.24 = (bf16[128,1024]{1,0:T(8,128)(2,1)S(1)}, bf16[128,1024]{1,0:T(8,128)(2,1)S(1)}, u32[]{:S(2)}, u32[]{:S(2)}) collective-permute-start(bf16[128,1024]{1,0:T(8,128)(2,1)S(1)} %gate.3), channel_id=1, source_target_pairs={{0,4},{4,0},{8,12},{12,8},{1,5},{5,1},{9,13},{13,9},{2,6},{6,2},{1... | collective-permute-start | bytes 786440 | tf_op jit(solution)/shard_map/ppermute | solution.py:426
  66.4 1.2 %collective-permute-done.24.refs_0_ = bf16[128,1024]{1,0:T(8,128)(2,1)S(1)} collective-permute-done((bf16[128,1024]{1,0:T(8,128)(2,1)S(1)}, bf16[128,1024]{1,0:T(8,128)(2,1)S(1)}, u32[]{:S(2)}, u32[]{:S(2)}) %collective-permute-start.24) | collective-permute-done | bytes 262176 | tf_op jit(solution)/shard_map/ppermute | solution.py:426
  67.6 2.3 %adam.3 = (f32[256,1024]{1,0:T(8,128)}, f32[256,1024]{1,0:T(8,128)}, f32[256,1024]{1,0:T(8,128)}, f32[8,128]{1,0:T(8,128)}) custom-call(f32[8,1024]{1,0:T(8,128)S(1)} %get-tuple-element.76.choices_ref, f32[384,1024]{1,0:T(8,128)S(1)} %get-tuple-element.78.state_ref, ...), custom_call_target="tpu_custom_call", output_to_operand_aliasing={{0}: (7, {}), {1}: (8, {}), {2}: (9, {})} | custom-call | bytes 1024 | tf_op jit(solution)/shard_map/adam/pallas_call | solution.py:358
  (60 shorter events, 5.0 us)
Async XLA Ops:
  0.6 11.8 %copy-start = (bf16[1,512,1024]{2,1,0:T(8,128)(2,1)S(1)}, bf16[1,512,1024]{2,1,0:T(8,128)(2,1)}, u32[]{:S(2)}) copy-start(bf16[1,512,1024]{2,1,0:T(8,128)(2,1)} %param.10) | copy-start | bytes 3145732
  0.6 11.8 %copy-start.8 = (s32[4]{0:T(128)S(1)}, s32[4]{0:T(128)}, u32[]{:S(2)}) copy-start(s32[4]{0:T(128)} %donor_ref.1) | copy-start | bytes 52
  0.7 11.7 %copy-start.9 = (f32[4]{0:T(128)S(1)}, f32[4]{0:T(128)}, u32[]{:S(2)}) copy-start(f32[4]{0:T(128)} %refs_0_.1) | copy-start | bytes 52
  0.7 11.7 %copy-start.10 = (f32[4]{0:T(128)S(1)}, f32[4]{0:T(128)}, u32[]{:S(2)}) copy-start(f32[4]{0:T(128)} %refs_1_.1) | copy-start | bytes 52
  0.7 11.7 %copy-start.11 = (s32[4]{0:T(128)S(1)}, s32[4]{0:T(128)}, u32[]{:S(2)}) copy-start(s32[4]{0:T(128)} %refs_2_.1) | copy-start | bytes 52
  4.0 12.1 %collective-permute-start.16 = (bf16[768,1024]{1,0:T(8,128)(2,1)}, bf16[768,1024]{1,0:T(8,128)(2,1)S(1)}, u32[]{:S(2)}, u32[]{:S(2)}) collective-permute-start(bf16[768,1024]{1,0:T(8,128)(2,1)} %get-tuple-element.77.own_ref), channel_id=1, source_target_pairs={{0,4},{4,0},{8,12},{12,8},{1,5},{5,1},{9,13},{13,9},{2,6},{6,2},{1... | collective-permute-start | bytes 4718600 | tf_op jit(solution)/shard_map/ppermute | solution.py:404
  4.1 14.0 %collective-permute-start.2 = (bf16[128,1024]{1,0:T(8,128)(2,1)}, bf16[128,1024]{1,0:T(8,128)(2,1)S(1)}, u32[]{:S(2)}, u32[]{:S(2)}) collective-permute-start(bf16[128,1024]{1,0:T(8,128)(2,1)} %get-tuple-element.51.after_ref.refs_0_), channel_id=1, source_target_pairs={{1,2},{2,1},{5,6},{6,5},{9,10},{10,9},{13,14},{14,13},{17,18},{18,... | collective-permute-start | bytes 786440 | tf_op jit(solution)/shard_map/ppermute | solution.py:401
  4.8 13.3 %collective-permute-start.3 = (bf16[128,1024]{1,0:T(8,128)(2,1)}, bf16[128,1024]{1,0:T(8,128)(2,1)S(1)}, u32[]{:S(2)}, u32[]{:S(2)}) collective-permute-start(bf16[128,1024]{1,0:T(8,128)(2,1)} %get-tuple-element.51.after_ref.refs_0_), channel_id=1, source_target_pairs={{0,1},{2,3},{1,0},{3,2},{4,5},{6,7},{5,4},{7,6},{8,9},{10,11},{9,8... | collective-permute-start | bytes 786440 | tf_op jit(solution)/shard_map/ppermute | solution.py:401
  10.1 11.5 %collective-permute-start = (bf16[128,1024]{1,0:T(8,128)(2,1)}, bf16[128,1024]{1,0:T(8,128)(2,1)S(1)}, u32[]{:S(2)}, u32[]{:S(2)}) collective-permute-start(bf16[128,1024]{1,0:T(8,128)(2,1)} %get-tuple-element.48.refs_1_), channel_id=1, source_target_pairs={{1,2},{2,1},{5,6},{6,5},{9,10},{10,9},{13,14},{14,13},{17,18},{18,... | collective-permute-start | bytes 786440 | tf_op jit(solution)/shard_map/ppermute | solution.py:401
  10.8 11.7 %collective-permute-start.1 = (bf16[128,1024]{1,0:T(8,128)(2,1)}, bf16[128,1024]{1,0:T(8,128)(2,1)}, u32[]{:S(2)}, u32[]{:S(2)}) collective-permute-start(bf16[128,1024]{1,0:T(8,128)(2,1)} %get-tuple-element.48.refs_1_), channel_id=1, source_target_pairs={{0,1},{2,3},{1,0},{3,2},{4,5},{6,7},{5,4},{7,6},{8,9},{10,11},{9,8... | collective-permute-start | bytes 786440 | tf_op jit(solution)/shard_map/ppermute | solution.py:401
  16.9 45.6 %collective-permute-start.17 = (bf16[768,1024]{1,0:T(8,128)(2,1)S(1)}, bf16[768,1024]{1,0:T(8,128)(2,1)S(1)}, u32[]{:S(2)}, u32[]{:S(2)}) collective-permute-start(bf16[768,1024]{1,0:T(8,128)(2,1)S(1)} %pick.1), channel_id=1, source_target_pairs={{0,8},{4,12},{8,0},{12,4},{1,9},{5,13},{9,1},{13,5},{2,10},{6,14},... | collective-permute-start | bytes 4718600 | tf_op jit(solution)/shard_map/ppermute | solution.py:405
  18.3 8.7 %collective-permute-start.6 = (bf16[128,1024]{1,0:T(8,128)(2,1)S(1)}, bf16[128,1024]{1,0:T(8,128)(2,1)S(1)}, u32[]{:S(2)}, u32[]{:S(2)}) collective-permute-start(bf16[128,1024]{1,0:T(8,128)(2,1)S(1)} %get-tuple-element.59), channel_id=1, source_target_pairs={{1,2},{2,1},{5,6},{6,5},{9,10},{10,9},{13,14},{14,13},{17,18},{18,... | collective-permute-start | bytes 786440 | tf_op jit(solution)/shard_map/ppermute | solution.py:401
  19.0 8.1 %collective-permute-start.7 = (bf16[128,1024]{1,0:T(8,128)(2,1)S(1)}, bf16[128,1024]{1,0:T(8,128)(2,1)S(1)}, u32[]{:S(2)}, u32[]{:S(2)}) collective-permute-start(bf16[128,1024]{1,0:T(8,128)(2,1)S(1)} %get-tuple-element.54.after_ref), channel_id=1, source_target_pairs={{0,1},{2,3},{1,0},{3,2},{4,5},{6,7},{5,4},{7,6},{8,9},{10,11},{9,8... | collective-permute-start | bytes 786440 | tf_op jit(solution)/shard_map/ppermute | solution.py:401
  23.6 7.0 %collective-permute-start.4 = (bf16[128,1024]{1,0:T(8,128)(2,1)S(1)}, bf16[128,1024]{1,0:T(8,128)(2,1)S(1)}, u32[]{:S(2)}, u32[]{:S(2)}) collective-permute-start(bf16[128,1024]{1,0:T(8,128)(2,1)S(1)} %get-tuple-element.55), channel_id=1, source_target_pairs={{1,2},{2,1},{5,6},{6,5},{9,10},{10,9},{13,14},{14,13},{17,18},{18,... | collective-permute-start | bytes 786440 | tf_op jit(solution)/shard_map/ppermute | solution.py:401
  24.3 8.4 %collective-permute-start.5 = (bf16[128,1024]{1,0:T(8,128)(2,1)S(1)}, bf16[128,1024]{1,0:T(8,128)(2,1)S(1)}, u32[]{:S(2)}, u32[]{:S(2)}) collective-permute-start(bf16[128,1024]{1,0:T(8,128)(2,1)S(1)} %get-tuple-element.57.after_ref), channel_id=1, source_target_pairs={{0,1},{2,3},{1,0},{3,2},{4,5},{6,7},{5,4},{7,6},{8,9},{10,11},{9,8... | collective-permute-start | bytes 786440 | tf_op jit(solution)/shard_map/ppermute | solution.py:401
  27.3 9.5 %collective-permute-start.10 = (bf16[128,1024]{1,0:T(8,128)(2,1)S(1)}, bf16[128,1024]{1,0:T(8,128)(2,1)S(1)}, u32[]{:S(2)}, u32[]{:S(2)}) collective-permute-start(bf16[128,1024]{1,0:T(8,128)(2,1)S(1)} %get-tuple-element.67), channel_id=1, source_target_pairs={{1,2},{2,1},{5,6},{6,5},{9,10},{10,9},{13,14},{14,13},{17,18},{18,... | collective-permute-start | bytes 786440 | tf_op jit(solution)/shard_map/ppermute | solution.py:401
  28.0 10.4 %collective-permute-start.11 = (bf16[128,1024]{1,0:T(8,128)(2,1)S(1)}, bf16[128,1024]{1,0:T(8,128)(2,1)S(1)}, u32[]{:S(2)}, u32[]{:S(2)}) collective-permute-start(bf16[128,1024]{1,0:T(8,128)(2,1)S(1)} %get-tuple-element.62.after_ref), channel_id=1, source_target_pairs={{0,1},{2,3},{1,0},{3,2},{4,5},{6,7},{5,4},{7,6},{8,9},{10,11},{9,8... | collective-permute-start | bytes 786440 | tf_op jit(solution)/shard_map/ppermute | solution.py:401
  32.9 7.5 %collective-permute-start.8 = (bf16[128,1024]{1,0:T(8,128)(2,1)S(1)}, bf16[128,1024]{1,0:T(8,128)(2,1)S(1)}, u32[]{:S(2)}, u32[]{:S(2)}) collective-permute-start(bf16[128,1024]{1,0:T(8,128)(2,1)S(1)} %get-tuple-element.63), channel_id=1, source_target_pairs={{1,2},{2,1},{5,6},{6,5},{9,10},{10,9},{13,14},{14,13},{17,18},{18,... | collective-permute-start | bytes 786440 | tf_op jit(solution)/shard_map/ppermute | solution.py:401
  33.6 8.9 %collective-permute-start.9 = (bf16[128,1024]{1,0:T(8,128)(2,1)S(1)}, bf16[128,1024]{1,0:T(8,128)(2,1)S(1)}, u32[]{:S(2)}, u32[]{:S(2)}) collective-permute-start(bf16[128,1024]{1,0:T(8,128)(2,1)S(1)} %get-tuple-element.65.after_ref), channel_id=1, source_target_pairs={{0,1},{2,3},{1,0},{3,2},{4,5},{6,7},{5,4},{7,6},{8,9},{10,11},{9,8... | collective-permute-start | bytes 786440 | tf_op jit(solution)/shard_map/ppermute | solution.py:401
  38.5 9.3 %collective-permute-start.14 = (bf16[128,1024]{1,0:T(8,128)(2,1)S(1)}, bf16[128,1024]{1,0:T(8,128)(2,1)S(1)}, u32[]{:S(2)}, u32[]{:S(2)}) collective-permute-start(bf16[128,1024]{1,0:T(8,128)(2,1)S(1)} %get-tuple-element.70.after_ref), channel_id=1, source_target_pairs={{0,1},{2,3},{1,0},{3,2},{4,5},{6,7},{5,4},{7,6},{8,9},{10,11},{9,8... | collective-permute-start | bytes 786440 | tf_op jit(solution)/shard_map/ppermute | solution.py:401
  39.8 8.1 %collective-permute-start.15 = (bf16[128,1024]{1,0:T(8,128)(2,1)S(1)}, bf16[128,1024]{1,0:T(8,128)(2,1)S(1)}, u32[]{:S(2)}, u32[]{:S(2)}) collective-permute-start(bf16[128,1024]{1,0:T(8,128)(2,1)S(1)} %get-tuple-element.74), channel_id=1, source_target_pairs={{1,2},{2,1},{5,6},{6,5},{9,10},{10,9},{13,14},{14,13},{17,18},{18,... | collective-permute-start | bytes 786440 | tf_op jit(solution)/shard_map/ppermute | solution.py:401
  42.7 13.1 %collective-permute-start.12 = (bf16[128,1024]{1,0:T(8,128)(2,1)S(1)}, bf16[128,1024]{1,0:T(8,128)(2,1)S(1)}, u32[]{:S(2)}, u32[]{:S(2)}) collective-permute-start(bf16[128,1024]{1,0:T(8,128)(2,1)S(1)} %get-tuple-element.71.after_ref), channel_id=1, source_target_pairs={{0,1},{2,3},{1,0},{3,2},{4,5},{6,7},{5,4},{7,6},{8,9},{10,11},{9,8... | collective-permute-start | bytes 786440 | tf_op jit(solution)/shard_map/ppermute | solution.py:401
  44.2 11.6 %collective-permute-start.13 = (bf16[128,1024]{1,0:T(8,128)(2,1)S(1)}, bf16[128,1024]{1,0:T(8,128)(2,1)S(1)}, u32[]{:S(2)}, u32[]{:S(2)}) collective-permute-start(bf16[128,1024]{1,0:T(8,128)(2,1)S(1)} %get-tuple-element.72), channel_id=1, source_target_pairs={{1,2},{2,1},{5,6},{6,5},{9,10},{10,9},{13,14},{14,13},{17,18},{18,... | collective-permute-start | bytes 786440 | tf_op jit(solution)/shard_map/ppermute | solution.py:401
  47.9 8.5 %copy-start.7 = (bf16[128,1024]{1,0:T(8,128)(2,1)S(1)}, bf16[128,1024]{1,0:T(8,128)(2,1)}, u32[]{:S(2)}) copy-start(bf16[128,1024]{1,0:T(8,128)(2,1)} %get-tuple-element.48.refs_1_) | copy-start | bytes 786436
  48.0 11.8 %collective-permute-start.21 = (bf16[128,1024]{1,0:T(8,128)(2,1)S(1)}, bf16[128,1024]{1,0:T(8,128)(2,1)S(1)}, u32[]{:S(2)}, u32[]{:S(2)}) collective-permute-start(bf16[128,1024]{1,0:T(8,128)(2,1)S(1)} %summed_grad.2.after_ref.own_ref), channel_id=1, source_target_pairs={{0,8},{4,12},{8,0},{12,4},{1,9},{5,13},{9,1},{13,5},{2,10},{6,14},... | collective-permute-start | bytes 786440 | tf_op jit(solution)/shard_map/ppermute | solution.py:424
  49.6 14.2 %collective-permute-start.20 = (bf16[128,1024]{1,0:T(8,128)(2,1)S(1)}, bf16[128,1024]{1,0:T(8,128)(2,1)S(1)}, u32[]{:S(2)}, u32[]{:S(2)}) collective-permute-start(bf16[128,1024]{1,0:T(8,128)(2,1)S(1)} %summed_grad.2.after_ref.own_ref), channel_id=1, source_target_pairs={{0,4},{4,0},{8,12},{12,8},{1,5},{5,1},{9,13},{13,9},{2,6},{6,2},{1... | collective-permute-start | bytes 786440 | tf_op jit(solution)/shard_map/ppermute | solution.py:423
  55.9 6.9 %copy-start.1 = (f32[1,256,1024]{2,1,0:T(8,128)S(1)}, f32[1,256,1024]{2,1,0:T(8,128)}, u32[]{:S(2)}) copy-start(f32[1,256,1024]{2,1,0:T(8,128)} %param.11) | copy-start | bytes 3145732
  56.0 9.5 %collective-permute-start.19 = (bf16[128,1024]{1,0:T(8,128)(2,1)S(1)}, bf16[128,1024]{1,0:T(8,128)(2,1)S(1)}, u32[]{:S(2)}, u32[]{:S(2)}) collective-permute-start(bf16[128,1024]{1,0:T(8,128)(2,1)S(1)} %summed_grad.3.after_ref.own_ref), channel_id=1, source_target_pairs={{0,8},{4,12},{8,0},{12,4},{1,9},{5,13},{9,1},{13,5},{2,10},{6,14},... | collective-permute-start | bytes 786440 | tf_op jit(solution)/shard_map/ppermute | solution.py:424
  59.9 3.9 %collective-permute-start.22 = (bf16[64,1024]{1,0:T(8,128)(2,1)S(1)}, bf16[64,1024]{1,0:T(8,128)(2,1)S(1)}, u32[]{:S(2)}, u32[]{:S(2)}) collective-permute-start(bf16[64,1024]{1,0:T(8,128)(2,1)S(1)} %get-tuple-element.81), channel_id=1, source_target_pairs={{0,4},{4,0},{8,12},{12,8},{1,5},{5,1},{9,13},{13,9},{2,6},{6,2},{1... | collective-permute-start | bytes 393224 | tf_op jit(solution)/shard_map/ppermute | solution.py:426
  62.4 1.4 %collective-permute-start.23 = (bf16[64,1024]{1,0:T(8,128)(2,1)S(1)}, bf16[64,1024]{1,0:T(8,128)(2,1)S(1)}, u32[]{:S(2)}, u32[]{:S(2)}) collective-permute-start(bf16[64,1024]{1,0:T(8,128)(2,1)S(1)} %get-tuple-element.82), channel_id=1, source_target_pairs={{0,4},{4,0},{8,12},{12,8},{1,5},{5,1},{9,13},{13,9},{2,6},{6,2},{1... | collective-permute-start | bytes 393224 | tf_op jit(solution)/shard_map/ppermute | solution.py:426
  62.5 4.0 %collective-permute-start.18 = (bf16[128,1024]{1,0:T(8,128)(2,1)S(1)}, bf16[128,1024]{1,0:T(8,128)(2,1)S(1)}, u32[]{:S(2)}, u32[]{:S(2)}) collective-permute-start(bf16[128,1024]{1,0:T(8,128)(2,1)S(1)} %summed_grad.3.after_ref.own_ref), channel_id=1, source_target_pairs={{0,4},{4,0},{8,12},{12,8},{1,5},{5,1},{9,13},{13,9},{2,6},{6,2},{1... | collective-permute-start | bytes 786440 | tf_op jit(solution)/shard_map/ppermute | solution.py:423
  65.5 2.1 %collective-permute-start.24 = (bf16[128,1024]{1,0:T(8,128)(2,1)S(1)}, bf16[128,1024]{1,0:T(8,128)(2,1)S(1)}, u32[]{:S(2)}, u32[]{:S(2)}) collective-permute-start(bf16[128,1024]{1,0:T(8,128)(2,1)S(1)} %gate.3), channel_id=1, source_target_pairs={{0,4},{4,0},{8,12},{12,8},{1,5},{5,1},{9,13},{13,9},{2,6},{6,2},{1... | collective-permute-start | bytes 786440 | tf_op jit(solution)/shard_map/ppermute | solution.py:426
  (5 other events, 21.0 us)

commit v14 on v13

--- a/solution.py
+++ b/solution.py
@@ -318,8 +318,9 @@
 
 def adam_kernel(start, size, hops, filled, choices_ref, state_ref, own_ref, mate_ref, across_ref, after_ref, *refs):
     far_refs, refs = refs[:hops], refs[hops + (3 if filled else 0):]
-    outs, (token_ref, stepped, sems) = refs[:3], refs[3:]
-    token_ref[...] = jnp.zeros_like(token_ref)
+    outs, tokens, (stepped, sems) = refs[:3], refs[3:-2], refs[-2:]
+    for token_ref in tokens:
+        token_ref[...] = jnp.zeros_like(token_ref)
     depth = own_ref.shape[1]
     writes = []
     piece, hop = 32, size // hops
@@ -353,12 +354,13 @@
         write.wait()
 
 
-def adam_update(start, size, rows, choices, state, grads, far, after, filled):
+def adam_update(start, size, rows, choices, state, grads, far, after, filled, tokens):
     depth = state.shape[1]
     return call(
         functools.partial(adam_kernel, start, size, len(far), bool(filled)), "adam",
-        [jax.ShapeDtypeStruct((rows, depth), jnp.float32)] * 3 + [jax.ShapeDtypeStruct((8, 128), jnp.float32)],
-        [VMEM] * 5 + [ANY] + [VMEM] * len(far) + [HBM] * len(filled), [HBM] * 3 + [VMEM],
+        [jax.ShapeDtypeStruct((rows, depth), jnp.float32)] * 3
+        + [jax.ShapeDtypeStruct((8, 128), jnp.float32)] * tokens,
+        [VMEM] * 5 + [ANY] + [VMEM] * len(far) + [HBM] * len(filled), [HBM] * 3 + [VMEM] * tokens,
         scratch=[pltpu.VMEM((3, size, depth), jnp.float32), pltpu.SemaphoreType.DMA((3 * (-(-size // 32)),))],
         aliases={6 + len(far) + k: k for k in range(len(filled))},
     )(choices, state, *grads, after, *far, *filled)
@@ -424,9 +426,11 @@
         across = lax.ppermute(grads[c], "member", swap_across)
         pieces = gate(across, computed, 2 if c == 0 and size % 64 == 0 else 1)
         far = [lax.ppermute(piece, "member", swap_mates) for piece in pieces]
-        *updated, computed = adam_update(
-            start, size, rows, choices, states[c], (grads[c], mate, across), far, computed, updated
+        last = c == len(steps_of) - 1
+        stepped = adam_update(
+            start, size, rows, choices, states[c], (grads[c], mate, across), far, computed, updated, int(not last)
         )
+        updated, computed = stepped[:3], stepped[-1]
     return (context_grad[None],) + tuple(array[None] for array in updated)
 
 

time: 70.5 us -> 70 us (level)
  no operation moved by 1% of the time
where the time goes in v14:
time: 70 us; the launch traced here: 69.3 us
  starting transfers between devices  39.6 us (57%)
  Pallas kernels  16.3 us (23%)
  waiting for transfers between devices  11 us (16%)
  local copies, waits for them, and re-layouts  1.37 us (2%)
  between operations  1 us (1%)
    ppermute x16, starting transfers between devices, on_device(): now[swap].append(lax.ppermute(blocks[swap], 'shard', swaps[swap]))  26.1 us
    ppermute x16, waiting for transfers between devices, on_device(): now[swap].append(lax.ppermute(blocks[swap], 'shard', swaps[swap]))  9.78 us
    ppermute x2, starting transfers between devices, on_device(): mate = lax.ppermute(grads[c], 'member', swap_mates)  6.69 us
    pallas_call x1, Pallas kernels, columns(): call(functools.partial(columns_kernel, n, scale, parts), 'context_grad',...  3.47 us
    ppermute x3, starting transfers between devices, on_device(): far = [lax.ppermute(piece, 'member', swap_mates) for piece in pieces]  3.45 us
    pallas_call x2, Pallas kernels, adam_update(): call(functools.partial(adam_kernel, start, size, len(far), bool(filled)),...  3.33 us
    pallas_call x1, Pallas kernels, halves(): call(functools.partial(halves_kernel, parts), 'halves', shapes, [HBM] * 3...  3.33 us
    pallas_call x1, Pallas kernels, partial_blocks(): call(functools.partial(partial_kernel, n, scale, parts, order), 'partial_...  2.38 us
  transfers between devices with their start and end apart: 25, of which 7 were waited for; matrix products, arithmetic and copies ran while one was open for 0% of the time, Pallas kernels for 16%

profile of v14, /device:TPU:1, one launch (start us, length us, event | category | flops | bytes accessed | tf_op | source)
XLA Modules:
  0.0 69.3 jit_solution(17568965412569305618)
XLA Ops:
  0.7 3.3 %halves.1 = (bf16[768,1024]{1,0:T(8,128)(2,1)}, bf16[128,1024]{1,0:T(8,128)(2,1)}, bf16[128,1024]{1,0:T(8,128)(2,1)}) custom-call(f32[256,1024]{1,0:T(8,128)} %bitcast.13, f32[256,1024]{1,0:T(8,128)} %bitcast.15, f32[256,1024]{1,0:T(8,128)} %bitcast.17), custom_call_target="tpu_custom_call" | custom-call | bytes 1024 | tf_op jit(solution)/shard_map/halves/pallas_call | solution.py:103
  4.8 5.3 %collective-permute-start.3 = (bf16[128,1024]{1,0:T(8,128)(2,1)}, bf16[128,1024]{1,0:T(8,128)(2,1)S(1)}, u32[]{:S(2)}, u32[]{:S(2)}) collective-permute-start(bf16[128,1024]{1,0:T(8,128)(2,1)} %get-tuple-element.51.after_ref.refs_0_), channel_id=1, source_target_pairs={{0,1},{2,3},{1,0},{3,2},{4,5},{6,7},{5,4},{7,6},{8,9},{10,11},{9,8... | collective-permute-start | bytes 786440 | tf_op jit(solution)/shard_map/ppermute | solution.py:403
  10.8 1.5 %collective-permute-start.1 = (bf16[128,1024]{1,0:T(8,128)(2,1)}, bf16[128,1024]{1,0:T(8,128)(2,1)}, u32[]{:S(2)}, u32[]{:S(2)}) collective-permute-start(bf16[128,1024]{1,0:T(8,128)(2,1)} %get-tuple-element.48.refs_1_), channel_id=1, source_target_pairs={{0,1},{2,3},{1,0},{3,2},{4,5},{6,7},{5,4},{7,6},{8,9},{10,11},{9,8... | collective-permute-start | bytes 786440 | tf_op jit(solution)/shard_map/ppermute | solution.py:403
  12.4 1.3 %copy-done.5 = bf16[1,512,1024]{2,1,0:T(8,128)(2,1)S(1)} copy-done((bf16[1,512,1024]{2,1,0:T(8,128)(2,1)S(1)}, bf16[1,512,1024]{2,1,0:T(8,128)(2,1)}, u32[]{:S(2)}) %copy-start.5) | copy-done | bytes 1048600
  13.7 2.4 %partial_blocks.1 = (f32[8,1024]{1,0:T(8,128)S(1)}, bf16[128,1024]{1,0:T(8,128)(2,1)S(1)}, bf16[128,1024]{1,0:T(8,128)(2,1)S(1)}, bf16[128,1024]{1,0:T(8,128)(2,...) custom-call(bf16[512,1024]{1,0:T(8,128)(2,1)S(1)} %bitcast.19, ...), custom_call_target="tpu_custom_call" | custom-call | bytes 1024 | tf_op jit(solution)/shard_map/partial_blocks/pallas_call | solution.py:167
  16.2 0.7 pick.1
  16.9 1.3 %collective-permute-start.17 = (bf16[768,1024]{1,0:T(8,128)(2,1)S(1)}, bf16[768,1024]{1,0:T(8,128)(2,1)S(1)}, u32[]{:S(2)}, u32[]{:S(2)}) collective-permute-start(bf16[768,1024]{1,0:T(8,128)(2,1)S(1)} %pick.1), channel_id=1, source_target_pairs={{0,8},{4,12},{8,0},{12,4},{1,9},{5,13},{9,1},{13,5},{2,10},{6,14},... | collective-permute-start | bytes 4718600 | tf_op jit(solution)/shard_map/ppermute | solution.py:407
  18.3 0.7 collective-permute-start.6
  19.0 2.6 %collective-permute-start.7 = (bf16[128,1024]{1,0:T(8,128)(2,1)S(1)}, bf16[128,1024]{1,0:T(8,128)(2,1)S(1)}, u32[]{:S(2)}, u32[]{:S(2)}) collective-permute-start(bf16[128,1024]{1,0:T(8,128)(2,1)S(1)} %get-tuple-element.54.after_ref), channel_id=1, source_target_pairs={{0,1},{2,3},{1,0},{3,2},{4,5},{6,7},{5,4},{7,6},{8,9},{10,11},{9,8... | collective-permute-start | bytes 786440 | tf_op jit(solution)/shard_map/ppermute | solution.py:403
  21.6 0.9 %collective-permute-done.1.arrived_too_ref.refs_3_ = bf16[128,1024]{1,0:T(8,128)(2,1)} collective-permute-done((bf16[128,1024]{1,0:T(8,128)(2,1)}, bf16[128,1024]{1,0:T(8,128)(2,1)}, u32[]{:S(2)}, u32[]{:S(2)}) %collective-permute-start.1) | collective-permute-done | bytes 262176 | tf_op jit(solution)/shard_map/ppermute | solution.py:403
  22.5 1.1 %to_send.7 = (bf16[128,1024]{1,0:T(8,128)(2,1)S(1)}, bf16[128,1024]{1,0:T(8,128)(2,1)S(1)}) custom-call(bf16[128,1024]{1,0:T(8,128)(2,1)S(1)} %collective-permute-done.arrived_ref.refs_5_, bf16[128,1024]{1,0:T(8,128)(2,1)S(1)} %get-tuple-element.49.term_ref, bf16[128,1024]{1,0:T(8,128)(2,1)} %collective-permute-done.1.arrived_too_ref.refs_3_, ...), custom_call_target="tpu_custom_call" | custom-call | flops 1342177280 | bytes 1024 | tf_op jit(solution)/shard_map/to_send/pallas_call | solution.py:194
  23.6 0.7 collective-permute-start.4
  24.3 2.7 %collective-permute-start.5 = (bf16[128,1024]{1,0:T(8,128)(2,1)S(1)}, bf16[128,1024]{1,0:T(8,128)(2,1)S(1)}, u32[]{:S(2)}, u32[]{:S(2)}) collective-permute-start(bf16[128,1024]{1,0:T(8,128)(2,1)S(1)} %get-tuple-element.57.after_ref), channel_id=1, source_target_pairs={{0,1},{2,3},{1,0},{3,2},{4,5},{6,7},{5,4},{7,6},{8,9},{10,11},{9,8... | collective-permute-start | bytes 786440 | tf_op jit(solution)/shard_map/ppermute | solution.py:403
  27.3 0.7 collective-permute-start.10
  28.0 2.7 %collective-permute-start.11 = (bf16[128,1024]{1,0:T(8,128)(2,1)S(1)}, bf16[128,1024]{1,0:T(8,128)(2,1)S(1)}, u32[]{:S(2)}, u32[]{:S(2)}) collective-permute-start(bf16[128,1024]{1,0:T(8,128)(2,1)S(1)} %get-tuple-element.62.after_ref), channel_id=1, source_target_pairs={{0,1},{2,3},{1,0},{3,2},{4,5},{6,7},{5,4},{7,6},{8,9},{10,11},{9,8... | collective-permute-start | bytes 786440 | tf_op jit(solution)/shard_map/ppermute | solution.py:403
  30.6 2.1 %collective-permute-done.5.arrived_too_ref.refs_7_ = bf16[128,1024]{1,0:T(8,128)(2,1)S(1)} collective-permute-done((bf16[128,1024]{1,0:T(8,128)(2,1)S(1)}, bf16[128,1024]{1,0:T(8,128)(2,1)S(1)}, u32[]{:S(2)}, u32[]{:S(2)}) %collective-permute-start.5) | collective-permute-done | bytes 262176 | tf_op jit(solution)/shard_map/ppermute | solution.py:403
  32.9 0.7 collective-permute-start.8
  33.6 3.2 %collective-permute-start.9 = (bf16[128,1024]{1,0:T(8,128)(2,1)S(1)}, bf16[128,1024]{1,0:T(8,128)(2,1)S(1)}, u32[]{:S(2)}, u32[]{:S(2)}) collective-permute-start(bf16[128,1024]{1,0:T(8,128)(2,1)S(1)} %get-tuple-element.65.after_ref), channel_id=1, source_target_pairs={{0,1},{2,3},{1,0},{3,2},{4,5},{6,7},{5,4},{7,6},{8,9},{10,11},{9,8... | collective-permute-start | bytes 786440 | tf_op jit(solution)/shard_map/ppermute | solution.py:403
  36.8 1.6 %collective-permute-done.11.arrived_too_ref.refs_10_ = bf16[128,1024]{1,0:T(8,128)(2,1)S(1)} collective-permute-done((bf16[128,1024]{1,0:T(8,128)(2,1)S(1)}, bf16[128,1024]{1,0:T(8,128)(2,1)S(1)}, u32[]{:S(2)}, u32[]{:S(2)}) %collective-permute-start.11) | collective-permute-done | bytes 262176 | tf_op jit(solution)/shard_map/ppermute | solution.py:403
  38.5 1.2 %collective-permute-start.14 = (bf16[128,1024]{1,0:T(8,128)(2,1)S(1)}, bf16[128,1024]{1,0:T(8,128)(2,1)S(1)}, u32[]{:S(2)}, u32[]{:S(2)}) collective-permute-start(bf16[128,1024]{1,0:T(8,128)(2,1)S(1)} %get-tuple-element.70.after_ref), channel_id=1, source_target_pairs={{0,1},{2,3},{1,0},{3,2},{4,5},{6,7},{5,4},{7,6},{8,9},{10,11},{9,8... | collective-permute-start | bytes 786440 | tf_op jit(solution)/shard_map/ppermute | solution.py:403
  40.4 2.1 %collective-permute-done.9.arrived_too_ref.refs_11_ = bf16[128,1024]{1,0:T(8,128)(2,1)S(1)} collective-permute-done((bf16[128,1024]{1,0:T(8,128)(2,1)S(1)}, bf16[128,1024]{1,0:T(8,128)(2,1)S(1)}, u32[]{:S(2)}, u32[]{:S(2)}) %collective-permute-start.9) | collective-permute-done | bytes 262176 | tf_op jit(solution)/shard_map/ppermute | solution.py:403
  42.7 1.5 %collective-permute-start.12 = (bf16[128,1024]{1,0:T(8,128)(2,1)S(1)}, bf16[128,1024]{1,0:T(8,128)(2,1)S(1)}, u32[]{:S(2)}, u32[]{:S(2)}) collective-permute-start(bf16[128,1024]{1,0:T(8,128)(2,1)S(1)} %get-tuple-element.71.after_ref), channel_id=1, source_target_pairs={{0,1},{2,3},{1,0},{3,2},{4,5},{6,7},{5,4},{7,6},{8,9},{10,11},{9,8... | collective-permute-start | bytes 786440 | tf_op jit(solution)/shard_map/ppermute | solution.py:403
  44.9 3.0 %collective-permute-done.14.one_ref = bf16[128,1024]{1,0:T(8,128)(2,1)S(1)} collective-permute-done((bf16[128,1024]{1,0:T(8,128)(2,1)S(1)}, bf16[128,1024]{1,0:T(8,128)(2,1)S(1)}, u32[]{:S(2)}, u32[]{:S(2)}) %collective-permute-start.14) | collective-permute-done | bytes 262176 | tf_op jit(solution)/shard_map/ppermute | solution.py:403
  48.0 1.6 %collective-permute-start.21 = (bf16[128,1024]{1,0:T(8,128)(2,1)S(1)}, bf16[128,1024]{1,0:T(8,128)(2,1)S(1)}, u32[]{:S(2)}, u32[]{:S(2)}) collective-permute-start(bf16[128,1024]{1,0:T(8,128)(2,1)S(1)} %summed_grad.2.after_ref.own_ref), channel_id=1, source_target_pairs={{0,8},{4,12},{8,0},{12,4},{1,9},{5,13},{9,1},{13,5},{2,10},{6,14},... | collective-permute-start | bytes 786440 | tf_op jit(solution)/shard_map/ppermute | solution.py:426
  49.6 6.3 %collective-permute-start.20 = (bf16[128,1024]{1,0:T(8,128)(2,1)S(1)}, bf16[128,1024]{1,0:T(8,128)(2,1)S(1)}, u32[]{:S(2)}, u32[]{:S(2)}) collective-permute-start(bf16[128,1024]{1,0:T(8,128)(2,1)S(1)} %summed_grad.2.after_ref.own_ref), channel_id=1, source_target_pairs={{0,4},{4,0},{8,12},{12,8},{1,5},{5,1},{9,13},{13,9},{2,6},{6,2},{1... | collective-permute-start | bytes 786440 | tf_op jit(solution)/shard_map/ppermute | solution.py:425
  56.3 3.5 %context_grad.1 = (bf16[512,1024]{1,0:T(8,128)(2,1)}, f32[8,128]{1,0:T(8,128)S(1)}) custom-call(s32[2]{0:T(128)S(1)} %pad_add_fusion.where_ref, bf16[512,1024]{1,0:T(8,128)(2,1)S(1)} %bitcast.12, bf16[128,1024]{1,0:T(8,128)(2,1)S(1)} %summed_grad.3.after_ref.own_ref, bf16[128,1024]{1,0:T(8,128)(2,1)S(1)} %copy-done.6, bf16[128,1024]{1,0:T(8,128)(2,1)S(1)} %copy-done.7, ...), custom_call_target="tpu_custom_call" | custom-call | bytes 1024 | tf_op jit(solution)/shard_map/context_grad/pallas_call | solution.py:262
  59.9 2.5 %collective-permute-start.22 = (bf16[64,1024]{1,0:T(8,128)(2,1)S(1)}, bf16[64,1024]{1,0:T(8,128)(2,1)S(1)}, u32[]{:S(2)}, u32[]{:S(2)}) collective-permute-start(bf16[64,1024]{1,0:T(8,128)(2,1)S(1)} %get-tuple-element.81), channel_id=1, source_target_pairs={{0,4},{4,0},{8,12},{12,8},{1,5},{5,1},{9,13},{13,9},{2,6},{6,2},{1... | collective-permute-start | bytes 393224 | tf_op jit(solution)/shard_map/ppermute | solution.py:428
  62.9 0.9 %taken_state.1 = (f32[384,1024]{1,0:T(8,128)S(1)}, f32[384,1024]{1,0:T(8,128)S(1)}) custom-call(s32[2]{0:T(128)S(1)} %pad_add_fusion.where_ref, s32[4]{0:T(128)S(1)} %copy-done.8, bf16[128,1024]{1,0:T(8,128)(2,1)S(1)} %get-tuple-element.71.after_ref, f32[256,1024]{1,0:T(8,128)S(1)} %bitcast.14, f32[256,1024]{1,0:T(8,128)S(1)} %bitcast.16, ...), custom_call_target="tpu_custom_call" | custom-call | bytes 1024 | tf_op jit(solution)/shard_map/taken_state/pallas_call | solution.py:311
  63.9 1.7 %adam.2 = (f32[256,1024]{1,0:T(8,128)}, f32[256,1024]{1,0:T(8,128)}, f32[256,1024]{1,0:T(8,128)}, f32[8,128]{1,0:T(8,128)S(1)}) custom-call(f32[8,1024]{1,0:T(8,128)S(1)} %get-tuple-element.76.choices_ref, f32[384,1024]{1,0:T(8,128)S(1)} %get-tuple-element.79.state_ref, bf16[128,1024]{1,0:T(8,128)(2,1)S(1)} %summed_grad.2.after_ref.own_ref, ...), custom_call_target="tpu_custom_call" | custom-call | bytes 1024 | tf_op jit(solution)/shard_map/adam/pallas_call | solution.py:359
  65.6 0.9 %collective-permute-start.24 = (bf16[128,1024]{1,0:T(8,128)(2,1)S(1)}, bf16[128,1024]{1,0:T(8,128)(2,1)S(1)}, u32[]{:S(2)}, u32[]{:S(2)}) collective-permute-start(bf16[128,1024]{1,0:T(8,128)(2,1)S(1)} %gate.3), channel_id=1, source_target_pairs={{0,4},{4,0},{8,12},{12,8},{1,5},{5,1},{9,13},{13,9},{2,6},{6,2},{1... | collective-permute-start | bytes 786440 | tf_op jit(solution)/shard_map/ppermute | solution.py:428
  66.4 1.2 %collective-permute-done.24.refs_0_ = bf16[128,1024]{1,0:T(8,128)(2,1)S(1)} collective-permute-done((bf16[128,1024]{1,0:T(8,128)(2,1)S(1)}, bf16[128,1024]{1,0:T(8,128)(2,1)S(1)}, u32[]{:S(2)}, u32[]{:S(2)}) %collective-permute-start.24) | collective-permute-done | bytes 262176 | tf_op jit(solution)/shard_map/ppermute | solution.py:428
  67.6 1.7 %adam.3 = (f32[256,1024]{1,0:T(8,128)}, f32[256,1024]{1,0:T(8,128)}, f32[256,1024]{1,0:T(8,128)}) custom-call(f32[8,1024]{1,0:T(8,128)S(1)} %get-tuple-element.76.choices_ref, f32[384,1024]{1,0:T(8,128)S(1)} %get-tuple-element.78.state_ref, ...), custom_call_target="tpu_custom_call", output_to_operand_aliasing={{0}: (7, {}), {1}: (8, {}), {2}: (9, {})} | custom-call | bytes 1024 | tf_op jit(solution)/shard_map/adam/pallas_call | solution.py:359
  (60 shorter events, 5.0 us)
Async XLA Ops:
  0.6 11.8 %copy-start = (bf16[1,512,1024]{2,1,0:T(8,128)(2,1)S(1)}, bf16[1,512,1024]{2,1,0:T(8,128)(2,1)}, u32[]{:S(2)}) copy-start(bf16[1,512,1024]{2,1,0:T(8,128)(2,1)} %param.10) | copy-start | bytes 3145732
  0.6 11.8 %copy-start.8 = (s32[4]{0:T(128)S(1)}, s32[4]{0:T(128)}, u32[]{:S(2)}) copy-start(s32[4]{0:T(128)} %donor_ref.1) | copy-start | bytes 52
  0.7 11.7 %copy-start.9 = (f32[4]{0:T(128)S(1)}, f32[4]{0:T(128)}, u32[]{:S(2)}) copy-start(f32[4]{0:T(128)} %refs_0_.1) | copy-start | bytes 52
  0.7 11.7 %copy-start.10 = (f32[4]{0:T(128)S(1)}, f32[4]{0:T(128)}, u32[]{:S(2)}) copy-start(f32[4]{0:T(128)} %refs_1_.1) | copy-start | bytes 52
  0.7 11.7 %copy-start.11 = (s32[4]{0:T(128)S(1)}, s32[4]{0:T(128)}, u32[]{:S(2)}) copy-start(s32[4]{0:T(128)} %refs_2_.1) | copy-start | bytes 52
  4.0 12.1 %collective-permute-start.16 = (bf16[768,1024]{1,0:T(8,128)(2,1)}, bf16[768,1024]{1,0:T(8,128)(2,1)S(1)}, u32[]{:S(2)}, u32[]{:S(2)}) collective-permute-start(bf16[768,1024]{1,0:T(8,128)(2,1)} %get-tuple-element.77.own_ref), channel_id=1, source_target_pairs={{0,4},{4,0},{8,12},{12,8},{1,5},{5,1},{9,13},{13,9},{2,6},{6,2},{1... | collective-permute-start | bytes 4718600 | tf_op jit(solution)/shard_map/ppermute | solution.py:406
  4.1 14.0 %collective-permute-start.2 = (bf16[128,1024]{1,0:T(8,128)(2,1)}, bf16[128,1024]{1,0:T(8,128)(2,1)S(1)}, u32[]{:S(2)}, u32[]{:S(2)}) collective-permute-start(bf16[128,1024]{1,0:T(8,128)(2,1)} %get-tuple-element.51.after_ref.refs_0_), channel_id=1, source_target_pairs={{1,2},{2,1},{5,6},{6,5},{9,10},{10,9},{13,14},{14,13},{17,18},{18,... | collective-permute-start | bytes 786440 | tf_op jit(solution)/shard_map/ppermute | solution.py:403
  4.8 13.3 %collective-permute-start.3 = (bf16[128,1024]{1,0:T(8,128)(2,1)}, bf16[128,1024]{1,0:T(8,128)(2,1)S(1)}, u32[]{:S(2)}, u32[]{:S(2)}) collective-permute-start(bf16[128,1024]{1,0:T(8,128)(2,1)} %get-tuple-element.51.after_ref.refs_0_), channel_id=1, source_target_pairs={{0,1},{2,3},{1,0},{3,2},{4,5},{6,7},{5,4},{7,6},{8,9},{10,11},{9,8... | collective-permute-start | bytes 786440 | tf_op jit(solution)/shard_map/ppermute | solution.py:403
  10.1 11.5 %collective-permute-start = (bf16[128,1024]{1,0:T(8,128)(2,1)}, bf16[128,1024]{1,0:T(8,128)(2,1)S(1)}, u32[]{:S(2)}, u32[]{:S(2)}) collective-permute-start(bf16[128,1024]{1,0:T(8,128)(2,1)} %get-tuple-element.48.refs_1_), channel_id=1, source_target_pairs={{1,2},{2,1},{5,6},{6,5},{9,10},{10,9},{13,14},{14,13},{17,18},{18,... | collective-permute-start | bytes 786440 | tf_op jit(solution)/shard_map/ppermute | solution.py:403
  10.8 11.7 %collective-permute-start.1 = (bf16[128,1024]{1,0:T(8,128)(2,1)}, bf16[128,1024]{1,0:T(8,128)(2,1)}, u32[]{:S(2)}, u32[]{:S(2)}) collective-permute-start(bf16[128,1024]{1,0:T(8,128)(2,1)} %get-tuple-element.48.refs_1_), channel_id=1, source_target_pairs={{0,1},{2,3},{1,0},{3,2},{4,5},{6,7},{5,4},{7,6},{8,9},{10,11},{9,8... | collective-permute-start | bytes 786440 | tf_op jit(solution)/shard_map/ppermute | solution.py:403
  16.9 45.6 %collective-permute-start.17 = (bf16[768,1024]{1,0:T(8,128)(2,1)S(1)}, bf16[768,1024]{1,0:T(8,128)(2,1)S(1)}, u32[]{:S(2)}, u32[]{:S(2)}) collective-permute-start(bf16[768,1024]{1,0:T(8,128)(2,1)S(1)} %pick.1), channel_id=1, source_target_pairs={{0,8},{4,12},{8,0},{12,4},{1,9},{5,13},{9,1},{13,5},{2,10},{6,14},... | collective-permute-start | bytes 4718600 | tf_op jit(solution)/shard_map/ppermute | solution.py:407
  18.3 8.7 %collective-permute-start.6 = (bf16[128,1024]{1,0:T(8,128)(2,1)S(1)}, bf16[128,1024]{1,0:T(8,128)(2,1)S(1)}, u32[]{:S(2)}, u32[]{:S(2)}) collective-permute-start(bf16[128,1024]{1,0:T(8,128)(2,1)S(1)} %get-tuple-element.59), channel_id=1, source_target_pairs={{1,2},{2,1},{5,6},{6,5},{9,10},{10,9},{13,14},{14,13},{17,18},{18,... | collective-permute-start | bytes 786440 | tf_op jit(solution)/shard_map/ppermute | solution.py:403
  19.0 8.1 %collective-permute-start.7 = (bf16[128,1024]{1,0:T(8,128)(2,1)S(1)}, bf16[128,1024]{1,0:T(8,128)(2,1)S(1)}, u32[]{:S(2)}, u32[]{:S(2)}) collective-permute-start(bf16[128,1024]{1,0:T(8,128)(2,1)S(1)} %get-tuple-element.54.after_ref), channel_id=1, source_target_pairs={{0,1},{2,3},{1,0},{3,2},{4,5},{6,7},{5,4},{7,6},{8,9},{10,11},{9,8... | collective-permute-start | bytes 786440 | tf_op jit(solution)/shard_map/ppermute | solution.py:403
  23.6 7.0 %collective-permute-start.4 = (bf16[128,1024]{1,0:T(8,128)(2,1)S(1)}, bf16[128,1024]{1,0:T(8,128)(2,1)S(1)}, u32[]{:S(2)}, u32[]{:S(2)}) collective-permute-start(bf16[128,1024]{1,0:T(8,128)(2,1)S(1)} %get-tuple-element.55), channel_id=1, source_target_pairs={{1,2},{2,1},{5,6},{6,5},{9,10},{10,9},{13,14},{14,13},{17,18},{18,... | collective-permute-start | bytes 786440 | tf_op jit(solution)/shard_map/ppermute | solution.py:403
  24.3 8.4 %collective-permute-start.5 = (bf16[128,1024]{1,0:T(8,128)(2,1)S(1)}, bf16[128,1024]{1,0:T(8,128)(2,1)S(1)}, u32[]{:S(2)}, u32[]{:S(2)}) collective-permute-start(bf16[128,1024]{1,0:T(8,128)(2,1)S(1)} %get-tuple-element.57.after_ref), channel_id=1, source_target_pairs={{0,1},{2,3},{1,0},{3,2},{4,5},{6,7},{5,4},{7,6},{8,9},{10,11},{9,8... | collective-permute-start | bytes 786440 | tf_op jit(solution)/shard_map/ppermute | solution.py:403
  27.3 9.5 %collective-permute-start.10 = (bf16[128,1024]{1,0:T(8,128)(2,1)S(1)}, bf16[128,1024]{1,0:T(8,128)(2,1)S(1)}, u32[]{:S(2)}, u32[]{:S(2)}) collective-permute-start(bf16[128,1024]{1,0:T(8,128)(2,1)S(1)} %get-tuple-element.67), channel_id=1, source_target_pairs={{1,2},{2,1},{5,6},{6,5},{9,10},{10,9},{13,14},{14,13},{17,18},{18,... | collective-permute-start | bytes 786440 | tf_op jit(solution)/shard_map/ppermute | solution.py:403
  28.0 10.4 %collective-permute-start.11 = (bf16[128,1024]{1,0:T(8,128)(2,1)S(1)}, bf16[128,1024]{1,0:T(8,128)(2,1)S(1)}, u32[]{:S(2)}, u32[]{:S(2)}) collective-permute-start(bf16[128,1024]{1,0:T(8,128)(2,1)S(1)} %get-tuple-element.62.after_ref), channel_id=1, source_target_pairs={{0,1},{2,3},{1,0},{3,2},{4,5},{6,7},{5,4},{7,6},{8,9},{10,11},{9,8... | collective-permute-start | bytes 786440 | tf_op jit(solution)/shard_map/ppermute | solution.py:403
  32.9 7.5 %collective-permute-start.8 = (bf16[128,1024]{1,0:T(8,128)(2,1)S(1)}, bf16[128,1024]{1,0:T(8,128)(2,1)S(1)}, u32[]{:S(2)}, u32[]{:S(2)}) collective-permute-start(bf16[128,1024]{1,0:T(8,128)(2,1)S(1)} %get-tuple-element.63), channel_id=1, source_target_pairs={{1,2},{2,1},{5,6},{6,5},{9,10},{10,9},{13,14},{14,13},{17,18},{18,... | collective-permute-start | bytes 786440 | tf_op jit(solution)/shard_map/ppermute | solution.py:403
  33.6 8.9 %collective-permute-start.9 = (bf16[128,1024]{1,0:T(8,128)(2,1)S(1)}, bf16[128,1024]{1,0:T(8,128)(2,1)S(1)}, u32[]{:S(2)}, u32[]{:S(2)}) collective-permute-start(bf16[128,1024]{1,0:T(8,128)(2,1)S(1)} %get-tuple-element.65.after_ref), channel_id=1, source_target_pairs={{0,1},{2,3},{1,0},{3,2},{4,5},{6,7},{5,4},{7,6},{8,9},{10,11},{9,8... | collective-permute-start | bytes 786440 | tf_op jit(solution)/shard_map/ppermute | solution.py:403
  38.5 9.3 %collective-permute-start.14 = (bf16[128,1024]{1,0:T(8,128)(2,1)S(1)}, bf16[128,1024]{1,0:T(8,128)(2,1)S(1)}, u32[]{:S(2)}, u32[]{:S(2)}) collective-permute-start(bf16[128,1024]{1,0:T(8,128)(2,1)S(1)} %get-tuple-element.70.after_ref), channel_id=1, source_target_pairs={{0,1},{2,3},{1,0},{3,2},{4,5},{6,7},{5,4},{7,6},{8,9},{10,11},{9,8... | collective-permute-start | bytes 786440 | tf_op jit(solution)/shard_map/ppermute | solution.py:403
  39.8 8.1 %collective-permute-start.15 = (bf16[128,1024]{1,0:T(8,128)(2,1)S(1)}, bf16[128,1024]{1,0:T(8,128)(2,1)S(1)}, u32[]{:S(2)}, u32[]{:S(2)}) collective-permute-start(bf16[128,1024]{1,0:T(8,128)(2,1)S(1)} %get-tuple-element.74), channel_id=1, source_target_pairs={{1,2},{2,1},{5,6},{6,5},{9,10},{10,9},{13,14},{14,13},{17,18},{18,... | collective-permute-start | bytes 786440 | tf_op jit(solution)/shard_map/ppermute | solution.py:403
  42.7 13.1 %collective-permute-start.12 = (bf16[128,1024]{1,0:T(8,128)(2,1)S(1)}, bf16[128,1024]{1,0:T(8,128)(2,1)S(1)}, u32[]{:S(2)}, u32[]{:S(2)}) collective-permute-start(bf16[128,1024]{1,0:T(8,128)(2,1)S(1)} %get-tuple-element.71.after_ref), channel_id=1, source_target_pairs={{0,1},{2,3},{1,0},{3,2},{4,5},{6,7},{5,4},{7,6},{8,9},{10,11},{9,8... | collective-permute-start | bytes 786440 | tf_op jit(solution)/shard_map/ppermute | solution.py:403
  44.2 11.6 %collective-permute-start.13 = (bf16[128,1024]{1,0:T(8,128)(2,1)S(1)}, bf16[128,1024]{1,0:T(8,128)(2,1)S(1)}, u32[]{:S(2)}, u32[]{:S(2)}) collective-permute-start(bf16[128,1024]{1,0:T(8,128)(2,1)S(1)} %get-tuple-element.72), channel_id=1, source_target_pairs={{1,2},{2,1},{5,6},{6,5},{9,10},{10,9},{13,14},{14,13},{17,18},{18,... | collective-permute-start | bytes 786440 | tf_op jit(solution)/shard_map/ppermute | solution.py:403
  47.9 8.5 %copy-start.7 = (bf16[128,1024]{1,0:T(8,128)(2,1)S(1)}, bf16[128,1024]{1,0:T(8,128)(2,1)}, u32[]{:S(2)}) copy-start(bf16[128,1024]{1,0:T(8,128)(2,1)} %get-tuple-element.48.refs_1_) | copy-start | bytes 786436
  48.0 11.8 %collective-permute-start.21 = (bf16[128,1024]{1,0:T(8,128)(2,1)S(1)}, bf16[128,1024]{1,0:T(8,128)(2,1)S(1)}, u32[]{:S(2)}, u32[]{:S(2)}) collective-permute-start(bf16[128,1024]{1,0:T(8,128)(2,1)S(1)} %summed_grad.2.after_ref.own_ref), channel_id=1, source_target_pairs={{0,8},{4,12},{8,0},{12,4},{1,9},{5,13},{9,1},{13,5},{2,10},{6,14},... | collective-permute-start | bytes 786440 | tf_op jit(solution)/shard_map/ppermute | solution.py:426
  49.6 14.3 %collective-permute-start.20 = (bf16[128,1024]{1,0:T(8,128)(2,1)S(1)}, bf16[128,1024]{1,0:T(8,128)(2,1)S(1)}, u32[]{:S(2)}, u32[]{:S(2)}) collective-permute-start(bf16[128,1024]{1,0:T(8,128)(2,1)S(1)} %summed_grad.2.after_ref.own_ref), channel_id=1, source_target_pairs={{0,4},{4,0},{8,12},{12,8},{1,5},{5,1},{9,13},{13,9},{2,6},{6,2},{1... | collective-permute-start | bytes 786440 | tf_op jit(solution)/shard_map/ppermute | solution.py:425
  55.9 6.9 %copy-start.1 = (f32[1,256,1024]{2,1,0:T(8,128)S(1)}, f32[1,256,1024]{2,1,0:T(8,128)}, u32[]{:S(2)}) copy-start(f32[1,256,1024]{2,1,0:T(8,128)} %param.11) | copy-start | bytes 3145732
  56.0 9.6 %collective-permute-start.19 = (bf16[128,1024]{1,0:T(8,128)(2,1)S(1)}, bf16[128,1024]{1,0:T(8,128)(2,1)S(1)}, u32[]{:S(2)}, u32[]{:S(2)}) collective-permute-start(bf16[128,1024]{1,0:T(8,128)(2,1)S(1)} %summed_grad.3.after_ref.own_ref), channel_id=1, source_target_pairs={{0,8},{4,12},{8,0},{12,4},{1,9},{5,13},{9,1},{13,5},{2,10},{6,14},... | collective-permute-start | bytes 786440 | tf_op jit(solution)/shard_map/ppermute | solution.py:426
  59.9 4.0 %collective-permute-start.22 = (bf16[64,1024]{1,0:T(8,128)(2,1)S(1)}, bf16[64,1024]{1,0:T(8,128)(2,1)S(1)}, u32[]{:S(2)}, u32[]{:S(2)}) collective-permute-start(bf16[64,1024]{1,0:T(8,128)(2,1)S(1)} %get-tuple-element.81), channel_id=1, source_target_pairs={{0,4},{4,0},{8,12},{12,8},{1,5},{5,1},{9,13},{13,9},{2,6},{6,2},{1... | collective-permute-start | bytes 393224 | tf_op jit(solution)/shard_map/ppermute | solution.py:428
  62.4 1.5 %collective-permute-start.23 = (bf16[64,1024]{1,0:T(8,128)(2,1)S(1)}, bf16[64,1024]{1,0:T(8,128)(2,1)S(1)}, u32[]{:S(2)}, u32[]{:S(2)}) collective-permute-start(bf16[64,1024]{1,0:T(8,128)(2,1)S(1)} %get-tuple-element.82), channel_id=1, source_target_pairs={{0,4},{4,0},{8,12},{12,8},{1,5},{5,1},{9,13},{13,9},{2,6},{6,2},{1... | collective-permute-start | bytes 393224 | tf_op jit(solution)/shard_map/ppermute | solution.py:428
  62.5 4.0 %collective-permute-start.18 = (bf16[128,1024]{1,0:T(8,128)(2,1)S(1)}, bf16[128,1024]{1,0:T(8,128)(2,1)S(1)}, u32[]{:S(2)}, u32[]{:S(2)}) collective-permute-start(bf16[128,1024]{1,0:T(8,128)(2,1)S(1)} %summed_grad.3.after_ref.own_ref), channel_id=1, source_target_pairs={{0,4},{4,0},{8,12},{12,8},{1,5},{5,1},{9,13},{13,9},{2,6},{6,2},{1... | collective-permute-start | bytes 786440 | tf_op jit(solution)/shard_map/ppermute | solution.py:425
  65.6 2.0 %collective-permute-start.24 = (bf16[128,1024]{1,0:T(8,128)(2,1)S(1)}, bf16[128,1024]{1,0:T(8,128)(2,1)S(1)}, u32[]{:S(2)}, u32[]{:S(2)}) collective-permute-start(bf16[128,1024]{1,0:T(8,128)(2,1)S(1)} %gate.3), channel_id=1, source_target_pairs={{0,4},{4,0},{8,12},{12,8},{1,5},{5,1},{9,13},{13,9},{2,6},{6,2},{1... | collective-permute-start | bytes 786440 | tf_op jit(solution)/shard_map/ppermute | solution.py:428
  (5 other events, 21.0 us)
